TPU v7x, 32 devices: a whole 2x2x4 slice. The times are simulated.
32 devices in a mesh: runs: 2 (over x), mesh: 16 (over z, y, core).
Axes of the slice: x: 2, y: 2, z: 4, core: 2. Of those that a mesh axis runs over, the one named last changes fastest.
Arguments:
- velocity: float32 [6, 256, 2048], P('runs', None, 'mesh'), parts along dimension 0, may hold values from -4 to 4
- magnetic: float32 [6, 256, 2048], P('runs', None, 'mesh'), parts along dimension 0, may hold values from -4 to 4
- mass_blocks: float32 [6, 6, 2048], P(None, None, 'mesh'), may hold values from -1 to 12, as said below
- stiff_blocks: float32 [6, 6, 2048], P(None, None, 'mesh'), may hold values from -2 to 24, as said below
- twist_blocks: float32 [6, 6, 2048], P(None, None, 'mesh'), may hold values from -0.00024414062 to 0.0029296875, as said below
- diffusivity: float32 [4096], P(('runs', 'mesh')), parts along dimension 0, may hold values from 1 to 8, as said below
- connectivity: int32 [6, 2048], P(None, 'mesh'), may hold values from 0 to 191
- ghost_lists: int32 [2, 512], P(None, 'mesh'), may hold values from 0 to 127, as said below
Outputs:
- new_velocity: float32 [6, 256, 2048], P('runs', None, 'mesh'), parts along dimension 0
- new_magnetic: float32 [6, 256, 2048], P('runs', None, 'mesh'), parts along dimension 0
There are 2 independent parts, one for each index of `runs`. A program takes and returns all parts, laid end to end along the dimension named above; an argument that names none is the same for every part. Nothing has to cross between parts.
Inputs may be any that keep to these rules, and one draw needn't show every extreme that they name: `mass_blocks`: symmetric blocks; each diagonal entry exceeds the sum of magnitudes of the other entries of its row. An element that names ghost slots appears on both neighbouring devices with the same blocks, so the assembled operators are symmetric positive definite. `stiff_blocks`: as mass_blocks. `twist_blocks`: as mass_blocks. An element shared by two devices has the same diffusivity on both. `ghost_lists`: within each row of one device the 32 entries are distinct; row 0 names nodes of the device below, row 1 nodes of the device above.
All inputs are finite; a program needn't handle non-finite values.
Results may differ from a plain program's by a relative error of at most 0.0001.
Values sent between devices are 32-bit elements; how exact they have to be, the bound alone decides.
No kernel may reach another device: no remote copies, remote signals or barrier semaphores. Data moves between devices by JAX's collectives and lax.ppermute only.
A program may use at most 64 MiB of HBM per device.

v0:
```python
import math

import jax
import jax.numpy as jnp
from jax import lax
from jax.sharding import PartitionSpec as P

ITERS = 3


time_step = 0.1
viscosity = 2.0
tilt_factor = 0.5
axial_factor = 1.0
lorentz_factor = 0.005
epsilon = 1e-06
highest = lax.Precision.HIGHEST


def extended(block, sides, width):
    for axis, dim in sides:
        count = lax.axis_size(axis)
        forward = [(i, i + 1) for i in range(count - 1)]
        backward = [(target, source) for source, target in forward]
        low = lax.ppermute(
            lax.slice_in_dim(block, block.shape[dim] - width, None, axis=dim), axis, forward
        )
        high = lax.ppermute(lax.slice_in_dim(block, 0, width, axis=dim), axis, backward)
        block = jnp.concatenate([low, block, high], axis=dim)
    return block


def transform_tables(coef_count, plane_count):
    mode_index = jnp.arange(coef_count, dtype=jnp.int32) // 2
    parity = jnp.arange(coef_count, dtype=jnp.int32) % 2
    planes = jnp.arange(plane_count, dtype=jnp.int32)
    phase_turns = planes[:, None] * mode_index[None, :] % plane_count
    angles = 2.0 * math.pi / plane_count * phase_turns.astype(jnp.float32)
    inverse = jnp.where(parity[None, :] == 0, jnp.cos(angles), jnp.sin(angles))
    weight = jnp.where(mode_index == 0, 1.0, 2.0).astype(jnp.float32) / plane_count
    forward = jnp.transpose(inverse * weight[None, :])
    return (inverse, forward)


def cross_product(first_field, second_field):
    return jnp.stack(
        [
            first_field[1] * second_field[2] - first_field[2] * second_field[1],
            first_field[2] * second_field[0] - first_field[0] * second_field[2],
            first_field[0] * second_field[1] - first_field[1] * second_field[0],
        ]
    )


def forcing_terms(velocity, magnetic):
    inverse, forward = transform_tables(velocity.shape[1], 2 * velocity.shape[1])
    plane_count = inverse.shape[0]
    phys_velocity = jnp.einsum("jc,kcn->kjn", inverse, velocity, precision=highest)
    phys_magnetic = jnp.einsum("jc,kcn->kjn", inverse, magnetic, precision=highest)
    induction = cross_product(phys_velocity, phys_magnetic)
    angles = (
        2.0 * math.pi / plane_count * jnp.arange(plane_count, dtype=jnp.int32).astype(jnp.float32)
    )
    rotation = jnp.stack(
        [
            tilt_factor * jnp.cos(angles),
            -tilt_factor * jnp.sin(angles),
            axial_factor * jnp.ones_like(angles),
        ]
    )[:, :, None]
    force_phys = -2.0 * cross_product(rotation, phys_velocity) - lorentz_factor * cross_product(
        phys_magnetic, induction
    )
    forcing_velocity = jnp.einsum("cj,kjn->kcn", forward, force_phys, precision=highest)
    forcing_magnetic = jnp.einsum("cj,kjn->kcn", forward, induction, precision=highest)
    return (forcing_velocity, forcing_magnetic)


def squared_modes(coef_count):
    mode_index = jnp.arange(coef_count, dtype=jnp.int32) // 2
    return (mode_index * mode_index).astype(jnp.float32)


def dense_operators(blocks, connectivity, node_count, width):
    node_range = jnp.arange(node_count, dtype=jnp.int32)
    width_range = jnp.arange(width, dtype=jnp.int32)
    columns = (connectivity[:, :, None] == width_range[None, None, :]).astype(jnp.float32)
    total = jnp.zeros((blocks.shape[0], node_count, width), jnp.float32)
    for row in range(6):
        targets = (connectivity[row][:, None] == node_range[None, :]).astype(jnp.float32)
        weighted = jnp.einsum("gbe,bew->gew", blocks[:, row], columns, precision=highest)
        total = total + jnp.einsum("en,gew->gnw", targets, weighted, precision=highest)
    return total


def local(
    velocity,
    magnetic,
    mass_blocks,
    stiff_blocks,
    twist_blocks,
    diffusivity,
    connectivity,
    ghost_lists,
):
    node_count = velocity.shape[-1]
    ghosts = ghost_lists.shape[-1]
    width = node_count + 2 * ghosts
    state_now = jnp.stack([velocity, magnetic])
    forcing = jnp.stack(list(forcing_terms(velocity, magnetic)))
    mode_square = squared_modes(velocity.shape[1])[None, None, :, None]
    all_blocks = jnp.stack(
        [
            mass_blocks,
            viscosity * stiff_blocks,
            diffusivity * stiff_blocks,
            viscosity * twist_blocks,
            diffusivity * twist_blocks,
        ]
    )
    operators = dense_operators(all_blocks, connectivity, node_count, width)
    mass_matrix = operators[0]
    stiff_matrices = operators[1:3]
    twist_matrices = operators[3:5]

    def with_ghosts(field_values):
        padded = extended(field_values, (("mesh", 3),), node_count)
        from_below = jnp.take(padded[..., :node_count], ghost_lists[0], axis=-1)
        from_above = jnp.take(padded[..., 2 * node_count :], ghost_lists[1], axis=-1)
        return jnp.concatenate([field_values, from_below, from_above], axis=-1)

    def mass_apply(widened):
        return jnp.einsum("fkcj,nj->fkcn", widened, mass_matrix, precision=highest)

    def diffusion_apply(widened):
        stiff_terms = jnp.einsum("fkcj,fnj->fkcn", widened, stiff_matrices, precision=highest)
        twist_terms = jnp.einsum("fkcj,fnj->fkcn", widened, twist_matrices, precision=highest)
        return stiff_terms + mode_square * twist_terms

    residual = mass_apply(with_ghosts(forcing)) - diffusion_apply(with_ghosts(state_now))
    solution = state_now

    def squares(vector):
        return lax.psum(jnp.sum(vector * vector, axis=-1), "mesh")

    direction = residual
    norm_now = squares(residual)
    for iteration in range(ITERS):
        operate_widened = with_ghosts(direction)
        image = mass_apply(operate_widened) / time_step + diffusion_apply(operate_widened)
        curvature = lax.psum(jnp.sum(direction * image, axis=-1), "mesh")
        step_size = norm_now / (curvature + epsilon)
        solution = solution + step_size[..., None] * direction
        residual = residual - step_size[..., None] * image
        if iteration + 1 < ITERS:
            norm_next = squares(residual)
            conjugacy = norm_next / (norm_now + epsilon)
            direction = residual + conjugacy[..., None] * direction
            norm_now = norm_next
    return (solution[0], solution[1])


def solution(mesh):
    in_specs = (
        P("runs", None, "mesh"),
        P("runs", None, "mesh"),
        P(None, None, "mesh"),
        P(None, None, "mesh"),
        P(None, None, "mesh"),
        P(("runs", "mesh")),
        P(None, "mesh"),
        P(None, "mesh"),
    )
    out_specs = (P("runs", None, "mesh"), P("runs", None, "mesh"))
    return jax.shard_map(local, mesh=mesh, in_specs=in_specs, out_specs=out_specs, check_vma=False)
```

profile of v0, /device:TPU:0, one launch (start us, length us, event | category | flops | bytes accessed | tf_op | source)
XLA Modules:
  0.0 359.7 jit_solution(11023500793550098156)
XLA Ops:
  0.6 1.2 copy.16
  2.0 1.1 pad_maximum_fusion.7
  3.1 1.3 collective-permute-start.3
  4.4 3.9 %collective-permute-start.2 = (f32[2,3,256,128]{2,3,1,0:T(8,128)}, f32[2,3,256,128]{2,3,1,0:T(8,128)}, u32[]{:S(2)}, u32[]{:S(2)}) collective-permute-start(f32[2,3,256,128]{2,3,1,0:T(8,128)} %pad_maximum_fusion.7), channel_id=1, source_target_pairs={{0,1},{1,2},{2,3},{3,4},{4,5},{5,6},{6,7},{7,8},{8,9},{9,10},{10,1... | collective-permute-start | bytes 2359304 | tf_op jit(solution)/shard_map/ppermute | solution.py:25
  8.5 3.1 convolution_bitcast_fusion
  11.6 3.1 convolution_bitcast_fusion.1
  15.1 3.4 convolution_bitcast_fusion.2
  18.5 13.4 %convolution_bitcast_fusion.3 = f32[1,3,256,128]{2,3,1,0:T(8,128)S(1)} fusion(f32[1,512,128]{2,1,0:T(8,128)S(1)} %get-tuple-element.23, f32[1,512,128]{2,1,0:T(8,128)S(1)} %get-tuple-element.24, f32[1,512,128]{2,1,0:T(8,128)S(1)} %get-tuple-element.22, f32[1,512,128]{2,1,0:T(8,128)S(1)} %multiply_subtract_fusion.2, ...), kind=kOutput, calls=%fused_computation.36 | convolution fusion | flops 607453184 | bytes 1968384 | tf_op jit(solution)/shard_map/cj,kjn->kcn/dot_general | solution.py:74
  32.0 0.9 pad_maximum_fusion.8
  32.9 1.3 collective-permute-start.1
  34.2 5.1 %collective-permute-start = (f32[2,3,256,128]{2,3,1,0:T(8,128)}, f32[2,3,256,128]{2,3,1,0:T(8,128)}, u32[]{:S(2)}, u32[]{:S(2)}) collective-permute-start(f32[2,3,256,128]{2,3,1,0:T(8,128)} %pad_maximum_fusion.8), channel_id=1, source_target_pairs={{0,1},{1,2},{2,3},{3,4},{4,5},{5,6},{6,7},{7,8},{8,9},{9,10},{10,1... | collective-permute-start | bytes 2359304 | tf_op jit(solution)/shard_map/ppermute | solution.py:25
  41.1 1.8 fusion.59
  43.2 1.8 fusion.61
  45.2 1.8 fusion.63
  47.0 1.5 copy.50
  48.7 1.8 fusion.65
  50.5 2.3 copy.48
  53.1 1.8 fusion.67
  54.8 1.5 copy.46
  57.8 1.2 convolution_add_fusion.3
  59.3 1.6 copy.54
  60.9 1.1 copy.52
  62.0 1.6 convolution_add_fusion.2
  64.5 1.9 copy.26
  67.2 1.7 copy.22
  69.7 2.1 copy.24
  72.7 1.7 copy.20
  76.3 0.9 fusion.11
  77.3 0.9 fusion.35
  78.2 1.0 fusion.8
  79.3 1.3 collective-permute-start.5
  80.6 4.3 %collective-permute-start.4 = (f32[2,3,256,128]{2,3,1,0:T(8,128)S(1)}, f32[2,3,256,128]{2,3,1,0:T(8,128)}, u32[]{:S(2)}, u32[]{:S(2)}) collective-permute-start(f32[2,3,256,128]{2,3,1,0:T(8,128)S(1)} %fusion.8), channel_id=1, source_target_pairs={{0,1},{1,2},{2,3},{3,4},{4,5},{5,6},{6,7},{7,8},{8,9},{9,10},{10,1... | collective-permute-start | bytes 2359304 | tf_op jit(solution)/shard_map/ppermute | solution.py:25
  86.4 1.7 copy.28
  89.0 0.9 fusion.56
  89.9 0.9 convolution_multiply_fusion.5
  90.9 2.0 multiply_reduce_fusion.3
  92.9 74.2 %all-reduce = (f32[2,3,256]{2,1,0:T(4,128)S(1)}, f32[2,3,256]{2,1,0:T(4,128)S(1)}) all-reduce(f32[2,3,256]{2,1,0:T(4,128)S(1)} %get-tuple-element.8, f32[2,3,256]{2,1,0:T(4,128)S(1)} %get-tuple-element.7), channel_id=1, replica_groups=mesh['runs'=2,'mesh'=16] {'mesh'}, use_global_device_ids=true, to_apply=%region_1.3 | all-reduce | flops 3072 | bytes 24576 | tf_op jit(solution)/shard_map/psum | solution.py:144
  167.1 1.3 multiply_reduce_fusion.2
  168.4 30.0 %psum.44 = f32[2,3,256]{2,1,0:T(4,128)S(1)} all-reduce(f32[2,3,256]{2,1,0:T(4,128)S(1)} %get-tuple-element.11), channel_id=1, replica_groups=mesh['runs'=2,'mesh'=16] {'mesh'}, use_global_device_ids=true, to_apply=%region_5.7 | all-reduce | flops 1536 | bytes 12288 | tf_op jit(solution)/shard_map/psum | solution.py:144
  198.5 1.3 collective-permute-start.7
  199.8 4.1 %collective-permute-start.6 = (f32[2,3,256,128]{2,3,1,0:T(8,128)S(1)}, f32[2,3,256,128]{2,3,1,0:T(8,128)}, u32[]{:S(2)}, u32[]{:S(2)}) collective-permute-start(f32[2,3,256,128]{2,3,1,0:T(8,128)S(1)} %multiply_add_fusion.2), channel_id=1, source_target_pairs={{0,1},{1,2},{2,3},{3,4},{4,5},{5,6},{6,7},{7,8},{8,9},{9,10},{10,1... | collective-permute-start | bytes 2359304 | tf_op jit(solution)/shard_map/ppermute | solution.py:25
  203.9 1.5 copy.34
  205.5 1.9 gather_fusion.7
  208.2 2.7 copy.32
  210.8 1.9 gather_fusion.6
  212.9 1.9 fusion.55
  214.8 0.9 convolution_multiply_fusion.3
  215.8 2.1 multiply_reduce_fusion.1
  217.9 40.7 %psum.45 = f32[2,3,256]{2,1,0:T(4,128)} all-reduce(f32[2,3,256]{2,1,0:T(4,128)S(1)} %get-tuple-element.49), channel_id=1, replica_groups=mesh['runs'=2,'mesh'=16] {'mesh'}, use_global_device_ids=true, to_apply=%region_7.9 | all-reduce | flops 1536 | bytes 12288 | tf_op jit(solution)/shard_map/psum | solution.py:151
  260.0 30.7 %psum.46 = f32[2,3,256]{2,1,0:T(4,128)} all-reduce(f32[2,3,256]{2,1,0:T(4,128)} %multiply_reduce_fusion), channel_id=1, replica_groups=mesh['runs'=2,'mesh'=16] {'mesh'}, use_global_device_ids=true, to_apply=%region_9.11 | all-reduce | flops 1536 | bytes 12288 | tf_op jit(solution)/shard_map/psum | solution.py:144
  291.4 1.3 multiply_add_fusion.1
  292.7 1.3 collective-permute-start.9
  294.0 4.0 %collective-permute-start.8 = (f32[2,3,256,128]{2,3,1,0:T(8,128)S(1)}, f32[2,3,256,128]{2,3,1,0:T(8,128)}, u32[]{:S(2)}, u32[]{:S(2)}) collective-permute-start(f32[2,3,256,128]{2,3,1,0:T(8,128)S(1)} %multiply_add_fusion.1), channel_id=1, source_target_pairs={{0,1},{1,2},{2,3},{3,4},{4,5},{5,6},{6,7},{7,8},{8,9},{9,10},{10,1... | collective-permute-start | bytes 2359304 | tf_op jit(solution)/shard_map/ppermute | solution.py:25
  298.0 1.5 copy.38
  299.5 2.7 gather_fusion.9
  302.2 1.7 fusion.73
  303.9 2.6 copy.36
  306.5 2.7 gather_fusion.8
  309.2 1.0 fusion.74
  310.2 2.0 fusion.19
  312.3 0.9 convolution_multiply_fusion.1
  313.3 1.7 fusion.10
  315.0 40.4 %psum.47 = f32[2,3,256]{2,1,0:T(4,128)S(1)} all-reduce(f32[2,3,256]{2,1,0:T(4,128)} %fusion.10), channel_id=1, replica_groups=mesh['runs'=2,'mesh'=16] {'mesh'}, use_global_device_ids=true, to_apply=%region_11.13 | all-reduce | flops 1536 | bytes 12288 | tf_op jit(solution)/shard_map/psum | solution.py:151
  356.1 1.5 multiply_add_fusion
  (129 shorter events, 18.2 us)
Async XLA Ops:
  0.6 1.2 copy-start.8
  2.0 76.2 %copy-start.3 = (f32[3,256,128]{1,2,0:T(8,128)}, f32[3,256,128]{1,2,0:T(8,128)S(1)}, u32[]{:S(2)}) copy-start(f32[3,256,128]{1,2,0:T(8,128)S(1)} %copy.17) | copy-start | bytes 1179652
  3.1 61.3 %collective-permute-start.3 = (f32[2,3,256,128]{2,3,1,0:T(8,128)}, f32[2,3,256,128]{2,3,1,0:T(8,128)}, u32[]{:S(2)}, u32[]{:S(2)}) collective-permute-start(f32[2,3,256,128]{2,3,1,0:T(8,128)} %pad_maximum_fusion.7), channel_id=1, source_target_pairs={{1,0},{2,1},{3,2},{4,3},{5,4},{6,5},{7,6},{8,7},{9,8},{10,9},{11,1... | collective-permute-start | bytes 2359304 | tf_op jit(solution)/shard_map/ppermute | solution.py:28
  4.4 65.3 %collective-permute-start.2 = (f32[2,3,256,128]{2,3,1,0:T(8,128)}, f32[2,3,256,128]{2,3,1,0:T(8,128)}, u32[]{:S(2)}, u32[]{:S(2)}) collective-permute-start(f32[2,3,256,128]{2,3,1,0:T(8,128)} %pad_maximum_fusion.7), channel_id=1, source_target_pairs={{0,1},{1,2},{2,3},{3,4},{4,5},{5,6},{6,7},{7,8},{8,9},{9,10},{10,1... | collective-permute-start | bytes 2359304 | tf_op jit(solution)/shard_map/ppermute | solution.py:25
  8.5 3.1 copy-start.9
  18.5 13.4 %copy-start.10 = (f32[1,3,256,128]{2,3,1,0:T(8,128)}, f32[1,3,256,128]{2,3,1,0:T(8,128)S(1)}, u32[]{:S(2)}) copy-start(f32[1,3,256,128]{2,3,1,0:T(8,128)S(1)} %convolution_bitcast_fusion.2) | copy-start | bytes 1179652
  31.9 7.9 %copy-start.12 = (f32[1,3,256,128]{2,3,1,0:T(8,128)}, f32[1,3,256,128]{2,3,1,0:T(8,128)S(1)}, u32[]{:S(2)}) copy-start(f32[1,3,256,128]{2,3,1,0:T(8,128)S(1)} %convolution_bitcast_fusion.3) | copy-start | bytes 1179652
  31.9 7.4 %copy-start.27 = (s32[6,128]{1,0:T(8,128)S(1)}, s32[6,128]{1,0:T(8,128)}, u32[]{:S(2)}) copy-start(s32[6,128]{1,0:T(8,128)} %param.16) | copy-start | bytes 9220
  31.9 7.6 %copy-start.31 = (s32[2,32]{1,0:T(2,128)S(1)}, s32[2,32]{1,0:T(2,128)}, u32[]{:S(2)}) copy-start(s32[2,32]{1,0:T(2,128)} %param.17) | copy-start | bytes 772
  32.0 7.7 %copy-start.19 = (f32[6,6,128]{2,1,0:T(8,128)S(1)}, f32[6,6,128]{2,1,0:T(8,128)}, u32[]{:S(2)}) copy-start(f32[6,6,128]{2,1,0:T(8,128)} %param.12) | copy-start | bytes 55300
  32.0 7.7 %copy-start.14 = (f32[6,6,128]{2,1,0:T(8,128)S(1)}, f32[6,6,128]{2,1,0:T(8,128)}, u32[]{:S(2)}) copy-start(f32[6,6,128]{2,1,0:T(8,128)} %param.13) | copy-start | bytes 55300
  32.0 7.7 %copy-start.30 = (f32[128]{0:T(128)S(1)}, f32[128]{0:T(128)}, u32[]{:S(2)}) copy-start(f32[128]{0:T(128)} %param.15) | copy-start | bytes 1540
  32.0 7.7 %copy-start.15 = (f32[6,6,128]{2,1,0:T(8,128)S(1)}, f32[6,6,128]{2,1,0:T(8,128)}, u32[]{:S(2)}) copy-start(f32[6,6,128]{2,1,0:T(8,128)} %param.14) | copy-start | bytes 55300
  32.9 34.2 %collective-permute-start.1 = (f32[2,3,256,128]{2,3,1,0:T(8,128)}, f32[2,3,256,128]{2,3,1,0:T(8,128)}, u32[]{:S(2)}, u32[]{:S(2)}) collective-permute-start(f32[2,3,256,128]{2,3,1,0:T(8,128)} %pad_maximum_fusion.8), channel_id=1, source_target_pairs={{1,0},{2,1},{3,2},{4,3},{5,4},{6,5},{7,6},{8,7},{9,8},{10,9},{11,1... | collective-permute-start | bytes 2359304 | tf_op jit(solution)/shard_map/ppermute | solution.py:28
  34.2 38.5 %collective-permute-start = (f32[2,3,256,128]{2,3,1,0:T(8,128)}, f32[2,3,256,128]{2,3,1,0:T(8,128)}, u32[]{:S(2)}, u32[]{:S(2)}) collective-permute-start(f32[2,3,256,128]{2,3,1,0:T(8,128)} %pad_maximum_fusion.8), channel_id=1, source_target_pairs={{0,1},{1,2},{2,3},{3,4},{4,5},{5,6},{6,7},{7,8},{8,9},{9,10},{10,1... | collective-permute-start | bytes 2359304 | tf_op jit(solution)/shard_map/ppermute | solution.py:25
  39.6 167.8 %copy-start.25 = (pred[32]{0:T(512)(128)(4,1)}, pred[32]{0:T(512)(128)(4,1)S(1)}, u32[]{:S(2)}) copy-start(pred[32]{0:T(512)(128)(4,1)S(1)} %get-tuple-element.42) | copy-start | bytes 100
  39.6 173.1 %copy-start.23 = (pred[32]{0:T(512)(128)(4,1)}, pred[32]{0:T(512)(128)(4,1)S(1)}, u32[]{:S(2)}) copy-start(pred[32]{0:T(512)(128)(4,1)S(1)} %get-tuple-element.13) | copy-start | bytes 100
  39.6 171.2 %copy-start.28 = (s32[1024]{0:T(1024)}, s32[1024]{0:T(1024)S(1)}, u32[]{:S(2)}) copy-start(s32[1024]{0:T(1024)S(1)} %pad_clamp_fusion.1) | copy-start | bytes 12292
  39.7 165.8 %copy-start.29 = (s32[1024]{0:T(1024)}, s32[1024]{0:T(1024)S(1)}, u32[]{:S(2)}) copy-start(s32[1024]{0:T(1024)S(1)} %pad_clamp_fusion) | copy-start | bytes 12292
  56.3 1.0 copy-start.7
  59.0 31.9 %copy-start.20 = (f32[256]{0:T(256)}, f32[256]{0:T(256)S(1)}, u32[]{:S(2)}) copy-start(f32[256]{0:T(256)S(1)} %multiply_convert_fusion) | copy-start | bytes 3076
  59.3 1.6 copy-start.4
  64.5 150.3 %copy-start.1 = (f32[5,128,192]{1,2,0:T(8,128)}, f32[5,128,192]{1,2,0:T(8,128)S(1)}, u32[]{:S(2)}) copy-start(f32[5,128,192]{1,2,0:T(8,128)S(1)} %fusion.9) | copy-start | bytes 1474564
  75.2 1.0 copy-start.11
  75.2 1.1 copy-start.13
  79.3 5.6 %collective-permute-start.5 = (f32[2,3,256,128]{2,3,1,0:T(8,128)S(1)}, f32[2,3,256,128]{2,3,1,0:T(8,128)S(1)}, u32[]{:S(2)}, u32[]{:S(2)}) collective-permute-start(f32[2,3,256,128]{2,3,1,0:T(8,128)S(1)} %fusion.8), channel_id=1, source_target_pairs={{1,0},{2,1},{3,2},{4,3},{5,4},{6,5},{7,6},{8,7},{9,8},{10,9},{11,1... | collective-permute-start | bytes 2359304 | tf_op jit(solution)/shard_map/ppermute | solution.py:28
  80.6 5.8 %collective-permute-start.4 = (f32[2,3,256,128]{2,3,1,0:T(8,128)S(1)}, f32[2,3,256,128]{2,3,1,0:T(8,128)}, u32[]{:S(2)}, u32[]{:S(2)}) collective-permute-start(f32[2,3,256,128]{2,3,1,0:T(8,128)S(1)} %fusion.8), channel_id=1, source_target_pairs={{0,1},{1,2},{2,3},{3,4},{4,5},{5,6},{6,7},{7,8},{8,9},{9,10},{10,1... | collective-permute-start | bytes 2359304 | tf_op jit(solution)/shard_map/ppermute | solution.py:25
  167.1 1.3 copy-start.16
  198.5 5.4 %collective-permute-start.7 = (f32[2,3,256,128]{2,3,1,0:T(8,128)S(1)}, f32[2,3,256,128]{2,3,1,0:T(8,128)S(1)}, u32[]{:S(2)}, u32[]{:S(2)}) collective-permute-start(f32[2,3,256,128]{2,3,1,0:T(8,128)S(1)} %multiply_add_fusion.2), channel_id=1, source_target_pairs={{1,0},{2,1},{3,2},{4,3},{5,4},{6,5},{7,6},{8,7},{9,8},{10,9},{11,1... | collective-permute-start | bytes 2359304 | tf_op jit(solution)/shard_map/ppermute | solution.py:28
  199.8 8.3 %collective-permute-start.6 = (f32[2,3,256,128]{2,3,1,0:T(8,128)S(1)}, f32[2,3,256,128]{2,3,1,0:T(8,128)}, u32[]{:S(2)}, u32[]{:S(2)}) collective-permute-start(f32[2,3,256,128]{2,3,1,0:T(8,128)S(1)} %multiply_add_fusion.2), channel_id=1, source_target_pairs={{0,1},{1,2},{2,3},{3,4},{4,5},{5,6},{6,7},{7,8},{8,9},{9,10},{10,1... | collective-permute-start | bytes 2359304 | tf_op jit(solution)/shard_map/ppermute | solution.py:25
  212.8 2.0 copy-start.6
  214.8 1.0 copy-start.21
  217.8 72.8 %copy-start = (f32[2,3,256,128]{2,3,1,0:T(8,128)}, f32[2,3,256,128]{2,3,1,0:T(8,128)S(1)}, u32[]{:S(2)}) copy-start(f32[2,3,256,128]{2,3,1,0:T(8,128)S(1)} %get-tuple-element.50) | copy-start | bytes 2359300
  291.4 1.3 copy-start.18
  292.7 5.3 %collective-permute-start.9 = (f32[2,3,256,128]{2,3,1,0:T(8,128)S(1)}, f32[2,3,256,128]{2,3,1,0:T(8,128)S(1)}, u32[]{:S(2)}, u32[]{:S(2)}) collective-permute-start(f32[2,3,256,128]{2,3,1,0:T(8,128)S(1)} %multiply_add_fusion.1), channel_id=1, source_target_pairs={{1,0},{2,1},{3,2},{4,3},{5,4},{6,5},{7,6},{8,7},{9,8},{10,9},{11,1... | collective-permute-start | bytes 2359304 | tf_op jit(solution)/shard_map/ppermute | solution.py:28
  294.0 9.8 %collective-permute-start.8 = (f32[2,3,256,128]{2,3,1,0:T(8,128)S(1)}, f32[2,3,256,128]{2,3,1,0:T(8,128)}, u32[]{:S(2)}, u32[]{:S(2)}) collective-permute-start(f32[2,3,256,128]{2,3,1,0:T(8,128)S(1)} %multiply_add_fusion.1), channel_id=1, source_target_pairs={{0,1},{1,2},{2,3},{3,4},{4,5},{5,6},{6,7},{7,8},{8,9},{9,10},{10,1... | collective-permute-start | bytes 2359304 | tf_op jit(solution)/shard_map/ppermute | solution.py:25
  299.5 2.7 copy-start.26
  306.5 2.7 copy-start.24
  310.2 2.1 copy-start.2
  310.2 2.1 copy-start.5
  312.3 1.0 copy-start.22
  313.3 42.8 %copy-start.17 = (f32[2,3,256]{2,1,0:T(4,128)S(1)}, f32[2,3,256]{2,1,0:T(4,128)}, u32[]{:S(2)}) copy-start(f32[2,3,256]{2,1,0:T(4,128)} %copy-done.16) | copy-start | bytes 18436
where the time goes:
time: 365 us; the launch traced here: 360 us
  blocking collectives  216 us (59%)
  matrix products  53.6 us (15%)
  local copies, waits for them, and re-layouts  46.9 us (13%)
  starting transfers between devices  27.8 us (8%)
  other arithmetic  13.7 us (4%)
    psum x3, blocking collectives, squares(): return lax.psum(jnp.sum(vector * vector, axis=-1), 'mesh')  135 us
    psum x2, blocking collectives, local(): curvature = lax.psum(jnp.sum(direction * image, axis=-1), 'mesh')  81.1 us
    ppermute x5, starting transfers between devices, extended(): lax.ppermute(lax.slice_in_dim(block, block.shape[dim] - width, None, axis...  21.4 us
    dot_general x1, matrix products, forcing_terms(): jnp.einsum('cj,kjn->kcn', forward, force_phys, precision=highest)  13.4 us
    ppermute x5, local copies, waits for them, and re-layouts, extended(): lax.ppermute(lax.slice_in_dim(block, block.shape[dim] - width, None, axis...  10.9 us
    dot_general x6, matrix products, dense_operators(): jnp.einsum('gbe,bew->gew', blocks[:, row], columns, precision=highest)  9.69 us
    dot_general x6, local copies, waits for them, and re-layouts, dense_operators(): jnp.einsum('gbe,bew->gew', blocks[:, row], columns, precision=highest)  8.25 us
  transfers between devices with their start and end apart: 10, of which 0 were waited for; matrix products, arithmetic and copies ran while one was open for 19% of the time, Pallas kernels for 0%

commit v1 on v0

v1 whole, which is shorter than its diff:
```python
import functools
import math

import jax
import jax.numpy as jnp
import ml_dtypes
import numpy as np
from jax import lax
from jax.experimental import pallas as pl
from jax.experimental.pallas import tpu as pltpu
from jax.sharding import PartitionSpec as P

viscosity = 2.0
inverse_step = 10.0
tilt_factor = 0.5
axial_factor = 1.0
lorentz_factor = 0.005
epsilon = 1e-06
basis_scale = 512.0

f32 = jnp.float32
bf16 = jnp.bfloat16
VMEM = pl.BlockSpec(memory_space=pltpu.VMEM)
SMEM = pl.BlockSpec(memory_space=pltpu.SMEM)


def split_table(table):
    high = table.astype(np.float32).astype(ml_dtypes.bfloat16)
    low = (table - high.astype(np.float64)).astype(np.float32).astype(ml_dtypes.bfloat16)
    return high, low


def transform_tables(coefs):
    planes = 2 * coefs
    mode = np.arange(coefs) // 2
    turns = (np.arange(planes)[:, None] * mode[None, :]) % planes
    angles = 2.0 * math.pi / planes * turns
    inverse = np.where(np.arange(coefs)[None, :] % 2 == 0, np.cos(angles), np.sin(angles))
    weight = np.where(mode == 0, 1.0, 2.0) / planes
    to_planes = np.concatenate(split_table(inverse.T.copy()), axis=0)
    to_coefs = np.concatenate(split_table(inverse * weight[None, :]), axis=0)
    phi = 2.0 * math.pi / planes * np.arange(planes)
    rows = np.zeros((8, planes), np.float32)
    rows[0] = -2.0 * tilt_factor * np.cos(phi)
    rows[1] = 2.0 * tilt_factor * np.sin(phi)
    rows[2] = -2.0 * axial_factor
    squares = np.zeros((8, coefs), np.float32)
    squares[:] = (mode * mode).astype(np.float32)[None, :]
    return to_planes, to_coefs, rows, squares


def halves(value):
    high = value.astype(bf16)
    return high, (value - high.astype(f32)).astype(bf16)


def dot(first, second):
    return lax.dot_general(first, second, (((1,), (0,)), ((), ())), preferred_element_type=f32)


def dot_nt(first, second):
    return lax.dot_general(first, second, (((1,), (1,)), ((), ())), preferred_element_type=f32)


def stacked_columns(value):
    high, low = halves(value)
    return jnp.concatenate([high, low, high], axis=1)


def stacked_rows(value):
    high, low = halves(value)
    return jnp.concatenate([high, high, low], axis=0)


def iota(shape, dim):
    return lax.broadcasted_iota(jnp.int32, shape, dim)


def element_sides(conn, nodes, ghosts):
    own = jnp.max((conn < nodes).astype(f32), axis=0, keepdims=True)
    low = jnp.max(((conn >= nodes) & (conn < nodes + ghosts)).astype(f32), axis=0, keepdims=True)
    high = jnp.max((conn >= nodes + ghosts).astype(f32), axis=0, keepdims=True)
    return own, low, high


def pack_matrix(conn, odd, nodes, ghosts):
    _, low, high = element_sides(conn, nodes, ghosts)
    node_of_row = iota((nodes, conn.shape[1]), 0)
    flag_low = jnp.zeros((nodes, conn.shape[1]), f32)
    flag_high = jnp.zeros((nodes, conn.shape[1]), f32)
    for a in range(conn.shape[0]):
        hit = node_of_row == conn[a : a + 1, :]
        flag_low = jnp.maximum(flag_low, jnp.where(hit, low, 0.0))
        flag_high = jnp.maximum(flag_high, jnp.where(hit, high, 0.0))
    flag_low = jnp.max(flag_low, axis=1, keepdims=True)
    flag_high = jnp.max(flag_high, axis=1, keepdims=True)
    before = (iota((nodes, nodes), 1) < iota((nodes, nodes), 0)).astype(bf16)
    lane = iota((nodes, nodes), 1)
    flags = jnp.where(lane == 0, flag_low, jnp.where(lane == 1, flag_high, 0.0))
    ranks = dot(before, flags.astype(bf16))
    rank_low = jnp.sum(jnp.where(lane == 0, ranks, 0.0), axis=1, keepdims=True).astype(jnp.int32)
    rank_high = jnp.sum(jnp.where(lane == 1, ranks, 0.0), axis=1, keepdims=True).astype(jnp.int32)
    rows = iota((nodes, 2 * ghosts), 1)
    low_row = rank_low + (1 - odd) * ghosts
    high_row = rank_high + odd * ghosts
    fits_low = (flag_low > 0.0) & (rank_low < ghosts) & (rows == low_row)
    fits_high = (flag_high > 0.0) & (rank_high < ghosts) & (rows == high_row)
    return jnp.where(fits_low | fits_high, 1.0, 0.0)


def to_row(column, size):
    eye = iota((size, size), 0) == iota((size, size), 1)
    return jnp.sum(jnp.where(eye, column, 0.0), axis=0, keepdims=True)


def to_column(row, size):
    eye = iota((size, size), 0) == iota((size, size), 1)
    return jnp.sum(jnp.where(eye, row, 0.0), axis=1, keepdims=True)


def slot_matrix(conn, lists, odd, low_valid, high_valid, nodes, ghosts):
    own, _, _ = element_sides(conn, nodes, ghosts)
    slot = iota((2 * ghosts, conn.shape[1]), 0) + nodes
    active = jnp.zeros((2 * ghosts, conn.shape[1]), f32)
    for a in range(conn.shape[0]):
        active = jnp.maximum(active, jnp.where(slot == conn[a : a + 1, :], own, 0.0))
    active = jnp.max(active, axis=1, keepdims=True)
    parts = []
    for side in range(2):
        flag = active[side * ghosts : (side + 1) * ghosts]
        node_row = lists[side : side + 1, :].astype(f32)
        node_column = to_column(node_row, ghosts)
        smaller = (node_row < node_column).astype(f32) * to_row(flag, ghosts)
        rank = jnp.sum(smaller, axis=1, keepdims=True).astype(jnp.int32)
        offset = (1 - odd) * ghosts if side == 0 else odd * ghosts
        valid = low_valid if side == 0 else high_valid
        live = (flag > 0.0) & (valid > 0)
        rows = iota((ghosts, 2 * ghosts), 1)
        parts.append(jnp.where(live & (rows == rank + offset), 1.0, 0.0))
    return jnp.concatenate(parts, axis=0)


def pack_kernel(info, velocity, magnetic, conn_ref, near_ref, far_ref, state_ref):
    nodes = velocity.shape[2]
    ghosts = near_ref.shape[1]
    pick = pack_matrix(conn_ref[...], info[0], nodes, ghosts)
    pick = jnp.transpose(pick).astype(bf16)
    for k in range(6):
        source = velocity if k < 3 else magnetic
        block = jnp.transpose(source[k % 3])
        state_ref[k] = block
        first, rest = halves(block)
        second = (block - first.astype(f32) - rest.astype(f32)).astype(bf16)
        packed = dot(pick, first) + dot(pick, rest) + dot(pick, second)
        near_ref[k] = packed[:ghosts]
        far_ref[k] = packed[ghosts:]


def to_planes(high, low, table):
    coefs = high.shape[1]
    return dot(high, table[:coefs]) + dot(low, table[:coefs]) + dot(high, table[coefs:])


def to_coefs(high, low, table):
    planes = high.shape[1]
    return dot(high, table[:planes]) + dot(low, table[:planes]) + dot(high, table[planes:])


def cross(a, b):
    return [
        a[1] * b[2] - a[2] * b[1],
        a[2] * b[0] - a[0] * b[2],
        a[0] * b[1] - a[1] * b[0],
    ]


def forcing(value, rows, planes_ref, coefs_ref, rotation_ref, phys_ref, high_ref, low_ref):
    planes = planes_ref.shape[1]
    high, low = halves(value)
    phys_ref[...] = to_planes(high, low, planes_ref)
    step_rows, step_lanes = 16, 256
    for row in range(0, rows, step_rows):
        for lane in range(0, planes, step_lanes):
            lanes = pl.ds(lane, step_lanes)
            u = [phys_ref[pl.ds(k * rows + row, step_rows), lanes] for k in range(3)]
            b = [phys_ref[pl.ds((3 + k) * rows + row, step_rows), lanes] for k in range(3)]
            turn = [rotation_ref[k : k + 1, lanes] for k in range(3)]
            induction = cross(u, b)
            twisted = cross(turn, u)
            lorentz = cross(b, induction)
            force = [twisted[k] - lorentz_factor * lorentz[k] for k in range(3)]
            for k, item in enumerate(force + induction):
                item_high, item_low = halves(item)
                at = pl.ds(k * rows + row, step_rows)
                high_ref[at, lanes] = item_high
                low_ref[at, lanes] = item_low
    return to_coefs(high_ref[...], low_ref[...], coefs_ref)


def build_kernel(
    info, state, planes_ref, coefs_ref, rotation_ref, squares_ref,
    mass_ref, stiff_ref, twist_ref, rates_ref, conn_ref, lists_ref,
    own_ref, ghost_ref, back_ref, mass_ghost_ref, rest_ghost_ref, residual_ref, packed_ref,
    phys_ref, high_ref, low_ref, force_ref, z_ref,
):
    nodes = state.shape[1]
    elements = conn_ref.shape[1]
    ghosts = lists_ref.shape[1]
    width = nodes + 2 * ghosts
    conn = conn_ref[...]
    pick = jnp.transpose(pack_matrix(conn, info[0], nodes, ghosts)).astype(bf16)
    remap = slot_matrix(conn, lists_ref[...], info[0], info[1], info[2], nodes, ghosts).astype(bf16)

    node_of_row = iota((nodes, elements), 0)
    hits = [node_of_row == conn[a : a + 1, :] for a in range(6)]
    rates = rates_ref[0:1, :]
    for g, block in enumerate((mass_ref, stiff_ref, twist_ref)):
        for b in range(6):
            total = jnp.zeros((nodes, elements), f32)
            for a in range(6):
                total = total + jnp.where(hits[a], block[a, b : b + 1, :], 0.0)
            lanes = pl.ds(b * elements, elements)
            z_ref[pl.ds(g * nodes, nodes), lanes] = total
            if g > 0:
                z_ref[pl.ds((g + 2) * nodes, nodes), lanes] = total * rates
    column = jnp.concatenate(
        [(iota((width, elements), 0) == conn[b : b + 1, :]).astype(bf16) for b in range(6)], axis=1
    )
    z = z_ref[...]
    first, second = halves(z)
    third = (z - first.astype(f32) - second.astype(f32)).astype(bf16)
    dense = dot_nt(first, column) + dot_nt(second, column) + dot_nt(third, column)
    mass, stiff, twist, rate_stiff, rate_twist = [dense[g * nodes : (g + 1) * nodes] for g in range(5)]

    def picked(pair):
        return [dot(pick, item).astype(bf16) for item in pair]

    def moved(pair):
        return [dot(item[:, nodes:], remap).astype(bf16) for item in pair]

    def triple(pair):
        return jnp.concatenate([pair[0], pair[1], pair[0]], axis=1)

    def own_part(pair):
        return [item[:, :nodes] for item in pair]

    mass_pair = halves(mass)
    mass_packed = picked(mass_pair)
    mass_own = jnp.concatenate([triple(own_part(mass_pair)), triple(own_part(mass_packed))], axis=0)
    mass_ghost_ref[...] = jnp.concatenate([triple(moved(mass_pair)), triple(moved(mass_packed))], axis=0)
    rest_own = []
    for f in range(2):
        still = viscosity * stiff if f == 0 else rate_stiff
        turn = viscosity * twist if f == 0 else rate_twist
        image = (inverse_step * mass + still) * (1.0 / basis_scale)
        turn_image = turn * (1.0 / basis_scale)
        pairs = [halves(image), halves(turn_image)]
        pairs = pairs + [picked(pair) for pair in pairs]
        own_ref[f] = jnp.concatenate([triple(own_part(pair)) for pair in pairs], axis=0)
        moves = [moved(pair) for pair in pairs]
        ghost_ref[f] = jnp.concatenate([triple(pair) for pair in moves], axis=0)
        back = [
            jnp.transpose(moves[i][0].astype(f32) + moves[i][1].astype(f32)) for i in range(2)
        ]
        back_ref[f] = jnp.concatenate([stacked_columns(item) for item in back], axis=0)
        pairs = [halves(still), halves(turn)]
        pairs = pairs + [picked(pair) for pair in pairs]
        rest_own.append(jnp.concatenate([triple(own_part(pair)) for pair in pairs], axis=0))
        rest_ghost_ref[f] = jnp.concatenate([triple(moved(pair)) for pair in pairs], axis=0)

    value = state[...].reshape(6 * nodes, state.shape[2])
    force_ref[...] = forcing(
        value, nodes, planes_ref, coefs_ref, rotation_ref, phys_ref, high_ref, low_ref
    )
    square = squares_ref[0:1, :]
    for k in range(6):
        from_force = dot(mass_own, stacked_rows(force_ref[pl.ds(k * nodes, nodes), :]))
        from_state = dot(rest_own[k // 3], stacked_rows(state[k]))
        residual_ref[k] = from_force[:nodes] - (from_state[:nodes] + square * from_state[nodes : 2 * nodes])
        packed = from_state[2 * nodes :]
        packed_ref[k] = from_force[nodes:] - (packed[: 2 * ghosts] + square * packed[2 * ghosts :])


def ghost_block(info, near, far, k):
    distant = jnp.where(info[3] > 0, far[k], 0.0)
    return jnp.concatenate([near[k], distant], axis=0)


def start_kernel(
    info, near, far, packed, planes_ref, coefs_ref, rotation_ref, squares_ref, mass_ghost, rest_ghost,
    near_out, far_out, force_out, phys_ref, high_ref, low_ref,
):
    ghosts = near.shape[1]
    count = 2 * ghosts
    nodes = mass_ghost.shape[0] - count
    blocks = [ghost_block(info, near, far, k) for k in range(6)]
    value = jnp.concatenate(blocks, axis=0)
    force = forcing(value, count, planes_ref, coefs_ref, rotation_ref, phys_ref, high_ref, low_ref)
    square = squares_ref[0:1, :]
    for k in range(6):
        item = force[k * count : (k + 1) * count]
        force_out[k] = item
        from_force = dot(mass_ghost[nodes:], stacked_rows(item))
        from_state = dot(rest_ghost[k // 3, 2 * nodes :], stacked_rows(blocks[k]))
        total = packed[k] + from_force - (from_state[:count] + square * from_state[count:])
        near_out[k] = total[:ghosts]
        far_out[k] = total[ghosts:]


def apply_own(own, value, k, square, nodes, count):
    image = dot(own[k // 3], stacked_rows(value))
    full = image[:nodes] + square * image[nodes : 2 * nodes]
    packed = image[2 * nodes : 2 * nodes + count] + square * image[2 * nodes + count :]
    return full, packed


def first_kernel(
    info, near, far, force, residual, mass_ghost, rest_ghost, own, squares_ref,
    vector_out, image_out, packed_out, moments_out,
):
    nodes = residual.shape[1]
    count = force.shape[1]
    square = squares_ref[0:1, :]
    for k in range(6):
        from_force = dot(mass_ghost[:nodes], stacked_rows(force[k]))
        from_state = dot(rest_ghost[k // 3, : 2 * nodes], stacked_rows(ghost_block(info, near, far, k)))
        total = residual[k] + from_force - (from_state[:nodes] + square * from_state[nodes:])
        vector_out[k] = total
        full, packed = apply_own(own, total, k, square, nodes, count)
        image_out[k] = full
        packed_out[k] = packed
        moments_out[k : k + 1, :] = jnp.sum(total * total, axis=0, keepdims=True)
    moments_out[6:8, :] = jnp.zeros((2, moments_out.shape[1]), f32)


def send_kernel(info, near, far, packed, ghost_ops, squares_ref, near_out, far_out):
    ghosts = near.shape[1]
    count = 2 * ghosts
    top = ghost_ops.shape[1] - 2 * count
    square = squares_ref[0:1, :]
    for k in range(6):
        image = dot(ghost_ops[k // 3, top:], stacked_rows(ghost_block(info, near, far, k)))
        total = packed[k] + image[:count] + square * image[count:]
        near_out[k] = total[:ghosts]
        far_out[k] = total[ghosts:]


def next_kernel(
    info, near, far, image, before, own, ghost_ops, squares_ref,
    vector_out, image_out, packed_out, moments_out,
):
    nodes = image.shape[1]
    count = 2 * near.shape[1]
    square = squares_ref[0:1, :]
    for k in range(6):
        part = dot(ghost_ops[k // 3, : 2 * nodes], stacked_rows(ghost_block(info, near, far, k)))
        total = image[k] + part[:nodes] + square * part[nodes:]
        vector_out[k] = total
        full, packed = apply_own(own, total, k, square, nodes, count)
        image_out[k] = full
        packed_out[k] = packed
        moments_out[k : k + 1, :] = jnp.sum(before[k] * total, axis=0, keepdims=True)
        moments_out[6 + k : 7 + k, :] = jnp.sum(total * total, axis=0, keepdims=True)
    moments_out[12:16, :] = jnp.zeros((4, moments_out.shape[1]), f32)


def last_kernel(
    info, near, far, image, before, own, ghost_ops, back_ops, squares_ref,
    vector_out, back_out, moments_out,
):
    nodes = image.shape[1]
    count = 2 * near.shape[1]
    square = squares_ref[0:1, :]
    for k in range(6):
        part = dot(ghost_ops[k // 3, : 2 * nodes], stacked_rows(ghost_block(info, near, far, k)))
        total = image[k] + part[:nodes] + square * part[nodes:]
        vector_out[k] = total
        rows = stacked_rows(total)
        after = dot(own[k // 3, : 2 * nodes], rows)
        after = after[:nodes] + square * after[nodes:]
        back = dot(back_ops[k // 3], rows)
        back_out[k] = back[:count] + square * back[count:]
        moments_out[k : k + 1, :] = jnp.sum(before[k] * total, axis=0, keepdims=True)
        moments_out[6 + k : 7 + k, :] = jnp.sum(total * total, axis=0, keepdims=True)
        moments_out[12 + k : 13 + k, :] = jnp.sum(after * total, axis=0, keepdims=True)
    moments_out[18:24, :] = jnp.zeros((6, moments_out.shape[1]), f32)


def join_kernel(info, near, far, back, first, second, third, out):
    out[0:6] = first[0:6]
    out[6:18] = second[0:12]
    out[18:36] = third[0:18]
    out[36:40] = jnp.zeros((4, out.shape[1]), f32)
    for k in range(6):
        part = ghost_block(info, near, far, k) * back[k]
        out[30 + k : 31 + k, :] += jnp.sum(part, axis=0, keepdims=True)


def finish_kernel(moments, velocity, magnetic, first, second, third, velocity_out, magnetic_out):
    m0, m1, m2, m3, m4, m5 = [moments[6 * j : 6 * j + 6, :] for j in range(6)]
    scale = basis_scale
    alpha0 = m0 / (scale * m1 + epsilon)
    q1 = -alpha0 * scale
    rr1 = m0 + 2.0 * q1 * m1 + q1 * q1 * m2
    beta0 = rr1 / (m0 + epsilon)
    p0 = 1.0 + beta0
    p1 = q1
    alpha1 = rr1 / (scale * (p0 * p0 * m1 + 2.0 * p0 * p1 * m2 + p1 * p1 * m3) + epsilon)
    step1 = alpha1 * scale
    r1 = q1 - step1 * p0
    r2 = -step1 * p1
    rr2 = m0 + r1 * r1 * m2 + r2 * r2 * m4 + 2.0 * (r1 * m1 + r2 * m2 + r1 * r2 * m3)
    beta1 = rr2 / (rr1 + epsilon)
    d0 = 1.0 + beta1 * p0
    d1 = r1 + beta1 * p1
    d2 = r2
    curve = d0 * d0 * m1 + d1 * d1 * m3 + d2 * d2 * m5
    curve = curve + 2.0 * (d0 * d1 * m2 + d0 * d2 * m3 + d1 * d2 * m4)
    alpha2 = rr2 / (scale * curve + epsilon)
    c0 = alpha0 + alpha1 * p0 + alpha2 * d0
    c1 = alpha1 * p1 + alpha2 * d1
    c2 = alpha2 * d2
    for k in range(6):
        source, out = (velocity, velocity_out) if k < 3 else (magnetic, magnetic_out)
        change = (
            c0[k : k + 1, :] * first[k] + c1[k : k + 1, :] * second[k] + c2[k : k + 1, :] * third[k]
        )
        out[k % 3] = source[k % 3] + jnp.transpose(change)


def call(kernel, outs, operands, scratch=(), flops=0, limit=24):
    specs = [SMEM if operand.dtype == jnp.int32 and operand.ndim == 1 else VMEM for operand in operands]
    single = not isinstance(outs, list)
    shapes = [outs] if single else outs
    moved = sum(math.prod(o.shape) * o.dtype.itemsize for o in list(operands) + shapes)
    result = pl.pallas_call(
        kernel,
        out_shape=outs,
        in_specs=specs,
        out_specs=VMEM if single else [VMEM] * len(outs),
        scratch_shapes=list(scratch),
        compiler_params=pltpu.CompilerParams(vmem_limit_bytes=limit * 1024 * 1024),
        cost_estimate=pl.CostEstimate(flops=flops, bytes_accessed=moved, transcendentals=0),
    )(*operands)
    return result


def shape(*sizes, dtype=f32):
    return jax.ShapeDtypeStruct(sizes, dtype)


def involution(pairs):
    return [edge for a, b in pairs for edge in ((a, b), (b, a))]


def local(runs, count, velocity, magnetic, mass_blocks, stiff_blocks, twist_blocks, diffusivity, conn, lists):
    coefs, nodes = velocity.shape[1:]
    ghosts = lists.shape[1]
    elements = conn.shape[1]
    both = 2 * ghosts
    planes = 2 * coefs
    index = lax.axis_index("mesh")
    odd = index % 2
    low_valid = (index > 0).astype(jnp.int32)
    high_valid = (index < count - 1).astype(jnp.int32)
    far_valid = jnp.where(odd == 1, high_valid, low_valid)
    info = jnp.stack([odd, low_valid, high_valid, far_valid]).astype(jnp.int32)

    near_pairs = [(i, i ^ 1) for i in range(count)]
    far_pairs = []
    for run in range(runs):
        base = run * count
        far_pairs += involution([(base + i, base + i + 1) for i in range(1, count - 1, 2)])
    if runs % 2 == 0:
        for run in range(0, runs, 2):
            for end in (0, count - 1):
                far_pairs += involution([(run * count + end, (run + 1) * count + end)])

    def swap_near(value):
        return lax.ppermute(value, "mesh", near_pairs)

    def swap_far(value):
        return lax.ppermute(value, ("runs", "mesh"), far_pairs)

    def swapped(value, even_mask, odd_mask):
        pairs = [(i, i ^ (odd_mask if i % 2 else even_mask)) for i in range(count)]
        return lax.ppermute(value, "mesh", pairs)

    plane_table, coef_table, rotation, squares = transform_tables(coefs)
    plane_table, coef_table = jnp.asarray(plane_table), jnp.asarray(coef_table)
    rotation, squares = jnp.asarray(rotation), jnp.asarray(squares)
    ends = shape(6, ghosts, coefs)
    whole = shape(6, nodes, coefs)
    packs = shape(6, both, coefs)

    near, far, state = call(pack_kernel, [ends, ends, whole], [info, velocity, magnetic, conn])
    near_state, far_state = swap_near(near), swap_far(far)

    rates = jnp.broadcast_to(diffusivity[None, :], (8, elements))
    own, ghost_ops, back_ops, mass_ghost, rest_ghost, residual, packed = call(
        build_kernel,
        [
            shape(2, 2 * nodes + 2 * both, 3 * nodes, dtype=bf16),
            shape(2, 2 * nodes + 2 * both, 3 * both, dtype=bf16),
            shape(2, 2 * both, 3 * nodes, dtype=bf16),
            shape(nodes + both, 3 * both, dtype=bf16),
            shape(2, 2 * nodes + 2 * both, 3 * both, dtype=bf16),
            whole,
            packs,
        ],
        [info, state, plane_table, coef_table, rotation, squares, mass_blocks, stiff_blocks, twist_blocks, rates, conn, lists],
        scratch=[
            pltpu.VMEM((6 * nodes, planes), f32),
            pltpu.VMEM((6 * nodes, planes), bf16),
            pltpu.VMEM((6 * nodes, planes), bf16),
            pltpu.VMEM((6 * nodes, coefs), f32),
            pltpu.VMEM((5 * nodes, 6 * elements), f32),
        ],
        flops=6_000_000_000,
    )
    near, far, force = call(
        start_kernel,
        [ends, ends, packs],
        [info, near_state, far_state, packed, plane_table, coef_table, rotation, squares, mass_ghost, rest_ghost],
        scratch=[
            pltpu.VMEM((6 * both, planes), f32),
            pltpu.VMEM((6 * both, planes), bf16),
            pltpu.VMEM((6 * both, planes), bf16),
        ],
        flops=1_000_000_000,
    )
    near_now, far_now = swap_near(near), swap_far(far)
    vector0, image, packed, moments0 = call(
        first_kernel,
        [whole, whole, packs, shape(8, coefs)],
        [info, near_state, far_state, force, residual, mass_ghost, rest_ghost, own, squares],
        flops=2_000_000_000,
    )
    near, far = call(
        send_kernel, [ends, ends], [info, near_now, far_now, packed, ghost_ops, squares], flops=100_000_000
    )
    near_next, far_next = swap_near(near), swap_far(far)
    vector1, image, packed, moments1 = call(
        next_kernel,
        [whole, whole, packs, shape(16, coefs)],
        [info, near_now, far_now, image, vector0, own, ghost_ops, squares],
        flops=2_000_000_000,
    )
    near, far = call(
        send_kernel, [ends, ends], [info, near_next, far_next, packed, ghost_ops, squares], flops=100_000_000
    )
    near_last, far_last = swap_near(near), swap_far(far)
    vector2, back, moments2 = call(
        last_kernel,
        [whole, packs, shape(24, coefs)],
        [info, near_next, far_next, image, vector1, own, ghost_ops, back_ops, squares],
        flops=2_000_000_000,
    )
    moments = call(
        join_kernel, shape(40, coefs), [info, near_last, far_last, back, moments0, moments1, moments2]
    )
    if count == 16:
        total = moments + swap_near(moments)
        terms = [swapped(total, e, o) for e, o in ((4, 2), (8, 6), (12, 10), (2, 14))]
        others = jnp.where(odd == 1, terms[3], total)
        half = others + terms[0] + terms[1] + terms[2]
        total = half + swap_near(half)
    else:
        total = lax.psum(moments, "mesh")
    new_velocity, new_magnetic = call(
        finish_kernel,
        [shape(3, coefs, nodes), shape(3, coefs, nodes)],
        [total, velocity, magnetic, vector0, vector1, vector2],
        flops=10_000_000,
    )
    return new_velocity, new_magnetic


def solution(mesh):
    in_specs = (
        P("runs", None, "mesh"),
        P("runs", None, "mesh"),
        P(None, None, "mesh"),
        P(None, None, "mesh"),
        P(None, None, "mesh"),
        P(("runs", "mesh")),
        P(None, "mesh"),
        P(None, "mesh"),
    )
    out_specs = (P("runs", None, "mesh"), P("runs", None, "mesh"))
    sizes = dict(mesh.shape)
    step = functools.partial(local, sizes["runs"], sizes["mesh"])
    return jax.shard_map(step, mesh=mesh, in_specs=in_specs, out_specs=out_specs, check_vma=False)
```

time: 365 us -> 57.4 us (0.16); the launches traced: 360 us -> 57.1 us
  blocking collectives: 216 us -> 0 us
  matrix products: 53.6 us -> 0 us
  local copies, waits for them, and re-layouts: 46.9 us -> 4.3 us
  Pallas kernels: 0 us -> 20.9 us
  other arithmetic: 13.7 us -> 0.11 us
  waiting for transfers between devices: 0.03 us -> 9.95 us
  starting transfers between devices: 27.8 us -> 21 us
    psum x5 -> x0, blocking collectives: 216 us -> none  [the longest x3 135 us: squares(): return lax.psum(jnp.sum(vector * vector, axis=-1), 'mesh')]
    dot_general x28 -> x0, matrix products: 53.6 us -> none  [the longest x1 13.4 us: forcing_terms(): jnp.einsum('cj,kjn->kcn', forward, force_phys, precision=highest)]
    pallas_call x0 -> x10, Pallas kernels: none -> 20.9 us  [call(): pl.pallas_call(kernel, out_shape=outs, in_specs=specs, out_specs=VMEM if...]
    ppermute x10 -> x0, local copies, waits for them, and re-layouts: 18.2 us -> none  [the longest x5 10.9 us: extended(): lax.ppermute(lax.slice_in_dim(block, block.shape[dim] - width, None, axis...]
    gather x10 -> x0, local copies, waits for them, and re-layouts: 14 us -> none  [the longest x5 6.99 us: with_ghosts(): from_above = jnp.take(padded[..., 2 * node_count:], ghost_lists[1], axis=-1)]
    ppermute x10 -> x14, waiting for transfers between devices: 0.03 us -> 9.95 us  [the longest x4 5.63 us: swap_far(): return lax.ppermute(value, ('runs', 'mesh'), far_pairs)]
    dot_general x6 -> x0, local copies, waits for them, and re-layouts: 8.25 us -> none  [dense_operators(): jnp.einsum('gbe,bew->gew', blocks[:, row], columns, precision=highest)]
    ppermute x10 -> x14, starting transfers between devices: 27.8 us -> 21 us  [the longest x4 7.1 us: swapped(): return lax.ppermute(value, 'mesh', pairs)]
  transfers between devices with their start and end apart: 10 -> 14, of which waited for: 0 -> 6; matrix products, arithmetic and copies ran while one was open for 19% -> 0% of each run, Pallas kernels for 0% -> 25%
where the time goes in v1:
time: 57.4 us; the launch traced here: 57.1 us
  starting transfers between devices  21 us (37%)
  Pallas kernels  20.9 us (36%)
  waiting for transfers between devices  9.95 us (17%)
  local copies, waits for them, and re-layouts  4.3 us (7%)
  between operations  0.87 us (2%)
    pallas_call x10, Pallas kernels, call(): pl.pallas_call(kernel, out_shape=outs, in_specs=specs, out_specs=VMEM if...  20.9 us
    ppermute x4, starting transfers between devices, swapped(): return lax.ppermute(value, 'mesh', pairs)  7.1 us
    ppermute x4, starting transfers between devices, swap_far(): return lax.ppermute(value, ('runs', 'mesh'), far_pairs)  7.06 us
    ppermute x6, starting transfers between devices, swap_near(): return lax.ppermute(value, 'mesh', near_pairs)  6.8 us
    ppermute x4, waiting for transfers between devices, swap_far(): return lax.ppermute(value, ('runs', 'mesh'), far_pairs)  5.63 us
    unnamed x28, local copies, waits for them, and re-layouts  4.3 us
    ppermute x4, waiting for transfers between devices, swapped(): return lax.ppermute(value, 'mesh', pairs)  2.57 us
    ppermute x6, waiting for transfers between devices, swap_near(): return lax.ppermute(value, 'mesh', near_pairs)  1.75 us
  transfers between devices with their start and end apart: 14, of which 6 were waited for; matrix products, arithmetic and copies ran while one was open for 0% of the time, Pallas kernels for 25%

profile of v1, /device:TPU:0, one launch (start us, length us, event | category | flops | bytes accessed | tf_op | source)
XLA Modules:
  0.0 57.1 jit_solution(7213551966209302998)
XLA Ops:
  0.6 0.0 copy-start.5
  0.7 0.1 pad_add_fusion.info
  0.7 0.6 %copy-done.5 = s32[6,128]{1,0:T(8,128)S(1)} copy-done((s32[6,128]{1,0:T(8,128)S(1)}, s32[6,128]{1,0:T(8,128)}, u32[]{:S(2)}) %copy-start.5) | copy-done | bytes 3096
  1.3 0.0 copy-start
  1.3 1.0 %copy-done = f32[3,256,128]{2,1,0:T(8,128)S(1)} copy-done((f32[3,256,128]{2,1,0:T(8,128)S(1)}, f32[3,256,128]{2,1,0:T(8,128)}, u32[]{:S(2)}) %copy-start) | copy-done | bytes 393240
  2.3 0.0 copy-start.2
  2.3 1.0 %copy-done.2 = f32[3,256,128]{2,1,0:T(8,128)S(1)} copy-done((f32[3,256,128]{2,1,0:T(8,128)S(1)}, f32[3,256,128]{2,1,0:T(8,128)}, u32[]{:S(2)}) %copy-start.2) | copy-done | bytes 393240
  3.3 0.0 copy-start.13
  3.3 0.0 copy-start.6
  3.3 0.0 copy-start.7
  3.3 0.0 copy-start.8
  3.3 0.0 copy-start.10
  3.4 0.0 copy-start.12
  3.4 1.3 %shard_map.131 = (f32[6,32,256]{2,1,0:T(8,128)S(1)}, f32[6,32,256]{2,1,0:T(8,128)S(1)}, f32[6,128,256]{2,1,0:T(8,128)S(1)}) custom-call(s32[4]{0:T(128)S(1)} %pad_add_fusion.info, f32[3,256,128]{2,1,0:T(8,128)S(1)} %copy-done, f32[3,256,128]{2,1,0:T(8,128)S(1)} %copy-done.2, s32[6,128]{1,0:T(8,128)S(1)} %copy-done.5), custom_call_target="tpu_custom_call" | custom-call | bytes 1969168 | tf_op jit(solution)/shard_map/pallas_call | solution.py:436
  4.7 0.0 copy-start.4
  4.7 0.5 collective-permute-start
  5.2 2.6 %collective-permute-start.1 = (f32[6,32,256]{2,1,0:T(8,128)S(1)}, f32[6,32,256]{2,1,0:T(8,128)S(1)}, u32[]{:S(2)}, u32[]{:S(2)}) collective-permute-start(f32[6,32,256]{2,1,0:T(8,128)S(1)} %get-tuple-element.31), channel_id=1, source_target_pairs={{1,2},{2,1},{3,4},{4,3},{5,6},{6,5},{7,8},{8,7},{9,10},{10,9},{11,... | collective-permute-start | bytes 589832 | tf_op jit(solution)/shard_map/ppermute | solution.py:483
  7.8 0.0 copy-done.13
  7.8 0.0 copy-done.6
  7.8 0.0 copy-done.7
  7.8 0.0 copy-done.8
  7.8 0.0 copy-done.10
  7.8 0.0 copy-done.12
  7.8 0.0 copy-done.4
  7.8 0.6 %copy-done.9 = s32[2,32]{1,0:T(2,128)S(1)} copy-done((s32[2,32]{1,0:T(2,128)S(1)}, s32[2,32]{1,0:T(2,128)}, u32[]{:S(2)}) %copy-start.9) | copy-done | bytes 280
  8.5 1.0 %copy-done.11 = bf16[512,512]{1,0:T(8,128)(2,1)S(1)} copy-done((bf16[512,512]{1,0:T(8,128)(2,1)S(1)}, bf16[512,512]{1,0:T(8,128)(2,1)}, u32[]{:S(2)}) %copy-start.11) | copy-done | bytes 524312
  9.5 7.2 %shard_map.132 = (bf16[2,384,384]{2,1,0:T(8,128)(2,1)S(1)}, bf16[2,384,192]{2,1,0:T(8,128)(2,1)S(1)}, bf16[2,128,384]{2,1,0:T(8,128)(2,1)S(1)}, bf16[192,192]{1,...) custom-call(s32[4]{0:T(128)S(1)} %pad_add_fusion.info, ...), custom_call_target="tpu_custom_call" | custom-call | flops 6000000000 | bytes 4551952 | tf_op jit(solution)/shard_map/pallas_call | solution.py:436
  16.7 0.0 collective-permute-done.near
  16.7 0.0 collective-permute-done.1.far
  16.7 2.2 %shard_map.133 = (f32[6,32,256]{2,1,0:T(8,128)S(1)}, f32[6,32,256]{2,1,0:T(8,128)S(1)}, f32[6,64,256]{2,1,0:T(8,128)S(1)}) custom-call(s32[4]{0:T(128)S(1)} %pad_add_fusion.info, f32[6,32,256]{2,1,0:T(8,128)S(1)} %collective-permute-done.near, f32[6,32,256]{2,1,0:T(8,128)S(1)} %collective-permute-done.1.far, f32[6,64,256]{2,1,0:T(8,128)S(1)} %get-tuple-element.33.packed, ...), custom_call_target="tpu_custom_call" | custom-call | flops 1000000000 | bytes 3014672 | tf_op jit(solution)/shard_map/pallas_call | solution.py:436
  19.0 0.2 collective-permute-start.2
  19.2 1.5 %collective-permute-start.3 = (f32[6,32,256]{2,1,0:T(8,128)S(1)}, f32[6,32,256]{2,1,0:T(8,128)S(1)}, u32[]{:S(2)}, u32[]{:S(2)}) collective-permute-start(f32[6,32,256]{2,1,0:T(8,128)S(1)} %get-tuple-element.37), channel_id=1, source_target_pairs={{1,2},{2,1},{3,4},{4,3},{5,6},{6,5},{7,8},{8,7},{9,10},{10,9},{11,... | collective-permute-start | bytes 589832 | tf_op jit(solution)/shard_map/ppermute | solution.py:483
  20.7 2.2 %shard_map.134 = (f32[6,128,256]{2,1,0:T(8,128)S(1)}, f32[6,128,256]{2,1,0:T(8,128)S(1)}, f32[6,64,256]{2,1,0:T(8,128)S(1)}, f32[8,256]{1,0:T(8,128)S(1)}) custom-call(s32[4]{0:T(128)S(1)} %pad_add_fusion.info, f32[6,32,256]{2,1,0:T(8,128)S(1)} %collective-permute-done.near, f32[6,32,256]{2,1,0:T(8,128)S(1)} %collective-permute-done.1.far, ...), custom_call_target="tpu_custom_call" | custom-call | flops 2000000000 | bytes 4513808 | tf_op jit(solution)/shard_map/pallas_call | solution.py:436
  22.8 0.0 collective-permute-done.2.near
  22.8 2.0 %collective-permute-done.3.far = f32[6,32,256]{2,1,0:T(8,128)S(1)} collective-permute-done((f32[6,32,256]{2,1,0:T(8,128)S(1)}, f32[6,32,256]{2,1,0:T(8,128)S(1)}, u32[]{:S(2)}, u32[]{:S(2)}) %collective-permute-start.3) | collective-permute-done | bytes 196640 | tf_op jit(solution)/shard_map/ppermute | solution.py:483
  24.8 0.8 %shard_map.135 = (f32[6,32,256]{2,1,0:T(8,128)S(1)}, f32[6,32,256]{2,1,0:T(8,128)S(1)}) custom-call(s32[4]{0:T(128)S(1)} %pad_add_fusion.info, f32[6,32,256]{2,1,0:T(8,128)S(1)} %collective-permute-done.2.near, f32[6,32,256]{2,1,0:T(8,128)S(1)} %collective-permute-done.3.far, f32[6,64,256]{2,1,0:T(8,128)S(1)} %get-tuple-element.41.packed, ...), custom_call_target="tpu_custom_call" | custom-call | flops 100000000 | bytes 1482768 | tf_op jit(solution)/shard_map/pallas_call | solution.py:436
  25.7 0.8 %collective-permute-start.4 = (f32[6,32,256]{2,1,0:T(8,128)S(1)}, f32[6,32,256]{2,1,0:T(8,128)S(1)}, u32[]{:S(2)}, u32[]{:S(2)}) collective-permute-start(f32[6,32,256]{2,1,0:T(8,128)S(1)} %get-tuple-element.43), channel_id=1, source_target_pairs={{0,1},{1,0},{2,3},{3,2},{4,5},{5,4},{6,7},{7,6},{8,9},{9,8},{10,11... | collective-permute-start | bytes 589832 | tf_op jit(solution)/shard_map/ppermute | solution.py:480
  26.4 1.5 %collective-permute-start.5 = (f32[6,32,256]{2,1,0:T(8,128)S(1)}, f32[6,32,256]{2,1,0:T(8,128)S(1)}, u32[]{:S(2)}, u32[]{:S(2)}) collective-permute-start(f32[6,32,256]{2,1,0:T(8,128)S(1)} %get-tuple-element.44), channel_id=1, source_target_pairs={{1,2},{2,1},{3,4},{4,3},{5,6},{6,5},{7,8},{8,7},{9,10},{10,9},{11,... | collective-permute-start | bytes 589832 | tf_op jit(solution)/shard_map/ppermute | solution.py:483
  27.9 2.1 %shard_map.136 = (f32[6,128,256]{2,1,0:T(8,128)S(1)}, f32[6,128,256]{2,1,0:T(8,128)S(1)}, f32[6,64,256]{2,1,0:T(8,128)S(1)}, f32[16,256]{1,0:T(8,128)S(1)}) custom-call(s32[4]{0:T(128)S(1)} %pad_add_fusion.info, f32[6,32,256]{2,1,0:T(8,128)S(1)} %collective-permute-done.2.near, f32[6,32,256]{2,1,0:T(8,128)S(1)} %collective-permute-done.3.far, ...), custom_call_target="tpu_custom_call" | custom-call | flops 2000000000 | bytes 4841488 | tf_op jit(solution)/shard_map/pallas_call | solution.py:436
  30.0 0.0 collective-permute-done.4.near
  30.0 2.1 %collective-permute-done.5.far = f32[6,32,256]{2,1,0:T(8,128)S(1)} collective-permute-done((f32[6,32,256]{2,1,0:T(8,128)S(1)}, f32[6,32,256]{2,1,0:T(8,128)S(1)}, u32[]{:S(2)}, u32[]{:S(2)}) %collective-permute-start.5) | collective-permute-done | bytes 196640 | tf_op jit(solution)/shard_map/ppermute | solution.py:483
  32.1 0.8 %shard_map.137 = (f32[6,32,256]{2,1,0:T(8,128)S(1)}, f32[6,32,256]{2,1,0:T(8,128)S(1)}) custom-call(s32[4]{0:T(128)S(1)} %pad_add_fusion.info, f32[6,32,256]{2,1,0:T(8,128)S(1)} %collective-permute-done.4.near, f32[6,32,256]{2,1,0:T(8,128)S(1)} %collective-permute-done.5.far, f32[6,64,256]{2,1,0:T(8,128)S(1)} %get-tuple-element.47.packed, ...), custom_call_target="tpu_custom_call" | custom-call | flops 100000000 | bytes 1482768 | tf_op jit(solution)/shard_map/pallas_call | solution.py:436
  32.9 1.7 %collective-permute-start.6 = (f32[6,32,256]{2,1,0:T(8,128)S(1)}, f32[6,32,256]{2,1,0:T(8,128)S(1)}, u32[]{:S(2)}, u32[]{:S(2)}) collective-permute-start(f32[6,32,256]{2,1,0:T(8,128)S(1)} %get-tuple-element.48), channel_id=1, source_target_pairs={{0,1},{1,0},{2,3},{3,2},{4,5},{5,4},{6,7},{7,6},{8,9},{9,8},{10,11... | collective-permute-start | bytes 589832 | tf_op jit(solution)/shard_map/ppermute | solution.py:480
  34.6 1.5 %collective-permute-start.7 = (f32[6,32,256]{2,1,0:T(8,128)S(1)}, f32[6,32,256]{2,1,0:T(8,128)S(1)}, u32[]{:S(2)}, u32[]{:S(2)}) collective-permute-start(f32[6,32,256]{2,1,0:T(8,128)S(1)} %get-tuple-element.49), channel_id=1, source_target_pairs={{1,2},{2,1},{3,4},{4,3},{5,6},{6,5},{7,8},{8,7},{9,10},{10,9},{11,... | collective-permute-start | bytes 589832 | tf_op jit(solution)/shard_map/ppermute | solution.py:483
  36.1 2.6 %shard_map.138 = (f32[6,128,256]{2,1,0:T(8,128)S(1)}, f32[6,64,256]{2,1,0:T(8,128)S(1)}, f32[24,256]{1,0:T(8,128)S(1)}) custom-call(s32[4]{0:T(128)S(1)} %pad_add_fusion.info, f32[6,32,256]{2,1,0:T(8,128)S(1)} %collective-permute-done.4.near, f32[6,32,256]{2,1,0:T(8,128)S(1)} %collective-permute-done.5.far, f32[6,128,256]{2,1,0:T(8,128)S(1)} %get-tuple-element.50.image, ...), custom_call_target="tpu_custom_call" | custom-call | flops 2000000000 | bytes 4259856 | tf_op jit(solution)/shard_map/pallas_call | solution.py:436
  38.7 0.0 collective-permute-done.6.near
  38.7 1.6 %collective-permute-done.7.far = f32[6,32,256]{2,1,0:T(8,128)S(1)} collective-permute-done((f32[6,32,256]{2,1,0:T(8,128)S(1)}, f32[6,32,256]{2,1,0:T(8,128)S(1)}, u32[]{:S(2)}, u32[]{:S(2)}) %collective-permute-start.7) | collective-permute-done | bytes 196640 | tf_op jit(solution)/shard_map/ppermute | solution.py:483
  40.2 0.6 %shard_map.139 = f32[40,256]{1,0:T(8,128)S(1)} custom-call(s32[4]{0:T(128)S(1)} %pad_add_fusion.info, f32[6,32,256]{2,1,0:T(8,128)S(1)} %collective-permute-done.6.near, f32[6,32,256]{2,1,0:T(8,128)S(1)} %collective-permute-done.7.far, f32[6,64,256]{2,1,0:T(8,128)S(1)} %get-tuple-element.53.back, f32[8,256]{1,0:T(8,128)S(1)} %get-tuple-element.54.first, ...), custom_call_target="tpu_custom_call" | custom-call | bytes 876560 | tf_op jit(solution)/shard_map/pallas_call | solution.py:436
  40.8 0.0 copy-start.1
  40.8 1.7 %collective-permute-start.8 = (f32[40,256]{1,0:T(8,128)S(1)}, f32[40,256]{1,0:T(8,128)S(1)}, u32[]{:S(2)}, u32[]{:S(2)}) collective-permute-start(f32[40,256]{1,0:T(8,128)S(1)} %shard_map.139), channel_id=1, source_target_pairs={{0,1},{1,0},{2,3},{3,2},{4,5},{5,4},{6,7},{7,6},{8,9},{9,8},{10,11... | collective-permute-start | bytes 122888 | tf_op jit(solution)/shard_map/ppermute | solution.py:480
  42.5 0.9 %collective-permute-done.8 = f32[40,256]{1,0:T(8,128)S(1)} collective-permute-done((f32[40,256]{1,0:T(8,128)S(1)}, f32[40,256]{1,0:T(8,128)S(1)}, u32[]{:S(2)}, u32[]{:S(2)}) %collective-permute-start.8) | collective-permute-done | bytes 40992 | tf_op jit(solution)/shard_map/ppermute | solution.py:480
  43.4 4.8 %collective-permute-start.12 = (f32[40,256]{1,0:T(8,128)S(1)}, f32[40,256]{1,0:T(8,128)S(1)}, u32[]{:S(2)}, u32[]{:S(2)}) collective-permute-start(f32[40,256]{1,0:T(8,128)S(1)} %add.20), channel_id=1, source_target_pairs={{0,12},{1,11},{2,14},{3,9},{4,8},{5,15},{6,10},{7,13},{8,4},{9,3},... | collective-permute-start | bytes 122888 | tf_op jit(solution)/shard_map/ppermute | solution.py:487
  48.2 0.0 collective-permute-start.11
  48.2 0.6 %collective-permute-start.10 = (f32[40,256]{1,0:T(8,128)S(1)}, f32[40,256]{1,0:T(8,128)S(1)}, u32[]{:S(2)}, u32[]{:S(2)}) collective-permute-start(f32[40,256]{1,0:T(8,128)S(1)} %add.20), channel_id=1, source_target_pairs={{0,4},{1,3},{2,6},{3,1},{4,0},{5,7},{6,2},{7,5},{8,12},{9,11},{10,... | collective-permute-start | bytes 122888 | tf_op jit(solution)/shard_map/ppermute | solution.py:487
  48.8 1.7 %collective-permute-start.9 = (f32[40,256]{1,0:T(8,128)S(1)}, f32[40,256]{1,0:T(8,128)S(1)}, u32[]{:S(2)}, u32[]{:S(2)}) collective-permute-start(f32[40,256]{1,0:T(8,128)S(1)} %add.20), channel_id=1, source_target_pairs={{0,2},{1,15},{2,0},{3,13},{4,6},{5,11},{6,4},{7,9},{8,10},{9,7},{1... | collective-permute-start | bytes 122888 | tf_op jit(solution)/shard_map/ppermute | solution.py:487
  50.5 0.0 collective-permute-done.12
  50.5 2.6 %collective-permute-done.11 = f32[40,256]{1,0:T(8,128)S(1)} collective-permute-done((f32[40,256]{1,0:T(8,128)S(1)}, f32[40,256]{1,0:T(8,128)S(1)}, u32[]{:S(2)}, u32[]{:S(2)}) %collective-permute-start.11) | collective-permute-done | bytes 40992 | tf_op jit(solution)/shard_map/ppermute | solution.py:487
  53.1 0.0 collective-permute-done.10
  53.1 0.0 collective-permute-done.9
  53.1 2.0 %collective-permute-start.13 = (f32[40,256]{1,0:T(8,128)S(1)}, f32[40,256]{1,0:T(8,128)S(1)}, u32[]{:S(2)}, u32[]{:S(2)}) collective-permute-start(f32[40,256]{1,0:T(8,128)S(1)} %add_add_fusion), channel_id=1, source_target_pairs={{0,1},{1,0},{2,3},{3,2},{4,5},{5,4},{6,7},{7,6},{8,9},{9,8},{10,11... | collective-permute-start | bytes 122888 | tf_op jit(solution)/shard_map/ppermute | solution.py:480
  55.1 0.9 %collective-permute-done.13 = f32[40,256]{1,0:T(8,128)S(1)} collective-permute-done((f32[40,256]{1,0:T(8,128)S(1)}, f32[40,256]{1,0:T(8,128)S(1)}, u32[]{:S(2)}, u32[]{:S(2)}) %collective-permute-start.13) | collective-permute-done | bytes 40992 | tf_op jit(solution)/shard_map/ppermute | solution.py:480
  55.9 0.0 copy-done.3
  55.9 0.0 copy-done.1
  56.0 1.1 %shard_map.140 = (f32[3,256,128]{2,1,0:T(8,128)}, f32[3,256,128]{2,1,0:T(8,128)}) custom-call(f32[40,256]{1,0:T(8,128)S(1)} %add.24.moments, f32[3,256,128]{2,1,0:T(8,128)S(1)} %copy-done.1, f32[3,256,128]{2,1,0:T(8,128)S(1)} %copy-done.3, f32[6,128,256]{2,1,0:T(8,128)S(1)} %get-tuple-element.46.before.first, ...), custom_call_target="tpu_custom_call" | custom-call | flops 10000000 | bytes 3973120 | tf_op jit(solution)/shard_map/pallas_call | solution.py:436
  (7 shorter events, 0.0 us)
Async XLA Ops:
  0.6 0.7 %copy-start.5 = (s32[6,128]{1,0:T(8,128)S(1)}, s32[6,128]{1,0:T(8,128)}, u32[]{:S(2)}) copy-start(s32[6,128]{1,0:T(8,128)} %conn_ref.3) | copy-start | bytes 9220
  1.3 1.0 %copy-start = (f32[3,256,128]{2,1,0:T(8,128)S(1)}, f32[3,256,128]{2,1,0:T(8,128)}, u32[]{:S(2)}) copy-start(f32[3,256,128]{2,1,0:T(8,128)} %velocity.3) | copy-start | bytes 1179652
  2.3 1.0 %copy-start.2 = (f32[3,256,128]{2,1,0:T(8,128)S(1)}, f32[3,256,128]{2,1,0:T(8,128)}, u32[]{:S(2)}) copy-start(f32[3,256,128]{2,1,0:T(8,128)} %magnetic.3) | copy-start | bytes 1179652
  3.3 4.5 %copy-start.13 = (f32[128]{0:T(128)S(1)}, f32[128]{0:T(128)}, u32[]{:S(2)}) copy-start(f32[128]{0:T(128)} %param.17) | copy-start | bytes 1540
  3.3 4.5 %copy-start.6 = (f32[6,6,128]{2,1,0:T(8,128)S(1)}, f32[6,6,128]{2,1,0:T(8,128)}, u32[]{:S(2)}) copy-start(f32[6,6,128]{2,1,0:T(8,128)} %mass_ref.1) | copy-start | bytes 55300
  3.3 4.5 %copy-start.7 = (f32[6,6,128]{2,1,0:T(8,128)S(1)}, f32[6,6,128]{2,1,0:T(8,128)}, u32[]{:S(2)}) copy-start(f32[6,6,128]{2,1,0:T(8,128)} %stiff_ref.1) | copy-start | bytes 55300
  3.3 4.5 %copy-start.8 = (f32[6,6,128]{2,1,0:T(8,128)S(1)}, f32[6,6,128]{2,1,0:T(8,128)}, u32[]{:S(2)}) copy-start(f32[6,6,128]{2,1,0:T(8,128)} %twist_ref.1) | copy-start | bytes 55300
  3.3 4.5 %copy-start.10 = (bf16[1024,256]{1,0:T(8,128)(2,1)S(1)}, bf16[1024,256]{1,0:T(8,128)(2,1)}, u32[]{:S(2)}) copy-start(bf16[1024,256]{1,0:T(8,128)(2,1)} %constant.30.clone.coefs_ref) | copy-start | bytes 1572868
  3.4 4.5 %copy-start.12 = (f32[8,512]{1,0:T(8,128)S(1)}, f32[8,512]{1,0:T(8,128)}, u32[]{:S(2)}) copy-start(f32[8,512]{1,0:T(8,128)} %constant.31.clone.rotation_ref) | copy-start | bytes 49156
  4.7 3.1 %copy-start.4 = (f32[8,256]{1,0:T(8,128)S(1)}, f32[8,256]{1,0:T(8,128)}, u32[]{:S(2)}) copy-start(f32[8,256]{1,0:T(8,128)} %constant.32.clone.squares_ref) | copy-start | bytes 24580
  4.7 12.0 %collective-permute-start = (f32[6,32,256]{2,1,0:T(8,128)S(1)}, f32[6,32,256]{2,1,0:T(8,128)S(1)}, u32[]{:S(2)}, u32[]{:S(2)}) collective-permute-start(f32[6,32,256]{2,1,0:T(8,128)S(1)} %get-tuple-element.30), channel_id=1, source_target_pairs={{0,1},{1,0},{2,3},{3,2},{4,5},{5,4},{6,7},{7,6},{8,9},{9,8},{10,11... | collective-permute-start | bytes 589832 | tf_op jit(solution)/shard_map/ppermute | solution.py:480
  5.2 11.5 %collective-permute-start.1 = (f32[6,32,256]{2,1,0:T(8,128)S(1)}, f32[6,32,256]{2,1,0:T(8,128)S(1)}, u32[]{:S(2)}, u32[]{:S(2)}) collective-permute-start(f32[6,32,256]{2,1,0:T(8,128)S(1)} %get-tuple-element.31), channel_id=1, source_target_pairs={{1,2},{2,1},{3,4},{4,3},{5,6},{6,5},{7,8},{8,7},{9,10},{10,9},{11,... | collective-permute-start | bytes 589832 | tf_op jit(solution)/shard_map/ppermute | solution.py:483
  7.8 0.7 %copy-start.9 = (s32[2,32]{1,0:T(2,128)S(1)}, s32[2,32]{1,0:T(2,128)}, u32[]{:S(2)}) copy-start(s32[2,32]{1,0:T(2,128)} %lists_ref.1) | copy-start | bytes 772
  8.5 1.0 %copy-start.11 = (bf16[512,512]{1,0:T(8,128)(2,1)S(1)}, bf16[512,512]{1,0:T(8,128)(2,1)}, u32[]{:S(2)}) copy-start(bf16[512,512]{1,0:T(8,128)(2,1)} %constant.29.clone.planes_ref) | copy-start | bytes 1572868
  19.0 3.9 %collective-permute-start.2 = (f32[6,32,256]{2,1,0:T(8,128)S(1)}, f32[6,32,256]{2,1,0:T(8,128)S(1)}, u32[]{:S(2)}, u32[]{:S(2)}) collective-permute-start(f32[6,32,256]{2,1,0:T(8,128)S(1)} %get-tuple-element.36), channel_id=1, source_target_pairs={{0,1},{1,0},{2,3},{3,2},{4,5},{5,4},{6,7},{7,6},{8,9},{9,8},{10,11... | collective-permute-start | bytes 589832 | tf_op jit(solution)/shard_map/ppermute | solution.py:480
  19.2 5.7 %collective-permute-start.3 = (f32[6,32,256]{2,1,0:T(8,128)S(1)}, f32[6,32,256]{2,1,0:T(8,128)S(1)}, u32[]{:S(2)}, u32[]{:S(2)}) collective-permute-start(f32[6,32,256]{2,1,0:T(8,128)S(1)} %get-tuple-element.37), channel_id=1, source_target_pairs={{1,2},{2,1},{3,4},{4,3},{5,6},{6,5},{7,8},{8,7},{9,10},{10,9},{11,... | collective-permute-start | bytes 589832 | tf_op jit(solution)/shard_map/ppermute | solution.py:483
  25.7 4.3 %collective-permute-start.4 = (f32[6,32,256]{2,1,0:T(8,128)S(1)}, f32[6,32,256]{2,1,0:T(8,128)S(1)}, u32[]{:S(2)}, u32[]{:S(2)}) collective-permute-start(f32[6,32,256]{2,1,0:T(8,128)S(1)} %get-tuple-element.43), channel_id=1, source_target_pairs={{0,1},{1,0},{2,3},{3,2},{4,5},{5,4},{6,7},{7,6},{8,9},{9,8},{10,11... | collective-permute-start | bytes 589832 | tf_op jit(solution)/shard_map/ppermute | solution.py:480
  26.4 5.7 %collective-permute-start.5 = (f32[6,32,256]{2,1,0:T(8,128)S(1)}, f32[6,32,256]{2,1,0:T(8,128)S(1)}, u32[]{:S(2)}, u32[]{:S(2)}) collective-permute-start(f32[6,32,256]{2,1,0:T(8,128)S(1)} %get-tuple-element.44), channel_id=1, source_target_pairs={{1,2},{2,1},{3,4},{4,3},{5,6},{6,5},{7,8},{8,7},{9,10},{10,9},{11,... | collective-permute-start | bytes 589832 | tf_op jit(solution)/shard_map/ppermute | solution.py:483
  32.9 5.8 %collective-permute-start.6 = (f32[6,32,256]{2,1,0:T(8,128)S(1)}, f32[6,32,256]{2,1,0:T(8,128)S(1)}, u32[]{:S(2)}, u32[]{:S(2)}) collective-permute-start(f32[6,32,256]{2,1,0:T(8,128)S(1)} %get-tuple-element.48), channel_id=1, source_target_pairs={{0,1},{1,0},{2,3},{3,2},{4,5},{5,4},{6,7},{7,6},{8,9},{9,8},{10,11... | collective-permute-start | bytes 589832 | tf_op jit(solution)/shard_map/ppermute | solution.py:480
  34.6 5.7 %collective-permute-start.7 = (f32[6,32,256]{2,1,0:T(8,128)S(1)}, f32[6,32,256]{2,1,0:T(8,128)S(1)}, u32[]{:S(2)}, u32[]{:S(2)}) collective-permute-start(f32[6,32,256]{2,1,0:T(8,128)S(1)} %get-tuple-element.49), channel_id=1, source_target_pairs={{1,2},{2,1},{3,4},{4,3},{5,6},{6,5},{7,8},{8,7},{9,10},{10,9},{11,... | collective-permute-start | bytes 589832 | tf_op jit(solution)/shard_map/ppermute | solution.py:483
  40.2 15.7 %copy-start.3 = (f32[3,256,128]{2,1,0:T(8,128)S(1)}, f32[3,256,128]{2,1,0:T(8,128)}, u32[]{:S(2)}) copy-start(f32[3,256,128]{2,1,0:T(8,128)} %magnetic.3) | copy-start | bytes 1179652
  40.8 15.1 %copy-start.1 = (f32[3,256,128]{2,1,0:T(8,128)S(1)}, f32[3,256,128]{2,1,0:T(8,128)}, u32[]{:S(2)}) copy-start(f32[3,256,128]{2,1,0:T(8,128)} %velocity.3) | copy-start | bytes 1179652
  40.8 2.6 %collective-permute-start.8 = (f32[40,256]{1,0:T(8,128)S(1)}, f32[40,256]{1,0:T(8,128)S(1)}, u32[]{:S(2)}, u32[]{:S(2)}) collective-permute-start(f32[40,256]{1,0:T(8,128)S(1)} %shard_map.139), channel_id=1, source_target_pairs={{0,1},{1,0},{2,3},{3,2},{4,5},{5,4},{6,7},{7,6},{8,9},{9,8},{10,11... | collective-permute-start | bytes 122888 | tf_op jit(solution)/shard_map/ppermute | solution.py:480
  43.4 7.1 %collective-permute-start.12 = (f32[40,256]{1,0:T(8,128)S(1)}, f32[40,256]{1,0:T(8,128)S(1)}, u32[]{:S(2)}, u32[]{:S(2)}) collective-permute-start(f32[40,256]{1,0:T(8,128)S(1)} %add.20), channel_id=1, source_target_pairs={{0,12},{1,11},{2,14},{3,9},{4,8},{5,15},{6,10},{7,13},{8,4},{9,3},... | collective-permute-start | bytes 122888 | tf_op jit(solution)/shard_map/ppermute | solution.py:487
  48.2 4.9 %collective-permute-start.11 = (f32[40,256]{1,0:T(8,128)S(1)}, f32[40,256]{1,0:T(8,128)S(1)}, u32[]{:S(2)}, u32[]{:S(2)}) collective-permute-start(f32[40,256]{1,0:T(8,128)S(1)} %add.20), channel_id=1, source_target_pairs={{0,8},{1,7},{2,10},{3,5},{4,12},{5,3},{6,14},{7,1},{8,0},{9,15},{1... | collective-permute-start | bytes 122888 | tf_op jit(solution)/shard_map/ppermute | solution.py:487
  48.2 4.9 %collective-permute-start.10 = (f32[40,256]{1,0:T(8,128)S(1)}, f32[40,256]{1,0:T(8,128)S(1)}, u32[]{:S(2)}, u32[]{:S(2)}) collective-permute-start(f32[40,256]{1,0:T(8,128)S(1)} %add.20), channel_id=1, source_target_pairs={{0,4},{1,3},{2,6},{3,1},{4,0},{5,7},{6,2},{7,5},{8,12},{9,11},{10,... | collective-permute-start | bytes 122888 | tf_op jit(solution)/shard_map/ppermute | solution.py:487
  48.8 4.3 %collective-permute-start.9 = (f32[40,256]{1,0:T(8,128)S(1)}, f32[40,256]{1,0:T(8,128)S(1)}, u32[]{:S(2)}, u32[]{:S(2)}) collective-permute-start(f32[40,256]{1,0:T(8,128)S(1)} %add.20), channel_id=1, source_target_pairs={{0,2},{1,15},{2,0},{3,13},{4,6},{5,11},{6,4},{7,9},{8,10},{9,7},{1... | collective-permute-start | bytes 122888 | tf_op jit(solution)/shard_map/ppermute | solution.py:487
  53.1 2.8 %collective-permute-start.13 = (f32[40,256]{1,0:T(8,128)S(1)}, f32[40,256]{1,0:T(8,128)S(1)}, u32[]{:S(2)}, u32[]{:S(2)}) collective-permute-start(f32[40,256]{1,0:T(8,128)S(1)} %add_add_fusion), channel_id=1, source_target_pairs={{0,1},{1,0},{2,3},{3,2},{4,5},{5,4},{6,7},{7,6},{8,9},{9,8},{10,11... | collective-permute-start | bytes 122888 | tf_op jit(solution)/shard_map/ppermute | solution.py:480

commit v2 on v1

v2 whole, which is shorter than its diff:
```python
import functools
import math

import jax
import jax.numpy as jnp
import ml_dtypes
import numpy as np
from jax import lax
from jax.experimental import pallas as pl
from jax.experimental.pallas import tpu as pltpu
from jax.sharding import PartitionSpec as P

viscosity = 2.0
inverse_step = 10.0
tilt_factor = 0.5
axial_factor = 1.0
lorentz_factor = 0.005
epsilon = 1e-06
basis_scale = 512.0

f32 = jnp.float32
bf16 = jnp.bfloat16
VMEM = pl.BlockSpec(memory_space=pltpu.VMEM)
SMEM = pl.BlockSpec(memory_space=pltpu.SMEM)


def split_table(table):
    high = table.astype(np.float32).astype(ml_dtypes.bfloat16)
    low = (table - high.astype(np.float64)).astype(np.float32).astype(ml_dtypes.bfloat16)
    return high, low


def transform_tables(coefs):
    planes = 2 * coefs
    mode = np.arange(coefs) // 2
    turns = (np.arange(planes)[:, None] * mode[None, :]) % planes
    angles = 2.0 * math.pi / planes * turns
    inverse = np.where(np.arange(coefs)[None, :] % 2 == 0, np.cos(angles), np.sin(angles))
    weight = np.where(mode == 0, 1.0, 2.0) / planes
    to_planes = np.concatenate(split_table(inverse.T.copy()), axis=0)
    to_coefs = np.concatenate(split_table(inverse * weight[None, :]), axis=0)
    phi = 2.0 * math.pi / planes * np.arange(planes)
    rows = np.zeros((8, planes), np.float32)
    rows[0] = -2.0 * tilt_factor * np.cos(phi)
    rows[1] = 2.0 * tilt_factor * np.sin(phi)
    rows[2] = -2.0 * axial_factor
    squares = np.zeros((8, coefs), np.float32)
    squares[:] = (mode * mode).astype(np.float32)[None, :]
    return to_planes, to_coefs, rows, squares


def halves(value):
    high = value.astype(bf16)
    return high, (value - high.astype(f32)).astype(bf16)


def dot(first, second):
    return lax.dot_general(first, second, (((1,), (0,)), ((), ())), preferred_element_type=f32)


def dot_nt(first, second):
    return lax.dot_general(first, second, (((1,), (1,)), ((), ())), preferred_element_type=f32)


def stacked_columns(value):
    high, low = halves(value)
    return jnp.concatenate([high, low, high], axis=1)


def stacked_rows(value):
    high, low = halves(value)
    return jnp.concatenate([high, high, low], axis=0)


def iota(shape, dim):
    return lax.broadcasted_iota(jnp.int32, shape, dim)


def one_hot(conn, first, count):
    row = iota((count, conn.shape[1]), 0) + first
    return jnp.concatenate([(row == conn[a : a + 1, :]).astype(bf16) for a in range(6)], axis=1)


def element_sides(conn, nodes, ghosts):
    own = jnp.max((conn < nodes).astype(f32), axis=0, keepdims=True)
    low = jnp.max(((conn >= nodes) & (conn < nodes + ghosts)).astype(f32), axis=0, keepdims=True)
    high = jnp.max((conn >= nodes + ghosts).astype(f32), axis=0, keepdims=True)
    return own, low, high


def eight_rows(items):
    row = iota((8, items[0].shape[1]), 0)
    total = jnp.zeros(row.shape, f32)
    for i, item in enumerate(items):
        total = jnp.where(row == i, item, total)
    return total


def pack_matrix(conn, odd, nodes, ghosts):
    _, low, high = element_sides(conn, nodes, ghosts)
    sides = eight_rows([low, high]).astype(bf16)
    sides = jnp.concatenate([sides] * 6, axis=1)
    named = dot_nt(sides, one_hot(conn, 0, nodes))
    flags = jnp.where(named > 0.0, 1.0, 0.0)
    before = (iota((nodes, nodes), 0) < iota((nodes, nodes), 1)).astype(bf16)
    ranks = dot(flags.astype(bf16), before).astype(jnp.int32)
    rows = iota((2 * ghosts, nodes), 0)
    picks = []
    for side in range(2):
        offset = (1 - odd) * ghosts if side == 0 else odd * ghosts
        rank = ranks[side : side + 1, :]
        rank = jnp.where((flags[side : side + 1, :] > 0.0) & (rank < ghosts), rank + offset, -1)
        picks.append(rows == rank)
    return jnp.where(picks[0] | picks[1], 1.0, 0.0).astype(bf16)


def slot_matrix(conn, lists, odd, low_valid, high_valid, nodes, ghosts):
    own, _, _ = element_sides(conn, nodes, ghosts)
    owns = jnp.concatenate([eight_rows([own]).astype(bf16)] * 6, axis=1)
    slots = one_hot(conn, nodes, 2 * ghosts)
    active_rows = jnp.where(dot_nt(owns, slots) > 0.0, 1.0, 0.0)
    active_columns = jnp.where(dot_nt(slots, owns) > 0.0, 1.0, 0.0)
    numbers = eight_rows([lists[0:1, :].astype(f32), lists[1:2, :].astype(f32)]).astype(bf16)
    eye = (iota((ghosts, ghosts), 0) == iota((ghosts, ghosts), 1)).astype(bf16)
    columns = dot_nt(eye, numbers)
    parts = []
    for side in range(2):
        span = slice(side * ghosts, (side + 1) * ghosts)
        smaller = (lists[side : side + 1, :].astype(f32) < columns[:, side : side + 1]).astype(bf16)
        rank = dot_nt(smaller, active_rows[:, span].astype(bf16))[:, 0:1].astype(jnp.int32)
        offset = (1 - odd) * ghosts if side == 0 else odd * ghosts
        valid = low_valid if side == 0 else high_valid
        live = (active_columns[span, 0:1] > 0.0) & (valid > 0)
        rows = iota((ghosts, 2 * ghosts), 1)
        parts.append(jnp.where(live & (rows == rank + offset), 1.0, 0.0))
    return jnp.concatenate(parts, axis=0).astype(bf16)


def pack_kernel(
    info, velocity, magnetic, conn_ref, near_ref, far_ref, state_ref, pick_ref, values, arrived
):
    nodes = velocity.shape[2]
    ghosts = near_ref.shape[1]
    copies = []
    for k in range(6):
        source = velocity if k < 3 else magnetic
        copy = pltpu.make_async_copy(source.at[k % 3], values.at[k], arrived.at[k])
        copy.start()
        copies.append(copy)
    pick = pack_matrix(conn_ref[...], info[0], nodes, ghosts)
    pick_ref[...] = pick
    for k in range(6):
        copies[k].wait()
        block = jnp.transpose(values[k])
        state_ref[k] = block
        first, rest = halves(block)
        second = (block - first.astype(f32) - rest.astype(f32)).astype(bf16)
        packed = dot(pick, first) + dot(pick, rest) + dot(pick, second)
        near_ref[k] = packed[:ghosts]
        far_ref[k] = packed[ghosts:]


def to_planes(high, low, table):
    coefs = high.shape[1]
    return dot(high, table[:coefs]) + dot(low, table[:coefs]) + dot(high, table[coefs:])


def to_coefs(high, low, table):
    planes = high.shape[1]
    return dot(high, table[:planes]) + dot(low, table[:planes]) + dot(high, table[planes:])


def cross(a, b):
    return [
        a[1] * b[2] - a[2] * b[1],
        a[2] * b[0] - a[0] * b[2],
        a[0] * b[1] - a[1] * b[0],
    ]


def forcing(value, rows, planes_ref, coefs_ref, rotation_ref, phys_ref, high_ref, low_ref):
    planes = planes_ref.shape[1]
    high, low = halves(value)
    phys_ref[...] = to_planes(high, low, planes_ref)
    step_rows, step_lanes = 16, 256
    for row in range(0, rows, step_rows):
        for lane in range(0, planes, step_lanes):
            lanes = pl.ds(lane, step_lanes)
            u = [phys_ref[pl.ds(k * rows + row, step_rows), lanes] for k in range(3)]
            b = [phys_ref[pl.ds((3 + k) * rows + row, step_rows), lanes] for k in range(3)]
            turn = [rotation_ref[k : k + 1, lanes] for k in range(3)]
            induction = cross(u, b)
            twisted = cross(turn, u)
            lorentz = cross(b, induction)
            force = [twisted[k] - lorentz_factor * lorentz[k] for k in range(3)]
            for k, item in enumerate(force + induction):
                item_high, item_low = halves(item)
                at = pl.ds(k * rows + row, step_rows)
                high_ref[at, lanes] = item_high
                low_ref[at, lanes] = item_low
    return to_coefs(high_ref[...], low_ref[...], coefs_ref)


def triple(pair):
    return jnp.concatenate([pair[0], pair[1], pair[0]], axis=1)


def build_kernel(
    info, state, pick_ref, planes_hbm, coefs_hbm, rotation_ref, squares_ref,
    mass_ref, stiff_ref, twist_ref, rates_ref, conn_ref, lists_ref,
    dense_ref, force_ref, mass_ghost_ref, rest_ghost_ref, packed_ref,
    planes_ref, coefs_ref, phys_ref, high_ref, low_ref, z_ref, arrived,
):
    nodes = state.shape[1]
    elements = conn_ref.shape[1]
    ghosts = lists_ref.shape[1]
    count = 2 * ghosts
    tables = [
        pltpu.make_async_copy(planes_hbm, planes_ref, arrived.at[0]),
        pltpu.make_async_copy(coefs_hbm, coefs_ref, arrived.at[1]),
    ]
    for copy in tables:
        copy.start()
    conn = conn_ref[...]
    pick = pick_ref[...]
    remap = slot_matrix(conn, lists_ref[...], info[0], info[1], info[2], nodes, ghosts)
    rates = rates_ref[0:1, :]
    step = 16
    for row in range(0, nodes, step):
        number = iota((step, elements), 0) + row
        hits = [(number == conn[a : a + 1, :]).astype(f32) for a in range(6)]
        for g, block in enumerate((mass_ref, stiff_ref, twist_ref)):
            for b in range(6):
                total = hits[0] * block[0, b : b + 1, :]
                for a in range(1, 6):
                    total = total + hits[a] * block[a, b : b + 1, :]
                lanes = pl.ds(b * elements, elements)
                z_ref[pl.ds(g * nodes + row, step), lanes] = total
                if g > 0:
                    z_ref[pl.ds((g + 2) * nodes + row, step), lanes] = total * rates
    arrives = lax.dot_general(
        remap, one_hot(conn, nodes, count), (((0,), (0,)), ((), ())), preferred_element_type=f32
    )
    column = jnp.concatenate([one_hot(conn, 0, nodes), arrives.astype(bf16)], axis=0)
    z = z_ref[...]
    first, second = halves(z)
    third = (z - first.astype(f32) - second.astype(f32)).astype(bf16)
    dense = dot_nt(first, column) + dot_nt(second, column) + dot_nt(third, column)
    dense_ref[...] = dense
    high, low = halves(dense)
    pairs = []
    for g in range(5):
        rows = slice(g * nodes, (g + 1) * nodes)
        factor = viscosity if g in (1, 2) else 1.0
        pairs.append([(factor * dot(pick, item[rows])).astype(bf16) for item in (high, low)])

    def own_part(pair):
        return triple([item[:, :nodes] for item in pair])

    def ghost_part(pair):
        return triple([item[:, nodes:] for item in pair])

    mass_own = own_part(pairs[0])
    mass_ghost_ref[...] = ghost_part(pairs[0])
    rest_own = []
    for f in range(2):
        used = (pairs[1], pairs[2]) if f == 0 else (pairs[3], pairs[4])
        rest_own.append(jnp.concatenate([own_part(pair) for pair in used], axis=0))
        rest_ghost_ref[f] = jnp.concatenate([ghost_part(pair) for pair in used], axis=0)

    for copy in tables:
        copy.wait()
    value = state[...].reshape(6 * nodes, state.shape[2])
    force_ref[...] = forcing(
        value, nodes, planes_ref, coefs_ref, rotation_ref, phys_ref, high_ref, low_ref
    ).reshape(force_ref.shape)
    square = squares_ref[0:1, :]
    for k in range(6):
        from_force = dot(mass_own, stacked_rows(force_ref[k]))
        from_state = dot(rest_own[k // 3], stacked_rows(state[k]))
        packed_ref[k] = from_force - (from_state[:count] + square * from_state[count:])


def ghost_block(info, near, far, k):
    distant = jnp.where(info[3] > 0, far[k], 0.0)
    return jnp.concatenate([near[k], distant], axis=0)


def start_kernel(
    info, near, far, packed, planes_ref, coefs_ref, rotation_ref, squares_ref, mass_ghost, rest_ghost,
    near_out, far_out, force_out, phys_ref, high_ref, low_ref,
):
    ghosts = near.shape[1]
    count = 2 * ghosts
    blocks = [ghost_block(info, near, far, k) for k in range(6)]
    value = jnp.concatenate(blocks, axis=0)
    force = forcing(value, count, planes_ref, coefs_ref, rotation_ref, phys_ref, high_ref, low_ref)
    square = squares_ref[0:1, :]
    for k in range(6):
        item = force[k * count : (k + 1) * count]
        force_out[k] = item
        from_force = dot(mass_ghost[...], stacked_rows(item))
        from_state = dot(rest_ghost[k // 3], stacked_rows(blocks[k]))
        total = packed[k] + from_force - (from_state[:count] + square * from_state[count:])
        near_out[k] = total[:ghosts]
        far_out[k] = total[ghosts:]


def apply_own(own, value, k, square, nodes, count):
    image = dot(own[k // 3], stacked_rows(value))
    full = image[:nodes] + square * image[nodes : 2 * nodes]
    packed = image[2 * nodes : 2 * nodes + count] + square * image[2 * nodes + count :]
    return full, packed


def first_kernel(
    info, near, far, force_ghost, force, state, dense_ref, pick_ref, squares_ref,
    own_ref, ghost_ref, back_ref, vector_out, image_out, packed_out, moments_out,
):
    nodes = state.shape[1]
    count = force_ghost.shape[1]
    square = squares_ref[0:1, :]
    pick = pick_ref[...]
    mass, stiff, twist, rate_stiff, rate_twist = [
        dense_ref[pl.ds(g * nodes, nodes), :] for g in range(5)
    ]
    mass_op = stacked_columns(mass)
    rest_ops = []
    for f in range(2):
        still = viscosity * stiff if f == 0 else rate_stiff
        turn = viscosity * twist if f == 0 else rate_twist
        rest_ops.append(jnp.concatenate([stacked_columns(still), stacked_columns(turn)], axis=0))
        image = (inverse_step * mass + still) * (1.0 / basis_scale)
        turn = turn * (1.0 / basis_scale)
        pairs = [halves(image), halves(turn)]
        pairs = pairs + [[dot(pick, item).astype(bf16) for item in pair] for pair in pairs]
        own_ref[f] = jnp.concatenate(
            [triple([item[:, :nodes] for item in pair]) for pair in pairs], axis=0
        )
        ghost_ref[f] = jnp.concatenate(
            [triple([item[:, nodes:] for item in pair]) for pair in pairs], axis=0
        )
        back = [jnp.transpose(item[:, nodes:]) for item in (image, turn)]
        back_ref[f] = jnp.concatenate([stacked_columns(item) for item in back], axis=0)
    for k in range(6):
        wide_force = jnp.concatenate([force[k], force_ghost[k]], axis=0)
        wide_state = jnp.concatenate([state[k], ghost_block(info, near, far, k)], axis=0)
        from_force = dot(mass_op, stacked_rows(wide_force))
        from_state = dot(rest_ops[k // 3], stacked_rows(wide_state))
        total = from_force - (from_state[:nodes] + square * from_state[nodes:])
        vector_out[k] = total
        full, packed = apply_own(own_ref, total, k, square, nodes, count)
        image_out[k] = full
        packed_out[k] = packed
        moments_out[k : k + 1, :] = jnp.sum(total * total, axis=0, keepdims=True)
    moments_out[6:8, :] = jnp.zeros((2, moments_out.shape[1]), f32)


def send_kernel(info, near, far, packed, ghost_ops, squares_ref, near_out, far_out):
    ghosts = near.shape[1]
    count = 2 * ghosts
    top = ghost_ops.shape[1] - 2 * count
    square = squares_ref[0:1, :]
    for k in range(6):
        image = dot(ghost_ops[k // 3, top:], stacked_rows(ghost_block(info, near, far, k)))
        total = packed[k] + image[:count] + square * image[count:]
        near_out[k] = total[:ghosts]
        far_out[k] = total[ghosts:]


def next_kernel(
    info, near, far, image, before, own, ghost_ops, squares_ref,
    vector_out, image_out, packed_out, moments_out,
):
    nodes = image.shape[1]
    count = 2 * near.shape[1]
    square = squares_ref[0:1, :]
    for k in range(6):
        part = dot(ghost_ops[k // 3, : 2 * nodes], stacked_rows(ghost_block(info, near, far, k)))
        total = image[k] + part[:nodes] + square * part[nodes:]
        vector_out[k] = total
        full, packed = apply_own(own, total, k, square, nodes, count)
        image_out[k] = full
        packed_out[k] = packed
        moments_out[k : k + 1, :] = jnp.sum(before[k] * total, axis=0, keepdims=True)
        moments_out[6 + k : 7 + k, :] = jnp.sum(total * total, axis=0, keepdims=True)
    moments_out[12:16, :] = jnp.zeros((4, moments_out.shape[1]), f32)


def last_kernel(
    info, near, far, near_last, image, before, own, ghost_ops, back_ops, squares_ref, first, second,
    vector_out, back_out, moments_out,
):
    nodes = image.shape[1]
    ghosts = near.shape[1]
    count = 2 * ghosts
    square = squares_ref[0:1, :]
    moments_out[0:6] = first[0:6]
    moments_out[6:18] = second[0:12]
    for k in range(6):
        part = dot(ghost_ops[k // 3, : 2 * nodes], stacked_rows(ghost_block(info, near, far, k)))
        total = image[k] + part[:nodes] + square * part[nodes:]
        vector_out[k] = total
        rows = stacked_rows(total)
        after = dot(own[k // 3, : 2 * nodes], rows)
        after = after[:nodes] + square * after[nodes:]
        back = dot(back_ops[k // 3], rows)
        back = back[:count] + square * back[count:]
        back_out[k] = back[ghosts:]
        moments_out[18 + k : 19 + k, :] = jnp.sum(before[k] * total, axis=0, keepdims=True)
        moments_out[24 + k : 25 + k, :] = jnp.sum(total * total, axis=0, keepdims=True)
        moments_out[30 + k : 31 + k, :] = jnp.sum(after * total, axis=0, keepdims=True) + jnp.sum(
            near_last[k] * back[:ghosts], axis=0, keepdims=True
        )
    moments_out[36:40, :] = jnp.zeros((4, moments_out.shape[1]), f32)


def join_kernel(weight, info, far, back, moments, *rest):
    out = rest[-1]
    total = moments[...]
    for other in rest[:-1]:
        total = total + other[...]
    out[...] = total
    for k in range(6):
        distant = jnp.where(info[3] > 0, far[k], 0.0)
        out[30 + k : 31 + k, :] += weight * jnp.sum(distant * back[k], axis=0, keepdims=True)


def finish_kernel(moments, other, velocity, magnetic, first, second, third, velocity_out, magnetic_out):
    total = moments[...] + other[...]
    m0, m1, m2, m3, m4, m5 = [total[6 * j : 6 * j + 6, :] for j in range(6)]
    scale = basis_scale
    alpha0 = m0 / (scale * m1 + epsilon)
    q1 = -alpha0 * scale
    rr1 = m0 + 2.0 * q1 * m1 + q1 * q1 * m2
    beta0 = rr1 / (m0 + epsilon)
    p0 = 1.0 + beta0
    p1 = q1
    alpha1 = rr1 / (scale * (p0 * p0 * m1 + 2.0 * p0 * p1 * m2 + p1 * p1 * m3) + epsilon)
    step1 = alpha1 * scale
    r1 = q1 - step1 * p0
    r2 = -step1 * p1
    rr2 = m0 + r1 * r1 * m2 + r2 * r2 * m4 + 2.0 * (r1 * m1 + r2 * m2 + r1 * r2 * m3)
    beta1 = rr2 / (rr1 + epsilon)
    d0 = 1.0 + beta1 * p0
    d1 = r1 + beta1 * p1
    d2 = r2
    curve = d0 * d0 * m1 + d1 * d1 * m3 + d2 * d2 * m5
    curve = curve + 2.0 * (d0 * d1 * m2 + d0 * d2 * m3 + d1 * d2 * m4)
    alpha2 = rr2 / (scale * curve + epsilon)
    c0 = alpha0 + alpha1 * p0 + alpha2 * d0
    c1 = alpha1 * p1 + alpha2 * d1
    c2 = alpha2 * d2
    for k in range(6):
        source, out = (velocity, velocity_out) if k < 3 else (magnetic, magnetic_out)
        change = (
            c0[k : k + 1, :] * first[k] + c1[k : k + 1, :] * second[k] + c2[k : k + 1, :] * third[k]
        )
        out[k % 3] = source[k % 3] + jnp.transpose(change)


def call(kernel, outs, operands, scratch=(), flops=0, limit=24, distant=()):
    specs = [SMEM if operand.dtype == jnp.int32 and operand.ndim == 1 else VMEM for operand in operands]
    for i in distant:
        specs[i] = pl.BlockSpec(memory_space=pl.ANY)
    single = not isinstance(outs, list)
    shapes = [outs] if single else outs
    moved = sum(math.prod(o.shape) * o.dtype.itemsize for o in list(operands) + shapes)
    return pl.pallas_call(
        kernel,
        out_shape=outs,
        in_specs=specs,
        out_specs=VMEM if single else [VMEM] * len(outs),
        scratch_shapes=list(scratch),
        compiler_params=pltpu.CompilerParams(vmem_limit_bytes=limit * 1024 * 1024),
        cost_estimate=pl.CostEstimate(flops=flops, bytes_accessed=moved, transcendentals=0),
    )(*operands)


def shape(*sizes, dtype=f32):
    return jax.ShapeDtypeStruct(sizes, dtype)


def involution(pairs):
    return [edge for a, b in pairs for edge in ((a, b), (b, a))]


def local(runs, count, velocity, magnetic, mass_blocks, stiff_blocks, twist_blocks, diffusivity, conn, lists):
    coefs, nodes = velocity.shape[1:]
    ghosts = lists.shape[1]
    elements = conn.shape[1]
    both = 2 * ghosts
    planes = 2 * coefs
    index = lax.axis_index("mesh")
    odd = index % 2
    low_valid = (index > 0).astype(jnp.int32)
    high_valid = (index < count - 1).astype(jnp.int32)
    far_valid = jnp.where(odd == 1, high_valid, low_valid)
    info = jnp.stack([odd, low_valid, high_valid, far_valid]).astype(jnp.int32)

    near_pairs = [(i, i ^ 1) for i in range(count)]
    far_pairs = []
    for run in range(runs):
        base = run * count
        far_pairs += involution([(base + i, base + i + 1) for i in range(1, count - 1, 2)])
    if runs % 2 == 0:
        for run in range(0, runs, 2):
            for end in (0, count - 1):
                far_pairs += involution([(run * count + end, (run + 1) * count + end)])

    def swap_near(value):
        return lax.ppermute(value, "mesh", near_pairs)

    def swap_far(value):
        return lax.ppermute(value, ("runs", "mesh"), far_pairs)

    plane_table, coef_table, rotation, squares = transform_tables(coefs)
    plane_table, coef_table = jnp.asarray(plane_table), jnp.asarray(coef_table)
    rotation, squares = jnp.asarray(rotation), jnp.asarray(squares)
    ends = shape(6, ghosts, coefs)
    whole = shape(6, nodes, coefs)
    packs = shape(6, both, coefs)

    def exchange(near, far):
        far = swap_far(far)
        return swap_near(near), far

    near, far, state, pick = call(
        pack_kernel,
        [ends, ends, whole, shape(both, nodes, dtype=bf16)],
        [info, velocity, magnetic, conn],
        scratch=[pltpu.VMEM((6, coefs, nodes), f32), pltpu.SemaphoreType.DMA((6,))],
        distant=(1, 2),
    )
    near_state, far_state = exchange(near, far)
    dense, force, mass_ghost, rest_ghost, packed = call(
        build_kernel,
        [
            shape(5 * nodes, nodes + both),
            whole,
            shape(both, 3 * both, dtype=bf16),
            shape(2, 2 * both, 3 * both, dtype=bf16),
            packs,
        ],
        [info, state, pick, plane_table, coef_table, rotation, squares]
        + [mass_blocks, stiff_blocks, twist_blocks, diffusivity.reshape(1, elements), conn, lists],
        scratch=[
            pltpu.VMEM(plane_table.shape, bf16),
            pltpu.VMEM(coef_table.shape, bf16),
            pltpu.VMEM((6 * nodes, planes), f32),
            pltpu.VMEM((6 * nodes, planes), bf16),
            pltpu.VMEM((6 * nodes, planes), bf16),
            pltpu.VMEM((5 * nodes, 6 * elements), f32),
            pltpu.SemaphoreType.DMA((2,)),
        ],
        flops=6_000_000_000,
        distant=(3, 4),
    )
    near, far, force_ghost = call(
        start_kernel,
        [ends, ends, packs],
        [info, near_state, far_state, packed, plane_table, coef_table, rotation, squares]
        + [mass_ghost, rest_ghost],
        scratch=[
            pltpu.VMEM((6 * both, planes), f32),
            pltpu.VMEM((6 * both, planes), bf16),
            pltpu.VMEM((6 * both, planes), bf16),
        ],
        flops=1_000_000_000,
    )
    near_now, far_now = exchange(near, far)
    own, ghost_ops, back_ops, vector0, image, packed, moments0 = call(
        first_kernel,
        [
            shape(2, 2 * nodes + 2 * both, 3 * nodes, dtype=bf16),
            shape(2, 2 * nodes + 2 * both, 3 * both, dtype=bf16),
            shape(2, 2 * both, 3 * nodes, dtype=bf16),
            whole,
            whole,
            packs,
            shape(8, coefs),
        ],
        [info, near_state, far_state, force_ghost, force, state, dense, pick, squares],
        flops=2_000_000_000,
    )
    near, far = call(
        send_kernel, [ends, ends], [info, near_now, far_now, packed, ghost_ops, squares], flops=100_000_000
    )
    near_next, far_next = exchange(near, far)
    vector1, image, packed, moments1 = call(
        next_kernel,
        [whole, whole, packs, shape(16, coefs)],
        [info, near_now, far_now, image, vector0, own, ghost_ops, squares],
        flops=2_000_000_000,
    )
    near, far = call(
        send_kernel, [ends, ends], [info, near_next, far_next, packed, ghost_ops, squares], flops=100_000_000
    )
    near_last, far_last = exchange(near, far)
    vector2, back, moments = call(
        last_kernel,
        [whole, ends, shape(40, coefs)],
        [info, near_next, far_next, near_last, image, vector1, own, ghost_ops, back_ops, squares]
        + [moments0, moments1],
        flops=2_000_000_000,
    )
    if count % 8 == 0 and count <= 16:
        joined = call(
            functools.partial(join_kernel, 2.0),
            shape(40, coefs),
            [info, far_last, back, moments, swap_near(moments)],
        )
        target = (2, 0, 3, 1)
        lines = count // 4
        half = None
        for step in range(lines):
            pairs = [(i, ((i // 4) ^ step) * 4 + target[i % 4]) for i in range(count)]
            term = lax.ppermute(joined, "mesh", pairs)
            half = term if half is None else half + term
        other = swap_near(half)
    else:
        joined = call(
            functools.partial(join_kernel, 1.0), shape(40, coefs), [info, far_last, back, moments]
        )
        half = lax.psum(joined, "mesh")
        other = jnp.zeros_like(half)
    new_velocity, new_magnetic = call(
        finish_kernel,
        [shape(3, coefs, nodes), shape(3, coefs, nodes)],
        [half, other, velocity, magnetic, vector0, vector1, vector2],
        flops=10_000_000,
    )
    return new_velocity, new_magnetic


def solution(mesh):
    in_specs = (
        P("runs", None, "mesh"),
        P("runs", None, "mesh"),
        P(None, None, "mesh"),
        P(None, None, "mesh"),
        P(None, None, "mesh"),
        P(("runs", "mesh")),
        P(None, "mesh"),
        P(None, "mesh"),
    )
    out_specs = (P("runs", None, "mesh"), P("runs", None, "mesh"))
    sizes = dict(mesh.shape)
    step = functools.partial(local, sizes["runs"], sizes["mesh"])
    return jax.shard_map(step, mesh=mesh, in_specs=in_specs, out_specs=out_specs, check_vma=False)
```

time: 57.4 us -> 56 us (0.976)
  Pallas kernels: 20.9 us -> 24.6 us
  waiting for transfers between devices: 9.95 us -> 6.99 us
  starting transfers between devices: 21 us -> 18.9 us
    pallas_call x10, Pallas kernels: 20.9 us -> 24.6 us  [call(): pl.pallas_call(kernel, out_shape=outs, in_specs=specs, out_specs=VMEM if...]
    ppermute x4, waiting for transfers between devices: 5.63 us -> 2.53 us  [swap_far(): return lax.ppermute(value, ('runs', 'mesh'), far_pairs)]
    ppermute x6, starting transfers between devices: 6.8 us -> 4.41 us  [swap_near(): return lax.ppermute(value, 'mesh', near_pairs)]
  transfers between devices with their start and end apart: 14 -> 14, of which waited for: 6 -> 5; matrix products, arithmetic and copies ran while one was open for 0% -> 0% of each run, Pallas kernels for 25% -> 28%
where the time goes in v2:
time: 56 us; the launch traced here: 55.7 us
  Pallas kernels  24.6 us (44%)
  starting transfers between devices  18.9 us (34%)
  waiting for transfers between devices  6.99 us (12%)
  local copies, waits for them, and re-layouts  4.31 us (8%)
  between operations  0.85 us (2%)
    pallas_call x10, Pallas kernels, call(): pl.pallas_call(kernel, out_shape=outs, in_specs=specs, out_specs=VMEM if...  24.6 us
    ppermute x4, starting transfers between devices, local(): term = lax.ppermute(joined, 'mesh', pairs)  7.44 us
    ppermute x4, starting transfers between devices, swap_far(): return lax.ppermute(value, ('runs', 'mesh'), far_pairs)  7.03 us
    ppermute x6, starting transfers between devices, swap_near(): return lax.ppermute(value, 'mesh', near_pairs)  4.41 us
    unnamed x28, local copies, waits for them, and re-layouts  4.31 us
    ppermute x4, waiting for transfers between devices, local(): term = lax.ppermute(joined, 'mesh', pairs)  2.92 us
    ppermute x4, waiting for transfers between devices, swap_far(): return lax.ppermute(value, ('runs', 'mesh'), far_pairs)  2.53 us
    ppermute x6, waiting for transfers between devices, swap_near(): return lax.ppermute(value, 'mesh', near_pairs)  1.55 us
  transfers between devices with their start and end apart: 14, of which 5 were waited for; matrix products, arithmetic and copies ran while one was open for 0% of the time, Pallas kernels for 28%

profile of v2, /device:TPU:0, one launch (start us, length us, event | category | flops | bytes accessed | tf_op | source)
XLA Modules:
  0.0 55.7 jit_solution(868579602603150704)
XLA Ops:
  0.6 0.0 copy-start.5
  0.7 0.1 pad_add_fusion.info
  0.7 0.6 %copy-done.5 = s32[6,128]{1,0:T(8,128)S(1)} copy-done((s32[6,128]{1,0:T(8,128)S(1)}, s32[6,128]{1,0:T(8,128)}, u32[]{:S(2)}) %copy-start.5) | copy-done | bytes 3096
  1.3 0.0 copy-start
  1.3 1.0 %copy-done = f32[3,256,128]{2,1,0:T(8,128)S(1)} copy-done((f32[3,256,128]{2,1,0:T(8,128)S(1)}, f32[3,256,128]{2,1,0:T(8,128)}, u32[]{:S(2)}) %copy-start) | copy-done | bytes 393240
  2.3 0.0 copy-start.2
  2.3 1.0 %copy-done.2 = f32[3,256,128]{2,1,0:T(8,128)S(1)} copy-done((f32[3,256,128]{2,1,0:T(8,128)S(1)}, f32[3,256,128]{2,1,0:T(8,128)}, u32[]{:S(2)}) %copy-start.2) | copy-done | bytes 393240
  3.3 0.0 copy-start.6
  3.3 0.0 copy-start.7
  3.3 0.0 copy-start.8
  3.3 0.0 copy-start.10
  3.3 0.0 copy-start.11
  3.4 0.0 copy-start.13
  3.4 3.6 %shard_map.131 = (f32[6,32,256]{2,1,0:T(8,128)S(1)}, f32[6,32,256]{2,1,0:T(8,128)S(1)}, f32[6,128,256]{2,1,0:T(8,128)S(1)}, bf16[64,128]{1,0:T(8,128)(2,1)S(1)}) custom-call(s32[4]{0:T(128)S(1)} %pad_add_fusion.info, f32[3,256,128]{2,1,0:T(8,128)S(1)} %copy-done, f32[3,256,128]{2,1,0:T(8,128)S(1)} %copy-done.2, s32[6,128]{1,0:T(8,128)S(1)} %copy-done.5), custom_call_target="tpu_custom_call" | custom-call | bytes 1985552 | tf_op jit(solution)/shard_map/pallas_call | solution.py:469
  7.0 0.0 copy-start.4
  7.0 0.5 collective-permute-start
  7.5 2.6 %collective-permute-start.1 = (f32[6,32,256]{2,1,0:T(8,128)S(1)}, f32[6,32,256]{2,1,0:T(8,128)S(1)}, u32[]{:S(2)}, u32[]{:S(2)}) collective-permute-start(f32[6,32,256]{2,1,0:T(8,128)S(1)} %get-tuple-element.33), channel_id=1, source_target_pairs={{1,2},{2,1},{3,4},{4,3},{5,6},{6,5},{7,8},{8,7},{9,10},{10,9},{11,... | collective-permute-start | bytes 589832 | tf_op jit(solution)/shard_map/ppermute | solution.py:515
  10.1 0.0 copy-done.6
  10.1 0.0 copy-done.7
  10.1 0.0 copy-done.8
  10.1 0.0 copy-done.10
  10.1 0.0 copy-done.11
  10.1 0.0 copy-done.13
  10.1 0.0 copy-done.4
  10.1 0.6 %copy-done.9 = s32[2,32]{1,0:T(2,128)S(1)} copy-done((s32[2,32]{1,0:T(2,128)S(1)}, s32[2,32]{1,0:T(2,128)}, u32[]{:S(2)}) %copy-start.9) | copy-done | bytes 280
  10.7 1.0 %copy-done.12 = bf16[512,512]{1,0:T(8,128)(2,1)S(1)} copy-done((bf16[512,512]{1,0:T(8,128)(2,1)S(1)}, bf16[512,512]{1,0:T(8,128)(2,1)}, u32[]{:S(2)}) %copy-start.12) | copy-done | bytes 524312
  11.8 6.5 %shard_map.132 = (f32[640,192]{1,0:T(8,128)S(1)}, f32[6,128,256]{2,1,0:T(8,128)S(1)}, bf16[64,192]{1,0:T(8,128)(2,1)S(1)}, bf16[2,128,192]{2,1,0:T(8,128)(2,1)S(1)}, f32[6,64,256]{2,1,0:T(8,128)S(1)}) custom-call(s32[4]{0:T(128)S(1)} %pad_add_fusion.info, f32[6,128,256]{2,1,0:T(8,128)S(1)} %get-tuple-element.34.state, ...), custom_call_target="tpu_custom_call" | custom-call | flops 6000000000 | bytes 3729168 | tf_op jit(solution)/shard_map/pallas_call | solution.py:469
  18.3 0.0 collective-permute-done.near
  18.3 0.0 collective-permute-done.1.far
  18.4 2.2 %shard_map.133 = (f32[6,32,256]{2,1,0:T(8,128)S(1)}, f32[6,32,256]{2,1,0:T(8,128)S(1)}, f32[6,64,256]{2,1,0:T(8,128)S(1)}) custom-call(s32[4]{0:T(128)S(1)} %pad_add_fusion.info, f32[6,32,256]{2,1,0:T(8,128)S(1)} %collective-permute-done.near, f32[6,32,256]{2,1,0:T(8,128)S(1)} %collective-permute-done.1.far, f32[6,64,256]{2,1,0:T(8,128)S(1)} %get-tuple-element.36.packed, ...), custom_call_target="tpu_custom_call" | custom-call | flops 1000000000 | bytes 2768912 | tf_op jit(solution)/shard_map/pallas_call | solution.py:469
  20.6 0.2 collective-permute-start.2
  20.8 1.5 %collective-permute-start.3 = (f32[6,32,256]{2,1,0:T(8,128)S(1)}, f32[6,32,256]{2,1,0:T(8,128)S(1)}, u32[]{:S(2)}, u32[]{:S(2)}) collective-permute-start(f32[6,32,256]{2,1,0:T(8,128)S(1)} %get-tuple-element.40), channel_id=1, source_target_pairs={{1,2},{2,1},{3,4},{4,3},{5,6},{6,5},{7,8},{8,7},{9,10},{10,9},{11,... | collective-permute-start | bytes 589832 | tf_op jit(solution)/shard_map/ppermute | solution.py:515
  22.3 4.2 %shard_map.134 = (bf16[2,384,384]{2,1,0:T(8,128)(2,1)S(1)}, bf16[2,384,192]{2,1,0:T(8,128)(2,1)S(1)}, bf16[2,128,384]{2,1,0:T(8,128)(2,1)S(1)}, f32[6,128,256]{2...) custom-call(s32[4]{0:T(128)S(1)} %pad_add_fusion.info, ...), custom_call_target="tpu_custom_call" | custom-call | flops 2000000000 | bytes 5931024 | tf_op jit(solution)/shard_map/pallas_call | solution.py:469
  26.5 0.0 collective-permute-done.2.near
  26.5 0.0 collective-permute-done.3.far
  26.5 0.8 %shard_map.135 = (f32[6,32,256]{2,1,0:T(8,128)S(1)}, f32[6,32,256]{2,1,0:T(8,128)S(1)}) custom-call(s32[4]{0:T(128)S(1)} %pad_add_fusion.info, f32[6,32,256]{2,1,0:T(8,128)S(1)} %collective-permute-done.2.near, f32[6,32,256]{2,1,0:T(8,128)S(1)} %collective-permute-done.3.far, f32[6,64,256]{2,1,0:T(8,128)S(1)} %get-tuple-element.44.packed, ...), custom_call_target="tpu_custom_call" | custom-call | flops 100000000 | bytes 1482768 | tf_op jit(solution)/shard_map/pallas_call | solution.py:469
  27.3 0.7 %collective-permute-start.4 = (f32[6,32,256]{2,1,0:T(8,128)S(1)}, f32[6,32,256]{2,1,0:T(8,128)S(1)}, u32[]{:S(2)}, u32[]{:S(2)}) collective-permute-start(f32[6,32,256]{2,1,0:T(8,128)S(1)} %get-tuple-element.46), channel_id=1, source_target_pairs={{0,1},{1,0},{2,3},{3,2},{4,5},{5,4},{6,7},{7,6},{8,9},{9,8},{10,11... | collective-permute-start | bytes 589832 | tf_op jit(solution)/shard_map/ppermute | solution.py:512
  28.0 1.5 %collective-permute-start.5 = (f32[6,32,256]{2,1,0:T(8,128)S(1)}, f32[6,32,256]{2,1,0:T(8,128)S(1)}, u32[]{:S(2)}, u32[]{:S(2)}) collective-permute-start(f32[6,32,256]{2,1,0:T(8,128)S(1)} %get-tuple-element.47), channel_id=1, source_target_pairs={{1,2},{2,1},{3,4},{4,3},{5,6},{6,5},{7,8},{8,7},{9,10},{10,9},{11,... | collective-permute-start | bytes 589832 | tf_op jit(solution)/shard_map/ppermute | solution.py:515
  29.5 2.1 %shard_map.136 = (f32[6,128,256]{2,1,0:T(8,128)S(1)}, f32[6,128,256]{2,1,0:T(8,128)S(1)}, f32[6,64,256]{2,1,0:T(8,128)S(1)}, f32[16,256]{1,0:T(8,128)S(1)}) custom-call(s32[4]{0:T(128)S(1)} %pad_add_fusion.info, f32[6,32,256]{2,1,0:T(8,128)S(1)} %collective-permute-done.2.near, f32[6,32,256]{2,1,0:T(8,128)S(1)} %collective-permute-done.3.far, ...), custom_call_target="tpu_custom_call" | custom-call | flops 2000000000 | bytes 4841488 | tf_op jit(solution)/shard_map/pallas_call | solution.py:469
  31.6 0.0 collective-permute-done.4.near
  31.6 2.1 %collective-permute-done.5.far = f32[6,32,256]{2,1,0:T(8,128)S(1)} collective-permute-done((f32[6,32,256]{2,1,0:T(8,128)S(1)}, f32[6,32,256]{2,1,0:T(8,128)S(1)}, u32[]{:S(2)}, u32[]{:S(2)}) %collective-permute-start.5) | collective-permute-done | bytes 196640 | tf_op jit(solution)/shard_map/ppermute | solution.py:515
  33.7 0.8 %shard_map.137 = (f32[6,32,256]{2,1,0:T(8,128)S(1)}, f32[6,32,256]{2,1,0:T(8,128)S(1)}) custom-call(s32[4]{0:T(128)S(1)} %pad_add_fusion.info, f32[6,32,256]{2,1,0:T(8,128)S(1)} %collective-permute-done.4.near, f32[6,32,256]{2,1,0:T(8,128)S(1)} %collective-permute-done.5.far, f32[6,64,256]{2,1,0:T(8,128)S(1)} %get-tuple-element.51.packed, ...), custom_call_target="tpu_custom_call" | custom-call | flops 100000000 | bytes 1482768 | tf_op jit(solution)/shard_map/pallas_call | solution.py:469
  34.5 1.7 %collective-permute-start.7 = (f32[6,32,256]{2,1,0:T(8,128)S(1)}, f32[6,32,256]{2,1,0:T(8,128)S(1)}, u32[]{:S(2)}, u32[]{:S(2)}) collective-permute-start(f32[6,32,256]{2,1,0:T(8,128)S(1)} %get-tuple-element.53), channel_id=1, source_target_pairs={{0,1},{1,0},{2,3},{3,2},{4,5},{5,4},{6,7},{7,6},{8,9},{9,8},{10,11... | collective-permute-start | bytes 589832 | tf_op jit(solution)/shard_map/ppermute | solution.py:512
  36.2 1.5 %collective-permute-start.6 = (f32[6,32,256]{2,1,0:T(8,128)S(1)}, f32[6,32,256]{2,1,0:T(8,128)S(1)}, u32[]{:S(2)}, u32[]{:S(2)}) collective-permute-start(f32[6,32,256]{2,1,0:T(8,128)S(1)} %get-tuple-element.52), channel_id=1, source_target_pairs={{1,2},{2,1},{3,4},{4,3},{5,6},{6,5},{7,8},{8,7},{9,10},{10,9},{11,... | collective-permute-start | bytes 589832 | tf_op jit(solution)/shard_map/ppermute | solution.py:515
  37.7 0.0 collective-permute-done.7.near_last
  37.7 2.6 %shard_map.138 = (f32[6,128,256]{2,1,0:T(8,128)S(1)}, f32[6,32,256]{2,1,0:T(8,128)S(1)}, f32[40,256]{1,0:T(8,128)S(1)}) custom-call(s32[4]{0:T(128)S(1)} %pad_add_fusion.info, f32[6,32,256]{2,1,0:T(8,128)S(1)} %collective-permute-done.4.near, f32[6,32,256]{2,1,0:T(8,128)S(1)} %collective-permute-done.5.far, ...), custom_call_target="tpu_custom_call" | custom-call | flops 2000000000 | bytes 4300816 | tf_op jit(solution)/shard_map/pallas_call | solution.py:469
  40.3 0.0 copy-start.1
  40.3 1.1 %collective-permute-start.8 = (f32[40,256]{1,0:T(8,128)S(1)}, f32[40,256]{1,0:T(8,128)S(1)}, u32[]{:S(2)}, u32[]{:S(2)}) collective-permute-start(f32[40,256]{1,0:T(8,128)S(1)} %get-tuple-element.60.moments), channel_id=1, source_target_pairs={{0,1},{1,0},{2,3},{3,2},{4,5},{5,4},{6,7},{7,6},{8,9},{9,8},{10,11... | collective-permute-start | bytes 122888 | tf_op jit(solution)/shard_map/ppermute | solution.py:512
  41.4 0.4 collective-permute-done.6.far
  41.8 0.4 collective-permute-done.8.rest_0_
  42.3 0.6 %shard_map.139 = f32[40,256]{1,0:T(8,128)S(1)} custom-call(s32[4]{0:T(128)S(1)} %pad_add_fusion.info, f32[6,32,256]{2,1,0:T(8,128)S(1)} %collective-permute-done.6.far, f32[6,32,256]{2,1,0:T(8,128)S(1)} %get-tuple-element.59.back, f32[40,256]{1,0:T(8,128)S(1)} %get-tuple-element.60.moments, f32[40,256]{1,0:T(8,128)S(1)} %collective-permute-done.8.rest_0_), custom_call_target="tpu_custom_call" | custom-call | bytes 516112 | tf_op jit(solution)/shard_map/pallas_call | solution.py:469
  42.9 5.2 %collective-permute-start.12 = (f32[40,256]{1,0:T(8,128)S(1)}, f32[40,256]{1,0:T(8,128)S(1)}, u32[]{:S(2)}, u32[]{:S(2)}) collective-permute-start(f32[40,256]{1,0:T(8,128)S(1)} %shard_map.139), channel_id=1, source_target_pairs={{0,14},{1,12},{2,15},{3,13},{4,10},{5,8},{6,11},{7,9},{8,6},{9,4},... | collective-permute-start | bytes 122888 | tf_op jit(solution)/shard_map/ppermute | solution.py:618
  48.0 0.5 collective-permute-start.11
  48.6 0.1 collective-permute-start.10
  48.7 1.6 %collective-permute-start.9 = (f32[40,256]{1,0:T(8,128)S(1)}, f32[40,256]{1,0:T(8,128)S(1)}, u32[]{:S(2)}, u32[]{:S(2)}) collective-permute-start(f32[40,256]{1,0:T(8,128)S(1)} %shard_map.139), channel_id=1, source_target_pairs={{0,2},{1,0},{2,3},{3,1},{4,6},{5,4},{6,7},{7,5},{8,10},{9,8},{10,1... | collective-permute-start | bytes 122888 | tf_op jit(solution)/shard_map/ppermute | solution.py:618
  50.3 0.0 collective-permute-done.12
  50.3 2.9 %collective-permute-done.11 = f32[40,256]{1,0:T(8,128)S(1)} collective-permute-done((f32[40,256]{1,0:T(8,128)S(1)}, f32[40,256]{1,0:T(8,128)S(1)}, u32[]{:S(2)}, u32[]{:S(2)}) %collective-permute-start.11) | collective-permute-done | bytes 40992 | tf_op jit(solution)/shard_map/ppermute | solution.py:618
  53.2 0.0 collective-permute-done.10
  53.2 0.0 collective-permute-done.9
  53.2 0.2 collective-permute-start.13
  53.4 1.1 %collective-permute-done.13.other = f32[40,256]{1,0:T(8,128)S(1)} collective-permute-done((f32[40,256]{1,0:T(8,128)S(1)}, f32[40,256]{1,0:T(8,128)S(1)}, u32[]{:S(2)}, u32[]{:S(2)}) %collective-permute-start.13) | collective-permute-done | bytes 40992 | tf_op jit(solution)/shard_map/ppermute | solution.py:512
  54.5 0.0 copy-done.3
  54.5 0.0 copy-done.1
  54.5 1.2 %shard_map.140 = (f32[3,256,128]{2,1,0:T(8,128)}, f32[3,256,128]{2,1,0:T(8,128)}) custom-call(f32[40,256]{1,0:T(8,128)S(1)} %add_add_fusion.moments, f32[40,256]{1,0:T(8,128)S(1)} %collective-permute-done.13.other, f32[3,256,128]{2,1,0:T(8,128)S(1)} %copy-done.1, f32[3,256,128]{2,1,0:T(8,128)S(1)} %copy-done.3, ...), custom_call_target="tpu_custom_call" | custom-call | flops 10000000 | bytes 4014080 | tf_op jit(solution)/shard_map/pallas_call | solution.py:469
  (4 shorter events, 0.0 us)
Async XLA Ops:
  0.6 0.7 %copy-start.5 = (s32[6,128]{1,0:T(8,128)S(1)}, s32[6,128]{1,0:T(8,128)}, u32[]{:S(2)}) copy-start(s32[6,128]{1,0:T(8,128)} %conn_ref.3) | copy-start | bytes 9220
  1.3 1.0 %copy-start = (f32[3,256,128]{2,1,0:T(8,128)S(1)}, f32[3,256,128]{2,1,0:T(8,128)}, u32[]{:S(2)}) copy-start(f32[3,256,128]{2,1,0:T(8,128)} %velocity.3) | copy-start | bytes 1179652
  2.3 1.0 %copy-start.2 = (f32[3,256,128]{2,1,0:T(8,128)S(1)}, f32[3,256,128]{2,1,0:T(8,128)}, u32[]{:S(2)}) copy-start(f32[3,256,128]{2,1,0:T(8,128)} %magnetic.3) | copy-start | bytes 1179652
  3.3 6.7 %copy-start.6 = (f32[6,6,128]{2,1,0:T(8,128)S(1)}, f32[6,6,128]{2,1,0:T(8,128)}, u32[]{:S(2)}) copy-start(f32[6,6,128]{2,1,0:T(8,128)} %mass_ref.1) | copy-start | bytes 55300
  3.3 6.7 %copy-start.7 = (f32[6,6,128]{2,1,0:T(8,128)S(1)}, f32[6,6,128]{2,1,0:T(8,128)}, u32[]{:S(2)}) copy-start(f32[6,6,128]{2,1,0:T(8,128)} %stiff_ref.1) | copy-start | bytes 55300
  3.3 6.7 %copy-start.8 = (f32[6,6,128]{2,1,0:T(8,128)S(1)}, f32[6,6,128]{2,1,0:T(8,128)}, u32[]{:S(2)}) copy-start(f32[6,6,128]{2,1,0:T(8,128)} %twist_ref.1) | copy-start | bytes 55300
  3.3 6.7 %copy-start.10 = (f32[128]{0:T(128)S(1)}, f32[128]{0:T(128)}, u32[]{:S(2)}) copy-start(f32[128]{0:T(128)} %param.17) | copy-start | bytes 1540
  3.3 6.8 %copy-start.11 = (bf16[1024,256]{1,0:T(8,128)(2,1)S(1)}, bf16[1024,256]{1,0:T(8,128)(2,1)}, u32[]{:S(2)}) copy-start(bf16[1024,256]{1,0:T(8,128)(2,1)} %constant.30.clone.coefs_hbm.coefs_ref) | copy-start | bytes 1572868
  3.4 6.7 %copy-start.13 = (f32[8,512]{1,0:T(8,128)S(1)}, f32[8,512]{1,0:T(8,128)}, u32[]{:S(2)}) copy-start(f32[8,512]{1,0:T(8,128)} %constant.31.clone.rotation_ref) | copy-start | bytes 49156
  7.0 3.1 %copy-start.4 = (f32[8,256]{1,0:T(8,128)S(1)}, f32[8,256]{1,0:T(8,128)}, u32[]{:S(2)}) copy-start(f32[8,256]{1,0:T(8,128)} %constant.32.clone.squares_ref) | copy-start | bytes 24580
  7.0 11.4 %collective-permute-start = (f32[6,32,256]{2,1,0:T(8,128)S(1)}, f32[6,32,256]{2,1,0:T(8,128)S(1)}, u32[]{:S(2)}, u32[]{:S(2)}) collective-permute-start(f32[6,32,256]{2,1,0:T(8,128)S(1)} %get-tuple-element.32), channel_id=1, source_target_pairs={{0,1},{1,0},{2,3},{3,2},{4,5},{5,4},{6,7},{7,6},{8,9},{9,8},{10,11... | collective-permute-start | bytes 589832 | tf_op jit(solution)/shard_map/ppermute | solution.py:512
  7.5 10.8 %collective-permute-start.1 = (f32[6,32,256]{2,1,0:T(8,128)S(1)}, f32[6,32,256]{2,1,0:T(8,128)S(1)}, u32[]{:S(2)}, u32[]{:S(2)}) collective-permute-start(f32[6,32,256]{2,1,0:T(8,128)S(1)} %get-tuple-element.33), channel_id=1, source_target_pairs={{1,2},{2,1},{3,4},{4,3},{5,6},{6,5},{7,8},{8,7},{9,10},{10,9},{11,... | collective-permute-start | bytes 589832 | tf_op jit(solution)/shard_map/ppermute | solution.py:515
  10.1 0.7 %copy-start.9 = (s32[2,32]{1,0:T(2,128)S(1)}, s32[2,32]{1,0:T(2,128)}, u32[]{:S(2)}) copy-start(s32[2,32]{1,0:T(2,128)} %lists_ref.1) | copy-start | bytes 772
  10.7 1.0 %copy-start.12 = (bf16[512,512]{1,0:T(8,128)(2,1)S(1)}, bf16[512,512]{1,0:T(8,128)(2,1)}, u32[]{:S(2)}) copy-start(bf16[512,512]{1,0:T(8,128)(2,1)} %constant.29.clone.planes_hbm.planes_ref) | copy-start | bytes 1572868
  20.6 5.9 %collective-permute-start.2 = (f32[6,32,256]{2,1,0:T(8,128)S(1)}, f32[6,32,256]{2,1,0:T(8,128)S(1)}, u32[]{:S(2)}, u32[]{:S(2)}) collective-permute-start(f32[6,32,256]{2,1,0:T(8,128)S(1)} %get-tuple-element.39), channel_id=1, source_target_pairs={{0,1},{1,0},{2,3},{3,2},{4,5},{5,4},{6,7},{7,6},{8,9},{9,8},{10,11... | collective-permute-start | bytes 589832 | tf_op jit(solution)/shard_map/ppermute | solution.py:512
  20.8 5.7 %collective-permute-start.3 = (f32[6,32,256]{2,1,0:T(8,128)S(1)}, f32[6,32,256]{2,1,0:T(8,128)S(1)}, u32[]{:S(2)}, u32[]{:S(2)}) collective-permute-start(f32[6,32,256]{2,1,0:T(8,128)S(1)} %get-tuple-element.40), channel_id=1, source_target_pairs={{1,2},{2,1},{3,4},{4,3},{5,6},{6,5},{7,8},{8,7},{9,10},{10,9},{11,... | collective-permute-start | bytes 589832 | tf_op jit(solution)/shard_map/ppermute | solution.py:515
  27.3 4.3 %collective-permute-start.4 = (f32[6,32,256]{2,1,0:T(8,128)S(1)}, f32[6,32,256]{2,1,0:T(8,128)S(1)}, u32[]{:S(2)}, u32[]{:S(2)}) collective-permute-start(f32[6,32,256]{2,1,0:T(8,128)S(1)} %get-tuple-element.46), channel_id=1, source_target_pairs={{0,1},{1,0},{2,3},{3,2},{4,5},{5,4},{6,7},{7,6},{8,9},{9,8},{10,11... | collective-permute-start | bytes 589832 | tf_op jit(solution)/shard_map/ppermute | solution.py:512
  28.0 5.7 %collective-permute-start.5 = (f32[6,32,256]{2,1,0:T(8,128)S(1)}, f32[6,32,256]{2,1,0:T(8,128)S(1)}, u32[]{:S(2)}, u32[]{:S(2)}) collective-permute-start(f32[6,32,256]{2,1,0:T(8,128)S(1)} %get-tuple-element.47), channel_id=1, source_target_pairs={{1,2},{2,1},{3,4},{4,3},{5,6},{6,5},{7,8},{8,7},{9,10},{10,9},{11,... | collective-permute-start | bytes 589832 | tf_op jit(solution)/shard_map/ppermute | solution.py:515
  34.5 3.2 %collective-permute-start.7 = (f32[6,32,256]{2,1,0:T(8,128)S(1)}, f32[6,32,256]{2,1,0:T(8,128)S(1)}, u32[]{:S(2)}, u32[]{:S(2)}) collective-permute-start(f32[6,32,256]{2,1,0:T(8,128)S(1)} %get-tuple-element.53), channel_id=1, source_target_pairs={{0,1},{1,0},{2,3},{3,2},{4,5},{5,4},{6,7},{7,6},{8,9},{9,8},{10,11... | collective-permute-start | bytes 589832 | tf_op jit(solution)/shard_map/ppermute | solution.py:512
  36.2 5.7 %collective-permute-start.6 = (f32[6,32,256]{2,1,0:T(8,128)S(1)}, f32[6,32,256]{2,1,0:T(8,128)S(1)}, u32[]{:S(2)}, u32[]{:S(2)}) collective-permute-start(f32[6,32,256]{2,1,0:T(8,128)S(1)} %get-tuple-element.52), channel_id=1, source_target_pairs={{1,2},{2,1},{3,4},{4,3},{5,6},{6,5},{7,8},{8,7},{9,10},{10,9},{11,... | collective-permute-start | bytes 589832 | tf_op jit(solution)/shard_map/ppermute | solution.py:515
  37.7 16.9 %copy-start.3 = (f32[3,256,128]{2,1,0:T(8,128)S(1)}, f32[3,256,128]{2,1,0:T(8,128)}, u32[]{:S(2)}) copy-start(f32[3,256,128]{2,1,0:T(8,128)} %magnetic.3) | copy-start | bytes 1179652
  40.3 14.3 %copy-start.1 = (f32[3,256,128]{2,1,0:T(8,128)S(1)}, f32[3,256,128]{2,1,0:T(8,128)}, u32[]{:S(2)}) copy-start(f32[3,256,128]{2,1,0:T(8,128)} %velocity.3) | copy-start | bytes 1179652
  40.3 2.0 %collective-permute-start.8 = (f32[40,256]{1,0:T(8,128)S(1)}, f32[40,256]{1,0:T(8,128)S(1)}, u32[]{:S(2)}, u32[]{:S(2)}) collective-permute-start(f32[40,256]{1,0:T(8,128)S(1)} %get-tuple-element.60.moments), channel_id=1, source_target_pairs={{0,1},{1,0},{2,3},{3,2},{4,5},{5,4},{6,7},{7,6},{8,9},{9,8},{10,11... | collective-permute-start | bytes 122888 | tf_op jit(solution)/shard_map/ppermute | solution.py:512
  42.9 7.4 %collective-permute-start.12 = (f32[40,256]{1,0:T(8,128)S(1)}, f32[40,256]{1,0:T(8,128)S(1)}, u32[]{:S(2)}, u32[]{:S(2)}) collective-permute-start(f32[40,256]{1,0:T(8,128)S(1)} %shard_map.139), channel_id=1, source_target_pairs={{0,14},{1,12},{2,15},{3,13},{4,10},{5,8},{6,11},{7,9},{8,6},{9,4},... | collective-permute-start | bytes 122888 | tf_op jit(solution)/shard_map/ppermute | solution.py:618
  48.0 5.2 %collective-permute-start.11 = (f32[40,256]{1,0:T(8,128)S(1)}, f32[40,256]{1,0:T(8,128)S(1)}, u32[]{:S(2)}, u32[]{:S(2)}) collective-permute-start(f32[40,256]{1,0:T(8,128)S(1)} %shard_map.139), channel_id=1, source_target_pairs={{0,10},{1,8},{2,11},{3,9},{4,14},{5,12},{6,15},{7,13},{8,2},{9,0},... | collective-permute-start | bytes 122888 | tf_op jit(solution)/shard_map/ppermute | solution.py:618
  48.6 4.6 %collective-permute-start.10 = (f32[40,256]{1,0:T(8,128)S(1)}, f32[40,256]{1,0:T(8,128)S(1)}, u32[]{:S(2)}, u32[]{:S(2)}) collective-permute-start(f32[40,256]{1,0:T(8,128)S(1)} %shard_map.139), channel_id=1, source_target_pairs={{0,6},{1,4},{2,7},{3,5},{4,2},{5,0},{6,3},{7,1},{8,14},{9,12},{10,... | collective-permute-start | bytes 122888 | tf_op jit(solution)/shard_map/ppermute | solution.py:618
  48.7 4.5 %collective-permute-start.9 = (f32[40,256]{1,0:T(8,128)S(1)}, f32[40,256]{1,0:T(8,128)S(1)}, u32[]{:S(2)}, u32[]{:S(2)}) collective-permute-start(f32[40,256]{1,0:T(8,128)S(1)} %shard_map.139), channel_id=1, source_target_pairs={{0,2},{1,0},{2,3},{3,1},{4,6},{5,4},{6,7},{7,5},{8,10},{9,8},{10,1... | collective-permute-start | bytes 122888 | tf_op jit(solution)/shard_map/ppermute | solution.py:618
  53.2 1.3 %collective-permute-start.13 = (f32[40,256]{1,0:T(8,128)S(1)}, f32[40,256]{1,0:T(8,128)S(1)}, u32[]{:S(2)}, u32[]{:S(2)}) collective-permute-start(f32[40,256]{1,0:T(8,128)S(1)} %add_add_fusion.moments), channel_id=1, source_target_pairs={{0,1},{1,0},{2,3},{3,2},{4,5},{5,4},{6,7},{7,6},{8,9},{9,8},{10,11... | collective-permute-start | bytes 122888 | tf_op jit(solution)/shard_map/ppermute | solution.py:512

commit v3 on v2

--- a/solution.py
+++ b/solution.py
@@ -114,50 +114,60 @@
     return jnp.where(picks[0] | picks[1], 1.0, 0.0).astype(bf16)
 
 
+def to_row(column, size):
+    eye = iota((size, size), 0) == iota((size, size), 1)
+    return jnp.sum(jnp.where(eye, column, 0.0), axis=0, keepdims=True)
+
+
+def to_column(row, size):
+    eye = iota((size, size), 0) == iota((size, size), 1)
+    return jnp.sum(jnp.where(eye, row, 0.0), axis=1, keepdims=True)
+
+
 def slot_matrix(conn, lists, odd, low_valid, high_valid, nodes, ghosts):
     own, _, _ = element_sides(conn, nodes, ghosts)
-    owns = jnp.concatenate([eight_rows([own]).astype(bf16)] * 6, axis=1)
-    slots = one_hot(conn, nodes, 2 * ghosts)
-    active_rows = jnp.where(dot_nt(owns, slots) > 0.0, 1.0, 0.0)
-    active_columns = jnp.where(dot_nt(slots, owns) > 0.0, 1.0, 0.0)
-    numbers = eight_rows([lists[0:1, :].astype(f32), lists[1:2, :].astype(f32)]).astype(bf16)
-    eye = (iota((ghosts, ghosts), 0) == iota((ghosts, ghosts), 1)).astype(bf16)
-    columns = dot_nt(eye, numbers)
+    slot = iota((2 * ghosts, conn.shape[1]), 0) + nodes
+    active = jnp.zeros((2 * ghosts, conn.shape[1]), f32)
+    for a in range(conn.shape[0]):
+        active = jnp.maximum(active, jnp.where(slot == conn[a : a + 1, :], own, 0.0))
+    active = jnp.max(active, axis=1, keepdims=True)
     parts = []
     for side in range(2):
-        span = slice(side * ghosts, (side + 1) * ghosts)
-        smaller = (lists[side : side + 1, :].astype(f32) < columns[:, side : side + 1]).astype(bf16)
-        rank = dot_nt(smaller, active_rows[:, span].astype(bf16))[:, 0:1].astype(jnp.int32)
+        flag = active[side * ghosts : (side + 1) * ghosts]
+        node_row = lists[side : side + 1, :].astype(f32)
+        node_column = to_column(node_row, ghosts)
+        smaller = (node_row < node_column).astype(f32) * to_row(flag, ghosts)
+        rank = jnp.sum(smaller, axis=1, keepdims=True).astype(jnp.int32)
         offset = (1 - odd) * ghosts if side == 0 else odd * ghosts
         valid = low_valid if side == 0 else high_valid
-        live = (active_columns[span, 0:1] > 0.0) & (valid > 0)
+        live = (flag > 0.0) & (valid > 0)
         rows = iota((ghosts, 2 * ghosts), 1)
         parts.append(jnp.where(live & (rows == rank + offset), 1.0, 0.0))
     return jnp.concatenate(parts, axis=0).astype(bf16)
 
 
-def pack_kernel(
-    info, velocity, magnetic, conn_ref, near_ref, far_ref, state_ref, pick_ref, values, arrived
-):
-    nodes = velocity.shape[2]
+def pack_field(field, at, pick, near_ref, far_ref, state_ref):
     ghosts = near_ref.shape[1]
-    copies = []
-    for k in range(6):
-        source = velocity if k < 3 else magnetic
-        copy = pltpu.make_async_copy(source.at[k % 3], values.at[k], arrived.at[k])
-        copy.start()
-        copies.append(copy)
-    pick = pack_matrix(conn_ref[...], info[0], nodes, ghosts)
-    pick_ref[...] = pick
-    for k in range(6):
-        copies[k].wait()
-        block = jnp.transpose(values[k])
-        state_ref[k] = block
+    for k in range(3):
+        block = jnp.transpose(field[k])
+        state_ref[at + k] = block
         first, rest = halves(block)
         second = (block - first.astype(f32) - rest.astype(f32)).astype(bf16)
         packed = dot(pick, first) + dot(pick, rest) + dot(pick, second)
-        near_ref[k] = packed[:ghosts]
-        far_ref[k] = packed[ghosts:]
+        near_ref[at + k] = packed[:ghosts]
+        far_ref[at + k] = packed[ghosts:]
+
+
+def pack_velocity_kernel(info, velocity, conn_ref, near_ref, far_ref, state_ref, pick_ref):
+    pick = pack_matrix(conn_ref[...], info[0], velocity.shape[2], near_ref.shape[1])
+    pick_ref[...] = pick
+    pack_field(velocity, 0, pick, near_ref, far_ref, state_ref)
+
+
+def pack_magnetic_kernel(
+    magnetic, pick_ref, near_in, far_in, state_in, near_ref, far_ref, state_ref
+):
+    pack_field(magnetic, 3, pick_ref[...], near_ref, far_ref, state_ref)
 
 
 def to_planes(high, low, table):
@@ -206,21 +216,13 @@
 
 
 def build_kernel(
-    info, state, pick_ref, planes_hbm, coefs_hbm, rotation_ref, squares_ref,
-    mass_ref, stiff_ref, twist_ref, rates_ref, conn_ref, lists_ref,
-    dense_ref, force_ref, mass_ghost_ref, rest_ghost_ref, packed_ref,
-    planes_ref, coefs_ref, phys_ref, high_ref, low_ref, z_ref, arrived,
+    info, pick_ref, mass_ref, stiff_ref, twist_ref, rates_ref, conn_ref, lists_ref,
+    dense_ref, mass_own_ref, rest_own_ref, mass_ghost_ref, rest_ghost_ref, z_ref,
 ):
-    nodes = state.shape[1]
+    nodes = pick_ref.shape[1]
     elements = conn_ref.shape[1]
     ghosts = lists_ref.shape[1]
     count = 2 * ghosts
-    tables = [
-        pltpu.make_async_copy(planes_hbm, planes_ref, arrived.at[0]),
-        pltpu.make_async_copy(coefs_hbm, coefs_ref, arrived.at[1]),
-    ]
-    for copy in tables:
-        copy.start()
     conn = conn_ref[...]
     pick = pick_ref[...]
     remap = slot_matrix(conn, lists_ref[...], info[0], info[1], info[2], nodes, ghosts)
@@ -260,23 +262,27 @@
     def ghost_part(pair):
         return triple([item[:, nodes:] for item in pair])
 
-    mass_own = own_part(pairs[0])
+    mass_own_ref[...] = own_part(pairs[0])
     mass_ghost_ref[...] = ghost_part(pairs[0])
-    rest_own = []
     for f in range(2):
         used = (pairs[1], pairs[2]) if f == 0 else (pairs[3], pairs[4])
-        rest_own.append(jnp.concatenate([own_part(pair) for pair in used], axis=0))
+        rest_own_ref[f] = jnp.concatenate([own_part(pair) for pair in used], axis=0)
         rest_ghost_ref[f] = jnp.concatenate([ghost_part(pair) for pair in used], axis=0)
 
-    for copy in tables:
-        copy.wait()
+
+def force_kernel(
+    state, planes_ref, coefs_ref, rotation_ref, squares_ref, mass_own, rest_own,
+    force_ref, packed_ref, phys_ref, high_ref, low_ref,
+):
+    nodes = state.shape[1]
+    count = packed_ref.shape[1]
     value = state[...].reshape(6 * nodes, state.shape[2])
     force_ref[...] = forcing(
         value, nodes, planes_ref, coefs_ref, rotation_ref, phys_ref, high_ref, low_ref
     ).reshape(force_ref.shape)
     square = squares_ref[0:1, :]
     for k in range(6):
-        from_force = dot(mass_own, stacked_rows(force_ref[k]))
+        from_force = dot(mass_own[...], stacked_rows(force_ref[k]))
         from_state = dot(rest_own[k // 3], stacked_rows(state[k]))
         packed_ref[k] = from_force - (from_state[:count] + square * from_state[count:])
 
@@ -459,10 +465,8 @@
         out[k % 3] = source[k % 3] + jnp.transpose(change)
 
 
-def call(kernel, outs, operands, scratch=(), flops=0, limit=24, distant=()):
+def call(kernel, outs, operands, scratch=(), flops=0, limit=24, aliases=None):
     specs = [SMEM if operand.dtype == jnp.int32 and operand.ndim == 1 else VMEM for operand in operands]
-    for i in distant:
-        specs[i] = pl.BlockSpec(memory_space=pl.ANY)
     single = not isinstance(outs, list)
     shapes = [outs] if single else outs
     moved = sum(math.prod(o.shape) * o.dtype.itemsize for o in list(operands) + shapes)
@@ -472,6 +476,7 @@
         in_specs=specs,
         out_specs=VMEM if single else [VMEM] * len(outs),
         scratch_shapes=list(scratch),
+        input_output_aliases=aliases or {},
         compiler_params=pltpu.CompilerParams(vmem_limit_bytes=limit * 1024 * 1024),
         cost_estimate=pl.CostEstimate(flops=flops, bytes_accessed=moved, transcendentals=0),
     )(*operands)
@@ -526,35 +531,40 @@
         return swap_near(near), far
 
     near, far, state, pick = call(
-        pack_kernel,
+        pack_velocity_kernel,
         [ends, ends, whole, shape(both, nodes, dtype=bf16)],
-        [info, velocity, magnetic, conn],
-        scratch=[pltpu.VMEM((6, coefs, nodes), f32), pltpu.SemaphoreType.DMA((6,))],
-        distant=(1, 2),
+        [info, velocity, conn],
+    )
+    near, far, state = call(
+        pack_magnetic_kernel,
+        [ends, ends, whole],
+        [magnetic, pick, near, far, state],
+        aliases={2: 0, 3: 1, 4: 2},
     )
     near_state, far_state = exchange(near, far)
-    dense, force, mass_ghost, rest_ghost, packed = call(
+    dense, mass_own, rest_own, mass_ghost, rest_ghost = call(
         build_kernel,
         [
             shape(5 * nodes, nodes + both),
-            whole,
+            shape(both, 3 * nodes, dtype=bf16),
+            shape(2, 2 * both, 3 * nodes, dtype=bf16),
             shape(both, 3 * both, dtype=bf16),
             shape(2, 2 * both, 3 * both, dtype=bf16),
-            packs,
         ],
-        [info, state, pick, plane_table, coef_table, rotation, squares]
-        + [mass_blocks, stiff_blocks, twist_blocks, diffusivity.reshape(1, elements), conn, lists],
+        [info, pick, mass_blocks, stiff_blocks, twist_blocks, diffusivity.reshape(1, elements), conn, lists],
+        scratch=[pltpu.VMEM((5 * nodes, 6 * elements), f32)],
+        flops=1_000_000_000,
+    )
+    force, packed = call(
+        force_kernel,
+        [whole, packs],
+        [state, plane_table, coef_table, rotation, squares, mass_own, rest_own],
         scratch=[
-            pltpu.VMEM(plane_table.shape, bf16),
-            pltpu.VMEM(coef_table.shape, bf16),
             pltpu.VMEM((6 * nodes, planes), f32),
             pltpu.VMEM((6 * nodes, planes), bf16),
             pltpu.VMEM((6 * nodes, planes), bf16),
-            pltpu.VMEM((5 * nodes, 6 * elements), f32),
-            pltpu.SemaphoreType.DMA((2,)),
         ],
-        flops=6_000_000_000,
-        distant=(3, 4),
+        flops=2_000_000_000,
     )
     near, far, force_ghost = call(
         start_kernel,

time: 56 us -> 50.2 us (0.90)
  Pallas kernels: 24.6 us -> 21.2 us
  local copies, waits for them, and re-layouts: 4.31 us -> 1.78 us
    pallas_call x10 -> x12, Pallas kernels: 24.6 us -> 21.2 us  [call(): pl.pallas_call(kernel, out_shape=outs, in_specs=specs, out_specs=VMEM if...]
    unnamed x28 -> x26, local copies, waits for them, and re-layouts: 4.31 us -> 1.78 us
where the time goes in v3:
time: 50.2 us; the launch traced here: 50 us
  Pallas kernels  21.2 us (42%)
  starting transfers between devices  19.3 us (38%)
  waiting for transfers between devices  6.79 us (14%)
  local copies, waits for them, and re-layouts  1.78 us (4%)
  between operations  0.89 us (2%)
    pallas_call x12, Pallas kernels, call(): pl.pallas_call(kernel, out_shape=outs, in_specs=specs, out_specs=VMEM if...  21.2 us
    ppermute x4, starting transfers between devices, local(): term = lax.ppermute(joined, 'mesh', pairs)  7.53 us
    ppermute x4, starting transfers between devices, swap_far(): return lax.ppermute(value, ('runs', 'mesh'), far_pairs)  7.07 us
    ppermute x6, starting transfers between devices, swap_near(): return lax.ppermute(value, 'mesh', near_pairs)  4.65 us
    ppermute x4, waiting for transfers between devices, local(): term = lax.ppermute(joined, 'mesh', pairs)  2.83 us
    ppermute x4, waiting for transfers between devices, swap_far(): return lax.ppermute(value, ('runs', 'mesh'), far_pairs)  2.52 us
    unnamed x26, local copies, waits for them, and re-layouts  1.78 us
    ppermute x6, waiting for transfers between devices, swap_near(): return lax.ppermute(value, 'mesh', near_pairs)  1.45 us
  transfers between devices with their start and end apart: 14, of which 5 were waited for; matrix products, arithmetic and copies ran while one was open for 0% of the time, Pallas kernels for 28%

profile of v3, /device:TPU:0, one launch (start us, length us, event | category | flops | bytes accessed | tf_op | source)
XLA Modules:
  0.0 50.0 jit_solution(9635643995301818039)
XLA Ops:
  0.6 0.0 copy-start
  0.7 0.1 pad_add_fusion.info
  0.7 1.0 %copy-done.1 = f32[3,256,128]{2,1,0:T(8,128)S(1)} copy-done((f32[3,256,128]{2,1,0:T(8,128)S(1)}, f32[3,256,128]{2,1,0:T(8,128)}, u32[]{:S(2)}) %copy-start.1) | copy-done | bytes 393240
  1.8 0.0 copy-start.4
  1.8 0.7 %copy-done.4 = s32[6,128]{1,0:T(8,128)S(1)} copy-done((s32[6,128]{1,0:T(8,128)S(1)}, s32[6,128]{1,0:T(8,128)}, u32[]{:S(2)}) %copy-start.4) | copy-done | bytes 3096
  2.5 1.1 %shard_map.131 = (f32[6,32,256]{2,1,0:T(8,128)S(1)}, f32[6,32,256]{2,1,0:T(8,128)S(1)}, f32[6,128,256]{2,1,0:T(8,128)S(1)}, bf16[64,128]{1,0:T(8,128)(2,1)S(1)}) custom-call(s32[4]{0:T(128)S(1)} %pad_add_fusion.info, f32[3,256,128]{2,1,0:T(8,128)S(1)} %copy-done.1, s32[6,128]{1,0:T(8,128)S(1)} %copy-done.4), custom_call_target="tpu_custom_call" | custom-call | bytes 1592336 | tf_op jit(solution)/shard_map/pallas_call | solution.py:473
  3.6 0.0 copy-done
  3.6 0.0 copy-start.5
  3.6 0.0 copy-start.6
  3.6 0.0 copy-start.7
  3.6 0.3 shard_map.132
  4.0 0.5 %collective-permute-start = (f32[6,32,256]{2,1,0:T(8,128)S(1)}, f32[6,32,256]{2,1,0:T(8,128)S(1)}, u32[]{:S(2)}, u32[]{:S(2)}) collective-permute-start(f32[6,32,256]{2,1,0:T(8,128)S(1)} %get-tuple-element.41), channel_id=1, source_target_pairs={{0,1},{1,0},{2,3},{3,2},{4,5},{5,4},{6,7},{7,6},{8,9},{9,8},{10,11... | collective-permute-start | bytes 589832 | tf_op jit(solution)/shard_map/ppermute | solution.py:517
  4.5 2.6 %collective-permute-start.1 = (f32[6,32,256]{2,1,0:T(8,128)S(1)}, f32[6,32,256]{2,1,0:T(8,128)S(1)}, u32[]{:S(2)}, u32[]{:S(2)}) collective-permute-start(f32[6,32,256]{2,1,0:T(8,128)S(1)} %get-tuple-element.42), channel_id=1, source_target_pairs={{1,2},{2,1},{3,4},{4,3},{5,6},{6,5},{7,8},{8,7},{9,10},{10,9},{11,... | collective-permute-start | bytes 589832 | tf_op jit(solution)/shard_map/ppermute | solution.py:520
  7.1 0.0 copy-done.5
  7.1 0.0 copy-done.6
  7.1 0.0 copy-done.7
  7.1 0.0 copy-done.8
  7.1 0.0 copy-done.9
  7.1 0.0 copy-start.3
  7.1 0.0 copy-start.10
  7.1 0.0 copy-start.11
  7.1 0.0 copy-start.12
  7.2 2.4 %shard_map.133 = (f32[640,192]{1,0:T(8,128)S(1)}, bf16[64,384]{1,0:T(8,128)(2,1)S(1)}, bf16[2,128,384]{2,1,0:T(8,128)(2,1)S(1)}, bf16[64,192]{1,0:T(8,128)(2,1)S(1)}, bf16[2,128,192]{2,1,0:T(8,128)(2,1)S(1)}) custom-call(s32[4]{0:T(128)S(1)} %pad_add_fusion.info, bf16[64,128]{1,0:T(8,128)(2,1)S(1)} %get-tuple-element.37.pick_ref, ...), custom_call_target="tpu_custom_call" | custom-call | flops 1000000000 | bytes 935696 | tf_op jit(solution)/shard_map/pallas_call | solution.py:473
  9.5 0.0 copy-done.3
  9.5 0.0 copy-done.10
  9.5 0.0 copy-done.11
  9.5 0.0 copy-done.12
  9.5 3.0 %shard_map.134 = (f32[6,128,256]{2,1,0:T(8,128)S(1)}, f32[6,64,256]{2,1,0:T(8,128)S(1)}) custom-call(f32[6,128,256]{2,1,0:T(8,128)S(1)} %get-tuple-element.43.state, bf16[512,512]{1,0:T(8,128)(2,1)S(1)} %copy-done.11, bf16[1024,256]{1,0:T(8,128)(2,1)S(1)} %copy-done.10, f32[8,512]{1,0:T(8,128)S(1)} %copy-done.12, f32[8,256]{1,0:T(8,128)S(1)} %copy-done.3, ...), custom_call_target="tpu_custom_call" | custom-call | flops 2000000000 | bytes 3284992 | tf_op jit(solution)/shard_map/pallas_call | solution.py:473
  12.6 0.0 collective-permute-done.near
  12.6 0.0 collective-permute-done.1.far
  12.6 2.2 %shard_map.135 = (f32[6,32,256]{2,1,0:T(8,128)S(1)}, f32[6,32,256]{2,1,0:T(8,128)S(1)}, f32[6,64,256]{2,1,0:T(8,128)S(1)}) custom-call(s32[4]{0:T(128)S(1)} %pad_add_fusion.info, f32[6,32,256]{2,1,0:T(8,128)S(1)} %collective-permute-done.near, f32[6,32,256]{2,1,0:T(8,128)S(1)} %collective-permute-done.1.far, f32[6,64,256]{2,1,0:T(8,128)S(1)} %get-tuple-element.46.packed, ...), custom_call_target="tpu_custom_call" | custom-call | flops 1000000000 | bytes 2768912 | tf_op jit(solution)/shard_map/pallas_call | solution.py:473
  14.8 0.2 collective-permute-start.2
  15.0 1.5 %collective-permute-start.3 = (f32[6,32,256]{2,1,0:T(8,128)S(1)}, f32[6,32,256]{2,1,0:T(8,128)S(1)}, u32[]{:S(2)}, u32[]{:S(2)}) collective-permute-start(f32[6,32,256]{2,1,0:T(8,128)S(1)} %get-tuple-element.50), channel_id=1, source_target_pairs={{1,2},{2,1},{3,4},{4,3},{5,6},{6,5},{7,8},{8,7},{9,10},{10,9},{11,... | collective-permute-start | bytes 589832 | tf_op jit(solution)/shard_map/ppermute | solution.py:520
  16.5 4.2 %shard_map.136 = (bf16[2,384,384]{2,1,0:T(8,128)(2,1)S(1)}, bf16[2,384,192]{2,1,0:T(8,128)(2,1)S(1)}, bf16[2,128,384]{2,1,0:T(8,128)(2,1)S(1)}, f32[6,128,256]{2...) custom-call(s32[4]{0:T(128)S(1)} %pad_add_fusion.info, ...), custom_call_target="tpu_custom_call" | custom-call | flops 2000000000 | bytes 5931024 | tf_op jit(solution)/shard_map/pallas_call | solution.py:473
  20.7 0.0 collective-permute-done.2.near
  20.7 0.0 collective-permute-done.3.far
  20.7 0.8 %shard_map.137 = (f32[6,32,256]{2,1,0:T(8,128)S(1)}, f32[6,32,256]{2,1,0:T(8,128)S(1)}) custom-call(s32[4]{0:T(128)S(1)} %pad_add_fusion.info, f32[6,32,256]{2,1,0:T(8,128)S(1)} %collective-permute-done.2.near, f32[6,32,256]{2,1,0:T(8,128)S(1)} %collective-permute-done.3.far, f32[6,64,256]{2,1,0:T(8,128)S(1)} %get-tuple-element.54.packed, ...), custom_call_target="tpu_custom_call" | custom-call | flops 100000000 | bytes 1482768 | tf_op jit(solution)/shard_map/pallas_call | solution.py:473
  21.6 0.8 %collective-permute-start.4 = (f32[6,32,256]{2,1,0:T(8,128)S(1)}, f32[6,32,256]{2,1,0:T(8,128)S(1)}, u32[]{:S(2)}, u32[]{:S(2)}) collective-permute-start(f32[6,32,256]{2,1,0:T(8,128)S(1)} %get-tuple-element.56), channel_id=1, source_target_pairs={{0,1},{1,0},{2,3},{3,2},{4,5},{5,4},{6,7},{7,6},{8,9},{9,8},{10,11... | collective-permute-start | bytes 589832 | tf_op jit(solution)/shard_map/ppermute | solution.py:517
  22.4 1.5 %collective-permute-start.5 = (f32[6,32,256]{2,1,0:T(8,128)S(1)}, f32[6,32,256]{2,1,0:T(8,128)S(1)}, u32[]{:S(2)}, u32[]{:S(2)}) collective-permute-start(f32[6,32,256]{2,1,0:T(8,128)S(1)} %get-tuple-element.57), channel_id=1, source_target_pairs={{1,2},{2,1},{3,4},{4,3},{5,6},{6,5},{7,8},{8,7},{9,10},{10,9},{11,... | collective-permute-start | bytes 589832 | tf_op jit(solution)/shard_map/ppermute | solution.py:520
  23.9 2.1 %shard_map.138 = (f32[6,128,256]{2,1,0:T(8,128)S(1)}, f32[6,128,256]{2,1,0:T(8,128)S(1)}, f32[6,64,256]{2,1,0:T(8,128)S(1)}, f32[16,256]{1,0:T(8,128)S(1)}) custom-call(s32[4]{0:T(128)S(1)} %pad_add_fusion.info, f32[6,32,256]{2,1,0:T(8,128)S(1)} %collective-permute-done.2.near, f32[6,32,256]{2,1,0:T(8,128)S(1)} %collective-permute-done.3.far, ...), custom_call_target="tpu_custom_call" | custom-call | flops 2000000000 | bytes 4841488 | tf_op jit(solution)/shard_map/pallas_call | solution.py:473
  26.0 0.0 collective-permute-done.4.near
  26.0 2.1 %collective-permute-done.5.far = f32[6,32,256]{2,1,0:T(8,128)S(1)} collective-permute-done((f32[6,32,256]{2,1,0:T(8,128)S(1)}, f32[6,32,256]{2,1,0:T(8,128)S(1)}, u32[]{:S(2)}, u32[]{:S(2)}) %collective-permute-start.5) | collective-permute-done | bytes 196640 | tf_op jit(solution)/shard_map/ppermute | solution.py:520
  28.1 0.8 %shard_map.139 = (f32[6,32,256]{2,1,0:T(8,128)S(1)}, f32[6,32,256]{2,1,0:T(8,128)S(1)}) custom-call(s32[4]{0:T(128)S(1)} %pad_add_fusion.info, f32[6,32,256]{2,1,0:T(8,128)S(1)} %collective-permute-done.4.near, f32[6,32,256]{2,1,0:T(8,128)S(1)} %collective-permute-done.5.far, f32[6,64,256]{2,1,0:T(8,128)S(1)} %get-tuple-element.61.packed, ...), custom_call_target="tpu_custom_call" | custom-call | flops 100000000 | bytes 1482768 | tf_op jit(solution)/shard_map/pallas_call | solution.py:473
  28.9 1.7 %collective-permute-start.7 = (f32[6,32,256]{2,1,0:T(8,128)S(1)}, f32[6,32,256]{2,1,0:T(8,128)S(1)}, u32[]{:S(2)}, u32[]{:S(2)}) collective-permute-start(f32[6,32,256]{2,1,0:T(8,128)S(1)} %get-tuple-element.63), channel_id=1, source_target_pairs={{0,1},{1,0},{2,3},{3,2},{4,5},{5,4},{6,7},{7,6},{8,9},{9,8},{10,11... | collective-permute-start | bytes 589832 | tf_op jit(solution)/shard_map/ppermute | solution.py:517
  30.6 1.5 %collective-permute-start.6 = (f32[6,32,256]{2,1,0:T(8,128)S(1)}, f32[6,32,256]{2,1,0:T(8,128)S(1)}, u32[]{:S(2)}, u32[]{:S(2)}) collective-permute-start(f32[6,32,256]{2,1,0:T(8,128)S(1)} %get-tuple-element.62), channel_id=1, source_target_pairs={{1,2},{2,1},{3,4},{4,3},{5,6},{6,5},{7,8},{8,7},{9,10},{10,9},{11,... | collective-permute-start | bytes 589832 | tf_op jit(solution)/shard_map/ppermute | solution.py:520
  32.0 0.0 collective-permute-done.7.near_last
  32.0 2.6 %shard_map.140 = (f32[6,128,256]{2,1,0:T(8,128)S(1)}, f32[6,32,256]{2,1,0:T(8,128)S(1)}, f32[40,256]{1,0:T(8,128)S(1)}) custom-call(s32[4]{0:T(128)S(1)} %pad_add_fusion.info, f32[6,32,256]{2,1,0:T(8,128)S(1)} %collective-permute-done.4.near, f32[6,32,256]{2,1,0:T(8,128)S(1)} %collective-permute-done.5.far, ...), custom_call_target="tpu_custom_call" | custom-call | flops 2000000000 | bytes 4300816 | tf_op jit(solution)/shard_map/pallas_call | solution.py:473
  34.6 0.0 copy-start.2
  34.6 1.1 %collective-permute-start.8 = (f32[40,256]{1,0:T(8,128)S(1)}, f32[40,256]{1,0:T(8,128)S(1)}, u32[]{:S(2)}, u32[]{:S(2)}) collective-permute-start(f32[40,256]{1,0:T(8,128)S(1)} %get-tuple-element.70.moments), channel_id=1, source_target_pairs={{0,1},{1,0},{2,3},{3,2},{4,5},{5,4},{6,7},{7,6},{8,9},{9,8},{10,11... | collective-permute-start | bytes 122888 | tf_op jit(solution)/shard_map/ppermute | solution.py:517
  35.8 0.4 collective-permute-done.6.far
  36.2 0.4 collective-permute-done.8.rest_0_
  36.7 0.6 %shard_map.141 = f32[40,256]{1,0:T(8,128)S(1)} custom-call(s32[4]{0:T(128)S(1)} %pad_add_fusion.info, f32[6,32,256]{2,1,0:T(8,128)S(1)} %collective-permute-done.6.far, f32[6,32,256]{2,1,0:T(8,128)S(1)} %get-tuple-element.69.back, f32[40,256]{1,0:T(8,128)S(1)} %get-tuple-element.70.moments, f32[40,256]{1,0:T(8,128)S(1)} %collective-permute-done.8.rest_0_), custom_call_target="tpu_custom_call" | custom-call | bytes 516112 | tf_op jit(solution)/shard_map/pallas_call | solution.py:473
  37.2 5.3 %collective-permute-start.12 = (f32[40,256]{1,0:T(8,128)S(1)}, f32[40,256]{1,0:T(8,128)S(1)}, u32[]{:S(2)}, u32[]{:S(2)}) collective-permute-start(f32[40,256]{1,0:T(8,128)S(1)} %shard_map.141), channel_id=1, source_target_pairs={{0,14},{1,12},{2,15},{3,13},{4,10},{5,8},{6,11},{7,9},{8,6},{9,4},... | collective-permute-start | bytes 122888 | tf_op jit(solution)/shard_map/ppermute | solution.py:628
  42.5 0.4 collective-permute-start.11
  43.0 0.1 collective-permute-start.10
  43.1 1.7 %collective-permute-start.9 = (f32[40,256]{1,0:T(8,128)S(1)}, f32[40,256]{1,0:T(8,128)S(1)}, u32[]{:S(2)}, u32[]{:S(2)}) collective-permute-start(f32[40,256]{1,0:T(8,128)S(1)} %shard_map.141), channel_id=1, source_target_pairs={{0,2},{1,0},{2,3},{3,1},{4,6},{5,4},{6,7},{7,5},{8,10},{9,8},{10,1... | collective-permute-start | bytes 122888 | tf_op jit(solution)/shard_map/ppermute | solution.py:628
  44.8 0.0 collective-permute-done.12
  44.8 2.8 %collective-permute-done.11 = f32[40,256]{1,0:T(8,128)S(1)} collective-permute-done((f32[40,256]{1,0:T(8,128)S(1)}, f32[40,256]{1,0:T(8,128)S(1)}, u32[]{:S(2)}, u32[]{:S(2)}) %collective-permute-start.11) | collective-permute-done | bytes 40992 | tf_op jit(solution)/shard_map/ppermute | solution.py:628
  47.6 0.0 collective-permute-done.10
  47.6 0.0 collective-permute-done.9
  47.6 0.3 collective-permute-start.13
  47.9 1.0 %collective-permute-done.13.other = f32[40,256]{1,0:T(8,128)S(1)} collective-permute-done((f32[40,256]{1,0:T(8,128)S(1)}, f32[40,256]{1,0:T(8,128)S(1)}, u32[]{:S(2)}, u32[]{:S(2)}) %collective-permute-start.13) | collective-permute-done | bytes 40992 | tf_op jit(solution)/shard_map/ppermute | solution.py:517
  48.9 0.0 copy-done.2
  48.9 1.1 %shard_map.142 = (f32[3,256,128]{2,1,0:T(8,128)}, f32[3,256,128]{2,1,0:T(8,128)}) custom-call(f32[40,256]{1,0:T(8,128)S(1)} %add_add_fusion.moments, f32[40,256]{1,0:T(8,128)S(1)} %collective-permute-done.13.other, f32[3,256,128]{2,1,0:T(8,128)S(1)} %copy-done.2, f32[3,256,128]{2,1,0:T(8,128)S(1)} %copy-done, ...), custom_call_target="tpu_custom_call" | custom-call | flops 10000000 | bytes 4014080 | tf_op jit(solution)/shard_map/pallas_call | solution.py:473
  (4 shorter events, 0.0 us)
Async XLA Ops:
  0.6 3.0 %copy-start = (f32[3,256,128]{2,1,0:T(8,128)S(1)}, f32[3,256,128]{2,1,0:T(8,128)}, u32[]{:S(2)}) copy-start(f32[3,256,128]{2,1,0:T(8,128)} %magnetic.3) | copy-start | bytes 1179652
  0.7 1.0 %copy-start.1 = (f32[3,256,128]{2,1,0:T(8,128)S(1)}, f32[3,256,128]{2,1,0:T(8,128)}, u32[]{:S(2)}) copy-start(f32[3,256,128]{2,1,0:T(8,128)} %velocity.3) | copy-start | bytes 1179652
  1.8 0.7 %copy-start.4 = (s32[6,128]{1,0:T(8,128)S(1)}, s32[6,128]{1,0:T(8,128)}, u32[]{:S(2)}) copy-start(s32[6,128]{1,0:T(8,128)} %conn_ref.3) | copy-start | bytes 9220
  3.6 3.5 %copy-start.5 = (f32[6,6,128]{2,1,0:T(8,128)S(1)}, f32[6,6,128]{2,1,0:T(8,128)}, u32[]{:S(2)}) copy-start(f32[6,6,128]{2,1,0:T(8,128)} %mass_ref.1) | copy-start | bytes 55300
  3.6 3.5 %copy-start.6 = (f32[6,6,128]{2,1,0:T(8,128)S(1)}, f32[6,6,128]{2,1,0:T(8,128)}, u32[]{:S(2)}) copy-start(f32[6,6,128]{2,1,0:T(8,128)} %stiff_ref.1) | copy-start | bytes 55300
  3.6 3.5 %copy-start.7 = (f32[6,6,128]{2,1,0:T(8,128)S(1)}, f32[6,6,128]{2,1,0:T(8,128)}, u32[]{:S(2)}) copy-start(f32[6,6,128]{2,1,0:T(8,128)} %twist_ref.1) | copy-start | bytes 55300
  4.0 8.6 %collective-permute-start = (f32[6,32,256]{2,1,0:T(8,128)S(1)}, f32[6,32,256]{2,1,0:T(8,128)S(1)}, u32[]{:S(2)}, u32[]{:S(2)}) collective-permute-start(f32[6,32,256]{2,1,0:T(8,128)S(1)} %get-tuple-element.41), channel_id=1, source_target_pairs={{0,1},{1,0},{2,3},{3,2},{4,5},{5,4},{6,7},{7,6},{8,9},{9,8},{10,11... | collective-permute-start | bytes 589832 | tf_op jit(solution)/shard_map/ppermute | solution.py:517
  4.5 2.6 %copy-start.8 = (s32[2,32]{1,0:T(2,128)S(1)}, s32[2,32]{1,0:T(2,128)}, u32[]{:S(2)}) copy-start(s32[2,32]{1,0:T(2,128)} %lists_ref.1) | copy-start | bytes 772
  4.5 2.6 %copy-start.9 = (f32[128]{0:T(128)S(1)}, f32[128]{0:T(128)}, u32[]{:S(2)}) copy-start(f32[128]{0:T(128)} %param.17) | copy-start | bytes 1540
  4.5 8.1 %collective-permute-start.1 = (f32[6,32,256]{2,1,0:T(8,128)S(1)}, f32[6,32,256]{2,1,0:T(8,128)S(1)}, u32[]{:S(2)}, u32[]{:S(2)}) collective-permute-start(f32[6,32,256]{2,1,0:T(8,128)S(1)} %get-tuple-element.42), channel_id=1, source_target_pairs={{1,2},{2,1},{3,4},{4,3},{5,6},{6,5},{7,8},{8,7},{9,10},{10,9},{11,... | collective-permute-start | bytes 589832 | tf_op jit(solution)/shard_map/ppermute | solution.py:520
  7.1 2.4 %copy-start.3 = (f32[8,256]{1,0:T(8,128)S(1)}, f32[8,256]{1,0:T(8,128)}, u32[]{:S(2)}) copy-start(f32[8,256]{1,0:T(8,128)} %constant.32.clone.squares_ref) | copy-start | bytes 24580
  7.1 2.4 %copy-start.10 = (bf16[1024,256]{1,0:T(8,128)(2,1)S(1)}, bf16[1024,256]{1,0:T(8,128)(2,1)}, u32[]{:S(2)}) copy-start(bf16[1024,256]{1,0:T(8,128)(2,1)} %constant.30.clone.coefs_ref) | copy-start | bytes 1572868
  7.1 2.4 %copy-start.11 = (bf16[512,512]{1,0:T(8,128)(2,1)S(1)}, bf16[512,512]{1,0:T(8,128)(2,1)}, u32[]{:S(2)}) copy-start(bf16[512,512]{1,0:T(8,128)(2,1)} %constant.29.clone.planes_ref) | copy-start | bytes 1572868
  7.1 2.4 %copy-start.12 = (f32[8,512]{1,0:T(8,128)S(1)}, f32[8,512]{1,0:T(8,128)}, u32[]{:S(2)}) copy-start(f32[8,512]{1,0:T(8,128)} %constant.31.clone.rotation_ref) | copy-start | bytes 49156
  14.8 5.9 %collective-permute-start.2 = (f32[6,32,256]{2,1,0:T(8,128)S(1)}, f32[6,32,256]{2,1,0:T(8,128)S(1)}, u32[]{:S(2)}, u32[]{:S(2)}) collective-permute-start(f32[6,32,256]{2,1,0:T(8,128)S(1)} %get-tuple-element.49), channel_id=1, source_target_pairs={{0,1},{1,0},{2,3},{3,2},{4,5},{5,4},{6,7},{7,6},{8,9},{9,8},{10,11... | collective-permute-start | bytes 589832 | tf_op jit(solution)/shard_map/ppermute | solution.py:517
  15.0 5.7 %collective-permute-start.3 = (f32[6,32,256]{2,1,0:T(8,128)S(1)}, f32[6,32,256]{2,1,0:T(8,128)S(1)}, u32[]{:S(2)}, u32[]{:S(2)}) collective-permute-start(f32[6,32,256]{2,1,0:T(8,128)S(1)} %get-tuple-element.50), channel_id=1, source_target_pairs={{1,2},{2,1},{3,4},{4,3},{5,6},{6,5},{7,8},{8,7},{9,10},{10,9},{11,... | collective-permute-start | bytes 589832 | tf_op jit(solution)/shard_map/ppermute | solution.py:520
  21.6 4.4 %collective-permute-start.4 = (f32[6,32,256]{2,1,0:T(8,128)S(1)}, f32[6,32,256]{2,1,0:T(8,128)S(1)}, u32[]{:S(2)}, u32[]{:S(2)}) collective-permute-start(f32[6,32,256]{2,1,0:T(8,128)S(1)} %get-tuple-element.56), channel_id=1, source_target_pairs={{0,1},{1,0},{2,3},{3,2},{4,5},{5,4},{6,7},{7,6},{8,9},{9,8},{10,11... | collective-permute-start | bytes 589832 | tf_op jit(solution)/shard_map/ppermute | solution.py:517
  22.4 5.7 %collective-permute-start.5 = (f32[6,32,256]{2,1,0:T(8,128)S(1)}, f32[6,32,256]{2,1,0:T(8,128)S(1)}, u32[]{:S(2)}, u32[]{:S(2)}) collective-permute-start(f32[6,32,256]{2,1,0:T(8,128)S(1)} %get-tuple-element.57), channel_id=1, source_target_pairs={{1,2},{2,1},{3,4},{4,3},{5,6},{6,5},{7,8},{8,7},{9,10},{10,9},{11,... | collective-permute-start | bytes 589832 | tf_op jit(solution)/shard_map/ppermute | solution.py:520
  28.9 3.2 %collective-permute-start.7 = (f32[6,32,256]{2,1,0:T(8,128)S(1)}, f32[6,32,256]{2,1,0:T(8,128)S(1)}, u32[]{:S(2)}, u32[]{:S(2)}) collective-permute-start(f32[6,32,256]{2,1,0:T(8,128)S(1)} %get-tuple-element.63), channel_id=1, source_target_pairs={{0,1},{1,0},{2,3},{3,2},{4,5},{5,4},{6,7},{7,6},{8,9},{9,8},{10,11... | collective-permute-start | bytes 589832 | tf_op jit(solution)/shard_map/ppermute | solution.py:517
  30.6 5.7 %collective-permute-start.6 = (f32[6,32,256]{2,1,0:T(8,128)S(1)}, f32[6,32,256]{2,1,0:T(8,128)S(1)}, u32[]{:S(2)}, u32[]{:S(2)}) collective-permute-start(f32[6,32,256]{2,1,0:T(8,128)S(1)} %get-tuple-element.62), channel_id=1, source_target_pairs={{1,2},{2,1},{3,4},{4,3},{5,6},{6,5},{7,8},{8,7},{9,10},{10,9},{11,... | collective-permute-start | bytes 589832 | tf_op jit(solution)/shard_map/ppermute | solution.py:520
  34.6 14.3 %copy-start.2 = (f32[3,256,128]{2,1,0:T(8,128)S(1)}, f32[3,256,128]{2,1,0:T(8,128)}, u32[]{:S(2)}) copy-start(f32[3,256,128]{2,1,0:T(8,128)} %velocity.3) | copy-start | bytes 1179652
  34.6 2.0 %collective-permute-start.8 = (f32[40,256]{1,0:T(8,128)S(1)}, f32[40,256]{1,0:T(8,128)S(1)}, u32[]{:S(2)}, u32[]{:S(2)}) collective-permute-start(f32[40,256]{1,0:T(8,128)S(1)} %get-tuple-element.70.moments), channel_id=1, source_target_pairs={{0,1},{1,0},{2,3},{3,2},{4,5},{5,4},{6,7},{7,6},{8,9},{9,8},{10,11... | collective-permute-start | bytes 122888 | tf_op jit(solution)/shard_map/ppermute | solution.py:517
  37.2 7.5 %collective-permute-start.12 = (f32[40,256]{1,0:T(8,128)S(1)}, f32[40,256]{1,0:T(8,128)S(1)}, u32[]{:S(2)}, u32[]{:S(2)}) collective-permute-start(f32[40,256]{1,0:T(8,128)S(1)} %shard_map.141), channel_id=1, source_target_pairs={{0,14},{1,12},{2,15},{3,13},{4,10},{5,8},{6,11},{7,9},{8,6},{9,4},... | collective-permute-start | bytes 122888 | tf_op jit(solution)/shard_map/ppermute | solution.py:628
  42.5 5.1 %collective-permute-start.11 = (f32[40,256]{1,0:T(8,128)S(1)}, f32[40,256]{1,0:T(8,128)S(1)}, u32[]{:S(2)}, u32[]{:S(2)}) collective-permute-start(f32[40,256]{1,0:T(8,128)S(1)} %shard_map.141), channel_id=1, source_target_pairs={{0,10},{1,8},{2,11},{3,9},{4,14},{5,12},{6,15},{7,13},{8,2},{9,0},... | collective-permute-start | bytes 122888 | tf_op jit(solution)/shard_map/ppermute | solution.py:628
  43.0 4.6 %collective-permute-start.10 = (f32[40,256]{1,0:T(8,128)S(1)}, f32[40,256]{1,0:T(8,128)S(1)}, u32[]{:S(2)}, u32[]{:S(2)}) collective-permute-start(f32[40,256]{1,0:T(8,128)S(1)} %shard_map.141), channel_id=1, source_target_pairs={{0,6},{1,4},{2,7},{3,5},{4,2},{5,0},{6,3},{7,1},{8,14},{9,12},{10,... | collective-permute-start | bytes 122888 | tf_op jit(solution)/shard_map/ppermute | solution.py:628
  43.1 4.5 %collective-permute-start.9 = (f32[40,256]{1,0:T(8,128)S(1)}, f32[40,256]{1,0:T(8,128)S(1)}, u32[]{:S(2)}, u32[]{:S(2)}) collective-permute-start(f32[40,256]{1,0:T(8,128)S(1)} %shard_map.141), channel_id=1, source_target_pairs={{0,2},{1,0},{2,3},{3,1},{4,6},{5,4},{6,7},{7,5},{8,10},{9,8},{10,1... | collective-permute-start | bytes 122888 | tf_op jit(solution)/shard_map/ppermute | solution.py:628
  47.6 1.3 %collective-permute-start.13 = (f32[40,256]{1,0:T(8,128)S(1)}, f32[40,256]{1,0:T(8,128)S(1)}, u32[]{:S(2)}, u32[]{:S(2)}) collective-permute-start(f32[40,256]{1,0:T(8,128)S(1)} %add_add_fusion.moments), channel_id=1, source_target_pairs={{0,1},{1,0},{2,3},{3,2},{4,5},{5,4},{6,7},{7,6},{8,9},{9,8},{10,11... | collective-permute-start | bytes 122888 | tf_op jit(solution)/shard_map/ppermute | solution.py:517

commit v4 on v3

--- a/solution.py
+++ b/solution.py
@@ -21,7 +21,6 @@
 f32 = jnp.float32
 bf16 = jnp.bfloat16
 VMEM = pl.BlockSpec(memory_space=pltpu.VMEM)
-SMEM = pl.BlockSpec(memory_space=pltpu.SMEM)
 
 
 def split_table(table):
@@ -106,6 +105,7 @@
     ranks = dot(flags.astype(bf16), before).astype(jnp.int32)
     rows = iota((2 * ghosts, nodes), 0)
     picks = []
+    odd = odd[:, :nodes].astype(jnp.int32)
     for side in range(2):
         offset = (1 - odd) * ghosts if side == 0 else odd * ghosts
         rank = ranks[side : side + 1, :]
@@ -124,7 +124,7 @@
     return jnp.sum(jnp.where(eye, row, 0.0), axis=1, keepdims=True)
 
 
-def slot_matrix(conn, lists, odd, low_valid, high_valid, nodes, ghosts):
+def slot_matrix(conn, lists, info, nodes, ghosts):
     own, _, _ = element_sides(conn, nodes, ghosts)
     slot = iota((2 * ghosts, conn.shape[1]), 0) + nodes
     active = jnp.zeros((2 * ghosts, conn.shape[1]), f32)
@@ -138,9 +138,9 @@
         node_column = to_column(node_row, ghosts)
         smaller = (node_row < node_column).astype(f32) * to_row(flag, ghosts)
         rank = jnp.sum(smaller, axis=1, keepdims=True).astype(jnp.int32)
+        odd = info[0:1, : 2 * ghosts].astype(jnp.int32)
         offset = (1 - odd) * ghosts if side == 0 else odd * ghosts
-        valid = low_valid if side == 0 else high_valid
-        live = (flag > 0.0) & (valid > 0)
+        live = (flag > 0.0) & (info[1 + side : 2 + side, : 2 * ghosts] > 0.0)
         rows = iota((ghosts, 2 * ghosts), 1)
         parts.append(jnp.where(live & (rows == rank + offset), 1.0, 0.0))
     return jnp.concatenate(parts, axis=0).astype(bf16)
@@ -159,7 +159,7 @@
 
 
 def pack_velocity_kernel(info, velocity, conn_ref, near_ref, far_ref, state_ref, pick_ref):
-    pick = pack_matrix(conn_ref[...], info[0], velocity.shape[2], near_ref.shape[1])
+    pick = pack_matrix(conn_ref[...], info[0:1, :], velocity.shape[2], near_ref.shape[1])
     pick_ref[...] = pick
     pack_field(velocity, 0, pick, near_ref, far_ref, state_ref)
 
@@ -225,7 +225,7 @@
     count = 2 * ghosts
     conn = conn_ref[...]
     pick = pick_ref[...]
-    remap = slot_matrix(conn, lists_ref[...], info[0], info[1], info[2], nodes, ghosts)
+    remap = slot_matrix(conn, lists_ref[...], info, nodes, ghosts)
     rates = rates_ref[0:1, :]
     step = 16
     for row in range(0, nodes, step):
@@ -288,7 +288,7 @@
 
 
 def ghost_block(info, near, far, k):
-    distant = jnp.where(info[3] > 0, far[k], 0.0)
+    distant = jnp.where(info[3:4, :] > 0.0, far[k], 0.0)
     return jnp.concatenate([near[k], distant], axis=0)
 
 
@@ -428,7 +428,7 @@
         total = total + other[...]
     out[...] = total
     for k in range(6):
-        distant = jnp.where(info[3] > 0, far[k], 0.0)
+        distant = jnp.where(info[3:4, :] > 0.0, far[k], 0.0)
         out[30 + k : 31 + k, :] += weight * jnp.sum(distant * back[k], axis=0, keepdims=True)
 
 
@@ -466,14 +466,13 @@
 
 
 def call(kernel, outs, operands, scratch=(), flops=0, limit=24, aliases=None):
-    specs = [SMEM if operand.dtype == jnp.int32 and operand.ndim == 1 else VMEM for operand in operands]
     single = not isinstance(outs, list)
     shapes = [outs] if single else outs
     moved = sum(math.prod(o.shape) * o.dtype.itemsize for o in list(operands) + shapes)
     return pl.pallas_call(
         kernel,
         out_shape=outs,
-        in_specs=specs,
+        in_specs=[VMEM] * len(operands),
         out_specs=VMEM if single else [VMEM] * len(outs),
         scratch_shapes=list(scratch),
         input_output_aliases=aliases or {},
@@ -501,7 +500,9 @@
     low_valid = (index > 0).astype(jnp.int32)
     high_valid = (index < count - 1).astype(jnp.int32)
     far_valid = jnp.where(odd == 1, high_valid, low_valid)
-    info = jnp.stack([odd, low_valid, high_valid, far_valid]).astype(jnp.int32)
+    zero = jnp.zeros_like(odd)
+    info = jnp.stack([odd, low_valid, high_valid, far_valid, zero, zero, zero, zero]).astype(f32)
+    info = jnp.broadcast_to(info[:, None], (8, coefs))
 
     near_pairs = [(i, i ^ 1) for i in range(count)]
     far_pairs = []

time: 50.2 us -> 47.7 us (0.950)
  Pallas kernels: 21.2 us -> 16.4 us
  waiting for transfers between devices: 6.79 us -> 7.94 us
  starting transfers between devices: 19.3 us -> 20.3 us
    pallas_call x12, Pallas kernels: 21.2 us -> 16.4 us  [call(): pl.pallas_call(kernel, out_shape=outs, in_specs=[VMEM] * len(operands), o...]
    ppermute x4, waiting for transfers between devices: 2.52 us -> 4.09 us  [swap_far(): return lax.ppermute(value, ('runs', 'mesh'), far_pairs)]
    ppermute x6, starting transfers between devices: 4.65 us -> 5.25 us  [swap_near(): return lax.ppermute(value, 'mesh', near_pairs)]
    unnamed x26 -> x28, local copies, waits for them, and re-layouts: 1.78 us -> 1.75 us
  transfers between devices with their start and end apart: 14 -> 14, of which waited for: 5 -> 5; matrix products, arithmetic and copies ran while one was open for 0% -> 0% of each run, Pallas kernels for 28% -> 25%
where the time goes in v4:
time: 47.7 us; the launch traced here: 47.5 us
  starting transfers between devices  20.3 us (43%)
  Pallas kernels  16.4 us (34%)
  waiting for transfers between devices  7.94 us (17%)
  local copies, waits for them, and re-layouts  1.92 us (4%)
  between operations  0.91 us (2%)
    pallas_call x12, Pallas kernels, call(): pl.pallas_call(kernel, out_shape=outs, in_specs=[VMEM] * len(operands), o...  16.4 us
    ppermute x4, starting transfers between devices, local(): term = lax.ppermute(joined, 'mesh', pairs)  7.96 us
    ppermute x4, starting transfers between devices, swap_far(): return lax.ppermute(value, ('runs', 'mesh'), far_pairs)  7.07 us
    ppermute x6, starting transfers between devices, swap_near(): return lax.ppermute(value, 'mesh', near_pairs)  5.25 us
    ppermute x4, waiting for transfers between devices, swap_far(): return lax.ppermute(value, ('runs', 'mesh'), far_pairs)  4.09 us
    ppermute x4, waiting for transfers between devices, local(): term = lax.ppermute(joined, 'mesh', pairs)  2.82 us
    unnamed x28, local copies, waits for them, and re-layouts  1.75 us
    ppermute x6, waiting for transfers between devices, swap_near(): return lax.ppermute(value, 'mesh', near_pairs)  1.02 us
  transfers between devices with their start and end apart: 14, of which 5 were waited for; matrix products, arithmetic and copies ran while one was open for 0% of the time, Pallas kernels for 25%

profile of v4, /device:TPU:0, one launch (start us, length us, event | category | flops | bytes accessed | tf_op | source)
XLA Modules:
  0.0 47.5 jit_solution(5573073668204102767)
XLA Ops:
  0.6 0.0 copy-start
  0.7 0.1 stack.22
  0.8 0.1 broadcast_in_dim.2.info
  0.8 1.0 %copy-done.1 = f32[3,256,128]{2,1,0:T(8,128)S(1)} copy-done((f32[3,256,128]{2,1,0:T(8,128)S(1)}, f32[3,256,128]{2,1,0:T(8,128)}, u32[]{:S(2)}) %copy-start.1) | copy-done | bytes 393240
  1.8 0.7 %copy-done.4 = s32[6,128]{1,0:T(8,128)S(1)} copy-done((s32[6,128]{1,0:T(8,128)S(1)}, s32[6,128]{1,0:T(8,128)}, u32[]{:S(2)}) %copy-start.4) | copy-done | bytes 3096
  2.5 0.6 %shard_map.131 = (f32[6,32,256]{2,1,0:T(8,128)S(1)}, f32[6,32,256]{2,1,0:T(8,128)S(1)}, f32[6,128,256]{2,1,0:T(8,128)S(1)}, bf16[64,128]{1,0:T(8,128)(2,1)S(1)}) custom-call(f32[8,256]{1,0:T(8,128)S(1)} %broadcast_in_dim.2.info, f32[3,256,128]{2,1,0:T(8,128)S(1)} %copy-done.1, s32[6,128]{1,0:T(8,128)S(1)} %copy-done.4), custom_call_target="tpu_custom_call" | custom-call | bytes 1600512 | tf_op jit(solution)/shard_map/pallas_call | solution.py:472
  3.1 0.0 copy-done
  3.1 0.0 copy-start.6
  3.1 0.0 copy-start.7
  3.2 0.0 copy-start.8
  3.2 0.3 shard_map.132
  3.5 0.0 copy-start.5
  3.5 0.5 %collective-permute-start = (f32[6,32,256]{2,1,0:T(8,128)S(1)}, f32[6,32,256]{2,1,0:T(8,128)S(1)}, u32[]{:S(2)}, u32[]{:S(2)}) collective-permute-start(f32[6,32,256]{2,1,0:T(8,128)S(1)} %get-tuple-element.41), channel_id=1, source_target_pairs={{0,1},{1,0},{2,3},{3,2},{4,5},{5,4},{6,7},{7,6},{8,9},{9,8},{10,11... | collective-permute-start | bytes 589832 | tf_op jit(solution)/shard_map/ppermute | solution.py:518
  4.0 2.6 %collective-permute-start.1 = (f32[6,32,256]{2,1,0:T(8,128)S(1)}, f32[6,32,256]{2,1,0:T(8,128)S(1)}, u32[]{:S(2)}, u32[]{:S(2)}) collective-permute-start(f32[6,32,256]{2,1,0:T(8,128)S(1)} %get-tuple-element.42), channel_id=1, source_target_pairs={{1,2},{2,1},{3,4},{4,3},{5,6},{6,5},{7,8},{8,7},{9,10},{10,9},{11,... | collective-permute-start | bytes 589832 | tf_op jit(solution)/shard_map/ppermute | solution.py:521
  6.6 0.0 copy-done.6
  6.6 0.0 copy-done.7
  6.6 0.0 copy-done.8
  6.6 0.0 copy-done.5
  6.6 0.0 copy-done.9
  6.7 0.0 copy-done.10
  6.7 0.0 copy-start.3
  6.7 0.0 copy-start.11
  6.7 0.0 copy-start.12
  6.7 0.0 copy-start.13
  6.7 1.8 %shard_map.133 = (f32[640,192]{1,0:T(8,128)S(1)}, bf16[64,384]{1,0:T(8,128)(2,1)S(1)}, bf16[2,128,384]{2,1,0:T(8,128)(2,1)S(1)}, bf16[64,192]{1,0:T(8,128)(2,1)S(1)}, bf16[2,128,192]{2,1,0:T(8,128)(2,1)S(1)}) custom-call(f32[8,256]{1,0:T(8,128)S(1)} %broadcast_in_dim.2.info, bf16[64,128]{1,0:T(8,128)(2,1)S(1)} %get-tuple-element.37.pick_ref, ...), custom_call_target="tpu_custom_call" | custom-call | flops 1000000000 | bytes 943872 | tf_op jit(solution)/shard_map/pallas_call | solution.py:472
  8.5 0.0 copy-done.11
  8.5 0.0 copy-done.12
  8.5 0.0 copy-done.13
  8.6 3.0 %shard_map.134 = (f32[6,128,256]{2,1,0:T(8,128)S(1)}, f32[6,64,256]{2,1,0:T(8,128)S(1)}) custom-call(f32[6,128,256]{2,1,0:T(8,128)S(1)} %get-tuple-element.43.state, bf16[512,512]{1,0:T(8,128)(2,1)S(1)} %copy-done.12, bf16[1024,256]{1,0:T(8,128)(2,1)S(1)} %copy-done.11, f32[8,512]{1,0:T(8,128)S(1)} %copy-done.13, f32[8,256]{1,0:T(8,128)S(1)} %copy-done.3, ...), custom_call_target="tpu_custom_call" | custom-call | flops 2000000000 | bytes 3284992 | tf_op jit(solution)/shard_map/pallas_call | solution.py:472
  11.6 0.0 collective-permute-done.near
  11.6 0.0 collective-permute-done.1.far
  11.6 1.7 %shard_map.135 = (f32[6,32,256]{2,1,0:T(8,128)S(1)}, f32[6,32,256]{2,1,0:T(8,128)S(1)}, f32[6,64,256]{2,1,0:T(8,128)S(1)}) custom-call(f32[8,256]{1,0:T(8,128)S(1)} %broadcast_in_dim.2.info, f32[6,32,256]{2,1,0:T(8,128)S(1)} %collective-permute-done.near, f32[6,32,256]{2,1,0:T(8,128)S(1)} %collective-permute-done.1.far, ...), custom_call_target="tpu_custom_call" | custom-call | flops 1000000000 | bytes 2777088 | tf_op jit(solution)/shard_map/pallas_call | solution.py:472
  13.3 0.2 collective-permute-start.2
  13.5 1.5 %collective-permute-start.3 = (f32[6,32,256]{2,1,0:T(8,128)S(1)}, f32[6,32,256]{2,1,0:T(8,128)S(1)}, u32[]{:S(2)}, u32[]{:S(2)}) collective-permute-start(f32[6,32,256]{2,1,0:T(8,128)S(1)} %get-tuple-element.50), channel_id=1, source_target_pairs={{1,2},{2,1},{3,4},{4,3},{5,6},{6,5},{7,8},{8,7},{9,10},{10,9},{11,... | collective-permute-start | bytes 589832 | tf_op jit(solution)/shard_map/ppermute | solution.py:521
  15.0 3.6 %shard_map.136 = (bf16[2,384,384]{2,1,0:T(8,128)(2,1)S(1)}, bf16[2,384,192]{2,1,0:T(8,128)(2,1)S(1)}, bf16[2,128,384]{2,1,0:T(8,128)(2,1)S(1)}, f32[6,128,256]{2...) custom-call(f32[8,256]{1,0:T(8,128)S(1)} %broadcast_in_dim.2.info, ...), custom_call_target="tpu_custom_call" | custom-call | flops 2000000000 | bytes 5939200 | tf_op jit(solution)/shard_map/pallas_call | solution.py:472
  18.6 0.0 collective-permute-done.2.near
  18.6 0.5 %collective-permute-done.3.far = f32[6,32,256]{2,1,0:T(8,128)S(1)} collective-permute-done((f32[6,32,256]{2,1,0:T(8,128)S(1)}, f32[6,32,256]{2,1,0:T(8,128)S(1)}, u32[]{:S(2)}, u32[]{:S(2)}) %collective-permute-start.3) | collective-permute-done | bytes 196640 | tf_op jit(solution)/shard_map/ppermute | solution.py:521
  19.2 0.3 shard_map.137
  19.4 1.4 %collective-permute-start.4 = (f32[6,32,256]{2,1,0:T(8,128)S(1)}, f32[6,32,256]{2,1,0:T(8,128)S(1)}, u32[]{:S(2)}, u32[]{:S(2)}) collective-permute-start(f32[6,32,256]{2,1,0:T(8,128)S(1)} %get-tuple-element.56), channel_id=1, source_target_pairs={{0,1},{1,0},{2,3},{3,2},{4,5},{5,4},{6,7},{7,6},{8,9},{9,8},{10,11... | collective-permute-start | bytes 589832 | tf_op jit(solution)/shard_map/ppermute | solution.py:518
  20.9 1.5 %collective-permute-start.5 = (f32[6,32,256]{2,1,0:T(8,128)S(1)}, f32[6,32,256]{2,1,0:T(8,128)S(1)}, u32[]{:S(2)}, u32[]{:S(2)}) collective-permute-start(f32[6,32,256]{2,1,0:T(8,128)S(1)} %get-tuple-element.57), channel_id=1, source_target_pairs={{1,2},{2,1},{3,4},{4,3},{5,6},{6,5},{7,8},{8,7},{9,10},{10,9},{11,... | collective-permute-start | bytes 589832 | tf_op jit(solution)/shard_map/ppermute | solution.py:521
  22.4 1.5 %shard_map.138 = (f32[6,128,256]{2,1,0:T(8,128)S(1)}, f32[6,128,256]{2,1,0:T(8,128)S(1)}, f32[6,64,256]{2,1,0:T(8,128)S(1)}, f32[16,256]{1,0:T(8,128)S(1)}) custom-call(f32[8,256]{1,0:T(8,128)S(1)} %broadcast_in_dim.2.info, f32[6,32,256]{2,1,0:T(8,128)S(1)} %collective-permute-done.2.near, f32[6,32,256]{2,1,0:T(8,128)S(1)} %collective-permute-done.3.far, ...), custom_call_target="tpu_custom_call" | custom-call | flops 2000000000 | bytes 4849664 | tf_op jit(solution)/shard_map/pallas_call | solution.py:472
  23.9 0.0 collective-permute-done.4.near
  23.9 2.6 %collective-permute-done.5.far = f32[6,32,256]{2,1,0:T(8,128)S(1)} collective-permute-done((f32[6,32,256]{2,1,0:T(8,128)S(1)}, f32[6,32,256]{2,1,0:T(8,128)S(1)}, u32[]{:S(2)}, u32[]{:S(2)}) %collective-permute-start.5) | collective-permute-done | bytes 196640 | tf_op jit(solution)/shard_map/ppermute | solution.py:521
  26.5 0.3 shard_map.139
  26.8 1.7 %collective-permute-start.7 = (f32[6,32,256]{2,1,0:T(8,128)S(1)}, f32[6,32,256]{2,1,0:T(8,128)S(1)}, u32[]{:S(2)}, u32[]{:S(2)}) collective-permute-start(f32[6,32,256]{2,1,0:T(8,128)S(1)} %get-tuple-element.63), channel_id=1, source_target_pairs={{0,1},{1,0},{2,3},{3,2},{4,5},{5,4},{6,7},{7,6},{8,9},{9,8},{10,11... | collective-permute-start | bytes 589832 | tf_op jit(solution)/shard_map/ppermute | solution.py:518
  28.5 1.5 %collective-permute-start.6 = (f32[6,32,256]{2,1,0:T(8,128)S(1)}, f32[6,32,256]{2,1,0:T(8,128)S(1)}, u32[]{:S(2)}, u32[]{:S(2)}) collective-permute-start(f32[6,32,256]{2,1,0:T(8,128)S(1)} %get-tuple-element.62), channel_id=1, source_target_pairs={{1,2},{2,1},{3,4},{4,3},{5,6},{6,5},{7,8},{8,7},{9,10},{10,9},{11,... | collective-permute-start | bytes 589832 | tf_op jit(solution)/shard_map/ppermute | solution.py:521
  30.0 0.0 collective-permute-done.7.near_last
  30.0 2.1 %shard_map.140 = (f32[6,128,256]{2,1,0:T(8,128)S(1)}, f32[6,32,256]{2,1,0:T(8,128)S(1)}, f32[40,256]{1,0:T(8,128)S(1)}) custom-call(f32[8,256]{1,0:T(8,128)S(1)} %broadcast_in_dim.2.info, f32[6,32,256]{2,1,0:T(8,128)S(1)} %collective-permute-done.4.near, f32[6,32,256]{2,1,0:T(8,128)S(1)} %collective-permute-done.5.far, ...), custom_call_target="tpu_custom_call" | custom-call | flops 2000000000 | bytes 4308992 | tf_op jit(solution)/shard_map/pallas_call | solution.py:472
  32.1 0.0 copy-start.2
  32.1 1.1 %collective-permute-start.8 = (f32[40,256]{1,0:T(8,128)S(1)}, f32[40,256]{1,0:T(8,128)S(1)}, u32[]{:S(2)}, u32[]{:S(2)}) collective-permute-start(f32[40,256]{1,0:T(8,128)S(1)} %get-tuple-element.70.moments), channel_id=1, source_target_pairs={{0,1},{1,0},{2,3},{3,2},{4,5},{5,4},{6,7},{7,6},{8,9},{9,8},{10,11... | collective-permute-start | bytes 122888 | tf_op jit(solution)/shard_map/ppermute | solution.py:518
  33.2 1.0 %collective-permute-done.6.far = f32[6,32,256]{2,1,0:T(8,128)S(1)} collective-permute-done((f32[6,32,256]{2,1,0:T(8,128)S(1)}, f32[6,32,256]{2,1,0:T(8,128)S(1)}, u32[]{:S(2)}, u32[]{:S(2)}) %collective-permute-start.6) | collective-permute-done | bytes 196640 | tf_op jit(solution)/shard_map/ppermute | solution.py:521
  34.2 0.0 collective-permute-done.8.rest_0_
  34.2 0.1 shard_map.141
  34.2 5.7 %collective-permute-start.12 = (f32[40,256]{1,0:T(8,128)S(1)}, f32[40,256]{1,0:T(8,128)S(1)}, u32[]{:S(2)}, u32[]{:S(2)}) collective-permute-start(f32[40,256]{1,0:T(8,128)S(1)} %shard_map.141), channel_id=1, source_target_pairs={{0,14},{1,12},{2,15},{3,13},{4,10},{5,8},{6,11},{7,9},{8,6},{9,4},... | collective-permute-start | bytes 122888 | tf_op jit(solution)/shard_map/ppermute | solution.py:629
  39.9 0.4 collective-permute-start.11
  40.4 0.1 collective-permute-start.10
  40.5 1.7 %collective-permute-start.9 = (f32[40,256]{1,0:T(8,128)S(1)}, f32[40,256]{1,0:T(8,128)S(1)}, u32[]{:S(2)}, u32[]{:S(2)}) collective-permute-start(f32[40,256]{1,0:T(8,128)S(1)} %shard_map.141), channel_id=1, source_target_pairs={{0,2},{1,0},{2,3},{3,1},{4,6},{5,4},{6,7},{7,5},{8,10},{9,8},{10,1... | collective-permute-start | bytes 122888 | tf_op jit(solution)/shard_map/ppermute | solution.py:629
  42.2 0.0 collective-permute-done.12
  42.2 2.8 %collective-permute-done.11 = f32[40,256]{1,0:T(8,128)S(1)} collective-permute-done((f32[40,256]{1,0:T(8,128)S(1)}, f32[40,256]{1,0:T(8,128)S(1)}, u32[]{:S(2)}, u32[]{:S(2)}) %collective-permute-start.11) | collective-permute-done | bytes 40992 | tf_op jit(solution)/shard_map/ppermute | solution.py:629
  45.0 0.0 collective-permute-done.10
  45.0 0.0 collective-permute-done.9
  45.0 0.3 collective-permute-start.13
  45.3 1.0 %collective-permute-done.13.other = f32[40,256]{1,0:T(8,128)S(1)} collective-permute-done((f32[40,256]{1,0:T(8,128)S(1)}, f32[40,256]{1,0:T(8,128)S(1)}, u32[]{:S(2)}, u32[]{:S(2)}) %collective-permute-start.13) | collective-permute-done | bytes 40992 | tf_op jit(solution)/shard_map/ppermute | solution.py:518
  46.3 1.1 %shard_map.142 = (f32[3,256,128]{2,1,0:T(8,128)}, f32[3,256,128]{2,1,0:T(8,128)}) custom-call(f32[40,256]{1,0:T(8,128)S(1)} %add_add_fusion.moments, f32[40,256]{1,0:T(8,128)S(1)} %collective-permute-done.13.other, f32[3,256,128]{2,1,0:T(8,128)S(1)} %copy-done.2, f32[3,256,128]{2,1,0:T(8,128)S(1)} %copy-done, ...), custom_call_target="tpu_custom_call" | custom-call | flops 10000000 | bytes 4014080 | tf_op jit(solution)/shard_map/pallas_call | solution.py:472
  (9 shorter events, 0.0 us)
Async XLA Ops:
  0.6 2.5 %copy-start = (f32[3,256,128]{2,1,0:T(8,128)S(1)}, f32[3,256,128]{2,1,0:T(8,128)}, u32[]{:S(2)}) copy-start(f32[3,256,128]{2,1,0:T(8,128)} %magnetic.3) | copy-start | bytes 1179652
  0.8 1.0 %copy-start.1 = (f32[3,256,128]{2,1,0:T(8,128)S(1)}, f32[3,256,128]{2,1,0:T(8,128)}, u32[]{:S(2)}) copy-start(f32[3,256,128]{2,1,0:T(8,128)} %velocity.3) | copy-start | bytes 1179652
  1.8 0.7 %copy-start.4 = (s32[6,128]{1,0:T(8,128)S(1)}, s32[6,128]{1,0:T(8,128)}, u32[]{:S(2)}) copy-start(s32[6,128]{1,0:T(8,128)} %conn_ref.3) | copy-start | bytes 9220
  3.1 3.5 %copy-start.6 = (f32[6,6,128]{2,1,0:T(8,128)S(1)}, f32[6,6,128]{2,1,0:T(8,128)}, u32[]{:S(2)}) copy-start(f32[6,6,128]{2,1,0:T(8,128)} %mass_ref.1) | copy-start | bytes 55300
  3.1 3.5 %copy-start.7 = (f32[6,6,128]{2,1,0:T(8,128)S(1)}, f32[6,6,128]{2,1,0:T(8,128)}, u32[]{:S(2)}) copy-start(f32[6,6,128]{2,1,0:T(8,128)} %stiff_ref.1) | copy-start | bytes 55300
  3.2 3.5 %copy-start.8 = (f32[6,6,128]{2,1,0:T(8,128)S(1)}, f32[6,6,128]{2,1,0:T(8,128)}, u32[]{:S(2)}) copy-start(f32[6,6,128]{2,1,0:T(8,128)} %twist_ref.1) | copy-start | bytes 55300
  3.5 3.1 %copy-start.5 = (s32[6,128]{1,0:T(8,128)S(1)}, s32[6,128]{1,0:T(8,128)}, u32[]{:S(2)}) copy-start(s32[6,128]{1,0:T(8,128)} %conn_ref.3) | copy-start | bytes 9220
  3.5 8.0 %collective-permute-start = (f32[6,32,256]{2,1,0:T(8,128)S(1)}, f32[6,32,256]{2,1,0:T(8,128)S(1)}, u32[]{:S(2)}, u32[]{:S(2)}) collective-permute-start(f32[6,32,256]{2,1,0:T(8,128)S(1)} %get-tuple-element.41), channel_id=1, source_target_pairs={{0,1},{1,0},{2,3},{3,2},{4,5},{5,4},{6,7},{7,6},{8,9},{9,8},{10,11... | collective-permute-start | bytes 589832 | tf_op jit(solution)/shard_map/ppermute | solution.py:518
  4.0 2.6 %copy-start.9 = (s32[2,32]{1,0:T(2,128)S(1)}, s32[2,32]{1,0:T(2,128)}, u32[]{:S(2)}) copy-start(s32[2,32]{1,0:T(2,128)} %lists_ref.1) | copy-start | bytes 772
  4.0 2.6 %copy-start.10 = (f32[128]{0:T(128)S(1)}, f32[128]{0:T(128)}, u32[]{:S(2)}) copy-start(f32[128]{0:T(128)} %param.17) | copy-start | bytes 1540
  4.0 7.5 %collective-permute-start.1 = (f32[6,32,256]{2,1,0:T(8,128)S(1)}, f32[6,32,256]{2,1,0:T(8,128)S(1)}, u32[]{:S(2)}, u32[]{:S(2)}) collective-permute-start(f32[6,32,256]{2,1,0:T(8,128)S(1)} %get-tuple-element.42), channel_id=1, source_target_pairs={{1,2},{2,1},{3,4},{4,3},{5,6},{6,5},{7,8},{8,7},{9,10},{10,9},{11,... | collective-permute-start | bytes 589832 | tf_op jit(solution)/shard_map/ppermute | solution.py:521
  6.7 1.9 %copy-start.3 = (f32[8,256]{1,0:T(8,128)S(1)}, f32[8,256]{1,0:T(8,128)}, u32[]{:S(2)}) copy-start(f32[8,256]{1,0:T(8,128)} %constant.33.clone.squares_ref) | copy-start | bytes 24580
  6.7 1.9 %copy-start.11 = (bf16[1024,256]{1,0:T(8,128)(2,1)S(1)}, bf16[1024,256]{1,0:T(8,128)(2,1)}, u32[]{:S(2)}) copy-start(bf16[1024,256]{1,0:T(8,128)(2,1)} %constant.31.clone.coefs_ref) | copy-start | bytes 1572868
  6.7 1.8 %copy-start.12 = (bf16[512,512]{1,0:T(8,128)(2,1)S(1)}, bf16[512,512]{1,0:T(8,128)(2,1)}, u32[]{:S(2)}) copy-start(bf16[512,512]{1,0:T(8,128)(2,1)} %constant.30.clone.planes_ref) | copy-start | bytes 1572868
  6.7 1.8 %copy-start.13 = (f32[8,512]{1,0:T(8,128)S(1)}, f32[8,512]{1,0:T(8,128)}, u32[]{:S(2)}) copy-start(f32[8,512]{1,0:T(8,128)} %constant.32.clone.rotation_ref) | copy-start | bytes 49156
  13.3 5.4 %collective-permute-start.2 = (f32[6,32,256]{2,1,0:T(8,128)S(1)}, f32[6,32,256]{2,1,0:T(8,128)S(1)}, u32[]{:S(2)}, u32[]{:S(2)}) collective-permute-start(f32[6,32,256]{2,1,0:T(8,128)S(1)} %get-tuple-element.49), channel_id=1, source_target_pairs={{0,1},{1,0},{2,3},{3,2},{4,5},{5,4},{6,7},{7,6},{8,9},{9,8},{10,11... | collective-permute-start | bytes 589832 | tf_op jit(solution)/shard_map/ppermute | solution.py:518
  13.5 5.7 %collective-permute-start.3 = (f32[6,32,256]{2,1,0:T(8,128)S(1)}, f32[6,32,256]{2,1,0:T(8,128)S(1)}, u32[]{:S(2)}, u32[]{:S(2)}) collective-permute-start(f32[6,32,256]{2,1,0:T(8,128)S(1)} %get-tuple-element.50), channel_id=1, source_target_pairs={{1,2},{2,1},{3,4},{4,3},{5,6},{6,5},{7,8},{8,7},{9,10},{10,9},{11,... | collective-permute-start | bytes 589832 | tf_op jit(solution)/shard_map/ppermute | solution.py:521
  19.4 4.5 %collective-permute-start.4 = (f32[6,32,256]{2,1,0:T(8,128)S(1)}, f32[6,32,256]{2,1,0:T(8,128)S(1)}, u32[]{:S(2)}, u32[]{:S(2)}) collective-permute-start(f32[6,32,256]{2,1,0:T(8,128)S(1)} %get-tuple-element.56), channel_id=1, source_target_pairs={{0,1},{1,0},{2,3},{3,2},{4,5},{5,4},{6,7},{7,6},{8,9},{9,8},{10,11... | collective-permute-start | bytes 589832 | tf_op jit(solution)/shard_map/ppermute | solution.py:518
  20.9 5.7 %collective-permute-start.5 = (f32[6,32,256]{2,1,0:T(8,128)S(1)}, f32[6,32,256]{2,1,0:T(8,128)S(1)}, u32[]{:S(2)}, u32[]{:S(2)}) collective-permute-start(f32[6,32,256]{2,1,0:T(8,128)S(1)} %get-tuple-element.57), channel_id=1, source_target_pairs={{1,2},{2,1},{3,4},{4,3},{5,6},{6,5},{7,8},{8,7},{9,10},{10,9},{11,... | collective-permute-start | bytes 589832 | tf_op jit(solution)/shard_map/ppermute | solution.py:521
  26.8 3.2 %collective-permute-start.7 = (f32[6,32,256]{2,1,0:T(8,128)S(1)}, f32[6,32,256]{2,1,0:T(8,128)S(1)}, u32[]{:S(2)}, u32[]{:S(2)}) collective-permute-start(f32[6,32,256]{2,1,0:T(8,128)S(1)} %get-tuple-element.63), channel_id=1, source_target_pairs={{0,1},{1,0},{2,3},{3,2},{4,5},{5,4},{6,7},{7,6},{8,9},{9,8},{10,11... | collective-permute-start | bytes 589832 | tf_op jit(solution)/shard_map/ppermute | solution.py:518
  28.5 5.7 %collective-permute-start.6 = (f32[6,32,256]{2,1,0:T(8,128)S(1)}, f32[6,32,256]{2,1,0:T(8,128)S(1)}, u32[]{:S(2)}, u32[]{:S(2)}) collective-permute-start(f32[6,32,256]{2,1,0:T(8,128)S(1)} %get-tuple-element.62), channel_id=1, source_target_pairs={{1,2},{2,1},{3,4},{4,3},{5,6},{6,5},{7,8},{8,7},{9,10},{10,9},{11,... | collective-permute-start | bytes 589832 | tf_op jit(solution)/shard_map/ppermute | solution.py:521
  32.1 14.2 %copy-start.2 = (f32[3,256,128]{2,1,0:T(8,128)S(1)}, f32[3,256,128]{2,1,0:T(8,128)}, u32[]{:S(2)}) copy-start(f32[3,256,128]{2,1,0:T(8,128)} %velocity.3) | copy-start | bytes 1179652
  32.1 2.1 %collective-permute-start.8 = (f32[40,256]{1,0:T(8,128)S(1)}, f32[40,256]{1,0:T(8,128)S(1)}, u32[]{:S(2)}, u32[]{:S(2)}) collective-permute-start(f32[40,256]{1,0:T(8,128)S(1)} %get-tuple-element.70.moments), channel_id=1, source_target_pairs={{0,1},{1,0},{2,3},{3,2},{4,5},{5,4},{6,7},{7,6},{8,9},{9,8},{10,11... | collective-permute-start | bytes 122888 | tf_op jit(solution)/shard_map/ppermute | solution.py:518
  34.2 8.0 %collective-permute-start.12 = (f32[40,256]{1,0:T(8,128)S(1)}, f32[40,256]{1,0:T(8,128)S(1)}, u32[]{:S(2)}, u32[]{:S(2)}) collective-permute-start(f32[40,256]{1,0:T(8,128)S(1)} %shard_map.141), channel_id=1, source_target_pairs={{0,14},{1,12},{2,15},{3,13},{4,10},{5,8},{6,11},{7,9},{8,6},{9,4},... | collective-permute-start | bytes 122888 | tf_op jit(solution)/shard_map/ppermute | solution.py:629
  39.9 5.1 %collective-permute-start.11 = (f32[40,256]{1,0:T(8,128)S(1)}, f32[40,256]{1,0:T(8,128)S(1)}, u32[]{:S(2)}, u32[]{:S(2)}) collective-permute-start(f32[40,256]{1,0:T(8,128)S(1)} %shard_map.141), channel_id=1, source_target_pairs={{0,10},{1,8},{2,11},{3,9},{4,14},{5,12},{6,15},{7,13},{8,2},{9,0},... | collective-permute-start | bytes 122888 | tf_op jit(solution)/shard_map/ppermute | solution.py:629
  40.4 4.6 %collective-permute-start.10 = (f32[40,256]{1,0:T(8,128)S(1)}, f32[40,256]{1,0:T(8,128)S(1)}, u32[]{:S(2)}, u32[]{:S(2)}) collective-permute-start(f32[40,256]{1,0:T(8,128)S(1)} %shard_map.141), channel_id=1, source_target_pairs={{0,6},{1,4},{2,7},{3,5},{4,2},{5,0},{6,3},{7,1},{8,14},{9,12},{10,... | collective-permute-start | bytes 122888 | tf_op jit(solution)/shard_map/ppermute | solution.py:629
  40.5 4.5 %collective-permute-start.9 = (f32[40,256]{1,0:T(8,128)S(1)}, f32[40,256]{1,0:T(8,128)S(1)}, u32[]{:S(2)}, u32[]{:S(2)}) collective-permute-start(f32[40,256]{1,0:T(8,128)S(1)} %shard_map.141), channel_id=1, source_target_pairs={{0,2},{1,0},{2,3},{3,1},{4,6},{5,4},{6,7},{7,5},{8,10},{9,8},{10,1... | collective-permute-start | bytes 122888 | tf_op jit(solution)/shard_map/ppermute | solution.py:629
  45.0 1.3 %collective-permute-start.13 = (f32[40,256]{1,0:T(8,128)S(1)}, f32[40,256]{1,0:T(8,128)S(1)}, u32[]{:S(2)}, u32[]{:S(2)}) collective-permute-start(f32[40,256]{1,0:T(8,128)S(1)} %add_add_fusion.moments), channel_id=1, source_target_pairs={{0,1},{1,0},{2,3},{3,2},{4,5},{5,4},{6,7},{7,6},{8,9},{9,8},{10,11... | collective-permute-start | bytes 122888 | tf_op jit(solution)/shard_map/ppermute | solution.py:518

commit v5 on v4

--- a/solution.py
+++ b/solution.py
@@ -293,7 +293,7 @@
 
 
 def start_kernel(
-    info, near, far, packed, planes_ref, coefs_ref, rotation_ref, squares_ref, mass_ghost, rest_ghost,
+    info, far, near, packed, planes_ref, coefs_ref, rotation_ref, squares_ref, mass_ghost, rest_ghost,
     near_out, far_out, force_out, phys_ref, high_ref, low_ref,
 ):
     ghosts = near.shape[1]
@@ -320,7 +320,7 @@
 
 
 def first_kernel(
-    info, near, far, force_ghost, force, state, dense_ref, pick_ref, squares_ref,
+    info, far, near, force_ghost, force, state, dense_ref, pick_ref, squares_ref,
     own_ref, ghost_ref, back_ref, vector_out, image_out, packed_out, moments_out,
 ):
     nodes = state.shape[1]
@@ -362,7 +362,7 @@
     moments_out[6:8, :] = jnp.zeros((2, moments_out.shape[1]), f32)
 
 
-def send_kernel(info, near, far, packed, ghost_ops, squares_ref, near_out, far_out):
+def send_kernel(info, far, near, packed, ghost_ops, squares_ref, near_out, far_out):
     ghosts = near.shape[1]
     count = 2 * ghosts
     top = ghost_ops.shape[1] - 2 * count
@@ -375,7 +375,7 @@
 
 
 def next_kernel(
-    info, near, far, image, before, own, ghost_ops, squares_ref,
+    info, far, near, image, before, own, ghost_ops, squares_ref,
     vector_out, image_out, packed_out, moments_out,
 ):
     nodes = image.shape[1]
@@ -394,7 +394,7 @@
 
 
 def last_kernel(
-    info, near, far, near_last, image, before, own, ghost_ops, back_ops, squares_ref, first, second,
+    info, far, near, image, before, own, ghost_ops, back_ops, squares_ref, first, second,
     vector_out, back_out, moments_out,
 ):
     nodes = image.shape[1]
@@ -412,16 +412,15 @@
         after = after[:nodes] + square * after[nodes:]
         back = dot(back_ops[k // 3], rows)
         back = back[:count] + square * back[count:]
-        back_out[k] = back[ghosts:]
+        back_out[k] = back
         moments_out[18 + k : 19 + k, :] = jnp.sum(before[k] * total, axis=0, keepdims=True)
         moments_out[24 + k : 25 + k, :] = jnp.sum(total * total, axis=0, keepdims=True)
-        moments_out[30 + k : 31 + k, :] = jnp.sum(after * total, axis=0, keepdims=True) + jnp.sum(
-            near_last[k] * back[:ghosts], axis=0, keepdims=True
-        )
+        moments_out[30 + k : 31 + k, :] = jnp.sum(after * total, axis=0, keepdims=True)
     moments_out[36:40, :] = jnp.zeros((4, moments_out.shape[1]), f32)
 
 
-def join_kernel(weight, info, far, back, moments, *rest):
+def join_kernel(far_weight, near_weight, info, far, near, back, moments, *rest):
+    ghosts = near.shape[1]
     out = rest[-1]
     total = moments[...]
     for other in rest[:-1]:
@@ -429,7 +428,9 @@
     out[...] = total
     for k in range(6):
         distant = jnp.where(info[3:4, :] > 0.0, far[k], 0.0)
-        out[30 + k : 31 + k, :] += weight * jnp.sum(distant * back[k], axis=0, keepdims=True)
+        crossing = far_weight * jnp.sum(distant * back[k, ghosts:], axis=0, keepdims=True)
+        crossing += near_weight * jnp.sum(near[k] * back[k, :ghosts], axis=0, keepdims=True)
+        out[30 + k : 31 + k, :] += crossing
 
 
 def finish_kernel(moments, other, velocity, magnetic, first, second, third, velocity_out, magnetic_out):
@@ -500,9 +501,9 @@
     low_valid = (index > 0).astype(jnp.int32)
     high_valid = (index < count - 1).astype(jnp.int32)
     far_valid = jnp.where(odd == 1, high_valid, low_valid)
-    zero = jnp.zeros_like(odd)
-    info = jnp.stack([odd, low_valid, high_valid, far_valid, zero, zero, zero, zero]).astype(f32)
-    info = jnp.broadcast_to(info[:, None], (8, coefs))
+    row = lax.broadcasted_iota(jnp.int32, (8, coefs), 0)
+    flags = jnp.where(row == 0, odd, jnp.where(row == 1, low_valid, jnp.where(row == 2, high_valid, far_valid)))
+    info = flags.astype(f32)
 
     near_pairs = [(i, i ^ 1) for i in range(count)]
     far_pairs = []
@@ -570,7 +571,7 @@
     near, far, force_ghost = call(
         start_kernel,
         [ends, ends, packs],
-        [info, near_state, far_state, packed, plane_table, coef_table, rotation, squares]
+        [info, far_state, near_state, packed, plane_table, coef_table, rotation, squares]
         + [mass_ghost, rest_ghost],
         scratch=[
             pltpu.VMEM((6 * both, planes), f32),
@@ -591,35 +592,35 @@
             packs,
             shape(8, coefs),
         ],
-        [info, near_state, far_state, force_ghost, force, state, dense, pick, squares],
+        [info, far_state, near_state, force_ghost, force, state, dense, pick, squares],
         flops=2_000_000_000,
     )
     near, far = call(
-        send_kernel, [ends, ends], [info, near_now, far_now, packed, ghost_ops, squares], flops=100_000_000
+        send_kernel, [ends, ends], [info, far_now, near_now, packed, ghost_ops, squares], flops=100_000_000
     )
     near_next, far_next = exchange(near, far)
     vector1, image, packed, moments1 = call(
         next_kernel,
         [whole, whole, packs, shape(16, coefs)],
-        [info, near_now, far_now, image, vector0, own, ghost_ops, squares],
+        [info, far_now, near_now, image, vector0, own, ghost_ops, squares],
         flops=2_000_000_000,
     )
     near, far = call(
-        send_kernel, [ends, ends], [info, near_next, far_next, packed, ghost_ops, squares], flops=100_000_000
+        send_kernel, [ends, ends], [info, far_next, near_next, packed, ghost_ops, squares], flops=100_000_000
     )
     near_last, far_last = exchange(near, far)
     vector2, back, moments = call(
         last_kernel,
-        [whole, ends, shape(40, coefs)],
-        [info, near_next, far_next, near_last, image, vector1, own, ghost_ops, back_ops, squares]
+        [whole, packs, shape(40, coefs)],
+        [info, far_next, near_next, image, vector1, own, ghost_ops, back_ops, squares]
         + [moments0, moments1],
         flops=2_000_000_000,
     )
     if count % 8 == 0 and count <= 16:
         joined = call(
-            functools.partial(join_kernel, 2.0),
+            functools.partial(join_kernel, 2.0, 2.0),
             shape(40, coefs),
-            [info, far_last, back, moments, swap_near(moments)],
+            [info, far_last, near_last, back, moments, swap_near(moments)],
         )
         target = (2, 0, 3, 1)
         lines = count // 4
@@ -631,7 +632,7 @@
         other = swap_near(half)
     else:
         joined = call(
-            functools.partial(join_kernel, 1.0), shape(40, coefs), [info, far_last, back, moments]
+            functools.partial(join_kernel, 1.0, 1.0), shape(40, coefs), [info, far_last, near_last, back, moments]
         )
         half = lax.psum(joined, "mesh")
         other = jnp.zeros_like(half)

time: 47.7 us -> 45.7 us (0.958)
  waiting for transfers between devices: 7.94 us -> 6.68 us
  starting transfers between devices: 20.3 us -> 19.2 us
    ppermute x4, waiting for transfers between devices: 4.09 us -> 1.04 us  [swap_far(): return lax.ppermute(value, ('runs', 'mesh'), far_pairs)]
    ppermute x4, starting transfers between devices: 7.96 us -> 5.35 us  [local(): term = lax.ppermute(joined, 'mesh', pairs)]
    ppermute x6, starting transfers between devices: 5.25 us -> 7.08 us  [swap_near(): return lax.ppermute(value, 'mesh', near_pairs)]
    ppermute x6, waiting for transfers between devices: 1.02 us -> 2.09 us  [swap_near(): return lax.ppermute(value, 'mesh', near_pairs)]
    ppermute x4, waiting for transfers between devices: 2.82 us -> 3.56 us  [local(): term = lax.ppermute(joined, 'mesh', pairs)]
    unnamed x28, local copies, waits for them, and re-layouts: 1.75 us -> 2.26 us
  transfers between devices with their start and end apart: 14 -> 14, of which waited for: 5 -> 6; matrix products, arithmetic and copies ran while one was open for 0% -> 0% of each run, Pallas kernels for 25% -> 26%
where the time goes in v5:
time: 45.7 us; the launch traced here: 45.5 us
  starting transfers between devices  19.2 us (42%)
  Pallas kernels  16.4 us (36%)
  waiting for transfers between devices  6.68 us (15%)
  local copies, waits for them, and re-layouts  2.26 us (5%)
  between operations  0.88 us (2%)
    pallas_call x12, Pallas kernels, call(): pl.pallas_call(kernel, out_shape=outs, in_specs=[VMEM] * len(operands), o...  16.4 us
    ppermute x6, starting transfers between devices, swap_near(): return lax.ppermute(value, 'mesh', near_pairs)  7.08 us
    ppermute x4, starting transfers between devices, swap_far(): return lax.ppermute(value, ('runs', 'mesh'), far_pairs)  6.77 us
    ppermute x4, starting transfers between devices, local(): term = lax.ppermute(joined, 'mesh', pairs)  5.35 us
    ppermute x4, waiting for transfers between devices, local(): term = lax.ppermute(joined, 'mesh', pairs)  3.56 us
    unnamed x28, local copies, waits for them, and re-layouts  2.26 us
    ppermute x6, waiting for transfers between devices, swap_near(): return lax.ppermute(value, 'mesh', near_pairs)  2.09 us
    ppermute x4, waiting for transfers between devices, swap_far(): return lax.ppermute(value, ('runs', 'mesh'), far_pairs)  1.04 us
  transfers between devices with their start and end apart: 14, of which 6 were waited for; matrix products, arithmetic and copies ran while one was open for 0% of the time, Pallas kernels for 26%

profile of v5, /device:TPU:0, one launch (start us, length us, event | category | flops | bytes accessed | tf_op | source)
XLA Modules:
  0.0 45.5 jit_solution(4450252284325847328)
XLA Ops:
  0.6 0.0 copy-start
  0.7 0.1 select_convert_fusion.info
  0.8 0.0 copy-start.1
  0.8 1.0 %copy-done.1 = f32[3,256,128]{2,1,0:T(8,128)S(1)} copy-done((f32[3,256,128]{2,1,0:T(8,128)S(1)}, f32[3,256,128]{2,1,0:T(8,128)}, u32[]{:S(2)}) %copy-start.1) | copy-done | bytes 393240
  1.8 0.0 copy-start.4
  1.8 0.7 %copy-done.4 = s32[6,128]{1,0:T(8,128)S(1)} copy-done((s32[6,128]{1,0:T(8,128)S(1)}, s32[6,128]{1,0:T(8,128)}, u32[]{:S(2)}) %copy-start.4) | copy-done | bytes 3096
  2.5 0.6 %shard_map.131 = (f32[6,32,256]{2,1,0:T(8,128)S(1)}, f32[6,32,256]{2,1,0:T(8,128)S(1)}, f32[6,128,256]{2,1,0:T(8,128)S(1)}, bf16[64,128]{1,0:T(8,128)(2,1)S(1)}) custom-call(f32[8,256]{1,0:T(8,128)S(1)} %select_convert_fusion.info, f32[3,256,128]{2,1,0:T(8,128)S(1)} %copy-done.1, s32[6,128]{1,0:T(8,128)S(1)} %copy-done.4), custom_call_target="tpu_custom_call" | custom-call | bytes 1600512 | tf_op jit(solution)/shard_map/pallas_call | solution.py:473
  3.1 0.0 copy-done
  3.1 0.0 copy-start.6
  3.1 0.0 copy-start.7
  3.1 0.0 copy-start.8
  3.1 0.3 shard_map.132
  3.4 0.0 copy-start.5
  3.5 3.0 %collective-permute-start = (f32[6,32,256]{2,1,0:T(8,128)S(1)}, f32[6,32,256]{2,1,0:T(8,128)S(1)}, u32[]{:S(2)}, u32[]{:S(2)}) collective-permute-start(f32[6,32,256]{2,1,0:T(8,128)S(1)} %get-tuple-element.41), channel_id=1, source_target_pairs={{1,2},{2,1},{3,4},{4,3},{5,6},{6,5},{7,8},{8,7},{9,10},{10,9},{11,... | collective-permute-start | bytes 589832 | tf_op jit(solution)/shard_map/ppermute | solution.py:522
  6.5 0.0 copy-start.9
  6.5 0.1 collective-permute-start.1
  6.6 0.0 copy-done.6
  6.6 0.0 copy-done.7
  6.6 0.0 copy-done.8
  6.6 0.0 copy-done.5
  6.6 0.5 %copy-done.9 = s32[2,32]{1,0:T(2,128)S(1)} copy-done((s32[2,32]{1,0:T(2,128)S(1)}, s32[2,32]{1,0:T(2,128)}, u32[]{:S(2)}) %copy-start.9) | copy-done | bytes 280
  7.1 0.0 copy-done.10
  7.2 0.0 copy-start.13
  7.2 1.8 %shard_map.133 = (f32[640,192]{1,0:T(8,128)S(1)}, bf16[64,384]{1,0:T(8,128)(2,1)S(1)}, bf16[2,128,384]{2,1,0:T(8,128)(2,1)S(1)}, bf16[64,192]{1,0:T(8,128)(2,1)S(1)}, bf16[2,128,192]{2,1,0:T(8,128)(2,1)S(1)}) custom-call(f32[8,256]{1,0:T(8,128)S(1)} %select_convert_fusion.info, bf16[64,128]{1,0:T(8,128)(2,1)S(1)} %get-tuple-element.37.pick_ref, ...), custom_call_target="tpu_custom_call" | custom-call | flops 1000000000 | bytes 943872 | tf_op jit(solution)/shard_map/pallas_call | solution.py:473
  9.0 0.0 copy-done.3
  9.0 0.0 copy-done.11
  9.0 0.0 copy-done.12
  9.0 0.0 copy-done.13
  9.0 3.0 %shard_map.134 = (f32[6,128,256]{2,1,0:T(8,128)S(1)}, f32[6,64,256]{2,1,0:T(8,128)S(1)}) custom-call(f32[6,128,256]{2,1,0:T(8,128)S(1)} %get-tuple-element.43.state, bf16[512,512]{1,0:T(8,128)(2,1)S(1)} %copy-done.12, bf16[1024,256]{1,0:T(8,128)(2,1)S(1)} %copy-done.11, f32[8,512]{1,0:T(8,128)S(1)} %copy-done.13, f32[8,256]{1,0:T(8,128)S(1)} %copy-done.3, ...), custom_call_target="tpu_custom_call" | custom-call | flops 2000000000 | bytes 3284992 | tf_op jit(solution)/shard_map/pallas_call | solution.py:473
  12.0 0.0 collective-permute-done.far
  12.0 0.0 collective-permute-done.1.near
  12.0 1.7 %shard_map.135 = (f32[6,32,256]{2,1,0:T(8,128)S(1)}, f32[6,32,256]{2,1,0:T(8,128)S(1)}, f32[6,64,256]{2,1,0:T(8,128)S(1)}) custom-call(f32[8,256]{1,0:T(8,128)S(1)} %select_convert_fusion.info, f32[6,32,256]{2,1,0:T(8,128)S(1)} %collective-permute-done.far, f32[6,32,256]{2,1,0:T(8,128)S(1)} %collective-permute-done.1.near, ...), custom_call_target="tpu_custom_call" | custom-call | flops 1000000000 | bytes 2777088 | tf_op jit(solution)/shard_map/pallas_call | solution.py:473
  13.7 1.1 %collective-permute-start.2 = (f32[6,32,256]{2,1,0:T(8,128)S(1)}, f32[6,32,256]{2,1,0:T(8,128)S(1)}, u32[]{:S(2)}, u32[]{:S(2)}) collective-permute-start(f32[6,32,256]{2,1,0:T(8,128)S(1)} %get-tuple-element.49), channel_id=1, source_target_pairs={{1,2},{2,1},{3,4},{4,3},{5,6},{6,5},{7,8},{8,7},{9,10},{10,9},{11,... | collective-permute-start | bytes 589832 | tf_op jit(solution)/shard_map/ppermute | solution.py:522
  14.8 0.8 %collective-permute-start.3 = (f32[6,32,256]{2,1,0:T(8,128)S(1)}, f32[6,32,256]{2,1,0:T(8,128)S(1)}, u32[]{:S(2)}, u32[]{:S(2)}) collective-permute-start(f32[6,32,256]{2,1,0:T(8,128)S(1)} %get-tuple-element.50), channel_id=1, source_target_pairs={{0,1},{1,0},{2,3},{3,2},{4,5},{5,4},{6,7},{7,6},{8,9},{9,8},{10,11... | collective-permute-start | bytes 589832 | tf_op jit(solution)/shard_map/ppermute | solution.py:519
  15.6 3.6 %shard_map.136 = (bf16[2,384,384]{2,1,0:T(8,128)(2,1)S(1)}, bf16[2,384,192]{2,1,0:T(8,128)(2,1)S(1)}, bf16[2,128,384]{2,1,0:T(8,128)(2,1)S(1)}, f32[6,128,256]{2...) custom-call(f32[8,256]{1,0:T(8,128)S(1)} %select_convert_fusion.info, ...), custom_call_target="tpu_custom_call" | custom-call | flops 2000000000 | bytes 5939200 | tf_op jit(solution)/shard_map/pallas_call | solution.py:473
  19.2 0.2 collective-permute-done.2.far
  19.5 0.0 collective-permute-done.3.near
  19.5 0.3 shard_map.137
  19.7 1.3 %collective-permute-start.4 = (f32[6,32,256]{2,1,0:T(8,128)S(1)}, f32[6,32,256]{2,1,0:T(8,128)S(1)}, u32[]{:S(2)}, u32[]{:S(2)}) collective-permute-start(f32[6,32,256]{2,1,0:T(8,128)S(1)} %get-tuple-element.56), channel_id=1, source_target_pairs={{1,2},{2,1},{3,4},{4,3},{5,6},{6,5},{7,8},{8,7},{9,10},{10,9},{11,... | collective-permute-start | bytes 589832 | tf_op jit(solution)/shard_map/ppermute | solution.py:522
  21.1 2.0 %collective-permute-start.5 = (f32[6,32,256]{2,1,0:T(8,128)S(1)}, f32[6,32,256]{2,1,0:T(8,128)S(1)}, u32[]{:S(2)}, u32[]{:S(2)}) collective-permute-start(f32[6,32,256]{2,1,0:T(8,128)S(1)} %get-tuple-element.57), channel_id=1, source_target_pairs={{0,1},{1,0},{2,3},{3,2},{4,5},{5,4},{6,7},{7,6},{8,9},{9,8},{10,11... | collective-permute-start | bytes 589832 | tf_op jit(solution)/shard_map/ppermute | solution.py:519
  23.1 1.6 %shard_map.138 = (f32[6,128,256]{2,1,0:T(8,128)S(1)}, f32[6,128,256]{2,1,0:T(8,128)S(1)}, f32[6,64,256]{2,1,0:T(8,128)S(1)}, f32[16,256]{1,0:T(8,128)S(1)}) custom-call(f32[8,256]{1,0:T(8,128)S(1)} %select_convert_fusion.info, f32[6,32,256]{2,1,0:T(8,128)S(1)} %collective-permute-done.2.far, f32[6,32,256]{2,1,0:T(8,128)S(1)} %collective-permute-done.3.near, ...), custom_call_target="tpu_custom_call" | custom-call | flops 2000000000 | bytes 4849664 | tf_op jit(solution)/shard_map/pallas_call | solution.py:473
  24.7 0.8 %collective-permute-done.4.far = f32[6,32,256]{2,1,0:T(8,128)S(1)} collective-permute-done((f32[6,32,256]{2,1,0:T(8,128)S(1)}, f32[6,32,256]{2,1,0:T(8,128)S(1)}, u32[]{:S(2)}, u32[]{:S(2)}) %collective-permute-start.4) | collective-permute-done | bytes 196640 | tf_op jit(solution)/shard_map/ppermute | solution.py:522
  25.5 0.0 collective-permute-done.5.near
  25.5 0.3 shard_map.139
  25.8 1.3 %collective-permute-start.6 = (f32[6,32,256]{2,1,0:T(8,128)S(1)}, f32[6,32,256]{2,1,0:T(8,128)S(1)}, u32[]{:S(2)}, u32[]{:S(2)}) collective-permute-start(f32[6,32,256]{2,1,0:T(8,128)S(1)} %get-tuple-element.62), channel_id=1, source_target_pairs={{1,2},{2,1},{3,4},{4,3},{5,6},{6,5},{7,8},{8,7},{9,10},{10,9},{11,... | collective-permute-start | bytes 589832 | tf_op jit(solution)/shard_map/ppermute | solution.py:522
  27.1 3.5 %collective-permute-start.7 = (f32[6,32,256]{2,1,0:T(8,128)S(1)}, f32[6,32,256]{2,1,0:T(8,128)S(1)}, u32[]{:S(2)}, u32[]{:S(2)}) collective-permute-start(f32[6,32,256]{2,1,0:T(8,128)S(1)} %get-tuple-element.63), channel_id=1, source_target_pairs={{0,1},{1,0},{2,3},{3,2},{4,5},{5,4},{6,7},{7,6},{8,9},{9,8},{10,11... | collective-permute-start | bytes 589832 | tf_op jit(solution)/shard_map/ppermute | solution.py:519
  30.6 2.0 %shard_map.140 = (f32[6,128,256]{2,1,0:T(8,128)S(1)}, f32[6,64,256]{2,1,0:T(8,128)S(1)}, f32[40,256]{1,0:T(8,128)S(1)}) custom-call(f32[8,256]{1,0:T(8,128)S(1)} %select_convert_fusion.info, f32[6,32,256]{2,1,0:T(8,128)S(1)} %collective-permute-done.4.far, f32[6,32,256]{2,1,0:T(8,128)S(1)} %collective-permute-done.5.near, ...), custom_call_target="tpu_custom_call" | custom-call | flops 2000000000 | bytes 4308992 | tf_op jit(solution)/shard_map/pallas_call | solution.py:473
  32.7 0.1 collective-permute-start.8
  32.8 1.2 %collective-permute-done.8.rest_0_ = f32[40,256]{1,0:T(8,128)S(1)} collective-permute-done((f32[40,256]{1,0:T(8,128)S(1)}, f32[40,256]{1,0:T(8,128)S(1)}, u32[]{:S(2)}, u32[]{:S(2)}) %collective-permute-start.8) | collective-permute-done | bytes 40992 | tf_op jit(solution)/shard_map/ppermute | solution.py:519
  34.0 0.0 collective-permute-done.6.far
  34.0 0.0 collective-permute-done.7.near
  34.0 0.1 shard_map.141
  34.1 3.0 %collective-permute-start.12 = (f32[40,256]{1,0:T(8,128)S(1)}, f32[40,256]{1,0:T(8,128)S(1)}, u32[]{:S(2)}, u32[]{:S(2)}) collective-permute-start(f32[40,256]{1,0:T(8,128)S(1)} %shard_map.141), channel_id=1, source_target_pairs={{0,14},{1,12},{2,15},{3,13},{4,10},{5,8},{6,11},{7,9},{8,6},{9,4},... | collective-permute-start | bytes 122888 | tf_op jit(solution)/shard_map/ppermute | solution.py:630
  37.0 1.8 %collective-permute-start.11 = (f32[40,256]{1,0:T(8,128)S(1)}, f32[40,256]{1,0:T(8,128)S(1)}, u32[]{:S(2)}, u32[]{:S(2)}) collective-permute-start(f32[40,256]{1,0:T(8,128)S(1)} %shard_map.141), channel_id=1, source_target_pairs={{0,10},{1,8},{2,11},{3,9},{4,14},{5,12},{6,15},{7,13},{8,2},{9,0},... | collective-permute-start | bytes 122888 | tf_op jit(solution)/shard_map/ppermute | solution.py:630
  38.9 0.1 collective-permute-start.10
  39.0 0.4 collective-permute-start.9
  39.4 0.0 collective-permute-done.12
  39.4 3.2 %collective-permute-done.11 = f32[40,256]{1,0:T(8,128)S(1)} collective-permute-done((f32[40,256]{1,0:T(8,128)S(1)}, f32[40,256]{1,0:T(8,128)S(1)}, u32[]{:S(2)}, u32[]{:S(2)}) %collective-permute-start.11) | collective-permute-done | bytes 40992 | tf_op jit(solution)/shard_map/ppermute | solution.py:630
  42.7 0.3 collective-permute-done.10
  43.0 0.0 collective-permute-done.9
  43.0 0.5 %collective-permute-start.13 = (f32[40,256]{1,0:T(8,128)S(1)}, f32[40,256]{1,0:T(8,128)S(1)}, u32[]{:S(2)}, u32[]{:S(2)}) collective-permute-start(f32[40,256]{1,0:T(8,128)S(1)} %add_add_fusion.moments), channel_id=1, source_target_pairs={{0,1},{1,0},{2,3},{3,2},{4,5},{5,4},{6,7},{7,6},{8,9},{9,8},{10,11... | collective-permute-start | bytes 122888 | tf_op jit(solution)/shard_map/ppermute | solution.py:519
  43.5 0.9 %collective-permute-done.13.other = f32[40,256]{1,0:T(8,128)S(1)} collective-permute-done((f32[40,256]{1,0:T(8,128)S(1)}, f32[40,256]{1,0:T(8,128)S(1)}, u32[]{:S(2)}, u32[]{:S(2)}) %collective-permute-start.13) | collective-permute-done | bytes 40992 | tf_op jit(solution)/shard_map/ppermute | solution.py:519
  44.4 0.0 copy-done.2
  44.4 1.1 %shard_map.142 = (f32[3,256,128]{2,1,0:T(8,128)}, f32[3,256,128]{2,1,0:T(8,128)}) custom-call(f32[40,256]{1,0:T(8,128)S(1)} %add_add_fusion.moments, f32[40,256]{1,0:T(8,128)S(1)} %collective-permute-done.13.other, f32[3,256,128]{2,1,0:T(8,128)S(1)} %copy-done.2, f32[3,256,128]{2,1,0:T(8,128)S(1)} %copy-done, ...), custom_call_target="tpu_custom_call" | custom-call | flops 10000000 | bytes 4014080 | tf_op jit(solution)/shard_map/pallas_call | solution.py:473
  (8 shorter events, 0.0 us)
Async XLA Ops:
  0.6 2.4 %copy-start = (f32[3,256,128]{2,1,0:T(8,128)S(1)}, f32[3,256,128]{2,1,0:T(8,128)}, u32[]{:S(2)}) copy-start(f32[3,256,128]{2,1,0:T(8,128)} %magnetic.3) | copy-start | bytes 1179652
  0.8 1.0 %copy-start.1 = (f32[3,256,128]{2,1,0:T(8,128)S(1)}, f32[3,256,128]{2,1,0:T(8,128)}, u32[]{:S(2)}) copy-start(f32[3,256,128]{2,1,0:T(8,128)} %velocity.3) | copy-start | bytes 1179652
  1.8 0.7 %copy-start.4 = (s32[6,128]{1,0:T(8,128)S(1)}, s32[6,128]{1,0:T(8,128)}, u32[]{:S(2)}) copy-start(s32[6,128]{1,0:T(8,128)} %conn_ref.3) | copy-start | bytes 9220
  3.1 3.5 %copy-start.6 = (f32[6,6,128]{2,1,0:T(8,128)S(1)}, f32[6,6,128]{2,1,0:T(8,128)}, u32[]{:S(2)}) copy-start(f32[6,6,128]{2,1,0:T(8,128)} %mass_ref.1) | copy-start | bytes 55300
  3.1 3.5 %copy-start.7 = (f32[6,6,128]{2,1,0:T(8,128)S(1)}, f32[6,6,128]{2,1,0:T(8,128)}, u32[]{:S(2)}) copy-start(f32[6,6,128]{2,1,0:T(8,128)} %stiff_ref.1) | copy-start | bytes 55300
  3.1 3.5 %copy-start.8 = (f32[6,6,128]{2,1,0:T(8,128)S(1)}, f32[6,6,128]{2,1,0:T(8,128)}, u32[]{:S(2)}) copy-start(f32[6,6,128]{2,1,0:T(8,128)} %twist_ref.1) | copy-start | bytes 55300
  3.4 3.2 %copy-start.5 = (s32[6,128]{1,0:T(8,128)S(1)}, s32[6,128]{1,0:T(8,128)}, u32[]{:S(2)}) copy-start(s32[6,128]{1,0:T(8,128)} %conn_ref.3) | copy-start | bytes 9220
  3.5 8.6 %collective-permute-start = (f32[6,32,256]{2,1,0:T(8,128)S(1)}, f32[6,32,256]{2,1,0:T(8,128)S(1)}, u32[]{:S(2)}, u32[]{:S(2)}) collective-permute-start(f32[6,32,256]{2,1,0:T(8,128)S(1)} %get-tuple-element.41), channel_id=1, source_target_pairs={{1,2},{2,1},{3,4},{4,3},{5,6},{6,5},{7,8},{8,7},{9,10},{10,9},{11,... | collective-permute-start | bytes 589832 | tf_op jit(solution)/shard_map/ppermute | solution.py:522
  6.5 0.7 %copy-start.9 = (s32[2,32]{1,0:T(2,128)S(1)}, s32[2,32]{1,0:T(2,128)}, u32[]{:S(2)}) copy-start(s32[2,32]{1,0:T(2,128)} %lists_ref.1) | copy-start | bytes 772
  6.5 0.7 %copy-start.10 = (f32[128]{0:T(128)S(1)}, f32[128]{0:T(128)}, u32[]{:S(2)}) copy-start(f32[128]{0:T(128)} %param.17) | copy-start | bytes 1540
  6.5 5.6 %collective-permute-start.1 = (f32[6,32,256]{2,1,0:T(8,128)S(1)}, f32[6,32,256]{2,1,0:T(8,128)S(1)}, u32[]{:S(2)}, u32[]{:S(2)}) collective-permute-start(f32[6,32,256]{2,1,0:T(8,128)S(1)} %get-tuple-element.42), channel_id=1, source_target_pairs={{0,1},{1,0},{2,3},{3,2},{4,5},{5,4},{6,7},{7,6},{8,9},{9,8},{10,11... | collective-permute-start | bytes 589832 | tf_op jit(solution)/shard_map/ppermute | solution.py:519
  7.1 1.8 %copy-start.3 = (f32[8,256]{1,0:T(8,128)S(1)}, f32[8,256]{1,0:T(8,128)}, u32[]{:S(2)}) copy-start(f32[8,256]{1,0:T(8,128)} %constant.35.clone.squares_ref) | copy-start | bytes 24580
  7.1 1.8 %copy-start.11 = (bf16[1024,256]{1,0:T(8,128)(2,1)S(1)}, bf16[1024,256]{1,0:T(8,128)(2,1)}, u32[]{:S(2)}) copy-start(bf16[1024,256]{1,0:T(8,128)(2,1)} %constant.33.clone.coefs_ref) | copy-start | bytes 1572868
  7.1 1.8 %copy-start.12 = (bf16[512,512]{1,0:T(8,128)(2,1)S(1)}, bf16[512,512]{1,0:T(8,128)(2,1)}, u32[]{:S(2)}) copy-start(bf16[512,512]{1,0:T(8,128)(2,1)} %constant.32.clone.planes_ref) | copy-start | bytes 1572868
  7.2 1.8 %copy-start.13 = (f32[8,512]{1,0:T(8,128)S(1)}, f32[8,512]{1,0:T(8,128)}, u32[]{:S(2)}) copy-start(f32[8,512]{1,0:T(8,128)} %constant.34.clone.rotation_ref) | copy-start | bytes 49156
  13.7 5.7 %collective-permute-start.2 = (f32[6,32,256]{2,1,0:T(8,128)S(1)}, f32[6,32,256]{2,1,0:T(8,128)S(1)}, u32[]{:S(2)}, u32[]{:S(2)}) collective-permute-start(f32[6,32,256]{2,1,0:T(8,128)S(1)} %get-tuple-element.49), channel_id=1, source_target_pairs={{1,2},{2,1},{3,4},{4,3},{5,6},{6,5},{7,8},{8,7},{9,10},{10,9},{11,... | collective-permute-start | bytes 589832 | tf_op jit(solution)/shard_map/ppermute | solution.py:522
  14.8 4.7 %collective-permute-start.3 = (f32[6,32,256]{2,1,0:T(8,128)S(1)}, f32[6,32,256]{2,1,0:T(8,128)S(1)}, u32[]{:S(2)}, u32[]{:S(2)}) collective-permute-start(f32[6,32,256]{2,1,0:T(8,128)S(1)} %get-tuple-element.50), channel_id=1, source_target_pairs={{0,1},{1,0},{2,3},{3,2},{4,5},{5,4},{6,7},{7,6},{8,9},{9,8},{10,11... | collective-permute-start | bytes 589832 | tf_op jit(solution)/shard_map/ppermute | solution.py:519
  19.7 5.7 %collective-permute-start.4 = (f32[6,32,256]{2,1,0:T(8,128)S(1)}, f32[6,32,256]{2,1,0:T(8,128)S(1)}, u32[]{:S(2)}, u32[]{:S(2)}) collective-permute-start(f32[6,32,256]{2,1,0:T(8,128)S(1)} %get-tuple-element.56), channel_id=1, source_target_pairs={{1,2},{2,1},{3,4},{4,3},{5,6},{6,5},{7,8},{8,7},{9,10},{10,9},{11,... | collective-permute-start | bytes 589832 | tf_op jit(solution)/shard_map/ppermute | solution.py:522
  21.1 4.4 %collective-permute-start.5 = (f32[6,32,256]{2,1,0:T(8,128)S(1)}, f32[6,32,256]{2,1,0:T(8,128)S(1)}, u32[]{:S(2)}, u32[]{:S(2)}) collective-permute-start(f32[6,32,256]{2,1,0:T(8,128)S(1)} %get-tuple-element.57), channel_id=1, source_target_pairs={{0,1},{1,0},{2,3},{3,2},{4,5},{5,4},{6,7},{7,6},{8,9},{9,8},{10,11... | collective-permute-start | bytes 589832 | tf_op jit(solution)/shard_map/ppermute | solution.py:519
  25.8 8.2 %collective-permute-start.6 = (f32[6,32,256]{2,1,0:T(8,128)S(1)}, f32[6,32,256]{2,1,0:T(8,128)S(1)}, u32[]{:S(2)}, u32[]{:S(2)}) collective-permute-start(f32[6,32,256]{2,1,0:T(8,128)S(1)} %get-tuple-element.62), channel_id=1, source_target_pairs={{1,2},{2,1},{3,4},{4,3},{5,6},{6,5},{7,8},{8,7},{9,10},{10,9},{11,... | collective-permute-start | bytes 589832 | tf_op jit(solution)/shard_map/ppermute | solution.py:522
  27.1 6.9 %collective-permute-start.7 = (f32[6,32,256]{2,1,0:T(8,128)S(1)}, f32[6,32,256]{2,1,0:T(8,128)S(1)}, u32[]{:S(2)}, u32[]{:S(2)}) collective-permute-start(f32[6,32,256]{2,1,0:T(8,128)S(1)} %get-tuple-element.63), channel_id=1, source_target_pairs={{0,1},{1,0},{2,3},{3,2},{4,5},{5,4},{6,7},{7,6},{8,9},{9,8},{10,11... | collective-permute-start | bytes 589832 | tf_op jit(solution)/shard_map/ppermute | solution.py:519
  32.7 1.3 %collective-permute-start.8 = (f32[40,256]{1,0:T(8,128)S(1)}, f32[40,256]{1,0:T(8,128)S(1)}, u32[]{:S(2)}, u32[]{:S(2)}) collective-permute-start(f32[40,256]{1,0:T(8,128)S(1)} %get-tuple-element.70.moments), channel_id=1, source_target_pairs={{0,1},{1,0},{2,3},{3,2},{4,5},{5,4},{6,7},{7,6},{8,9},{9,8},{10,11... | collective-permute-start | bytes 122888 | tf_op jit(solution)/shard_map/ppermute | solution.py:519
  34.0 10.4 %copy-start.2 = (f32[3,256,128]{2,1,0:T(8,128)S(1)}, f32[3,256,128]{2,1,0:T(8,128)}, u32[]{:S(2)}) copy-start(f32[3,256,128]{2,1,0:T(8,128)} %velocity.3) | copy-start | bytes 1179652
  34.1 5.4 %collective-permute-start.12 = (f32[40,256]{1,0:T(8,128)S(1)}, f32[40,256]{1,0:T(8,128)S(1)}, u32[]{:S(2)}, u32[]{:S(2)}) collective-permute-start(f32[40,256]{1,0:T(8,128)S(1)} %shard_map.141), channel_id=1, source_target_pairs={{0,14},{1,12},{2,15},{3,13},{4,10},{5,8},{6,11},{7,9},{8,6},{9,4},... | collective-permute-start | bytes 122888 | tf_op jit(solution)/shard_map/ppermute | solution.py:630
  37.0 5.6 %collective-permute-start.11 = (f32[40,256]{1,0:T(8,128)S(1)}, f32[40,256]{1,0:T(8,128)S(1)}, u32[]{:S(2)}, u32[]{:S(2)}) collective-permute-start(f32[40,256]{1,0:T(8,128)S(1)} %shard_map.141), channel_id=1, source_target_pairs={{0,10},{1,8},{2,11},{3,9},{4,14},{5,12},{6,15},{7,13},{8,2},{9,0},... | collective-permute-start | bytes 122888 | tf_op jit(solution)/shard_map/ppermute | solution.py:630
  38.9 4.1 %collective-permute-start.10 = (f32[40,256]{1,0:T(8,128)S(1)}, f32[40,256]{1,0:T(8,128)S(1)}, u32[]{:S(2)}, u32[]{:S(2)}) collective-permute-start(f32[40,256]{1,0:T(8,128)S(1)} %shard_map.141), channel_id=1, source_target_pairs={{0,6},{1,4},{2,7},{3,5},{4,2},{5,0},{6,3},{7,1},{8,14},{9,12},{10,... | collective-permute-start | bytes 122888 | tf_op jit(solution)/shard_map/ppermute | solution.py:630
  39.0 4.0 %collective-permute-start.9 = (f32[40,256]{1,0:T(8,128)S(1)}, f32[40,256]{1,0:T(8,128)S(1)}, u32[]{:S(2)}, u32[]{:S(2)}) collective-permute-start(f32[40,256]{1,0:T(8,128)S(1)} %shard_map.141), channel_id=1, source_target_pairs={{0,2},{1,0},{2,3},{3,1},{4,6},{5,4},{6,7},{7,5},{8,10},{9,8},{10,1... | collective-permute-start | bytes 122888 | tf_op jit(solution)/shard_map/ppermute | solution.py:630
  43.0 1.4 %collective-permute-start.13 = (f32[40,256]{1,0:T(8,128)S(1)}, f32[40,256]{1,0:T(8,128)S(1)}, u32[]{:S(2)}, u32[]{:S(2)}) collective-permute-start(f32[40,256]{1,0:T(8,128)S(1)} %add_add_fusion.moments), channel_id=1, source_target_pairs={{0,1},{1,0},{2,3},{3,2},{4,5},{5,4},{6,7},{7,6},{8,9},{9,8},{10,11... | collective-permute-start | bytes 122888 | tf_op jit(solution)/shard_map/ppermute | solution.py:519

commit v6 on v5

--- a/solution.py
+++ b/solution.py
@@ -158,10 +158,13 @@
         far_ref[at + k] = packed[ghosts:]
 
 
-def pack_velocity_kernel(info, velocity, conn_ref, near_ref, far_ref, state_ref, pick_ref):
-    pick = pack_matrix(conn_ref[...], info[0:1, :], velocity.shape[2], near_ref.shape[1])
-    pick_ref[...] = pick
-    pack_field(velocity, 0, pick, near_ref, far_ref, state_ref)
+def pick_kernel(info, conn_ref, pick_ref):
+    rows, nodes = pick_ref.shape
+    pick_ref[...] = pack_matrix(conn_ref[...], info[0:1, :], nodes, rows // 2)
+
+
+def pack_velocity_kernel(velocity, pick_ref, near_ref, far_ref, state_ref):
+    pack_field(velocity, 0, pick_ref[...], near_ref, far_ref, state_ref)
 
 
 def pack_magnetic_kernel(
@@ -374,52 +377,82 @@
         far_out[k] = total[ghosts:]
 
 
-def next_kernel(
-    info, far, near, image, before, own, ghost_ops, squares_ref,
-    vector_out, image_out, packed_out, moments_out,
-):
-    nodes = image.shape[1]
-    count = 2 * near.shape[1]
-    square = squares_ref[0:1, :]
-    for k in range(6):
-        part = dot(ghost_ops[k // 3, : 2 * nodes], stacked_rows(ghost_block(info, near, far, k)))
-        total = image[k] + part[:nodes] + square * part[nodes:]
-        vector_out[k] = total
-        full, packed = apply_own(own, total, k, square, nodes, count)
-        image_out[k] = full
-        packed_out[k] = packed
-        moments_out[k : k + 1, :] = jnp.sum(before[k] * total, axis=0, keepdims=True)
-        moments_out[6 + k : 7 + k, :] = jnp.sum(total * total, axis=0, keepdims=True)
-    moments_out[12:16, :] = jnp.zeros((4, moments_out.shape[1]), f32)
-
-
-def last_kernel(
-    info, far, near, image, before, own, ghost_ops, back_ops, squares_ref, first, second,
-    vector_out, back_out, moments_out,
+def combine(image, square):
+    half = image.shape[0] // 2
+    return image[:half] + square * image[half:]
+
+
+def near_only(near):
+    return stacked_rows(jnp.concatenate([near, jnp.zeros_like(near)], axis=0))
+
+
+def far_only(info, far):
+    distant = jnp.where(info[3:4, :] > 0.0, far, 0.0)
+    return stacked_rows(jnp.concatenate([jnp.zeros_like(far), distant], axis=0))
+
+
+def second_kernel(
+    info, far, near, near_next, image, own, ghost_ops, squares_ref, vector_out, far_out, packed_near
 ):
     nodes = image.shape[1]
     ghosts = near.shape[1]
-    count = 2 * ghosts
+    square = squares_ref[0:1, :]
+    for k in range(6):
+        ops = ghost_ops[k // 3, : 2 * nodes]
+        total = image[k] + combine(dot(ops, stacked_rows(ghost_block(info, near, far, k))), square)
+        vector_out[k] = total
+        packed = dot(own[k // 3, 2 * nodes :], stacked_rows(total))
+        packed = combine(packed + dot(ghost_ops[k // 3, 2 * nodes :], near_only(near_next[k])), square)
+        packed_near[k] = packed[:ghosts]
+        far_out[k] = packed[ghosts:]
+
+
+def spread_kernel(
+    vector, before, near, own, ghost_ops, back_ops, squares_ref, image_out, back_out, moments_out
+):
+    nodes = vector.shape[1]
+    ghosts = near.shape[1]
+    square = squares_ref[0:1, :]
+    for k in range(6):
+        value = vector[k]
+        rows = stacked_rows(value)
+        image = dot(own[k // 3, : 2 * nodes], rows)
+        image_out[k] = combine(image + dot(ghost_ops[k // 3, : 2 * nodes], near_only(near[k])), square)
+        back_out[k] = combine(dot(back_ops[k // 3], rows), square)[ghosts:]
+        moments_out[k : k + 1, :] = jnp.sum(before[k] * value, axis=0, keepdims=True)
+        moments_out[6 + k : 7 + k, :] = jnp.sum(value * value, axis=0, keepdims=True)
+    moments_out[12:16, :] = jnp.zeros((4, moments_out.shape[1]), f32)
+
+
+def third_kernel(info, far, image, packed_near, ghost_ops, squares_ref, vector_out, near_out):
+    nodes = image.shape[1]
+    ghosts = far.shape[1]
+    square = squares_ref[0:1, :]
+    for k in range(6):
+        part = dot(ghost_ops[k // 3], far_only(info, far[k]))
+        vector_out[k] = image[k] + combine(part[: 2 * nodes], square)
+        near_out[k] = packed_near[k] + combine(part[2 * nodes :], square)[:ghosts]
+
+
+def last_kernel(
+    vector, before, own, back_ops, squares_ref, first, second, back_out, moments_out
+):
+    nodes = vector.shape[1]
     square = squares_ref[0:1, :]
     moments_out[0:6] = first[0:6]
     moments_out[6:18] = second[0:12]
     for k in range(6):
-        part = dot(ghost_ops[k // 3, : 2 * nodes], stacked_rows(ghost_block(info, near, far, k)))
-        total = image[k] + part[:nodes] + square * part[nodes:]
-        vector_out[k] = total
-        rows = stacked_rows(total)
-        after = dot(own[k // 3, : 2 * nodes], rows)
-        after = after[:nodes] + square * after[nodes:]
-        back = dot(back_ops[k // 3], rows)
-        back = back[:count] + square * back[count:]
-        back_out[k] = back
-        moments_out[18 + k : 19 + k, :] = jnp.sum(before[k] * total, axis=0, keepdims=True)
-        moments_out[24 + k : 25 + k, :] = jnp.sum(total * total, axis=0, keepdims=True)
-        moments_out[30 + k : 31 + k, :] = jnp.sum(after * total, axis=0, keepdims=True)
+        value = vector[k]
+        rows = stacked_rows(value)
+        after = combine(dot(own[k // 3, : 2 * nodes], rows), square)
+        back_out[k] = combine(dot(back_ops[k // 3], rows), square)
+        moments_out[18 + k : 19 + k, :] = jnp.sum(before[k] * value, axis=0, keepdims=True)
+        moments_out[24 + k : 25 + k, :] = jnp.sum(value * value, axis=0, keepdims=True)
+        moments_out[30 + k : 31 + k, :] = jnp.sum(after * value, axis=0, keepdims=True)
     moments_out[36:40, :] = jnp.zeros((4, moments_out.shape[1]), f32)
 
 
-def join_kernel(far_weight, near_weight, info, far, near, back, moments, *rest):
+def join_kernel(far_weight, near_weight, info, far, sent, near, back, moments, *rest):
     ghosts = near.shape[1]
     out = rest[-1]
     total = moments[...]
@@ -427,7 +460,7 @@
         total = total + other[...]
     out[...] = total
     for k in range(6):
-        distant = jnp.where(info[3:4, :] > 0.0, far[k], 0.0)
+        distant = jnp.where(info[3:4, :] > 0.0, far[k] + sent[k], 0.0)
         crossing = far_weight * jnp.sum(distant * back[k, ghosts:], axis=0, keepdims=True)
         crossing += near_weight * jnp.sum(near[k] * back[k, :ghosts], axis=0, keepdims=True)
         out[30 + k : 31 + k, :] += crossing
@@ -466,10 +499,10 @@
         out[k % 3] = source[k % 3] + jnp.transpose(change)
 
 
-def call(kernel, outs, operands, scratch=(), flops=0, limit=24, aliases=None):
+def call(kernel, outs, operands, scratch=(), flops=0, limit=24, aliases=None, moved=None):
     single = not isinstance(outs, list)
     shapes = [outs] if single else outs
-    moved = sum(math.prod(o.shape) * o.dtype.itemsize for o in list(operands) + shapes)
+    moved = moved or sum(math.prod(o.shape) * o.dtype.itemsize for o in list(operands) + shapes)
     return pl.pallas_call(
         kernel,
         out_shape=outs,
@@ -528,20 +561,24 @@
     whole = shape(6, nodes, coefs)
     packs = shape(6, both, coefs)
 
+    def swap_far_beside(value):
+        return lax.ppermute(value, ("runs", "mesh"), far_pairs[::-1])
+
     def exchange(near, far):
         far = swap_far(far)
         return swap_near(near), far
 
-    near, far, state, pick = call(
-        pack_velocity_kernel,
-        [ends, ends, whole, shape(both, nodes, dtype=bf16)],
-        [info, velocity, conn],
+    pick = call(pick_kernel, shape(both, nodes, dtype=bf16), [info, conn], flops=100_000_000, moved=1000)
+    near, far, state = call(
+        pack_velocity_kernel, [ends, ends, whole], [velocity, pick], flops=100_000_000, moved=1000
     )
     near, far, state = call(
         pack_magnetic_kernel,
         [ends, ends, whole],
         [magnetic, pick, near, far, state],
         aliases={2: 0, 3: 1, 4: 2},
+        flops=100_000_000,
+        moved=1000,
     )
     near_state, far_state = exchange(near, far)
     dense, mass_own, rest_own, mass_ghost, rest_ghost = call(
@@ -599,28 +636,34 @@
         send_kernel, [ends, ends], [info, far_now, near_now, packed, ghost_ops, squares], flops=100_000_000
     )
     near_next, far_next = exchange(near, far)
-    vector1, image, packed, moments1 = call(
-        next_kernel,
-        [whole, whole, packs, shape(16, coefs)],
-        [info, far_now, near_now, image, vector0, own, ghost_ops, squares],
-        flops=2_000_000_000,
-    )
-    near, far = call(
-        send_kernel, [ends, ends], [info, far_next, near_next, packed, ghost_ops, squares], flops=100_000_000
-    )
-    near_last, far_last = exchange(near, far)
-    vector2, back, moments = call(
+    vector1, far, packed_near = call(
+        second_kernel,
+        [whole, ends, ends],
+        [info, far_now, near_now, near_next, image, own, ghost_ops, squares],
+        flops=1_000_000_000,
+    )
+    far_last = swap_far_beside(far)
+    image, back1, moments1 = call(
+        spread_kernel,
+        [whole, ends, shape(16, coefs)],
+        [vector1, vector0, near_next, own, ghost_ops, back_ops, squares],
+        flops=1_000_000_000,
+    )
+    vector2, near = call(
+        third_kernel, [whole, ends], [info, far_next, image, packed_near, ghost_ops, squares], flops=500_000_000
+    )
+    near_last = swap_near(near)
+    back, moments = call(
         last_kernel,
-        [whole, packs, shape(40, coefs)],
-        [info, far_next, near_next, image, vector1, own, ghost_ops, back_ops, squares]
-        + [moments0, moments1],
-        flops=2_000_000_000,
+        [packs, shape(40, coefs)],
+        [vector2, vector1, own, back_ops, squares, moments0, moments1],
+        flops=1_000_000_000,
     )
     if count % 8 == 0 and count <= 16:
         joined = call(
             functools.partial(join_kernel, 2.0, 2.0),
             shape(40, coefs),
-            [info, far_last, near_last, back, moments, swap_near(moments)],
+            [info, far_last, back1, near_last, back, moments, swap_near(moments)],
         )
         target = (2, 0, 3, 1)
         lines = count // 4
@@ -632,7 +675,7 @@
         other = swap_near(half)
     else:
         joined = call(
-            functools.partial(join_kernel, 1.0, 1.0), shape(40, coefs), [info, far_last, near_last, back, moments]
+            functools.partial(join_kernel, 1.0, 1.0), shape(40, coefs), [info, far_last, back1, near_last, back, moments]
         )
         half = lax.psum(joined, "mesh")
         other = jnp.zeros_like(half)

time: 45.7 us -> 44.5 us (0.974)
  local copies, waits for them, and re-layouts: 2.26 us -> 1.61 us
    ppermute x4 -> x3, starting transfers between devices: 6.77 us -> 5.59 us  [swap_far(): return lax.ppermute(value, ('runs', 'mesh'), far_pairs)]
    ppermute x0 -> x1, starting transfers between devices: none -> 1.13 us  [swap_far_beside(): return lax.ppermute(value, ('runs', 'mesh'), far_pairs[::-1])]
    ppermute x6, starting transfers between devices: 7.08 us -> 6.19 us  [swap_near(): return lax.ppermute(value, 'mesh', near_pairs)]
    ppermute x4, starting transfers between devices: 5.35 us -> 6.09 us  [local(): term = lax.ppermute(joined, 'mesh', pairs)]
    unnamed x28 -> x26, local copies, waits for them, and re-layouts: 2.26 us -> 1.61 us
    pallas_call x12 -> x14, Pallas kernels: 16.4 us -> 16.1 us  [call(): pl.pallas_call(kernel, out_shape=outs, in_specs=[VMEM] * len(operands), o...]
    ppermute x4 -> x3, waiting for transfers between devices: 1.04 us -> 1.01 us  [swap_far(): return lax.ppermute(value, ('runs', 'mesh'), far_pairs)]
  transfers between devices with their start and end apart: 14 -> 14, of which waited for: 6 -> 6; matrix products, arithmetic and copies ran while one was open for 0% -> 0% of each run, Pallas kernels for 26% -> 27%
where the time goes in v6:
time: 44.5 us; the launch traced here: 44.3 us
  starting transfers between devices  19 us (43%)
  Pallas kernels  16.1 us (36%)
  waiting for transfers between devices  6.56 us (15%)
  local copies, waits for them, and re-layouts  1.61 us (4%)
  between operations  0.87 us (2%)
    pallas_call x14, Pallas kernels, call(): pl.pallas_call(kernel, out_shape=outs, in_specs=[VMEM] * len(operands), o...  16.1 us
    ppermute x6, starting transfers between devices, swap_near(): return lax.ppermute(value, 'mesh', near_pairs)  6.19 us
    ppermute x4, starting transfers between devices, local(): term = lax.ppermute(joined, 'mesh', pairs)  6.09 us
    ppermute x3, starting transfers between devices, swap_far(): return lax.ppermute(value, ('runs', 'mesh'), far_pairs)  5.59 us
    ppermute x4, waiting for transfers between devices, local(): term = lax.ppermute(joined, 'mesh', pairs)  3.47 us
    ppermute x6, waiting for transfers between devices, swap_near(): return lax.ppermute(value, 'mesh', near_pairs)  2.09 us
    unnamed x26, local copies, waits for them, and re-layouts  1.61 us
    ppermute x1, starting transfers between devices, swap_far_beside(): return lax.ppermute(value, ('runs', 'mesh'), far_pairs[::-1])  1.13 us
  transfers between devices with their start and end apart: 14, of which 6 were waited for; matrix products, arithmetic and copies ran while one was open for 0% of the time, Pallas kernels for 27%

profile of v6, /device:TPU:0, one launch (start us, length us, event | category | flops | bytes accessed | tf_op | source)
XLA Modules:
  0.0 44.3 jit_solution(14359418869649153518)
XLA Ops:
  0.6 0.0 copy-start.1
  0.7 0.1 select_convert_fusion.info
  0.8 0.0 copy-start.6
  0.8 0.7 %copy-done.6 = s32[6,128]{1,0:T(8,128)S(1)} copy-done((s32[6,128]{1,0:T(8,128)S(1)}, s32[6,128]{1,0:T(8,128)}, u32[]{:S(2)}) %copy-start.6) | copy-done | bytes 3096
  1.5 0.0 copy-start
  1.5 0.3 shard_map.131.pick_ref
  1.8 0.0 copy-done.1
  1.8 0.3 shard_map.132
  2.1 0.4 copy-done
  2.5 0.0 copy-start.3
  2.5 0.0 copy-start.4
  2.5 0.0 copy-start.5
  2.5 0.3 shard_map.133
  2.8 0.0 copy-start.7
  2.9 3.0 %collective-permute-start = (f32[6,32,256]{2,1,0:T(8,128)S(1)}, f32[6,32,256]{2,1,0:T(8,128)S(1)}, u32[]{:S(2)}, u32[]{:S(2)}) collective-permute-start(f32[6,32,256]{2,1,0:T(8,128)S(1)} %get-tuple-element.40), channel_id=1, source_target_pairs={{1,2},{2,1},{3,4},{4,3},{5,6},{6,5},{7,8},{8,7},{9,10},{10,9},{11,... | collective-permute-start | bytes 589832 | tf_op jit(solution)/shard_map/ppermute | solution.py:555
  5.9 0.1 collective-permute-start.1
  6.0 0.0 copy-done.3
  6.0 0.0 copy-done.4
  6.0 0.0 copy-done.5
  6.0 0.0 copy-done.7
  6.0 0.5 %copy-done.8 = s32[2,32]{1,0:T(2,128)S(1)} copy-done((s32[2,32]{1,0:T(2,128)S(1)}, s32[2,32]{1,0:T(2,128)}, u32[]{:S(2)}) %copy-start.8) | copy-done | bytes 280
  6.5 0.0 copy-done.9
  6.5 0.0 copy-start.12
  6.6 1.8 %shard_map.134 = (f32[640,192]{1,0:T(8,128)S(1)}, bf16[64,384]{1,0:T(8,128)(2,1)S(1)}, bf16[2,128,384]{2,1,0:T(8,128)(2,1)S(1)}, bf16[64,192]{1,0:T(8,128)(2,1)S(1)}, bf16[2,128,192]{2,1,0:T(8,128)(2,1)S(1)}) custom-call(f32[8,256]{1,0:T(8,128)S(1)} %select_convert_fusion.info, bf16[64,128]{1,0:T(8,128)(2,1)S(1)} %shard_map.131.pick_ref, ...), custom_call_target="tpu_custom_call" | custom-call | flops 1000000000 | bytes 943872 | tf_op jit(solution)/shard_map/pallas_call | solution.py:506
  8.4 0.0 copy-done.2
  8.4 0.0 copy-done.10
  8.4 0.0 copy-done.11
  8.4 0.0 copy-done.12
  8.4 3.0 %shard_map.135 = (f32[6,128,256]{2,1,0:T(8,128)S(1)}, f32[6,64,256]{2,1,0:T(8,128)S(1)}) custom-call(f32[6,128,256]{2,1,0:T(8,128)S(1)} %get-tuple-element.42.state, bf16[512,512]{1,0:T(8,128)(2,1)S(1)} %copy-done.11, bf16[1024,256]{1,0:T(8,128)(2,1)S(1)} %copy-done.10, f32[8,512]{1,0:T(8,128)S(1)} %copy-done.12, f32[8,256]{1,0:T(8,128)S(1)} %copy-done.2, ...), custom_call_target="tpu_custom_call" | custom-call | flops 2000000000 | bytes 3284992 | tf_op jit(solution)/shard_map/pallas_call | solution.py:506
  11.4 0.0 collective-permute-done.far
  11.4 0.0 collective-permute-done.1.near
  11.4 1.7 %shard_map.136 = (f32[6,32,256]{2,1,0:T(8,128)S(1)}, f32[6,32,256]{2,1,0:T(8,128)S(1)}, f32[6,64,256]{2,1,0:T(8,128)S(1)}) custom-call(f32[8,256]{1,0:T(8,128)S(1)} %select_convert_fusion.info, f32[6,32,256]{2,1,0:T(8,128)S(1)} %collective-permute-done.far, f32[6,32,256]{2,1,0:T(8,128)S(1)} %collective-permute-done.1.near, ...), custom_call_target="tpu_custom_call" | custom-call | flops 1000000000 | bytes 2777088 | tf_op jit(solution)/shard_map/pallas_call | solution.py:506
  13.1 1.1 %collective-permute-start.2 = (f32[6,32,256]{2,1,0:T(8,128)S(1)}, f32[6,32,256]{2,1,0:T(8,128)S(1)}, u32[]{:S(2)}, u32[]{:S(2)}) collective-permute-start(f32[6,32,256]{2,1,0:T(8,128)S(1)} %get-tuple-element.48), channel_id=1, source_target_pairs={{1,2},{2,1},{3,4},{4,3},{5,6},{6,5},{7,8},{8,7},{9,10},{10,9},{11,... | collective-permute-start | bytes 589832 | tf_op jit(solution)/shard_map/ppermute | solution.py:555
  14.2 0.8 %collective-permute-start.3 = (f32[6,32,256]{2,1,0:T(8,128)S(1)}, f32[6,32,256]{2,1,0:T(8,128)S(1)}, u32[]{:S(2)}, u32[]{:S(2)}) collective-permute-start(f32[6,32,256]{2,1,0:T(8,128)S(1)} %get-tuple-element.49), channel_id=1, source_target_pairs={{0,1},{1,0},{2,3},{3,2},{4,5},{5,4},{6,7},{7,6},{8,9},{9,8},{10,11... | collective-permute-start | bytes 589832 | tf_op jit(solution)/shard_map/ppermute | solution.py:552
  15.0 3.6 %shard_map.137 = (bf16[2,384,384]{2,1,0:T(8,128)(2,1)S(1)}, bf16[2,384,192]{2,1,0:T(8,128)(2,1)S(1)}, bf16[2,128,384]{2,1,0:T(8,128)(2,1)S(1)}, f32[6,128,256]{2...) custom-call(f32[8,256]{1,0:T(8,128)S(1)} %select_convert_fusion.info, ...), custom_call_target="tpu_custom_call" | custom-call | flops 2000000000 | bytes 5939200 | tf_op jit(solution)/shard_map/pallas_call | solution.py:506
  18.6 0.2 collective-permute-done.2.far
  18.9 0.0 collective-permute-done.3.near
  18.9 0.3 shard_map.138
  19.1 0.9 %collective-permute-start.4 = (f32[6,32,256]{2,1,0:T(8,128)S(1)}, f32[6,32,256]{2,1,0:T(8,128)S(1)}, u32[]{:S(2)}, u32[]{:S(2)}) collective-permute-start(f32[6,32,256]{2,1,0:T(8,128)S(1)} %get-tuple-element.55), channel_id=1, source_target_pairs={{0,1},{1,0},{2,3},{3,2},{4,5},{5,4},{6,7},{7,6},{8,9},{9,8},{10,11... | collective-permute-start | bytes 589832 | tf_op jit(solution)/shard_map/ppermute | solution.py:552
  20.0 1.5 %collective-permute-start.6 = (f32[6,32,256]{2,1,0:T(8,128)S(1)}, f32[6,32,256]{2,1,0:T(8,128)S(1)}, u32[]{:S(2)}, u32[]{:S(2)}) collective-permute-start(f32[6,32,256]{2,1,0:T(8,128)S(1)} %get-tuple-element.63), channel_id=1, source_target_pairs={{1,2},{2,1},{3,4},{4,3},{5,6},{6,5},{7,8},{8,7},{9,10},{10,9},{11,... | collective-permute-start | bytes 589832 | tf_op jit(solution)/shard_map/ppermute | solution.py:555
  21.5 0.0 collective-permute-done.4.near_next.near
  21.5 1.2 %shard_map.139 = (f32[6,128,256]{2,1,0:T(8,128)S(1)}, f32[6,32,256]{2,1,0:T(8,128)S(1)}, f32[6,32,256]{2,1,0:T(8,128)S(1)}) custom-call(f32[8,256]{1,0:T(8,128)S(1)} %select_convert_fusion.info, f32[6,32,256]{2,1,0:T(8,128)S(1)} %collective-permute-done.2.far, f32[6,32,256]{2,1,0:T(8,128)S(1)} %collective-permute-done.3.near, ...), custom_call_target="tpu_custom_call" | custom-call | flops 1000000000 | bytes 3457024 | tf_op jit(solution)/shard_map/pallas_call | solution.py:506
  22.8 1.1 %collective-permute-start.5 = (f32[6,32,256]{2,1,0:T(8,128)S(1)}, f32[6,32,256]{2,1,0:T(8,128)S(1)}, u32[]{:S(2)}, u32[]{:S(2)}) collective-permute-start(f32[6,32,256]{2,1,0:T(8,128)S(1)} %get-tuple-element.58), channel_id=1, source_target_pairs={{31,15},{15,31},{16,0},{0,16},{30,29},{29,30},{28,27},{27,28},{26,... | collective-permute-start | bytes 589832 | tf_op jit(solution)/shard_map/ppermute | solution.py:565
  23.9 1.0 %shard_map.140 = (f32[6,128,256]{2,1,0:T(8,128)S(1)}, f32[6,32,256]{2,1,0:T(8,128)S(1)}, f32[16,256]{1,0:T(8,128)S(1)}) custom-call(f32[6,128,256]{2,1,0:T(8,128)S(1)} %get-tuple-element.59.vector.before.second, f32[6,128,256]{2,1,0:T(8,128)S(1)} %get-tuple-element.60.before.first, f32[6,32,256]{2,1,0:T(8,128)S(1)} %collective-permute-done.4.near_next.near, ...), custom_call_target="tpu_custom_call" | custom-call | flops 1000000000 | bytes 3858432 | tf_op jit(solution)/shard_map/pallas_call | solution.py:506
  24.9 0.8 %collective-permute-done.6.far = f32[6,32,256]{2,1,0:T(8,128)S(1)} collective-permute-done((f32[6,32,256]{2,1,0:T(8,128)S(1)}, f32[6,32,256]{2,1,0:T(8,128)S(1)}, u32[]{:S(2)}, u32[]{:S(2)}) %collective-permute-start.6) | collective-permute-done | bytes 196640 | tf_op jit(solution)/shard_map/ppermute | solution.py:555
  25.7 0.5 %shard_map.141 = (f32[6,128,256]{2,1,0:T(8,128)S(1)}, f32[6,32,256]{2,1,0:T(8,128)S(1)}) custom-call(f32[8,256]{1,0:T(8,128)S(1)} %select_convert_fusion.info, f32[6,32,256]{2,1,0:T(8,128)S(1)} %collective-permute-done.6.far, f32[6,128,256]{2,1,0:T(8,128)S(1)} %get-tuple-element.64.image, f32[6,32,256]{2,1,0:T(8,128)S(1)} %get-tuple-element.65.packed_near, ...), custom_call_target="tpu_custom_call" | custom-call | flops 500000000 | bytes 2473984 | tf_op jit(solution)/shard_map/pallas_call | solution.py:506
  26.2 3.8 %collective-permute-start.7 = (f32[6,32,256]{2,1,0:T(8,128)S(1)}, f32[6,32,256]{2,1,0:T(8,128)S(1)}, u32[]{:S(2)}, u32[]{:S(2)}) collective-permute-start(f32[6,32,256]{2,1,0:T(8,128)S(1)} %get-tuple-element.66), channel_id=1, source_target_pairs={{0,1},{1,0},{2,3},{3,2},{4,5},{5,4},{6,7},{7,6},{8,9},{9,8},{10,11... | collective-permute-start | bytes 589832 | tf_op jit(solution)/shard_map/ppermute | solution.py:552
  30.0 0.8 %shard_map.142 = (f32[6,64,256]{2,1,0:T(8,128)S(1)}, f32[40,256]{1,0:T(8,128)S(1)}) custom-call(f32[6,128,256]{2,1,0:T(8,128)S(1)} %get-tuple-element.67.vector.third, f32[6,128,256]{2,1,0:T(8,128)S(1)} %get-tuple-element.59.vector.before.second, bf16[2,384,384]{2,1,0:T(8,128)(2,1)S(1)} %get-tuple-element.57.own, ...), custom_call_target="tpu_custom_call" | custom-call | flops 1000000000 | bytes 2826240 | tf_op jit(solution)/shard_map/pallas_call | solution.py:506
  30.8 0.1 collective-permute-start.8
  30.9 1.2 %collective-permute-done.8.rest_0_ = f32[40,256]{1,0:T(8,128)S(1)} collective-permute-done((f32[40,256]{1,0:T(8,128)S(1)}, f32[40,256]{1,0:T(8,128)S(1)}, u32[]{:S(2)}, u32[]{:S(2)}) %collective-permute-start.8) | collective-permute-done | bytes 40992 | tf_op jit(solution)/shard_map/ppermute | solution.py:552
  32.1 0.0 collective-permute-done.5.far
  32.1 0.0 collective-permute-done.7.near
  32.1 0.1 shard_map.143
  32.2 3.8 %collective-permute-start.12 = (f32[40,256]{1,0:T(8,128)S(1)}, f32[40,256]{1,0:T(8,128)S(1)}, u32[]{:S(2)}, u32[]{:S(2)}) collective-permute-start(f32[40,256]{1,0:T(8,128)S(1)} %shard_map.143), channel_id=1, source_target_pairs={{0,14},{1,12},{2,15},{3,13},{4,10},{5,8},{6,11},{7,9},{8,6},{9,4},... | collective-permute-start | bytes 122888 | tf_op jit(solution)/shard_map/ppermute | solution.py:673
  36.0 1.2 %collective-permute-start.11 = (f32[40,256]{1,0:T(8,128)S(1)}, f32[40,256]{1,0:T(8,128)S(1)}, u32[]{:S(2)}, u32[]{:S(2)}) collective-permute-start(f32[40,256]{1,0:T(8,128)S(1)} %shard_map.143), channel_id=1, source_target_pairs={{0,10},{1,8},{2,11},{3,9},{4,14},{5,12},{6,15},{7,13},{8,2},{9,0},... | collective-permute-start | bytes 122888 | tf_op jit(solution)/shard_map/ppermute | solution.py:673
  37.2 0.1 collective-permute-start.10
  37.3 1.0 %collective-permute-start.9 = (f32[40,256]{1,0:T(8,128)S(1)}, f32[40,256]{1,0:T(8,128)S(1)}, u32[]{:S(2)}, u32[]{:S(2)}) collective-permute-start(f32[40,256]{1,0:T(8,128)S(1)} %shard_map.143), channel_id=1, source_target_pairs={{0,2},{1,0},{2,3},{3,1},{4,6},{5,4},{6,7},{7,5},{8,10},{9,8},{10,1... | collective-permute-start | bytes 122888 | tf_op jit(solution)/shard_map/ppermute | solution.py:673
  38.3 0.0 collective-permute-done.12
  38.3 2.3 %collective-permute-done.11 = f32[40,256]{1,0:T(8,128)S(1)} collective-permute-done((f32[40,256]{1,0:T(8,128)S(1)}, f32[40,256]{1,0:T(8,128)S(1)}, u32[]{:S(2)}, u32[]{:S(2)}) %collective-permute-start.11) | collective-permute-done | bytes 40992 | tf_op jit(solution)/shard_map/ppermute | solution.py:673
  40.5 1.2 %collective-permute-done.10 = f32[40,256]{1,0:T(8,128)S(1)} collective-permute-done((f32[40,256]{1,0:T(8,128)S(1)}, f32[40,256]{1,0:T(8,128)S(1)}, u32[]{:S(2)}, u32[]{:S(2)}) %collective-permute-start.10) | collective-permute-done | bytes 40992 | tf_op jit(solution)/shard_map/ppermute | solution.py:673
  41.7 0.0 collective-permute-done.9
  41.8 0.5 %collective-permute-start.13 = (f32[40,256]{1,0:T(8,128)S(1)}, f32[40,256]{1,0:T(8,128)S(1)}, u32[]{:S(2)}, u32[]{:S(2)}) collective-permute-start(f32[40,256]{1,0:T(8,128)S(1)} %add_add_fusion.moments), channel_id=1, source_target_pairs={{0,1},{1,0},{2,3},{3,2},{4,5},{5,4},{6,7},{7,6},{8,9},{9,8},{10,11... | collective-permute-start | bytes 122888 | tf_op jit(solution)/shard_map/ppermute | solution.py:552
  42.3 0.9 %collective-permute-done.13.other = f32[40,256]{1,0:T(8,128)S(1)} collective-permute-done((f32[40,256]{1,0:T(8,128)S(1)}, f32[40,256]{1,0:T(8,128)S(1)}, u32[]{:S(2)}, u32[]{:S(2)}) %collective-permute-start.13) | collective-permute-done | bytes 40992 | tf_op jit(solution)/shard_map/ppermute | solution.py:552
  43.2 1.1 %shard_map.144 = (f32[3,256,128]{2,1,0:T(8,128)}, f32[3,256,128]{2,1,0:T(8,128)}) custom-call(f32[40,256]{1,0:T(8,128)S(1)} %add_add_fusion.moments, f32[40,256]{1,0:T(8,128)S(1)} %collective-permute-done.13.other, f32[3,256,128]{2,1,0:T(8,128)S(1)} %copy-done.1, f32[3,256,128]{2,1,0:T(8,128)S(1)} %copy-done, ...), custom_call_target="tpu_custom_call" | custom-call | flops 10000000 | bytes 4014080 | tf_op jit(solution)/shard_map/pallas_call | solution.py:506
  (8 shorter events, 0.0 us)
Async XLA Ops:
  0.6 1.2 %copy-start.1 = (f32[3,256,128]{2,1,0:T(8,128)S(1)}, f32[3,256,128]{2,1,0:T(8,128)}, u32[]{:S(2)}) copy-start(f32[3,256,128]{2,1,0:T(8,128)} %velocity.3) | copy-start | bytes 1179652
  0.8 0.7 %copy-start.6 = (s32[6,128]{1,0:T(8,128)S(1)}, s32[6,128]{1,0:T(8,128)}, u32[]{:S(2)}) copy-start(s32[6,128]{1,0:T(8,128)} %conn_ref.3) | copy-start | bytes 9220
  1.5 1.0 %copy-start = (f32[3,256,128]{2,1,0:T(8,128)S(1)}, f32[3,256,128]{2,1,0:T(8,128)}, u32[]{:S(2)}) copy-start(f32[3,256,128]{2,1,0:T(8,128)} %magnetic.3) | copy-start | bytes 1179652
  2.5 3.5 %copy-start.3 = (f32[6,6,128]{2,1,0:T(8,128)S(1)}, f32[6,6,128]{2,1,0:T(8,128)}, u32[]{:S(2)}) copy-start(f32[6,6,128]{2,1,0:T(8,128)} %mass_ref.1) | copy-start | bytes 55300
  2.5 3.5 %copy-start.4 = (f32[6,6,128]{2,1,0:T(8,128)S(1)}, f32[6,6,128]{2,1,0:T(8,128)}, u32[]{:S(2)}) copy-start(f32[6,6,128]{2,1,0:T(8,128)} %stiff_ref.1) | copy-start | bytes 55300
  2.5 3.5 %copy-start.5 = (f32[6,6,128]{2,1,0:T(8,128)S(1)}, f32[6,6,128]{2,1,0:T(8,128)}, u32[]{:S(2)}) copy-start(f32[6,6,128]{2,1,0:T(8,128)} %twist_ref.1) | copy-start | bytes 55300
  2.8 3.2 %copy-start.7 = (s32[6,128]{1,0:T(8,128)S(1)}, s32[6,128]{1,0:T(8,128)}, u32[]{:S(2)}) copy-start(s32[6,128]{1,0:T(8,128)} %conn_ref.3) | copy-start | bytes 9220
  2.9 8.5 %collective-permute-start = (f32[6,32,256]{2,1,0:T(8,128)S(1)}, f32[6,32,256]{2,1,0:T(8,128)S(1)}, u32[]{:S(2)}, u32[]{:S(2)}) collective-permute-start(f32[6,32,256]{2,1,0:T(8,128)S(1)} %get-tuple-element.40), channel_id=1, source_target_pairs={{1,2},{2,1},{3,4},{4,3},{5,6},{6,5},{7,8},{8,7},{9,10},{10,9},{11,... | collective-permute-start | bytes 589832 | tf_op jit(solution)/shard_map/ppermute | solution.py:555
  5.9 0.7 %copy-start.8 = (s32[2,32]{1,0:T(2,128)S(1)}, s32[2,32]{1,0:T(2,128)}, u32[]{:S(2)}) copy-start(s32[2,32]{1,0:T(2,128)} %lists_ref.1) | copy-start | bytes 772
  5.9 0.7 %copy-start.9 = (f32[128]{0:T(128)S(1)}, f32[128]{0:T(128)}, u32[]{:S(2)}) copy-start(f32[128]{0:T(128)} %param.17) | copy-start | bytes 1540
  5.9 5.6 %collective-permute-start.1 = (f32[6,32,256]{2,1,0:T(8,128)S(1)}, f32[6,32,256]{2,1,0:T(8,128)S(1)}, u32[]{:S(2)}, u32[]{:S(2)}) collective-permute-start(f32[6,32,256]{2,1,0:T(8,128)S(1)} %get-tuple-element.41), channel_id=1, source_target_pairs={{0,1},{1,0},{2,3},{3,2},{4,5},{5,4},{6,7},{7,6},{8,9},{9,8},{10,11... | collective-permute-start | bytes 589832 | tf_op jit(solution)/shard_map/ppermute | solution.py:552
  6.5 1.8 %copy-start.2 = (f32[8,256]{1,0:T(8,128)S(1)}, f32[8,256]{1,0:T(8,128)}, u32[]{:S(2)}) copy-start(f32[8,256]{1,0:T(8,128)} %constant.35.clone.squares_ref) | copy-start | bytes 24580
  6.5 1.8 %copy-start.10 = (bf16[1024,256]{1,0:T(8,128)(2,1)S(1)}, bf16[1024,256]{1,0:T(8,128)(2,1)}, u32[]{:S(2)}) copy-start(bf16[1024,256]{1,0:T(8,128)(2,1)} %constant.33.clone.coefs_ref) | copy-start | bytes 1572868
  6.5 1.8 %copy-start.11 = (bf16[512,512]{1,0:T(8,128)(2,1)S(1)}, bf16[512,512]{1,0:T(8,128)(2,1)}, u32[]{:S(2)}) copy-start(bf16[512,512]{1,0:T(8,128)(2,1)} %constant.32.clone.planes_ref) | copy-start | bytes 1572868
  6.5 1.8 %copy-start.12 = (f32[8,512]{1,0:T(8,128)S(1)}, f32[8,512]{1,0:T(8,128)}, u32[]{:S(2)}) copy-start(f32[8,512]{1,0:T(8,128)} %constant.34.clone.rotation_ref) | copy-start | bytes 49156
  13.1 5.7 %collective-permute-start.2 = (f32[6,32,256]{2,1,0:T(8,128)S(1)}, f32[6,32,256]{2,1,0:T(8,128)S(1)}, u32[]{:S(2)}, u32[]{:S(2)}) collective-permute-start(f32[6,32,256]{2,1,0:T(8,128)S(1)} %get-tuple-element.48), channel_id=1, source_target_pairs={{1,2},{2,1},{3,4},{4,3},{5,6},{6,5},{7,8},{8,7},{9,10},{10,9},{11,... | collective-permute-start | bytes 589832 | tf_op jit(solution)/shard_map/ppermute | solution.py:555
  14.2 4.6 %collective-permute-start.3 = (f32[6,32,256]{2,1,0:T(8,128)S(1)}, f32[6,32,256]{2,1,0:T(8,128)S(1)}, u32[]{:S(2)}, u32[]{:S(2)}) collective-permute-start(f32[6,32,256]{2,1,0:T(8,128)S(1)} %get-tuple-element.49), channel_id=1, source_target_pairs={{0,1},{1,0},{2,3},{3,2},{4,5},{5,4},{6,7},{7,6},{8,9},{9,8},{10,11... | collective-permute-start | bytes 589832 | tf_op jit(solution)/shard_map/ppermute | solution.py:552
  19.1 2.4 %collective-permute-start.4 = (f32[6,32,256]{2,1,0:T(8,128)S(1)}, f32[6,32,256]{2,1,0:T(8,128)S(1)}, u32[]{:S(2)}, u32[]{:S(2)}) collective-permute-start(f32[6,32,256]{2,1,0:T(8,128)S(1)} %get-tuple-element.55), channel_id=1, source_target_pairs={{0,1},{1,0},{2,3},{3,2},{4,5},{5,4},{6,7},{7,6},{8,9},{9,8},{10,11... | collective-permute-start | bytes 589832 | tf_op jit(solution)/shard_map/ppermute | solution.py:552
  20.0 5.7 %collective-permute-start.6 = (f32[6,32,256]{2,1,0:T(8,128)S(1)}, f32[6,32,256]{2,1,0:T(8,128)S(1)}, u32[]{:S(2)}, u32[]{:S(2)}) collective-permute-start(f32[6,32,256]{2,1,0:T(8,128)S(1)} %get-tuple-element.63), channel_id=1, source_target_pairs={{1,2},{2,1},{3,4},{4,3},{5,6},{6,5},{7,8},{8,7},{9,10},{10,9},{11,... | collective-permute-start | bytes 589832 | tf_op jit(solution)/shard_map/ppermute | solution.py:555
  22.8 9.3 %collective-permute-start.5 = (f32[6,32,256]{2,1,0:T(8,128)S(1)}, f32[6,32,256]{2,1,0:T(8,128)S(1)}, u32[]{:S(2)}, u32[]{:S(2)}) collective-permute-start(f32[6,32,256]{2,1,0:T(8,128)S(1)} %get-tuple-element.58), channel_id=1, source_target_pairs={{31,15},{15,31},{16,0},{0,16},{30,29},{29,30},{28,27},{27,28},{26,... | collective-permute-start | bytes 589832 | tf_op jit(solution)/shard_map/ppermute | solution.py:565
  26.2 5.9 %collective-permute-start.7 = (f32[6,32,256]{2,1,0:T(8,128)S(1)}, f32[6,32,256]{2,1,0:T(8,128)S(1)}, u32[]{:S(2)}, u32[]{:S(2)}) collective-permute-start(f32[6,32,256]{2,1,0:T(8,128)S(1)} %get-tuple-element.66), channel_id=1, source_target_pairs={{0,1},{1,0},{2,3},{3,2},{4,5},{5,4},{6,7},{7,6},{8,9},{9,8},{10,11... | collective-permute-start | bytes 589832 | tf_op jit(solution)/shard_map/ppermute | solution.py:552
  30.8 1.3 %collective-permute-start.8 = (f32[40,256]{1,0:T(8,128)S(1)}, f32[40,256]{1,0:T(8,128)S(1)}, u32[]{:S(2)}, u32[]{:S(2)}) collective-permute-start(f32[40,256]{1,0:T(8,128)S(1)} %get-tuple-element.71.moments), channel_id=1, source_target_pairs={{0,1},{1,0},{2,3},{3,2},{4,5},{5,4},{6,7},{7,6},{8,9},{9,8},{10,11... | collective-permute-start | bytes 122888 | tf_op jit(solution)/shard_map/ppermute | solution.py:552
  32.2 6.1 %collective-permute-start.12 = (f32[40,256]{1,0:T(8,128)S(1)}, f32[40,256]{1,0:T(8,128)S(1)}, u32[]{:S(2)}, u32[]{:S(2)}) collective-permute-start(f32[40,256]{1,0:T(8,128)S(1)} %shard_map.143), channel_id=1, source_target_pairs={{0,14},{1,12},{2,15},{3,13},{4,10},{5,8},{6,11},{7,9},{8,6},{9,4},... | collective-permute-start | bytes 122888 | tf_op jit(solution)/shard_map/ppermute | solution.py:673
  36.0 4.5 %collective-permute-start.11 = (f32[40,256]{1,0:T(8,128)S(1)}, f32[40,256]{1,0:T(8,128)S(1)}, u32[]{:S(2)}, u32[]{:S(2)}) collective-permute-start(f32[40,256]{1,0:T(8,128)S(1)} %shard_map.143), channel_id=1, source_target_pairs={{0,10},{1,8},{2,11},{3,9},{4,14},{5,12},{6,15},{7,13},{8,2},{9,0},... | collective-permute-start | bytes 122888 | tf_op jit(solution)/shard_map/ppermute | solution.py:673
  37.2 4.5 %collective-permute-start.10 = (f32[40,256]{1,0:T(8,128)S(1)}, f32[40,256]{1,0:T(8,128)S(1)}, u32[]{:S(2)}, u32[]{:S(2)}) collective-permute-start(f32[40,256]{1,0:T(8,128)S(1)} %shard_map.143), channel_id=1, source_target_pairs={{0,6},{1,4},{2,7},{3,5},{4,2},{5,0},{6,3},{7,1},{8,14},{9,12},{10,... | collective-permute-start | bytes 122888 | tf_op jit(solution)/shard_map/ppermute | solution.py:673
  37.3 4.4 %collective-permute-start.9 = (f32[40,256]{1,0:T(8,128)S(1)}, f32[40,256]{1,0:T(8,128)S(1)}, u32[]{:S(2)}, u32[]{:S(2)}) collective-permute-start(f32[40,256]{1,0:T(8,128)S(1)} %shard_map.143), channel_id=1, source_target_pairs={{0,2},{1,0},{2,3},{3,1},{4,6},{5,4},{6,7},{7,5},{8,10},{9,8},{10,1... | collective-permute-start | bytes 122888 | tf_op jit(solution)/shard_map/ppermute | solution.py:673
  41.8 1.4 %collective-permute-start.13 = (f32[40,256]{1,0:T(8,128)S(1)}, f32[40,256]{1,0:T(8,128)S(1)}, u32[]{:S(2)}, u32[]{:S(2)}) collective-permute-start(f32[40,256]{1,0:T(8,128)S(1)} %add_add_fusion.moments), channel_id=1, source_target_pairs={{0,1},{1,0},{2,3},{3,2},{4,5},{5,4},{6,7},{7,6},{8,9},{9,8},{10,11... | collective-permute-start | bytes 122888 | tf_op jit(solution)/shard_map/ppermute | solution.py:552

commit v7 on v6

--- a/solution.py
+++ b/solution.py
@@ -173,16 +173,6 @@
     pack_field(magnetic, 3, pick_ref[...], near_ref, far_ref, state_ref)
 
 
-def to_planes(high, low, table):
-    coefs = high.shape[1]
-    return dot(high, table[:coefs]) + dot(low, table[:coefs]) + dot(high, table[coefs:])
-
-
-def to_coefs(high, low, table):
-    planes = high.shape[1]
-    return dot(high, table[:planes]) + dot(low, table[:planes]) + dot(high, table[planes:])
-
-
 def cross(a, b):
     return [
         a[1] * b[2] - a[2] * b[1],
@@ -191,27 +181,29 @@
     ]
 
 
-def forcing(value, rows, planes_ref, coefs_ref, rotation_ref, phys_ref, high_ref, low_ref):
+def forcing(value, rows, planes_ref, coefs_ref, rotation_ref):
+    coefs = value.shape[1]
     planes = planes_ref.shape[1]
     high, low = halves(value)
-    phys_ref[...] = to_planes(high, low, planes_ref)
-    step_rows, step_lanes = 16, 256
-    for row in range(0, rows, step_rows):
-        for lane in range(0, planes, step_lanes):
-            lanes = pl.ds(lane, step_lanes)
-            u = [phys_ref[pl.ds(k * rows + row, step_rows), lanes] for k in range(3)]
-            b = [phys_ref[pl.ds((3 + k) * rows + row, step_rows), lanes] for k in range(3)]
-            turn = [rotation_ref[k : k + 1, lanes] for k in range(3)]
-            induction = cross(u, b)
-            twisted = cross(turn, u)
-            lorentz = cross(b, induction)
-            force = [twisted[k] - lorentz_factor * lorentz[k] for k in range(3)]
-            for k, item in enumerate(force + induction):
-                item_high, item_low = halves(item)
-                at = pl.ds(k * rows + row, step_rows)
-                high_ref[at, lanes] = item_high
-                low_ref[at, lanes] = item_low
-    return to_coefs(high_ref[...], low_ref[...], coefs_ref)
+    part = planes // 2
+    total = None
+    for first in range(0, planes, part):
+        lanes = slice(first, first + part)
+        table = planes_ref[:coefs, lanes]
+        phys = dot(high, table) + dot(low, table) + dot(high, planes_ref[coefs:, lanes])
+        u = [phys[k * rows : (k + 1) * rows] for k in range(3)]
+        b = [phys[(3 + k) * rows : (4 + k) * rows] for k in range(3)]
+        turn = [rotation_ref[k : k + 1, lanes] for k in range(3)]
+        induction = cross(u, b)
+        twisted = cross(turn, u)
+        lorentz = cross(b, induction)
+        force = [twisted[k] - lorentz_factor * lorentz[k] for k in range(3)]
+        item_high, item_low = halves(jnp.concatenate(force + induction, axis=0))
+        table = coefs_ref[lanes]
+        term = dot(item_high, table) + dot(item_low, table)
+        term = term + dot(item_high, coefs_ref[planes + first : planes + first + part])
+        total = term if total is None else total + term
+    return total
 
 
 def triple(pair):
@@ -275,13 +267,13 @@
 
 def force_kernel(
     state, planes_ref, coefs_ref, rotation_ref, squares_ref, mass_own, rest_own,
-    force_ref, packed_ref, phys_ref, high_ref, low_ref,
+    force_ref, packed_ref,
 ):
     nodes = state.shape[1]
     count = packed_ref.shape[1]
     value = state[...].reshape(6 * nodes, state.shape[2])
     force_ref[...] = forcing(
-        value, nodes, planes_ref, coefs_ref, rotation_ref, phys_ref, high_ref, low_ref
+        value, nodes, planes_ref, coefs_ref, rotation_ref
     ).reshape(force_ref.shape)
     square = squares_ref[0:1, :]
     for k in range(6):
@@ -297,13 +289,13 @@
 
 def start_kernel(
     info, far, near, packed, planes_ref, coefs_ref, rotation_ref, squares_ref, mass_ghost, rest_ghost,
-    near_out, far_out, force_out, phys_ref, high_ref, low_ref,
+    near_out, far_out, force_out,
 ):
     ghosts = near.shape[1]
     count = 2 * ghosts
     blocks = [ghost_block(info, near, far, k) for k in range(6)]
     value = jnp.concatenate(blocks, axis=0)
-    force = forcing(value, count, planes_ref, coefs_ref, rotation_ref, phys_ref, high_ref, low_ref)
+    force = forcing(value, count, planes_ref, coefs_ref, rotation_ref)
     square = squares_ref[0:1, :]
     for k in range(6):
         item = force[k * count : (k + 1) * count]
@@ -392,7 +384,8 @@
 
 
 def second_kernel(
-    info, far, near, near_next, image, own, ghost_ops, squares_ref, vector_out, far_out, packed_near
+    info, far, near, near_next, image, before, own, ghost_ops, back_ops, squares_ref,
+    vector_out, far_out, packed_near, image_out, back_out, moments_out,
 ):
     nodes = image.shape[1]
     ghosts = near.shape[1]
@@ -401,26 +394,15 @@
         ops = ghost_ops[k // 3, : 2 * nodes]
         total = image[k] + combine(dot(ops, stacked_rows(ghost_block(info, near, far, k))), square)
         vector_out[k] = total
-        packed = dot(own[k // 3, 2 * nodes :], stacked_rows(total))
-        packed = combine(packed + dot(ghost_ops[k // 3, 2 * nodes :], near_only(near_next[k])), square)
+        rows = stacked_rows(total)
+        after = dot(own[k // 3], rows) + dot(ghost_ops[k // 3], near_only(near_next[k]))
+        image_out[k] = combine(after[: 2 * nodes], square)
+        packed = combine(after[2 * nodes :], square)
         packed_near[k] = packed[:ghosts]
         far_out[k] = packed[ghosts:]
-
-
-def spread_kernel(
-    vector, before, near, own, ghost_ops, back_ops, squares_ref, image_out, back_out, moments_out
-):
-    nodes = vector.shape[1]
-    ghosts = near.shape[1]
-    square = squares_ref[0:1, :]
-    for k in range(6):
-        value = vector[k]
-        rows = stacked_rows(value)
-        image = dot(own[k // 3, : 2 * nodes], rows)
-        image_out[k] = combine(image + dot(ghost_ops[k // 3, : 2 * nodes], near_only(near[k])), square)
         back_out[k] = combine(dot(back_ops[k // 3], rows), square)[ghosts:]
-        moments_out[k : k + 1, :] = jnp.sum(before[k] * value, axis=0, keepdims=True)
-        moments_out[6 + k : 7 + k, :] = jnp.sum(value * value, axis=0, keepdims=True)
+        moments_out[k : k + 1, :] = jnp.sum(before[k] * total, axis=0, keepdims=True)
+        moments_out[6 + k : 7 + k, :] = jnp.sum(total * total, axis=0, keepdims=True)
     moments_out[12:16, :] = jnp.zeros((4, moments_out.shape[1]), f32)
 
 
@@ -528,7 +510,6 @@
     ghosts = lists.shape[1]
     elements = conn.shape[1]
     both = 2 * ghosts
-    planes = 2 * coefs
     index = lax.axis_index("mesh")
     odd = index % 2
     low_valid = (index > 0).astype(jnp.int32)
@@ -598,11 +579,6 @@
         force_kernel,
         [whole, packs],
         [state, plane_table, coef_table, rotation, squares, mass_own, rest_own],
-        scratch=[
-            pltpu.VMEM((6 * nodes, planes), f32),
-            pltpu.VMEM((6 * nodes, planes), bf16),
-            pltpu.VMEM((6 * nodes, planes), bf16),
-        ],
         flops=2_000_000_000,
     )
     near, far, force_ghost = call(
@@ -610,11 +586,6 @@
         [ends, ends, packs],
         [info, far_state, near_state, packed, plane_table, coef_table, rotation, squares]
         + [mass_ghost, rest_ghost],
-        scratch=[
-            pltpu.VMEM((6 * both, planes), f32),
-            pltpu.VMEM((6 * both, planes), bf16),
-            pltpu.VMEM((6 * both, planes), bf16),
-        ],
         flops=1_000_000_000,
     )
     near_now, far_now = exchange(near, far)
@@ -636,19 +607,13 @@
         send_kernel, [ends, ends], [info, far_now, near_now, packed, ghost_ops, squares], flops=100_000_000
     )
     near_next, far_next = exchange(near, far)
-    vector1, far, packed_near = call(
+    vector1, far, packed_near, image, back1, moments1 = call(
         second_kernel,
-        [whole, ends, ends],
-        [info, far_now, near_now, near_next, image, own, ghost_ops, squares],
+        [whole, ends, ends, whole, ends, shape(16, coefs)],
+        [info, far_now, near_now, near_next, image, vector0, own, ghost_ops, back_ops, squares],
         flops=1_000_000_000,
     )
     far_last = swap_far_beside(far)
-    image, back1, moments1 = call(
-        spread_kernel,
-        [whole, ends, shape(16, coefs)],
-        [vector1, vector0, near_next, own, ghost_ops, back_ops, squares],
-        flops=1_000_000_000,
-    )
     vector2, near = call(
         third_kernel, [whole, ends], [info, far_next, image, packed_near, ghost_ops, squares], flops=500_000_000
     )

time: 44.5 us -> 43.1 us (0.969)
  starting transfers between devices: 19 us -> 18.2 us
  Pallas kernels: 16.1 us -> 15.5 us
    ppermute x6, starting transfers between devices: 6.19 us -> 4.37 us  [swap_near(): return lax.ppermute(value, 'mesh', near_pairs)]
    ppermute x4, starting transfers between devices: 6.09 us -> 7.14 us  [local(): term = lax.ppermute(joined, 'mesh', pairs)]
    pallas_call x14 -> x13, Pallas kernels: 16.1 us -> 15.5 us  [call(): pl.pallas_call(kernel, out_shape=outs, in_specs=[VMEM] * len(operands), o...]
  transfers between devices with their start and end apart: 14 -> 14, of which waited for: 6 -> 4; matrix products, arithmetic and copies ran while one was open for 0% -> 0% of each run, Pallas kernels for 27% -> 27%
where the time goes in v7:
time: 43.1 us; the launch traced here: 42.9 us
  starting transfers between devices  18.2 us (42%)
  Pallas kernels  15.5 us (36%)
  waiting for transfers between devices  6.64 us (15%)
  local copies, waits for them, and re-layouts  1.61 us (4%)
  between operations  0.88 us (2%)
    pallas_call x13, Pallas kernels, call(): pl.pallas_call(kernel, out_shape=outs, in_specs=[VMEM] * len(operands), o...  15.5 us
    ppermute x4, starting transfers between devices, local(): term = lax.ppermute(joined, 'mesh', pairs)  7.14 us
    ppermute x3, starting transfers between devices, swap_far(): return lax.ppermute(value, ('runs', 'mesh'), far_pairs)  5.58 us
    ppermute x6, starting transfers between devices, swap_near(): return lax.ppermute(value, 'mesh', near_pairs)  4.37 us
    ppermute x4, waiting for transfers between devices, local(): term = lax.ppermute(joined, 'mesh', pairs)  3.47 us
    ppermute x6, waiting for transfers between devices, swap_near(): return lax.ppermute(value, 'mesh', near_pairs)  2.33 us
    unnamed x26, local copies, waits for them, and re-layouts  1.61 us
    ppermute x1, starting transfers between devices, swap_far_beside(): return lax.ppermute(value, ('runs', 'mesh'), far_pairs[::-1])  1.13 us
  transfers between devices with their start and end apart: 14, of which 4 were waited for; matrix products, arithmetic and copies ran while one was open for 0% of the time, Pallas kernels for 27%

profile of v7, /device:TPU:0, one launch (start us, length us, event | category | flops | bytes accessed | tf_op | source)
XLA Modules:
  0.0 42.9 jit_solution(1491165265345649400)
XLA Ops:
  0.6 0.0 copy-start.1
  0.7 0.1 select_convert_fusion.info
  0.8 0.0 copy-start.6
  0.8 0.7 %copy-done.6 = s32[6,128]{1,0:T(8,128)S(1)} copy-done((s32[6,128]{1,0:T(8,128)S(1)}, s32[6,128]{1,0:T(8,128)}, u32[]{:S(2)}) %copy-start.6) | copy-done | bytes 3096
  1.5 0.0 copy-start
  1.5 0.3 shard_map.131.pick_ref
  1.8 0.0 copy-done.1
  1.8 0.3 shard_map.132
  2.1 0.4 copy-done
  2.5 0.0 copy-start.3
  2.5 0.0 copy-start.4
  2.5 0.0 copy-start.5
  2.5 0.3 shard_map.133
  2.8 0.0 copy-start.7
  2.9 3.0 %collective-permute-start = (f32[6,32,256]{2,1,0:T(8,128)S(1)}, f32[6,32,256]{2,1,0:T(8,128)S(1)}, u32[]{:S(2)}, u32[]{:S(2)}) collective-permute-start(f32[6,32,256]{2,1,0:T(8,128)S(1)} %get-tuple-element.40), channel_id=1, source_target_pairs={{1,2},{2,1},{3,4},{4,3},{5,6},{6,5},{7,8},{8,7},{9,10},{10,9},{11,... | collective-permute-start | bytes 589832 | tf_op jit(solution)/shard_map/ppermute | solution.py:536
  5.9 0.0 copy-start.8
  5.9 0.1 collective-permute-start.1
  6.0 0.0 copy-done.3
  6.0 0.0 copy-done.4
  6.0 0.0 copy-done.5
  6.0 0.0 copy-done.7
  6.0 0.5 %copy-done.8 = s32[2,32]{1,0:T(2,128)S(1)} copy-done((s32[2,32]{1,0:T(2,128)S(1)}, s32[2,32]{1,0:T(2,128)}, u32[]{:S(2)}) %copy-start.8) | copy-done | bytes 280
  6.5 0.0 copy-done.9
  6.5 0.0 copy-start.12
  6.6 1.8 %shard_map.134 = (f32[640,192]{1,0:T(8,128)S(1)}, bf16[64,384]{1,0:T(8,128)(2,1)S(1)}, bf16[2,128,384]{2,1,0:T(8,128)(2,1)S(1)}, bf16[64,192]{1,0:T(8,128)(2,1)S(1)}, bf16[2,128,192]{2,1,0:T(8,128)(2,1)S(1)}) custom-call(f32[8,256]{1,0:T(8,128)S(1)} %select_convert_fusion.info, bf16[64,128]{1,0:T(8,128)(2,1)S(1)} %shard_map.131.pick_ref, ...), custom_call_target="tpu_custom_call" | custom-call | flops 1000000000 | bytes 943872 | tf_op jit(solution)/shard_map/pallas_call | solution.py:488
  8.4 0.0 copy-done.2
  8.4 0.0 copy-done.10
  8.4 0.0 copy-done.11
  8.4 0.0 copy-done.12
  8.4 2.6 %shard_map.135 = (f32[6,128,256]{2,1,0:T(8,128)S(1)}, f32[6,64,256]{2,1,0:T(8,128)S(1)}) custom-call(f32[6,128,256]{2,1,0:T(8,128)S(1)} %get-tuple-element.42.state, bf16[512,512]{1,0:T(8,128)(2,1)S(1)} %copy-done.11, bf16[1024,256]{1,0:T(8,128)(2,1)S(1)} %copy-done.10, f32[8,512]{1,0:T(8,128)S(1)} %copy-done.12, f32[8,256]{1,0:T(8,128)S(1)} %copy-done.2, ...), custom_call_target="tpu_custom_call" | custom-call | flops 2000000000 | bytes 3284992 | tf_op jit(solution)/shard_map/pallas_call | solution.py:488
  11.0 0.0 collective-permute-done.far
  11.0 0.0 collective-permute-done.1.near
  11.0 1.5 %shard_map.136 = (f32[6,32,256]{2,1,0:T(8,128)S(1)}, f32[6,32,256]{2,1,0:T(8,128)S(1)}, f32[6,64,256]{2,1,0:T(8,128)S(1)}) custom-call(f32[8,256]{1,0:T(8,128)S(1)} %select_convert_fusion.info, f32[6,32,256]{2,1,0:T(8,128)S(1)} %collective-permute-done.far, f32[6,32,256]{2,1,0:T(8,128)S(1)} %collective-permute-done.1.near, ...), custom_call_target="tpu_custom_call" | custom-call | flops 1000000000 | bytes 2777088 | tf_op jit(solution)/shard_map/pallas_call | solution.py:488
  12.5 1.1 %collective-permute-start.2 = (f32[6,32,256]{2,1,0:T(8,128)S(1)}, f32[6,32,256]{2,1,0:T(8,128)S(1)}, u32[]{:S(2)}, u32[]{:S(2)}) collective-permute-start(f32[6,32,256]{2,1,0:T(8,128)S(1)} %get-tuple-element.48), channel_id=1, source_target_pairs={{1,2},{2,1},{3,4},{4,3},{5,6},{6,5},{7,8},{8,7},{9,10},{10,9},{11,... | collective-permute-start | bytes 589832 | tf_op jit(solution)/shard_map/ppermute | solution.py:536
  13.5 1.2 %collective-permute-start.3 = (f32[6,32,256]{2,1,0:T(8,128)S(1)}, f32[6,32,256]{2,1,0:T(8,128)S(1)}, u32[]{:S(2)}, u32[]{:S(2)}) collective-permute-start(f32[6,32,256]{2,1,0:T(8,128)S(1)} %get-tuple-element.49), channel_id=1, source_target_pairs={{0,1},{1,0},{2,3},{3,2},{4,5},{5,4},{6,7},{7,6},{8,9},{9,8},{10,11... | collective-permute-start | bytes 589832 | tf_op jit(solution)/shard_map/ppermute | solution.py:533
  14.7 3.6 %shard_map.137 = (bf16[2,384,384]{2,1,0:T(8,128)(2,1)S(1)}, bf16[2,384,192]{2,1,0:T(8,128)(2,1)S(1)}, bf16[2,128,384]{2,1,0:T(8,128)(2,1)S(1)}, f32[6,128,256]{2...) custom-call(f32[8,256]{1,0:T(8,128)S(1)} %select_convert_fusion.info, ...), custom_call_target="tpu_custom_call" | custom-call | flops 2000000000 | bytes 5939200 | tf_op jit(solution)/shard_map/pallas_call | solution.py:488
  18.4 0.0 collective-permute-done.2.far
  18.4 0.0 collective-permute-done.3.near
  18.4 0.3 shard_map.138
  18.7 1.1 %collective-permute-start.4 = (f32[6,32,256]{2,1,0:T(8,128)S(1)}, f32[6,32,256]{2,1,0:T(8,128)S(1)}, u32[]{:S(2)}, u32[]{:S(2)}) collective-permute-start(f32[6,32,256]{2,1,0:T(8,128)S(1)} %get-tuple-element.55), channel_id=1, source_target_pairs={{0,1},{1,0},{2,3},{3,2},{4,5},{5,4},{6,7},{7,6},{8,9},{9,8},{10,11... | collective-permute-start | bytes 589832 | tf_op jit(solution)/shard_map/ppermute | solution.py:533
  19.8 1.5 %collective-permute-start.6 = (f32[6,32,256]{2,1,0:T(8,128)S(1)}, f32[6,32,256]{2,1,0:T(8,128)S(1)}, u32[]{:S(2)}, u32[]{:S(2)}) collective-permute-start(f32[6,32,256]{2,1,0:T(8,128)S(1)} %get-tuple-element.62), channel_id=1, source_target_pairs={{1,2},{2,1},{3,4},{4,3},{5,6},{6,5},{7,8},{8,7},{9,10},{10,9},{11,... | collective-permute-start | bytes 589832 | tf_op jit(solution)/shard_map/ppermute | solution.py:536
  21.3 0.0 collective-permute-done.4.near_next
  21.3 2.2 %shard_map.139 = (f32[6,128,256]{2,1,0:T(8,128)S(1)}, f32[6,32,256]{2,1,0:T(8,128)S(1)}, f32[6,32,256]{2,1,0:T(8,128)S(1)}, f32[6,128,256]{2,1,0:T(8,128)S(1)}, ...) custom-call(f32[8,256]{1,0:T(8,128)S(1)} %select_convert_fusion.info, f32[6,32,256]{2,1,0:T(8,128)S(1)} %collective-permute-done.2.far, ...), custom_call_target="tpu_custom_call" | custom-call | flops 1000000000 | bytes 5439488 | tf_op jit(solution)/shard_map/pallas_call | solution.py:488
  23.5 1.1 %collective-permute-start.5 = (f32[6,32,256]{2,1,0:T(8,128)S(1)}, f32[6,32,256]{2,1,0:T(8,128)S(1)}, u32[]{:S(2)}, u32[]{:S(2)}) collective-permute-start(f32[6,32,256]{2,1,0:T(8,128)S(1)} %get-tuple-element.60), channel_id=1, source_target_pairs={{31,15},{15,31},{16,0},{0,16},{30,29},{29,30},{28,27},{27,28},{26,... | collective-permute-start | bytes 589832 | tf_op jit(solution)/shard_map/ppermute | solution.py:546
  24.6 0.8 %collective-permute-done.6.far = f32[6,32,256]{2,1,0:T(8,128)S(1)} collective-permute-done((f32[6,32,256]{2,1,0:T(8,128)S(1)}, f32[6,32,256]{2,1,0:T(8,128)S(1)}, u32[]{:S(2)}, u32[]{:S(2)}) %collective-permute-start.6) | collective-permute-done | bytes 196640 | tf_op jit(solution)/shard_map/ppermute | solution.py:536
  25.5 0.5 %shard_map.140 = (f32[6,128,256]{2,1,0:T(8,128)S(1)}, f32[6,32,256]{2,1,0:T(8,128)S(1)}) custom-call(f32[8,256]{1,0:T(8,128)S(1)} %select_convert_fusion.info, f32[6,32,256]{2,1,0:T(8,128)S(1)} %collective-permute-done.6.far, f32[6,128,256]{2,1,0:T(8,128)S(1)} %get-tuple-element.63.image, f32[6,32,256]{2,1,0:T(8,128)S(1)} %get-tuple-element.64.packed_near, ...), custom_call_target="tpu_custom_call" | custom-call | flops 500000000 | bytes 2473984 | tf_op jit(solution)/shard_map/pallas_call | solution.py:488
  26.0 1.7 %collective-permute-start.7 = (f32[6,32,256]{2,1,0:T(8,128)S(1)}, f32[6,32,256]{2,1,0:T(8,128)S(1)}, u32[]{:S(2)}, u32[]{:S(2)}) collective-permute-start(f32[6,32,256]{2,1,0:T(8,128)S(1)} %get-tuple-element.65), channel_id=1, source_target_pairs={{0,1},{1,0},{2,3},{3,2},{4,5},{5,4},{6,7},{7,6},{8,9},{9,8},{10,11... | collective-permute-start | bytes 589832 | tf_op jit(solution)/shard_map/ppermute | solution.py:533
  27.6 0.8 %shard_map.141 = (f32[6,64,256]{2,1,0:T(8,128)S(1)}, f32[40,256]{1,0:T(8,128)S(1)}) custom-call(f32[6,128,256]{2,1,0:T(8,128)S(1)} %get-tuple-element.66.vector.third, f32[6,128,256]{2,1,0:T(8,128)S(1)} %get-tuple-element.67.before.second, bf16[2,384,384]{2,1,0:T(8,128)(2,1)S(1)} %get-tuple-element.58.own, ...), custom_call_target="tpu_custom_call" | custom-call | flops 1000000000 | bytes 2826240 | tf_op jit(solution)/shard_map/pallas_call | solution.py:488
  28.5 0.1 collective-permute-start.8
  28.6 1.2 %collective-permute-done.8.rest_0_ = f32[40,256]{1,0:T(8,128)S(1)} collective-permute-done((f32[40,256]{1,0:T(8,128)S(1)}, f32[40,256]{1,0:T(8,128)S(1)}, u32[]{:S(2)}, u32[]{:S(2)}) %collective-permute-start.8) | collective-permute-done | bytes 40992 | tf_op jit(solution)/shard_map/ppermute | solution.py:533
  29.8 0.0 collective-permute-done.5.far
  29.8 0.0 collective-permute-done.7.near
  29.8 0.1 shard_map.142
  29.9 4.9 %collective-permute-start.12 = (f32[40,256]{1,0:T(8,128)S(1)}, f32[40,256]{1,0:T(8,128)S(1)}, u32[]{:S(2)}, u32[]{:S(2)}) collective-permute-start(f32[40,256]{1,0:T(8,128)S(1)} %shard_map.142), channel_id=1, source_target_pairs={{0,14},{1,12},{2,15},{3,13},{4,10},{5,8},{6,11},{7,9},{8,6},{9,4},... | collective-permute-start | bytes 122888 | tf_op jit(solution)/shard_map/ppermute | solution.py:638
  34.7 1.2 %collective-permute-start.11 = (f32[40,256]{1,0:T(8,128)S(1)}, f32[40,256]{1,0:T(8,128)S(1)}, u32[]{:S(2)}, u32[]{:S(2)}) collective-permute-start(f32[40,256]{1,0:T(8,128)S(1)} %shard_map.142), channel_id=1, source_target_pairs={{0,10},{1,8},{2,11},{3,9},{4,14},{5,12},{6,15},{7,13},{8,2},{9,0},... | collective-permute-start | bytes 122888 | tf_op jit(solution)/shard_map/ppermute | solution.py:638
  35.9 0.2 collective-permute-start.10
  36.1 0.9 %collective-permute-start.9 = (f32[40,256]{1,0:T(8,128)S(1)}, f32[40,256]{1,0:T(8,128)S(1)}, u32[]{:S(2)}, u32[]{:S(2)}) collective-permute-start(f32[40,256]{1,0:T(8,128)S(1)} %shard_map.142), channel_id=1, source_target_pairs={{0,2},{1,0},{2,3},{3,1},{4,6},{5,4},{6,7},{7,5},{8,10},{9,8},{10,1... | collective-permute-start | bytes 122888 | tf_op jit(solution)/shard_map/ppermute | solution.py:638
  37.0 0.0 collective-permute-done.12
  37.0 3.5 %collective-permute-done.11 = f32[40,256]{1,0:T(8,128)S(1)} collective-permute-done((f32[40,256]{1,0:T(8,128)S(1)}, f32[40,256]{1,0:T(8,128)S(1)}, u32[]{:S(2)}, u32[]{:S(2)}) %collective-permute-start.11) | collective-permute-done | bytes 40992 | tf_op jit(solution)/shard_map/ppermute | solution.py:638
  40.5 0.0 collective-permute-done.10
  40.5 0.0 collective-permute-done.9
  40.5 0.2 collective-permute-start.13
  40.7 1.1 %collective-permute-done.13.other = f32[40,256]{1,0:T(8,128)S(1)} collective-permute-done((f32[40,256]{1,0:T(8,128)S(1)}, f32[40,256]{1,0:T(8,128)S(1)}, u32[]{:S(2)}, u32[]{:S(2)}) %collective-permute-start.13) | collective-permute-done | bytes 40992 | tf_op jit(solution)/shard_map/ppermute | solution.py:533
  41.8 1.2 %shard_map.143 = (f32[3,256,128]{2,1,0:T(8,128)}, f32[3,256,128]{2,1,0:T(8,128)}) custom-call(f32[40,256]{1,0:T(8,128)S(1)} %add_add_fusion.moments, f32[40,256]{1,0:T(8,128)S(1)} %collective-permute-done.13.other, f32[3,256,128]{2,1,0:T(8,128)S(1)} %copy-done.1, f32[3,256,128]{2,1,0:T(8,128)S(1)} %copy-done, ...), custom_call_target="tpu_custom_call" | custom-call | flops 10000000 | bytes 4014080 | tf_op jit(solution)/shard_map/pallas_call | solution.py:488
  (7 shorter events, 0.0 us)
Async XLA Ops:
  0.6 1.2 %copy-start.1 = (f32[3,256,128]{2,1,0:T(8,128)S(1)}, f32[3,256,128]{2,1,0:T(8,128)}, u32[]{:S(2)}) copy-start(f32[3,256,128]{2,1,0:T(8,128)} %velocity.3) | copy-start | bytes 1179652
  0.8 0.7 %copy-start.6 = (s32[6,128]{1,0:T(8,128)S(1)}, s32[6,128]{1,0:T(8,128)}, u32[]{:S(2)}) copy-start(s32[6,128]{1,0:T(8,128)} %conn_ref.3) | copy-start | bytes 9220
  1.5 1.0 %copy-start = (f32[3,256,128]{2,1,0:T(8,128)S(1)}, f32[3,256,128]{2,1,0:T(8,128)}, u32[]{:S(2)}) copy-start(f32[3,256,128]{2,1,0:T(8,128)} %magnetic.3) | copy-start | bytes 1179652
  2.5 3.5 %copy-start.3 = (f32[6,6,128]{2,1,0:T(8,128)S(1)}, f32[6,6,128]{2,1,0:T(8,128)}, u32[]{:S(2)}) copy-start(f32[6,6,128]{2,1,0:T(8,128)} %mass_ref.1) | copy-start | bytes 55300
  2.5 3.5 %copy-start.4 = (f32[6,6,128]{2,1,0:T(8,128)S(1)}, f32[6,6,128]{2,1,0:T(8,128)}, u32[]{:S(2)}) copy-start(f32[6,6,128]{2,1,0:T(8,128)} %stiff_ref.1) | copy-start | bytes 55300
  2.5 3.5 %copy-start.5 = (f32[6,6,128]{2,1,0:T(8,128)S(1)}, f32[6,6,128]{2,1,0:T(8,128)}, u32[]{:S(2)}) copy-start(f32[6,6,128]{2,1,0:T(8,128)} %twist_ref.1) | copy-start | bytes 55300
  2.8 3.2 %copy-start.7 = (s32[6,128]{1,0:T(8,128)S(1)}, s32[6,128]{1,0:T(8,128)}, u32[]{:S(2)}) copy-start(s32[6,128]{1,0:T(8,128)} %conn_ref.3) | copy-start | bytes 9220
  2.9 8.1 %collective-permute-start = (f32[6,32,256]{2,1,0:T(8,128)S(1)}, f32[6,32,256]{2,1,0:T(8,128)S(1)}, u32[]{:S(2)}, u32[]{:S(2)}) collective-permute-start(f32[6,32,256]{2,1,0:T(8,128)S(1)} %get-tuple-element.40), channel_id=1, source_target_pairs={{1,2},{2,1},{3,4},{4,3},{5,6},{6,5},{7,8},{8,7},{9,10},{10,9},{11,... | collective-permute-start | bytes 589832 | tf_op jit(solution)/shard_map/ppermute | solution.py:536
  5.9 0.7 %copy-start.8 = (s32[2,32]{1,0:T(2,128)S(1)}, s32[2,32]{1,0:T(2,128)}, u32[]{:S(2)}) copy-start(s32[2,32]{1,0:T(2,128)} %lists_ref.1) | copy-start | bytes 772
  5.9 0.7 %copy-start.9 = (f32[128]{0:T(128)S(1)}, f32[128]{0:T(128)}, u32[]{:S(2)}) copy-start(f32[128]{0:T(128)} %param.17) | copy-start | bytes 1540
  5.9 5.1 %collective-permute-start.1 = (f32[6,32,256]{2,1,0:T(8,128)S(1)}, f32[6,32,256]{2,1,0:T(8,128)S(1)}, u32[]{:S(2)}, u32[]{:S(2)}) collective-permute-start(f32[6,32,256]{2,1,0:T(8,128)S(1)} %get-tuple-element.41), channel_id=1, source_target_pairs={{0,1},{1,0},{2,3},{3,2},{4,5},{5,4},{6,7},{7,6},{8,9},{9,8},{10,11... | collective-permute-start | bytes 589832 | tf_op jit(solution)/shard_map/ppermute | solution.py:533
  6.5 1.8 %copy-start.2 = (f32[8,256]{1,0:T(8,128)S(1)}, f32[8,256]{1,0:T(8,128)}, u32[]{:S(2)}) copy-start(f32[8,256]{1,0:T(8,128)} %constant.35.clone.squares_ref) | copy-start | bytes 24580
  6.5 1.8 %copy-start.10 = (bf16[1024,256]{1,0:T(8,128)(2,1)S(1)}, bf16[1024,256]{1,0:T(8,128)(2,1)}, u32[]{:S(2)}) copy-start(bf16[1024,256]{1,0:T(8,128)(2,1)} %constant.33.clone.coefs_ref) | copy-start | bytes 1572868
  6.5 1.8 %copy-start.11 = (bf16[512,512]{1,0:T(8,128)(2,1)S(1)}, bf16[512,512]{1,0:T(8,128)(2,1)}, u32[]{:S(2)}) copy-start(bf16[512,512]{1,0:T(8,128)(2,1)} %constant.32.clone.planes_ref) | copy-start | bytes 1572868
  6.5 1.8 %copy-start.12 = (f32[8,512]{1,0:T(8,128)S(1)}, f32[8,512]{1,0:T(8,128)}, u32[]{:S(2)}) copy-start(f32[8,512]{1,0:T(8,128)} %constant.34.clone.rotation_ref) | copy-start | bytes 49156
  12.5 5.9 %collective-permute-start.2 = (f32[6,32,256]{2,1,0:T(8,128)S(1)}, f32[6,32,256]{2,1,0:T(8,128)S(1)}, u32[]{:S(2)}, u32[]{:S(2)}) collective-permute-start(f32[6,32,256]{2,1,0:T(8,128)S(1)} %get-tuple-element.48), channel_id=1, source_target_pairs={{1,2},{2,1},{3,4},{4,3},{5,6},{6,5},{7,8},{8,7},{9,10},{10,9},{11,... | collective-permute-start | bytes 589832 | tf_op jit(solution)/shard_map/ppermute | solution.py:536
  13.5 4.9 %collective-permute-start.3 = (f32[6,32,256]{2,1,0:T(8,128)S(1)}, f32[6,32,256]{2,1,0:T(8,128)S(1)}, u32[]{:S(2)}, u32[]{:S(2)}) collective-permute-start(f32[6,32,256]{2,1,0:T(8,128)S(1)} %get-tuple-element.49), channel_id=1, source_target_pairs={{0,1},{1,0},{2,3},{3,2},{4,5},{5,4},{6,7},{7,6},{8,9},{9,8},{10,11... | collective-permute-start | bytes 589832 | tf_op jit(solution)/shard_map/ppermute | solution.py:533
  18.7 2.6 %collective-permute-start.4 = (f32[6,32,256]{2,1,0:T(8,128)S(1)}, f32[6,32,256]{2,1,0:T(8,128)S(1)}, u32[]{:S(2)}, u32[]{:S(2)}) collective-permute-start(f32[6,32,256]{2,1,0:T(8,128)S(1)} %get-tuple-element.55), channel_id=1, source_target_pairs={{0,1},{1,0},{2,3},{3,2},{4,5},{5,4},{6,7},{7,6},{8,9},{9,8},{10,11... | collective-permute-start | bytes 589832 | tf_op jit(solution)/shard_map/ppermute | solution.py:533
  19.8 5.7 %collective-permute-start.6 = (f32[6,32,256]{2,1,0:T(8,128)S(1)}, f32[6,32,256]{2,1,0:T(8,128)S(1)}, u32[]{:S(2)}, u32[]{:S(2)}) collective-permute-start(f32[6,32,256]{2,1,0:T(8,128)S(1)} %get-tuple-element.62), channel_id=1, source_target_pairs={{1,2},{2,1},{3,4},{4,3},{5,6},{6,5},{7,8},{8,7},{9,10},{10,9},{11,... | collective-permute-start | bytes 589832 | tf_op jit(solution)/shard_map/ppermute | solution.py:536
  23.5 6.3 %collective-permute-start.5 = (f32[6,32,256]{2,1,0:T(8,128)S(1)}, f32[6,32,256]{2,1,0:T(8,128)S(1)}, u32[]{:S(2)}, u32[]{:S(2)}) collective-permute-start(f32[6,32,256]{2,1,0:T(8,128)S(1)} %get-tuple-element.60), channel_id=1, source_target_pairs={{31,15},{15,31},{16,0},{0,16},{30,29},{29,30},{28,27},{27,28},{26,... | collective-permute-start | bytes 589832 | tf_op jit(solution)/shard_map/ppermute | solution.py:546
  26.0 3.8 %collective-permute-start.7 = (f32[6,32,256]{2,1,0:T(8,128)S(1)}, f32[6,32,256]{2,1,0:T(8,128)S(1)}, u32[]{:S(2)}, u32[]{:S(2)}) collective-permute-start(f32[6,32,256]{2,1,0:T(8,128)S(1)} %get-tuple-element.65), channel_id=1, source_target_pairs={{0,1},{1,0},{2,3},{3,2},{4,5},{5,4},{6,7},{7,6},{8,9},{9,8},{10,11... | collective-permute-start | bytes 589832 | tf_op jit(solution)/shard_map/ppermute | solution.py:533
  28.5 1.3 %collective-permute-start.8 = (f32[40,256]{1,0:T(8,128)S(1)}, f32[40,256]{1,0:T(8,128)S(1)}, u32[]{:S(2)}, u32[]{:S(2)}) collective-permute-start(f32[40,256]{1,0:T(8,128)S(1)} %get-tuple-element.71.moments), channel_id=1, source_target_pairs={{0,1},{1,0},{2,3},{3,2},{4,5},{5,4},{6,7},{7,6},{8,9},{9,8},{10,11... | collective-permute-start | bytes 122888 | tf_op jit(solution)/shard_map/ppermute | solution.py:533
  29.9 7.1 %collective-permute-start.12 = (f32[40,256]{1,0:T(8,128)S(1)}, f32[40,256]{1,0:T(8,128)S(1)}, u32[]{:S(2)}, u32[]{:S(2)}) collective-permute-start(f32[40,256]{1,0:T(8,128)S(1)} %shard_map.142), channel_id=1, source_target_pairs={{0,14},{1,12},{2,15},{3,13},{4,10},{5,8},{6,11},{7,9},{8,6},{9,4},... | collective-permute-start | bytes 122888 | tf_op jit(solution)/shard_map/ppermute | solution.py:638
  34.7 5.7 %collective-permute-start.11 = (f32[40,256]{1,0:T(8,128)S(1)}, f32[40,256]{1,0:T(8,128)S(1)}, u32[]{:S(2)}, u32[]{:S(2)}) collective-permute-start(f32[40,256]{1,0:T(8,128)S(1)} %shard_map.142), channel_id=1, source_target_pairs={{0,10},{1,8},{2,11},{3,9},{4,14},{5,12},{6,15},{7,13},{8,2},{9,0},... | collective-permute-start | bytes 122888 | tf_op jit(solution)/shard_map/ppermute | solution.py:638
  35.9 4.6 %collective-permute-start.10 = (f32[40,256]{1,0:T(8,128)S(1)}, f32[40,256]{1,0:T(8,128)S(1)}, u32[]{:S(2)}, u32[]{:S(2)}) collective-permute-start(f32[40,256]{1,0:T(8,128)S(1)} %shard_map.142), channel_id=1, source_target_pairs={{0,6},{1,4},{2,7},{3,5},{4,2},{5,0},{6,3},{7,1},{8,14},{9,12},{10,... | collective-permute-start | bytes 122888 | tf_op jit(solution)/shard_map/ppermute | solution.py:638
  36.1 4.4 %collective-permute-start.9 = (f32[40,256]{1,0:T(8,128)S(1)}, f32[40,256]{1,0:T(8,128)S(1)}, u32[]{:S(2)}, u32[]{:S(2)}) collective-permute-start(f32[40,256]{1,0:T(8,128)S(1)} %shard_map.142), channel_id=1, source_target_pairs={{0,2},{1,0},{2,3},{3,1},{4,6},{5,4},{6,7},{7,5},{8,10},{9,8},{10,1... | collective-permute-start | bytes 122888 | tf_op jit(solution)/shard_map/ppermute | solution.py:638
  40.5 1.3 %collective-permute-start.13 = (f32[40,256]{1,0:T(8,128)S(1)}, f32[40,256]{1,0:T(8,128)S(1)}, u32[]{:S(2)}, u32[]{:S(2)}) collective-permute-start(f32[40,256]{1,0:T(8,128)S(1)} %add_add_fusion.moments), channel_id=1, source_target_pairs={{0,1},{1,0},{2,3},{3,2},{4,5},{5,4},{6,7},{7,6},{8,9},{9,8},{10,11... | collective-permute-start | bytes 122888 | tf_op jit(solution)/shard_map/ppermute | solution.py:533

commit v8 on v7

--- a/solution.py
+++ b/solution.py
@@ -241,8 +241,7 @@
     column = jnp.concatenate([one_hot(conn, 0, nodes), arrives.astype(bf16)], axis=0)
     z = z_ref[...]
     first, second = halves(z)
-    third = (z - first.astype(f32) - second.astype(f32)).astype(bf16)
-    dense = dot_nt(first, column) + dot_nt(second, column) + dot_nt(third, column)
+    dense = dot_nt(first, column) + dot_nt(second, column)
     dense_ref[...] = dense
     high, low = halves(dense)
     pairs = []
@@ -437,19 +436,23 @@
 def join_kernel(far_weight, near_weight, info, far, sent, near, back, moments, *rest):
     ghosts = near.shape[1]
     out = rest[-1]
+    half = out.shape[1]
     total = moments[...]
     for other in rest[:-1]:
         total = total + other[...]
-    out[...] = total
+    out[0:36] = total[:36, :half]
+    out[36:72] = total[:36, half:]
     for k in range(6):
         distant = jnp.where(info[3:4, :] > 0.0, far[k] + sent[k], 0.0)
         crossing = far_weight * jnp.sum(distant * back[k, ghosts:], axis=0, keepdims=True)
         crossing += near_weight * jnp.sum(near[k] * back[k, :ghosts], axis=0, keepdims=True)
-        out[30 + k : 31 + k, :] += crossing
+        out[30 + k : 31 + k, :] += crossing[:, :half]
+        out[66 + k : 67 + k, :] += crossing[:, half:]
 
 
 def finish_kernel(moments, other, velocity, magnetic, first, second, third, velocity_out, magnetic_out):
     total = moments[...] + other[...]
+    total = jnp.concatenate([total[:36], total[36:]], axis=1)
     m0, m1, m2, m3, m4, m5 = [total[6 * j : 6 * j + 6, :] for j in range(6)]
     scale = basis_scale
     alpha0 = m0 / (scale * m1 + epsilon)
@@ -627,7 +630,7 @@
     if count % 8 == 0 and count <= 16:
         joined = call(
             functools.partial(join_kernel, 2.0, 2.0),
-            shape(40, coefs),
+            shape(72, coefs // 2),
             [info, far_last, back1, near_last, back, moments, swap_near(moments)],
         )
         target = (2, 0, 3, 1)
@@ -640,7 +643,7 @@
         other = swap_near(half)
     else:
         joined = call(
-            functools.partial(join_kernel, 1.0, 1.0), shape(40, coefs), [info, far_last, back1, near_last, back, moments]
+            functools.partial(join_kernel, 1.0, 1.0), shape(72, coefs // 2), [info, far_last, back1, near_last, back, moments]
         )
         half = lax.psum(joined, "mesh")
         other = jnp.zeros_like(half)

time: 43.1 us -> 42.8 us (level)
  transfers between devices with their start and end apart: 14 -> 14, of which waited for: 4 -> 4; matrix products, arithmetic and copies ran while one was open for 0% -> 0% of each run, Pallas kernels for 27% -> 26%
where the time goes in v8:
time: 42.8 us; the launch traced here: 42.7 us
  starting transfers between devices  18.5 us (43%)
  Pallas kernels  15.2 us (36%)
  waiting for transfers between devices  6.35 us (15%)
  local copies, waits for them, and re-layouts  1.61 us (4%)
  between operations  0.88 us (2%)
    pallas_call x13, Pallas kernels, call(): pl.pallas_call(kernel, out_shape=outs, in_specs=[VMEM] * len(operands), o...  15.2 us
    ppermute x4, starting transfers between devices, local(): term = lax.ppermute(joined, 'mesh', pairs)  7.08 us
    ppermute x3, starting transfers between devices, swap_far(): return lax.ppermute(value, ('runs', 'mesh'), far_pairs)  5.58 us
    ppermute x6, starting transfers between devices, swap_near(): return lax.ppermute(value, 'mesh', near_pairs)  4.7 us
    ppermute x4, waiting for transfers between devices, local(): term = lax.ppermute(joined, 'mesh', pairs)  3.27 us
    ppermute x6, waiting for transfers between devices, swap_near(): return lax.ppermute(value, 'mesh', near_pairs)  2.24 us
    unnamed x26, local copies, waits for them, and re-layouts  1.61 us
    ppermute x1, starting transfers between devices, swap_far_beside(): return lax.ppermute(value, ('runs', 'mesh'), far_pairs[::-1])  1.13 us
  transfers between devices with their start and end apart: 14, of which 4 were waited for; matrix products, arithmetic and copies ran while one was open for 0% of the time, Pallas kernels for 26%

profile of v8, /device:TPU:0, one launch (start us, length us, event | category | flops | bytes accessed | tf_op | source)
XLA Modules:
  0.0 42.7 jit_solution(8055625287842838779)
XLA Ops:
  0.6 0.0 copy-start.1
  0.7 0.1 select_convert_fusion.info
  0.8 0.0 copy-start.6
  0.8 0.7 %copy-done.6 = s32[6,128]{1,0:T(8,128)S(1)} copy-done((s32[6,128]{1,0:T(8,128)S(1)}, s32[6,128]{1,0:T(8,128)}, u32[]{:S(2)}) %copy-start.6) | copy-done | bytes 3096
  1.5 0.0 copy-start
  1.5 0.3 shard_map.131.pick_ref
  1.8 0.0 copy-done.1
  1.8 0.3 shard_map.132
  2.1 0.4 copy-done
  2.5 0.0 copy-start.3
  2.5 0.0 copy-start.4
  2.5 0.0 copy-start.5
  2.5 0.3 shard_map.133
  2.8 0.0 copy-start.7
  2.9 3.0 %collective-permute-start = (f32[6,32,256]{2,1,0:T(8,128)S(1)}, f32[6,32,256]{2,1,0:T(8,128)S(1)}, u32[]{:S(2)}, u32[]{:S(2)}) collective-permute-start(f32[6,32,256]{2,1,0:T(8,128)S(1)} %get-tuple-element.40), channel_id=1, source_target_pairs={{1,2},{2,1},{3,4},{4,3},{5,6},{6,5},{7,8},{8,7},{9,10},{10,9},{11,... | collective-permute-start | bytes 589832 | tf_op jit(solution)/shard_map/ppermute | solution.py:539
  5.9 0.0 copy-start.8
  5.9 0.1 collective-permute-start.1
  6.0 0.0 copy-done.3
  6.0 0.0 copy-done.4
  6.0 0.0 copy-done.5
  6.0 0.0 copy-done.7
  6.0 0.5 %copy-done.8 = s32[2,32]{1,0:T(2,128)S(1)} copy-done((s32[2,32]{1,0:T(2,128)S(1)}, s32[2,32]{1,0:T(2,128)}, u32[]{:S(2)}) %copy-start.8) | copy-done | bytes 280
  6.5 0.0 copy-done.9
  6.5 0.0 copy-start.12
  6.6 1.6 %shard_map.134 = (f32[640,192]{1,0:T(8,128)S(1)}, bf16[64,384]{1,0:T(8,128)(2,1)S(1)}, bf16[2,128,384]{2,1,0:T(8,128)(2,1)S(1)}, bf16[64,192]{1,0:T(8,128)(2,1)S(1)}, bf16[2,128,192]{2,1,0:T(8,128)(2,1)S(1)}) custom-call(f32[8,256]{1,0:T(8,128)S(1)} %select_convert_fusion.info, bf16[64,128]{1,0:T(8,128)(2,1)S(1)} %shard_map.131.pick_ref, ...), custom_call_target="tpu_custom_call" | custom-call | flops 1000000000 | bytes 943872 | tf_op jit(solution)/shard_map/pallas_call | solution.py:491
  8.1 0.0 copy-done.2
  8.1 0.0 copy-done.10
  8.1 0.0 copy-done.11
  8.1 0.0 copy-done.12
  8.2 2.6 %shard_map.135 = (f32[6,128,256]{2,1,0:T(8,128)S(1)}, f32[6,64,256]{2,1,0:T(8,128)S(1)}) custom-call(f32[6,128,256]{2,1,0:T(8,128)S(1)} %get-tuple-element.42.state, bf16[512,512]{1,0:T(8,128)(2,1)S(1)} %copy-done.11, bf16[1024,256]{1,0:T(8,128)(2,1)S(1)} %copy-done.10, f32[8,512]{1,0:T(8,128)S(1)} %copy-done.12, f32[8,256]{1,0:T(8,128)S(1)} %copy-done.2, ...), custom_call_target="tpu_custom_call" | custom-call | flops 2000000000 | bytes 3284992 | tf_op jit(solution)/shard_map/pallas_call | solution.py:491
  10.7 0.0 collective-permute-done.far
  10.7 0.0 collective-permute-done.1.near
  10.8 1.5 %shard_map.136 = (f32[6,32,256]{2,1,0:T(8,128)S(1)}, f32[6,32,256]{2,1,0:T(8,128)S(1)}, f32[6,64,256]{2,1,0:T(8,128)S(1)}) custom-call(f32[8,256]{1,0:T(8,128)S(1)} %select_convert_fusion.info, f32[6,32,256]{2,1,0:T(8,128)S(1)} %collective-permute-done.far, f32[6,32,256]{2,1,0:T(8,128)S(1)} %collective-permute-done.1.near, ...), custom_call_target="tpu_custom_call" | custom-call | flops 1000000000 | bytes 2777088 | tf_op jit(solution)/shard_map/pallas_call | solution.py:491
  12.2 1.1 %collective-permute-start.2 = (f32[6,32,256]{2,1,0:T(8,128)S(1)}, f32[6,32,256]{2,1,0:T(8,128)S(1)}, u32[]{:S(2)}, u32[]{:S(2)}) collective-permute-start(f32[6,32,256]{2,1,0:T(8,128)S(1)} %get-tuple-element.48), channel_id=1, source_target_pairs={{1,2},{2,1},{3,4},{4,3},{5,6},{6,5},{7,8},{8,7},{9,10},{10,9},{11,... | collective-permute-start | bytes 589832 | tf_op jit(solution)/shard_map/ppermute | solution.py:539
  13.3 1.4 %collective-permute-start.3 = (f32[6,32,256]{2,1,0:T(8,128)S(1)}, f32[6,32,256]{2,1,0:T(8,128)S(1)}, u32[]{:S(2)}, u32[]{:S(2)}) collective-permute-start(f32[6,32,256]{2,1,0:T(8,128)S(1)} %get-tuple-element.49), channel_id=1, source_target_pairs={{0,1},{1,0},{2,3},{3,2},{4,5},{5,4},{6,7},{7,6},{8,9},{9,8},{10,11... | collective-permute-start | bytes 589832 | tf_op jit(solution)/shard_map/ppermute | solution.py:536
  14.7 3.6 %shard_map.137 = (bf16[2,384,384]{2,1,0:T(8,128)(2,1)S(1)}, bf16[2,384,192]{2,1,0:T(8,128)(2,1)S(1)}, bf16[2,128,384]{2,1,0:T(8,128)(2,1)S(1)}, f32[6,128,256]{2...) custom-call(f32[8,256]{1,0:T(8,128)S(1)} %select_convert_fusion.info, ...), custom_call_target="tpu_custom_call" | custom-call | flops 2000000000 | bytes 5939200 | tf_op jit(solution)/shard_map/pallas_call | solution.py:491
  18.4 0.0 collective-permute-done.2.far
  18.4 0.0 collective-permute-done.3.near
  18.4 0.3 shard_map.138
  18.7 1.1 %collective-permute-start.4 = (f32[6,32,256]{2,1,0:T(8,128)S(1)}, f32[6,32,256]{2,1,0:T(8,128)S(1)}, u32[]{:S(2)}, u32[]{:S(2)}) collective-permute-start(f32[6,32,256]{2,1,0:T(8,128)S(1)} %get-tuple-element.55), channel_id=1, source_target_pairs={{0,1},{1,0},{2,3},{3,2},{4,5},{5,4},{6,7},{7,6},{8,9},{9,8},{10,11... | collective-permute-start | bytes 589832 | tf_op jit(solution)/shard_map/ppermute | solution.py:536
  19.8 1.5 %collective-permute-start.6 = (f32[6,32,256]{2,1,0:T(8,128)S(1)}, f32[6,32,256]{2,1,0:T(8,128)S(1)}, u32[]{:S(2)}, u32[]{:S(2)}) collective-permute-start(f32[6,32,256]{2,1,0:T(8,128)S(1)} %get-tuple-element.62), channel_id=1, source_target_pairs={{1,2},{2,1},{3,4},{4,3},{5,6},{6,5},{7,8},{8,7},{9,10},{10,9},{11,... | collective-permute-start | bytes 589832 | tf_op jit(solution)/shard_map/ppermute | solution.py:539
  21.3 0.0 collective-permute-done.4.near_next
  21.3 2.2 %shard_map.139 = (f32[6,128,256]{2,1,0:T(8,128)S(1)}, f32[6,32,256]{2,1,0:T(8,128)S(1)}, f32[6,32,256]{2,1,0:T(8,128)S(1)}, f32[6,128,256]{2,1,0:T(8,128)S(1)}, ...) custom-call(f32[8,256]{1,0:T(8,128)S(1)} %select_convert_fusion.info, f32[6,32,256]{2,1,0:T(8,128)S(1)} %collective-permute-done.2.far, ...), custom_call_target="tpu_custom_call" | custom-call | flops 1000000000 | bytes 5439488 | tf_op jit(solution)/shard_map/pallas_call | solution.py:491
  23.5 1.1 %collective-permute-start.5 = (f32[6,32,256]{2,1,0:T(8,128)S(1)}, f32[6,32,256]{2,1,0:T(8,128)S(1)}, u32[]{:S(2)}, u32[]{:S(2)}) collective-permute-start(f32[6,32,256]{2,1,0:T(8,128)S(1)} %get-tuple-element.60), channel_id=1, source_target_pairs={{31,15},{15,31},{16,0},{0,16},{30,29},{29,30},{28,27},{27,28},{26,... | collective-permute-start | bytes 589832 | tf_op jit(solution)/shard_map/ppermute | solution.py:549
  24.6 0.8 %collective-permute-done.6.far = f32[6,32,256]{2,1,0:T(8,128)S(1)} collective-permute-done((f32[6,32,256]{2,1,0:T(8,128)S(1)}, f32[6,32,256]{2,1,0:T(8,128)S(1)}, u32[]{:S(2)}, u32[]{:S(2)}) %collective-permute-start.6) | collective-permute-done | bytes 196640 | tf_op jit(solution)/shard_map/ppermute | solution.py:539
  25.5 0.5 %shard_map.140 = (f32[6,128,256]{2,1,0:T(8,128)S(1)}, f32[6,32,256]{2,1,0:T(8,128)S(1)}) custom-call(f32[8,256]{1,0:T(8,128)S(1)} %select_convert_fusion.info, f32[6,32,256]{2,1,0:T(8,128)S(1)} %collective-permute-done.6.far, f32[6,128,256]{2,1,0:T(8,128)S(1)} %get-tuple-element.63.image, f32[6,32,256]{2,1,0:T(8,128)S(1)} %get-tuple-element.64.packed_near, ...), custom_call_target="tpu_custom_call" | custom-call | flops 500000000 | bytes 2473984 | tf_op jit(solution)/shard_map/pallas_call | solution.py:491
  26.0 1.7 %collective-permute-start.7 = (f32[6,32,256]{2,1,0:T(8,128)S(1)}, f32[6,32,256]{2,1,0:T(8,128)S(1)}, u32[]{:S(2)}, u32[]{:S(2)}) collective-permute-start(f32[6,32,256]{2,1,0:T(8,128)S(1)} %get-tuple-element.65), channel_id=1, source_target_pairs={{0,1},{1,0},{2,3},{3,2},{4,5},{5,4},{6,7},{7,6},{8,9},{9,8},{10,11... | collective-permute-start | bytes 589832 | tf_op jit(solution)/shard_map/ppermute | solution.py:536
  27.6 0.8 %shard_map.141 = (f32[6,64,256]{2,1,0:T(8,128)S(1)}, f32[40,256]{1,0:T(8,128)S(1)}) custom-call(f32[6,128,256]{2,1,0:T(8,128)S(1)} %get-tuple-element.66.vector.third, f32[6,128,256]{2,1,0:T(8,128)S(1)} %get-tuple-element.67.before.second, bf16[2,384,384]{2,1,0:T(8,128)(2,1)S(1)} %get-tuple-element.58.own, ...), custom_call_target="tpu_custom_call" | custom-call | flops 1000000000 | bytes 2826240 | tf_op jit(solution)/shard_map/pallas_call | solution.py:491
  28.5 0.1 collective-permute-start.8
  28.6 1.2 %collective-permute-done.8.rest_0_ = f32[40,256]{1,0:T(8,128)S(1)} collective-permute-done((f32[40,256]{1,0:T(8,128)S(1)}, f32[40,256]{1,0:T(8,128)S(1)}, u32[]{:S(2)}, u32[]{:S(2)}) %collective-permute-start.8) | collective-permute-done | bytes 40992 | tf_op jit(solution)/shard_map/ppermute | solution.py:536
  29.8 0.0 collective-permute-done.5.far
  29.8 0.0 collective-permute-done.7.near
  29.8 0.1 shard_map.142
  29.9 4.8 %collective-permute-start.12 = (f32[72,128]{1,0:T(8,128)S(1)}, f32[72,128]{1,0:T(8,128)S(1)}, u32[]{:S(2)}, u32[]{:S(2)}) collective-permute-start(f32[72,128]{1,0:T(8,128)S(1)} %shard_map.142), channel_id=1, source_target_pairs={{0,14},{1,12},{2,15},{3,13},{4,10},{5,8},{6,11},{7,9},{8,6},{9,4},... | collective-permute-start | bytes 110600 | tf_op jit(solution)/shard_map/ppermute | solution.py:641
  34.7 1.2 %collective-permute-start.11 = (f32[72,128]{1,0:T(8,128)S(1)}, f32[72,128]{1,0:T(8,128)S(1)}, u32[]{:S(2)}, u32[]{:S(2)}) collective-permute-start(f32[72,128]{1,0:T(8,128)S(1)} %shard_map.142), channel_id=1, source_target_pairs={{0,10},{1,8},{2,11},{3,9},{4,14},{5,12},{6,15},{7,13},{8,2},{9,0},... | collective-permute-start | bytes 110600 | tf_op jit(solution)/shard_map/ppermute | solution.py:641
  35.9 0.2 collective-permute-start.10
  36.1 0.9 %collective-permute-start.9 = (f32[72,128]{1,0:T(8,128)S(1)}, f32[72,128]{1,0:T(8,128)S(1)}, u32[]{:S(2)}, u32[]{:S(2)}) collective-permute-start(f32[72,128]{1,0:T(8,128)S(1)} %shard_map.142), channel_id=1, source_target_pairs={{0,2},{1,0},{2,3},{3,1},{4,6},{5,4},{6,7},{7,5},{8,10},{9,8},{10,1... | collective-permute-start | bytes 110600 | tf_op jit(solution)/shard_map/ppermute | solution.py:641
  36.9 0.0 collective-permute-done.12
  36.9 3.3 %collective-permute-done.11 = f32[72,128]{1,0:T(8,128)S(1)} collective-permute-done((f32[72,128]{1,0:T(8,128)S(1)}, f32[72,128]{1,0:T(8,128)S(1)}, u32[]{:S(2)}, u32[]{:S(2)}) %collective-permute-start.11) | collective-permute-done | bytes 36896 | tf_op jit(solution)/shard_map/ppermute | solution.py:641
  40.2 0.0 collective-permute-done.10
  40.2 0.0 collective-permute-done.9
  40.2 0.3 collective-permute-start.13
  40.5 1.0 %collective-permute-done.13.other = f32[72,128]{1,0:T(8,128)S(1)} collective-permute-done((f32[72,128]{1,0:T(8,128)S(1)}, f32[72,128]{1,0:T(8,128)S(1)}, u32[]{:S(2)}, u32[]{:S(2)}) %collective-permute-start.13) | collective-permute-done | bytes 36896 | tf_op jit(solution)/shard_map/ppermute | solution.py:536
  41.5 1.2 %shard_map.143 = (f32[3,256,128]{2,1,0:T(8,128)}, f32[3,256,128]{2,1,0:T(8,128)}) custom-call(f32[72,128]{1,0:T(8,128)S(1)} %add_add_fusion.moments, f32[72,128]{1,0:T(8,128)S(1)} %collective-permute-done.13.other, f32[3,256,128]{2,1,0:T(8,128)S(1)} %copy-done.1, f32[3,256,128]{2,1,0:T(8,128)S(1)} %copy-done, ...), custom_call_target="tpu_custom_call" | custom-call | flops 10000000 | bytes 4005888 | tf_op jit(solution)/shard_map/pallas_call | solution.py:491
  (7 shorter events, 0.0 us)
Async XLA Ops:
  0.6 1.2 %copy-start.1 = (f32[3,256,128]{2,1,0:T(8,128)S(1)}, f32[3,256,128]{2,1,0:T(8,128)}, u32[]{:S(2)}) copy-start(f32[3,256,128]{2,1,0:T(8,128)} %velocity.3) | copy-start | bytes 1179652
  0.8 0.7 %copy-start.6 = (s32[6,128]{1,0:T(8,128)S(1)}, s32[6,128]{1,0:T(8,128)}, u32[]{:S(2)}) copy-start(s32[6,128]{1,0:T(8,128)} %conn_ref.3) | copy-start | bytes 9220
  1.5 1.0 %copy-start = (f32[3,256,128]{2,1,0:T(8,128)S(1)}, f32[3,256,128]{2,1,0:T(8,128)}, u32[]{:S(2)}) copy-start(f32[3,256,128]{2,1,0:T(8,128)} %magnetic.3) | copy-start | bytes 1179652
  2.5 3.5 %copy-start.3 = (f32[6,6,128]{2,1,0:T(8,128)S(1)}, f32[6,6,128]{2,1,0:T(8,128)}, u32[]{:S(2)}) copy-start(f32[6,6,128]{2,1,0:T(8,128)} %mass_ref.1) | copy-start | bytes 55300
  2.5 3.5 %copy-start.4 = (f32[6,6,128]{2,1,0:T(8,128)S(1)}, f32[6,6,128]{2,1,0:T(8,128)}, u32[]{:S(2)}) copy-start(f32[6,6,128]{2,1,0:T(8,128)} %stiff_ref.1) | copy-start | bytes 55300
  2.5 3.5 %copy-start.5 = (f32[6,6,128]{2,1,0:T(8,128)S(1)}, f32[6,6,128]{2,1,0:T(8,128)}, u32[]{:S(2)}) copy-start(f32[6,6,128]{2,1,0:T(8,128)} %twist_ref.1) | copy-start | bytes 55300
  2.8 3.2 %copy-start.7 = (s32[6,128]{1,0:T(8,128)S(1)}, s32[6,128]{1,0:T(8,128)}, u32[]{:S(2)}) copy-start(s32[6,128]{1,0:T(8,128)} %conn_ref.3) | copy-start | bytes 9220
  2.9 7.9 %collective-permute-start = (f32[6,32,256]{2,1,0:T(8,128)S(1)}, f32[6,32,256]{2,1,0:T(8,128)S(1)}, u32[]{:S(2)}, u32[]{:S(2)}) collective-permute-start(f32[6,32,256]{2,1,0:T(8,128)S(1)} %get-tuple-element.40), channel_id=1, source_target_pairs={{1,2},{2,1},{3,4},{4,3},{5,6},{6,5},{7,8},{8,7},{9,10},{10,9},{11,... | collective-permute-start | bytes 589832 | tf_op jit(solution)/shard_map/ppermute | solution.py:539
  5.9 0.7 %copy-start.8 = (s32[2,32]{1,0:T(2,128)S(1)}, s32[2,32]{1,0:T(2,128)}, u32[]{:S(2)}) copy-start(s32[2,32]{1,0:T(2,128)} %lists_ref.1) | copy-start | bytes 772
  5.9 0.7 %copy-start.9 = (f32[128]{0:T(128)S(1)}, f32[128]{0:T(128)}, u32[]{:S(2)}) copy-start(f32[128]{0:T(128)} %param.17) | copy-start | bytes 1540
  5.9 4.9 %collective-permute-start.1 = (f32[6,32,256]{2,1,0:T(8,128)S(1)}, f32[6,32,256]{2,1,0:T(8,128)S(1)}, u32[]{:S(2)}, u32[]{:S(2)}) collective-permute-start(f32[6,32,256]{2,1,0:T(8,128)S(1)} %get-tuple-element.41), channel_id=1, source_target_pairs={{0,1},{1,0},{2,3},{3,2},{4,5},{5,4},{6,7},{7,6},{8,9},{9,8},{10,11... | collective-permute-start | bytes 589832 | tf_op jit(solution)/shard_map/ppermute | solution.py:536
  6.5 1.6 %copy-start.2 = (f32[8,256]{1,0:T(8,128)S(1)}, f32[8,256]{1,0:T(8,128)}, u32[]{:S(2)}) copy-start(f32[8,256]{1,0:T(8,128)} %constant.35.clone.squares_ref) | copy-start | bytes 24580
  6.5 1.6 %copy-start.10 = (bf16[1024,256]{1,0:T(8,128)(2,1)S(1)}, bf16[1024,256]{1,0:T(8,128)(2,1)}, u32[]{:S(2)}) copy-start(bf16[1024,256]{1,0:T(8,128)(2,1)} %constant.33.clone.coefs_ref) | copy-start | bytes 1572868
  6.5 1.6 %copy-start.11 = (bf16[512,512]{1,0:T(8,128)(2,1)S(1)}, bf16[512,512]{1,0:T(8,128)(2,1)}, u32[]{:S(2)}) copy-start(bf16[512,512]{1,0:T(8,128)(2,1)} %constant.32.clone.planes_ref) | copy-start | bytes 1572868
  6.5 1.6 %copy-start.12 = (f32[8,512]{1,0:T(8,128)S(1)}, f32[8,512]{1,0:T(8,128)}, u32[]{:S(2)}) copy-start(f32[8,512]{1,0:T(8,128)} %constant.34.clone.rotation_ref) | copy-start | bytes 49156
  12.2 6.2 %collective-permute-start.2 = (f32[6,32,256]{2,1,0:T(8,128)S(1)}, f32[6,32,256]{2,1,0:T(8,128)S(1)}, u32[]{:S(2)}, u32[]{:S(2)}) collective-permute-start(f32[6,32,256]{2,1,0:T(8,128)S(1)} %get-tuple-element.48), channel_id=1, source_target_pairs={{1,2},{2,1},{3,4},{4,3},{5,6},{6,5},{7,8},{8,7},{9,10},{10,9},{11,... | collective-permute-start | bytes 589832 | tf_op jit(solution)/shard_map/ppermute | solution.py:539
  13.3 5.1 %collective-permute-start.3 = (f32[6,32,256]{2,1,0:T(8,128)S(1)}, f32[6,32,256]{2,1,0:T(8,128)S(1)}, u32[]{:S(2)}, u32[]{:S(2)}) collective-permute-start(f32[6,32,256]{2,1,0:T(8,128)S(1)} %get-tuple-element.49), channel_id=1, source_target_pairs={{0,1},{1,0},{2,3},{3,2},{4,5},{5,4},{6,7},{7,6},{8,9},{9,8},{10,11... | collective-permute-start | bytes 589832 | tf_op jit(solution)/shard_map/ppermute | solution.py:536
  18.7 2.6 %collective-permute-start.4 = (f32[6,32,256]{2,1,0:T(8,128)S(1)}, f32[6,32,256]{2,1,0:T(8,128)S(1)}, u32[]{:S(2)}, u32[]{:S(2)}) collective-permute-start(f32[6,32,256]{2,1,0:T(8,128)S(1)} %get-tuple-element.55), channel_id=1, source_target_pairs={{0,1},{1,0},{2,3},{3,2},{4,5},{5,4},{6,7},{7,6},{8,9},{9,8},{10,11... | collective-permute-start | bytes 589832 | tf_op jit(solution)/shard_map/ppermute | solution.py:536
  19.8 5.7 %collective-permute-start.6 = (f32[6,32,256]{2,1,0:T(8,128)S(1)}, f32[6,32,256]{2,1,0:T(8,128)S(1)}, u32[]{:S(2)}, u32[]{:S(2)}) collective-permute-start(f32[6,32,256]{2,1,0:T(8,128)S(1)} %get-tuple-element.62), channel_id=1, source_target_pairs={{1,2},{2,1},{3,4},{4,3},{5,6},{6,5},{7,8},{8,7},{9,10},{10,9},{11,... | collective-permute-start | bytes 589832 | tf_op jit(solution)/shard_map/ppermute | solution.py:539
  23.5 6.3 %collective-permute-start.5 = (f32[6,32,256]{2,1,0:T(8,128)S(1)}, f32[6,32,256]{2,1,0:T(8,128)S(1)}, u32[]{:S(2)}, u32[]{:S(2)}) collective-permute-start(f32[6,32,256]{2,1,0:T(8,128)S(1)} %get-tuple-element.60), channel_id=1, source_target_pairs={{31,15},{15,31},{16,0},{0,16},{30,29},{29,30},{28,27},{27,28},{26,... | collective-permute-start | bytes 589832 | tf_op jit(solution)/shard_map/ppermute | solution.py:549
  26.0 3.8 %collective-permute-start.7 = (f32[6,32,256]{2,1,0:T(8,128)S(1)}, f32[6,32,256]{2,1,0:T(8,128)S(1)}, u32[]{:S(2)}, u32[]{:S(2)}) collective-permute-start(f32[6,32,256]{2,1,0:T(8,128)S(1)} %get-tuple-element.65), channel_id=1, source_target_pairs={{0,1},{1,0},{2,3},{3,2},{4,5},{5,4},{6,7},{7,6},{8,9},{9,8},{10,11... | collective-permute-start | bytes 589832 | tf_op jit(solution)/shard_map/ppermute | solution.py:536
  28.5 1.3 %collective-permute-start.8 = (f32[40,256]{1,0:T(8,128)S(1)}, f32[40,256]{1,0:T(8,128)S(1)}, u32[]{:S(2)}, u32[]{:S(2)}) collective-permute-start(f32[40,256]{1,0:T(8,128)S(1)} %get-tuple-element.71.moments), channel_id=1, source_target_pairs={{0,1},{1,0},{2,3},{3,2},{4,5},{5,4},{6,7},{7,6},{8,9},{9,8},{10,11... | collective-permute-start | bytes 122888 | tf_op jit(solution)/shard_map/ppermute | solution.py:536
  29.9 7.1 %collective-permute-start.12 = (f32[72,128]{1,0:T(8,128)S(1)}, f32[72,128]{1,0:T(8,128)S(1)}, u32[]{:S(2)}, u32[]{:S(2)}) collective-permute-start(f32[72,128]{1,0:T(8,128)S(1)} %shard_map.142), channel_id=1, source_target_pairs={{0,14},{1,12},{2,15},{3,13},{4,10},{5,8},{6,11},{7,9},{8,6},{9,4},... | collective-permute-start | bytes 110600 | tf_op jit(solution)/shard_map/ppermute | solution.py:641
  34.7 5.5 %collective-permute-start.11 = (f32[72,128]{1,0:T(8,128)S(1)}, f32[72,128]{1,0:T(8,128)S(1)}, u32[]{:S(2)}, u32[]{:S(2)}) collective-permute-start(f32[72,128]{1,0:T(8,128)S(1)} %shard_map.142), channel_id=1, source_target_pairs={{0,10},{1,8},{2,11},{3,9},{4,14},{5,12},{6,15},{7,13},{8,2},{9,0},... | collective-permute-start | bytes 110600 | tf_op jit(solution)/shard_map/ppermute | solution.py:641
  35.9 4.3 %collective-permute-start.10 = (f32[72,128]{1,0:T(8,128)S(1)}, f32[72,128]{1,0:T(8,128)S(1)}, u32[]{:S(2)}, u32[]{:S(2)}) collective-permute-start(f32[72,128]{1,0:T(8,128)S(1)} %shard_map.142), channel_id=1, source_target_pairs={{0,6},{1,4},{2,7},{3,5},{4,2},{5,0},{6,3},{7,1},{8,14},{9,12},{10,... | collective-permute-start | bytes 110600 | tf_op jit(solution)/shard_map/ppermute | solution.py:641
  36.1 4.1 %collective-permute-start.9 = (f32[72,128]{1,0:T(8,128)S(1)}, f32[72,128]{1,0:T(8,128)S(1)}, u32[]{:S(2)}, u32[]{:S(2)}) collective-permute-start(f32[72,128]{1,0:T(8,128)S(1)} %shard_map.142), channel_id=1, source_target_pairs={{0,2},{1,0},{2,3},{3,1},{4,6},{5,4},{6,7},{7,5},{8,10},{9,8},{10,1... | collective-permute-start | bytes 110600 | tf_op jit(solution)/shard_map/ppermute | solution.py:641
  40.2 1.3 %collective-permute-start.13 = (f32[72,128]{1,0:T(8,128)S(1)}, f32[72,128]{1,0:T(8,128)S(1)}, u32[]{:S(2)}, u32[]{:S(2)}) collective-permute-start(f32[72,128]{1,0:T(8,128)S(1)} %add_add_fusion.moments), channel_id=1, source_target_pairs={{0,1},{1,0},{2,3},{3,2},{4,5},{5,4},{6,7},{7,6},{8,9},{9,8},{10,11... | collective-permute-start | bytes 110600 | tf_op jit(solution)/shard_map/ppermute | solution.py:536

commit v9 on v8

--- a/solution.py
+++ b/solution.py
@@ -17,6 +17,7 @@
 lorentz_factor = 0.005
 epsilon = 1e-06
 basis_scale = 512.0
+residual_scale = 2.0**-8
 
 f32 = jnp.float32
 bf16 = jnp.bfloat16
@@ -247,7 +248,7 @@
     pairs = []
     for g in range(5):
         rows = slice(g * nodes, (g + 1) * nodes)
-        factor = viscosity if g in (1, 2) else 1.0
+        factor = residual_scale * (viscosity if g in (1, 2) else 1.0)
         pairs.append([(factor * dot(pick, item[rows])).astype(bf16) for item in (high, low)])
 
     def own_part(pair):
@@ -324,12 +325,13 @@
     mass, stiff, twist, rate_stiff, rate_twist = [
         dense_ref[pl.ds(g * nodes, nodes), :] for g in range(5)
     ]
-    mass_op = stacked_columns(mass)
+    mass_op = stacked_columns(residual_scale * mass)
     rest_ops = []
     for f in range(2):
         still = viscosity * stiff if f == 0 else rate_stiff
         turn = viscosity * twist if f == 0 else rate_twist
-        rest_ops.append(jnp.concatenate([stacked_columns(still), stacked_columns(turn)], axis=0))
+        rest = [stacked_columns(residual_scale * item) for item in (still, turn)]
+        rest_ops.append(jnp.concatenate(rest, axis=0))
         image = (inverse_step * mass + still) * (1.0 / basis_scale)
         turn = turn * (1.0 / basis_scale)
         pairs = [halves(image), halves(turn)]
@@ -455,27 +457,30 @@
     total = jnp.concatenate([total[:36], total[36:]], axis=1)
     m0, m1, m2, m3, m4, m5 = [total[6 * j : 6 * j + 6, :] for j in range(6)]
     scale = basis_scale
-    alpha0 = m0 / (scale * m1 + epsilon)
+    small = epsilon * residual_scale * residual_scale
+    alpha0 = m0 / (scale * m1 + small)
     q1 = -alpha0 * scale
-    rr1 = m0 + 2.0 * q1 * m1 + q1 * q1 * m2
-    beta0 = rr1 / (m0 + epsilon)
+    rr1 = jnp.maximum(m0 + 2.0 * q1 * m1 + q1 * q1 * m2, 0.0)
+    beta0 = rr1 / (m0 + small)
     p0 = 1.0 + beta0
     p1 = q1
-    alpha1 = rr1 / (scale * (p0 * p0 * m1 + 2.0 * p0 * p1 * m2 + p1 * p1 * m3) + epsilon)
+    alpha1 = rr1 / (scale * (p0 * p0 * m1 + 2.0 * p0 * p1 * m2 + p1 * p1 * m3) + small)
     step1 = alpha1 * scale
     r1 = q1 - step1 * p0
     r2 = -step1 * p1
     rr2 = m0 + r1 * r1 * m2 + r2 * r2 * m4 + 2.0 * (r1 * m1 + r2 * m2 + r1 * r2 * m3)
-    beta1 = rr2 / (rr1 + epsilon)
+    rr2 = jnp.maximum(rr2, 0.0)
+    beta1 = rr2 / (rr1 + small)
     d0 = 1.0 + beta1 * p0
     d1 = r1 + beta1 * p1
     d2 = r2
     curve = d0 * d0 * m1 + d1 * d1 * m3 + d2 * d2 * m5
     curve = curve + 2.0 * (d0 * d1 * m2 + d0 * d2 * m3 + d1 * d2 * m4)
-    alpha2 = rr2 / (scale * curve + epsilon)
-    c0 = alpha0 + alpha1 * p0 + alpha2 * d0
-    c1 = alpha1 * p1 + alpha2 * d1
-    c2 = alpha2 * d2
+    alpha2 = rr2 / (scale * curve + small)
+    back = 1.0 / residual_scale
+    c0 = back * (alpha0 + alpha1 * p0 + alpha2 * d0)
+    c1 = back * (alpha1 * p1 + alpha2 * d1)
+    c2 = back * (alpha2 * d2)
     for k in range(6):
         source, out = (velocity, velocity_out) if k < 3 else (magnetic, magnetic_out)
         change = (

time: 42.8 us -> 42.8 us (level)
  no operation moved by 1% of the time
where the time goes in v9:
time: 42.8 us; the launch traced here: 42.7 us
  starting transfers between devices  18.5 us (43%)
  Pallas kernels  15.2 us (36%)
  waiting for transfers between devices  6.35 us (15%)
  local copies, waits for them, and re-layouts  1.61 us (4%)
  between operations  0.88 us (2%)
    pallas_call x13, Pallas kernels, call(): pl.pallas_call(kernel, out_shape=outs, in_specs=[VMEM] * len(operands), o...  15.2 us
    ppermute x4, starting transfers between devices, local(): term = lax.ppermute(joined, 'mesh', pairs)  7.08 us
    ppermute x3, starting transfers between devices, swap_far(): return lax.ppermute(value, ('runs', 'mesh'), far_pairs)  5.58 us
    ppermute x6, starting transfers between devices, swap_near(): return lax.ppermute(value, 'mesh', near_pairs)  4.7 us
    ppermute x4, waiting for transfers between devices, local(): term = lax.ppermute(joined, 'mesh', pairs)  3.27 us
    ppermute x6, waiting for transfers between devices, swap_near(): return lax.ppermute(value, 'mesh', near_pairs)  2.24 us
    unnamed x26, local copies, waits for them, and re-layouts  1.61 us
    ppermute x1, starting transfers between devices, swap_far_beside(): return lax.ppermute(value, ('runs', 'mesh'), far_pairs[::-1])  1.13 us
  transfers between devices with their start and end apart: 14, of which 4 were waited for; matrix products, arithmetic and copies ran while one was open for 0% of the time, Pallas kernels for 26%

profile of v9, /device:TPU:0, one launch (start us, length us, event | category | flops | bytes accessed | tf_op | source)
XLA Modules:
  0.0 42.7 jit_solution(662324781154099892)
XLA Ops:
  0.6 0.0 copy-start.1
  0.7 0.1 select_convert_fusion.info
  0.8 0.0 copy-start.6
  0.8 0.7 %copy-done.6 = s32[6,128]{1,0:T(8,128)S(1)} copy-done((s32[6,128]{1,0:T(8,128)S(1)}, s32[6,128]{1,0:T(8,128)}, u32[]{:S(2)}) %copy-start.6) | copy-done | bytes 3096
  1.5 0.0 copy-start
  1.5 0.3 shard_map.131.pick_ref
  1.8 0.0 copy-done.1
  1.8 0.3 shard_map.132
  2.1 0.4 copy-done
  2.5 0.0 copy-start.3
  2.5 0.0 copy-start.4
  2.5 0.0 copy-start.5
  2.5 0.3 shard_map.133
  2.8 0.0 copy-start.7
  2.9 3.0 %collective-permute-start = (f32[6,32,256]{2,1,0:T(8,128)S(1)}, f32[6,32,256]{2,1,0:T(8,128)S(1)}, u32[]{:S(2)}, u32[]{:S(2)}) collective-permute-start(f32[6,32,256]{2,1,0:T(8,128)S(1)} %get-tuple-element.40), channel_id=1, source_target_pairs={{1,2},{2,1},{3,4},{4,3},{5,6},{6,5},{7,8},{8,7},{9,10},{10,9},{11,... | collective-permute-start | bytes 589832 | tf_op jit(solution)/shard_map/ppermute | solution.py:544
  5.9 0.0 copy-start.8
  5.9 0.1 collective-permute-start.1
  6.0 0.0 copy-done.3
  6.0 0.0 copy-done.4
  6.0 0.0 copy-done.5
  6.0 0.0 copy-done.7
  6.0 0.5 %copy-done.8 = s32[2,32]{1,0:T(2,128)S(1)} copy-done((s32[2,32]{1,0:T(2,128)S(1)}, s32[2,32]{1,0:T(2,128)}, u32[]{:S(2)}) %copy-start.8) | copy-done | bytes 280
  6.5 0.0 copy-done.9
  6.5 0.0 copy-start.12
  6.6 1.6 %shard_map.134 = (f32[640,192]{1,0:T(8,128)S(1)}, bf16[64,384]{1,0:T(8,128)(2,1)S(1)}, bf16[2,128,384]{2,1,0:T(8,128)(2,1)S(1)}, bf16[64,192]{1,0:T(8,128)(2,1)S(1)}, bf16[2,128,192]{2,1,0:T(8,128)(2,1)S(1)}) custom-call(f32[8,256]{1,0:T(8,128)S(1)} %select_convert_fusion.info, bf16[64,128]{1,0:T(8,128)(2,1)S(1)} %shard_map.131.pick_ref, ...), custom_call_target="tpu_custom_call" | custom-call | flops 1000000000 | bytes 943872 | tf_op jit(solution)/shard_map/pallas_call | solution.py:496
  8.1 0.0 copy-done.2
  8.1 0.0 copy-done.10
  8.1 0.0 copy-done.11
  8.1 0.0 copy-done.12
  8.2 2.6 %shard_map.135 = (f32[6,128,256]{2,1,0:T(8,128)S(1)}, f32[6,64,256]{2,1,0:T(8,128)S(1)}) custom-call(f32[6,128,256]{2,1,0:T(8,128)S(1)} %get-tuple-element.42.state, bf16[512,512]{1,0:T(8,128)(2,1)S(1)} %copy-done.11, bf16[1024,256]{1,0:T(8,128)(2,1)S(1)} %copy-done.10, f32[8,512]{1,0:T(8,128)S(1)} %copy-done.12, f32[8,256]{1,0:T(8,128)S(1)} %copy-done.2, ...), custom_call_target="tpu_custom_call" | custom-call | flops 2000000000 | bytes 3284992 | tf_op jit(solution)/shard_map/pallas_call | solution.py:496
  10.7 0.0 collective-permute-done.far
  10.7 0.0 collective-permute-done.1.near
  10.8 1.5 %shard_map.136 = (f32[6,32,256]{2,1,0:T(8,128)S(1)}, f32[6,32,256]{2,1,0:T(8,128)S(1)}, f32[6,64,256]{2,1,0:T(8,128)S(1)}) custom-call(f32[8,256]{1,0:T(8,128)S(1)} %select_convert_fusion.info, f32[6,32,256]{2,1,0:T(8,128)S(1)} %collective-permute-done.far, f32[6,32,256]{2,1,0:T(8,128)S(1)} %collective-permute-done.1.near, ...), custom_call_target="tpu_custom_call" | custom-call | flops 1000000000 | bytes 2777088 | tf_op jit(solution)/shard_map/pallas_call | solution.py:496
  12.2 1.1 %collective-permute-start.2 = (f32[6,32,256]{2,1,0:T(8,128)S(1)}, f32[6,32,256]{2,1,0:T(8,128)S(1)}, u32[]{:S(2)}, u32[]{:S(2)}) collective-permute-start(f32[6,32,256]{2,1,0:T(8,128)S(1)} %get-tuple-element.48), channel_id=1, source_target_pairs={{1,2},{2,1},{3,4},{4,3},{5,6},{6,5},{7,8},{8,7},{9,10},{10,9},{11,... | collective-permute-start | bytes 589832 | tf_op jit(solution)/shard_map/ppermute | solution.py:544
  13.3 1.4 %collective-permute-start.3 = (f32[6,32,256]{2,1,0:T(8,128)S(1)}, f32[6,32,256]{2,1,0:T(8,128)S(1)}, u32[]{:S(2)}, u32[]{:S(2)}) collective-permute-start(f32[6,32,256]{2,1,0:T(8,128)S(1)} %get-tuple-element.49), channel_id=1, source_target_pairs={{0,1},{1,0},{2,3},{3,2},{4,5},{5,4},{6,7},{7,6},{8,9},{9,8},{10,11... | collective-permute-start | bytes 589832 | tf_op jit(solution)/shard_map/ppermute | solution.py:541
  14.7 3.6 %shard_map.137 = (bf16[2,384,384]{2,1,0:T(8,128)(2,1)S(1)}, bf16[2,384,192]{2,1,0:T(8,128)(2,1)S(1)}, bf16[2,128,384]{2,1,0:T(8,128)(2,1)S(1)}, f32[6,128,256]{2...) custom-call(f32[8,256]{1,0:T(8,128)S(1)} %select_convert_fusion.info, ...), custom_call_target="tpu_custom_call" | custom-call | flops 2000000000 | bytes 5939200 | tf_op jit(solution)/shard_map/pallas_call | solution.py:496
  18.4 0.0 collective-permute-done.2.far
  18.4 0.0 collective-permute-done.3.near
  18.4 0.3 shard_map.138
  18.7 1.1 %collective-permute-start.4 = (f32[6,32,256]{2,1,0:T(8,128)S(1)}, f32[6,32,256]{2,1,0:T(8,128)S(1)}, u32[]{:S(2)}, u32[]{:S(2)}) collective-permute-start(f32[6,32,256]{2,1,0:T(8,128)S(1)} %get-tuple-element.55), channel_id=1, source_target_pairs={{0,1},{1,0},{2,3},{3,2},{4,5},{5,4},{6,7},{7,6},{8,9},{9,8},{10,11... | collective-permute-start | bytes 589832 | tf_op jit(solution)/shard_map/ppermute | solution.py:541
  19.8 1.5 %collective-permute-start.6 = (f32[6,32,256]{2,1,0:T(8,128)S(1)}, f32[6,32,256]{2,1,0:T(8,128)S(1)}, u32[]{:S(2)}, u32[]{:S(2)}) collective-permute-start(f32[6,32,256]{2,1,0:T(8,128)S(1)} %get-tuple-element.62), channel_id=1, source_target_pairs={{1,2},{2,1},{3,4},{4,3},{5,6},{6,5},{7,8},{8,7},{9,10},{10,9},{11,... | collective-permute-start | bytes 589832 | tf_op jit(solution)/shard_map/ppermute | solution.py:544
  21.3 0.0 collective-permute-done.4.near_next
  21.3 2.2 %shard_map.139 = (f32[6,128,256]{2,1,0:T(8,128)S(1)}, f32[6,32,256]{2,1,0:T(8,128)S(1)}, f32[6,32,256]{2,1,0:T(8,128)S(1)}, f32[6,128,256]{2,1,0:T(8,128)S(1)}, ...) custom-call(f32[8,256]{1,0:T(8,128)S(1)} %select_convert_fusion.info, f32[6,32,256]{2,1,0:T(8,128)S(1)} %collective-permute-done.2.far, ...), custom_call_target="tpu_custom_call" | custom-call | flops 1000000000 | bytes 5439488 | tf_op jit(solution)/shard_map/pallas_call | solution.py:496
  23.5 1.1 %collective-permute-start.5 = (f32[6,32,256]{2,1,0:T(8,128)S(1)}, f32[6,32,256]{2,1,0:T(8,128)S(1)}, u32[]{:S(2)}, u32[]{:S(2)}) collective-permute-start(f32[6,32,256]{2,1,0:T(8,128)S(1)} %get-tuple-element.60), channel_id=1, source_target_pairs={{31,15},{15,31},{16,0},{0,16},{30,29},{29,30},{28,27},{27,28},{26,... | collective-permute-start | bytes 589832 | tf_op jit(solution)/shard_map/ppermute | solution.py:554
  24.6 0.8 %collective-permute-done.6.far = f32[6,32,256]{2,1,0:T(8,128)S(1)} collective-permute-done((f32[6,32,256]{2,1,0:T(8,128)S(1)}, f32[6,32,256]{2,1,0:T(8,128)S(1)}, u32[]{:S(2)}, u32[]{:S(2)}) %collective-permute-start.6) | collective-permute-done | bytes 196640 | tf_op jit(solution)/shard_map/ppermute | solution.py:544
  25.5 0.5 %shard_map.140 = (f32[6,128,256]{2,1,0:T(8,128)S(1)}, f32[6,32,256]{2,1,0:T(8,128)S(1)}) custom-call(f32[8,256]{1,0:T(8,128)S(1)} %select_convert_fusion.info, f32[6,32,256]{2,1,0:T(8,128)S(1)} %collective-permute-done.6.far, f32[6,128,256]{2,1,0:T(8,128)S(1)} %get-tuple-element.63.image, f32[6,32,256]{2,1,0:T(8,128)S(1)} %get-tuple-element.64.packed_near, ...), custom_call_target="tpu_custom_call" | custom-call | flops 500000000 | bytes 2473984 | tf_op jit(solution)/shard_map/pallas_call | solution.py:496
  26.0 1.7 %collective-permute-start.7 = (f32[6,32,256]{2,1,0:T(8,128)S(1)}, f32[6,32,256]{2,1,0:T(8,128)S(1)}, u32[]{:S(2)}, u32[]{:S(2)}) collective-permute-start(f32[6,32,256]{2,1,0:T(8,128)S(1)} %get-tuple-element.65), channel_id=1, source_target_pairs={{0,1},{1,0},{2,3},{3,2},{4,5},{5,4},{6,7},{7,6},{8,9},{9,8},{10,11... | collective-permute-start | bytes 589832 | tf_op jit(solution)/shard_map/ppermute | solution.py:541
  27.6 0.8 %shard_map.141 = (f32[6,64,256]{2,1,0:T(8,128)S(1)}, f32[40,256]{1,0:T(8,128)S(1)}) custom-call(f32[6,128,256]{2,1,0:T(8,128)S(1)} %get-tuple-element.66.vector.third, f32[6,128,256]{2,1,0:T(8,128)S(1)} %get-tuple-element.67.before.second, bf16[2,384,384]{2,1,0:T(8,128)(2,1)S(1)} %get-tuple-element.58.own, ...), custom_call_target="tpu_custom_call" | custom-call | flops 1000000000 | bytes 2826240 | tf_op jit(solution)/shard_map/pallas_call | solution.py:496
  28.5 0.1 collective-permute-start.8
  28.6 1.2 %collective-permute-done.8.rest_0_ = f32[40,256]{1,0:T(8,128)S(1)} collective-permute-done((f32[40,256]{1,0:T(8,128)S(1)}, f32[40,256]{1,0:T(8,128)S(1)}, u32[]{:S(2)}, u32[]{:S(2)}) %collective-permute-start.8) | collective-permute-done | bytes 40992 | tf_op jit(solution)/shard_map/ppermute | solution.py:541
  29.8 0.0 collective-permute-done.5.far
  29.8 0.0 collective-permute-done.7.near
  29.8 0.1 shard_map.142
  29.9 4.8 %collective-permute-start.12 = (f32[72,128]{1,0:T(8,128)S(1)}, f32[72,128]{1,0:T(8,128)S(1)}, u32[]{:S(2)}, u32[]{:S(2)}) collective-permute-start(f32[72,128]{1,0:T(8,128)S(1)} %shard_map.142), channel_id=1, source_target_pairs={{0,14},{1,12},{2,15},{3,13},{4,10},{5,8},{6,11},{7,9},{8,6},{9,4},... | collective-permute-start | bytes 110600 | tf_op jit(solution)/shard_map/ppermute | solution.py:646
  34.7 1.2 %collective-permute-start.11 = (f32[72,128]{1,0:T(8,128)S(1)}, f32[72,128]{1,0:T(8,128)S(1)}, u32[]{:S(2)}, u32[]{:S(2)}) collective-permute-start(f32[72,128]{1,0:T(8,128)S(1)} %shard_map.142), channel_id=1, source_target_pairs={{0,10},{1,8},{2,11},{3,9},{4,14},{5,12},{6,15},{7,13},{8,2},{9,0},... | collective-permute-start | bytes 110600 | tf_op jit(solution)/shard_map/ppermute | solution.py:646
  35.9 0.2 collective-permute-start.10
  36.1 0.9 %collective-permute-start.9 = (f32[72,128]{1,0:T(8,128)S(1)}, f32[72,128]{1,0:T(8,128)S(1)}, u32[]{:S(2)}, u32[]{:S(2)}) collective-permute-start(f32[72,128]{1,0:T(8,128)S(1)} %shard_map.142), channel_id=1, source_target_pairs={{0,2},{1,0},{2,3},{3,1},{4,6},{5,4},{6,7},{7,5},{8,10},{9,8},{10,1... | collective-permute-start | bytes 110600 | tf_op jit(solution)/shard_map/ppermute | solution.py:646
  36.9 0.0 collective-permute-done.12
  36.9 3.3 %collective-permute-done.11 = f32[72,128]{1,0:T(8,128)S(1)} collective-permute-done((f32[72,128]{1,0:T(8,128)S(1)}, f32[72,128]{1,0:T(8,128)S(1)}, u32[]{:S(2)}, u32[]{:S(2)}) %collective-permute-start.11) | collective-permute-done | bytes 36896 | tf_op jit(solution)/shard_map/ppermute | solution.py:646
  40.2 0.0 collective-permute-done.10
  40.2 0.0 collective-permute-done.9
  40.2 0.3 collective-permute-start.13
  40.5 1.0 %collective-permute-done.13.other = f32[72,128]{1,0:T(8,128)S(1)} collective-permute-done((f32[72,128]{1,0:T(8,128)S(1)}, f32[72,128]{1,0:T(8,128)S(1)}, u32[]{:S(2)}, u32[]{:S(2)}) %collective-permute-start.13) | collective-permute-done | bytes 36896 | tf_op jit(solution)/shard_map/ppermute | solution.py:541
  41.5 1.2 %shard_map.143 = (f32[3,256,128]{2,1,0:T(8,128)}, f32[3,256,128]{2,1,0:T(8,128)}) custom-call(f32[72,128]{1,0:T(8,128)S(1)} %add_add_fusion.moments, f32[72,128]{1,0:T(8,128)S(1)} %collective-permute-done.13.other, f32[3,256,128]{2,1,0:T(8,128)S(1)} %copy-done.1, f32[3,256,128]{2,1,0:T(8,128)S(1)} %copy-done, ...), custom_call_target="tpu_custom_call" | custom-call | flops 10000000 | bytes 4005888 | tf_op jit(solution)/shard_map/pallas_call | solution.py:496
  (7 shorter events, 0.0 us)
Async XLA Ops:
  0.6 1.2 %copy-start.1 = (f32[3,256,128]{2,1,0:T(8,128)S(1)}, f32[3,256,128]{2,1,0:T(8,128)}, u32[]{:S(2)}) copy-start(f32[3,256,128]{2,1,0:T(8,128)} %velocity.3) | copy-start | bytes 1179652
  0.8 0.7 %copy-start.6 = (s32[6,128]{1,0:T(8,128)S(1)}, s32[6,128]{1,0:T(8,128)}, u32[]{:S(2)}) copy-start(s32[6,128]{1,0:T(8,128)} %conn_ref.3) | copy-start | bytes 9220
  1.5 1.0 %copy-start = (f32[3,256,128]{2,1,0:T(8,128)S(1)}, f32[3,256,128]{2,1,0:T(8,128)}, u32[]{:S(2)}) copy-start(f32[3,256,128]{2,1,0:T(8,128)} %magnetic.3) | copy-start | bytes 1179652
  2.5 3.5 %copy-start.3 = (f32[6,6,128]{2,1,0:T(8,128)S(1)}, f32[6,6,128]{2,1,0:T(8,128)}, u32[]{:S(2)}) copy-start(f32[6,6,128]{2,1,0:T(8,128)} %mass_ref.1) | copy-start | bytes 55300
  2.5 3.5 %copy-start.4 = (f32[6,6,128]{2,1,0:T(8,128)S(1)}, f32[6,6,128]{2,1,0:T(8,128)}, u32[]{:S(2)}) copy-start(f32[6,6,128]{2,1,0:T(8,128)} %stiff_ref.1) | copy-start | bytes 55300
  2.5 3.5 %copy-start.5 = (f32[6,6,128]{2,1,0:T(8,128)S(1)}, f32[6,6,128]{2,1,0:T(8,128)}, u32[]{:S(2)}) copy-start(f32[6,6,128]{2,1,0:T(8,128)} %twist_ref.1) | copy-start | bytes 55300
  2.8 3.2 %copy-start.7 = (s32[6,128]{1,0:T(8,128)S(1)}, s32[6,128]{1,0:T(8,128)}, u32[]{:S(2)}) copy-start(s32[6,128]{1,0:T(8,128)} %conn_ref.3) | copy-start | bytes 9220
  2.9 7.9 %collective-permute-start = (f32[6,32,256]{2,1,0:T(8,128)S(1)}, f32[6,32,256]{2,1,0:T(8,128)S(1)}, u32[]{:S(2)}, u32[]{:S(2)}) collective-permute-start(f32[6,32,256]{2,1,0:T(8,128)S(1)} %get-tuple-element.40), channel_id=1, source_target_pairs={{1,2},{2,1},{3,4},{4,3},{5,6},{6,5},{7,8},{8,7},{9,10},{10,9},{11,... | collective-permute-start | bytes 589832 | tf_op jit(solution)/shard_map/ppermute | solution.py:544
  5.9 0.7 %copy-start.8 = (s32[2,32]{1,0:T(2,128)S(1)}, s32[2,32]{1,0:T(2,128)}, u32[]{:S(2)}) copy-start(s32[2,32]{1,0:T(2,128)} %lists_ref.1) | copy-start | bytes 772
  5.9 0.7 %copy-start.9 = (f32[128]{0:T(128)S(1)}, f32[128]{0:T(128)}, u32[]{:S(2)}) copy-start(f32[128]{0:T(128)} %param.17) | copy-start | bytes 1540
  5.9 4.9 %collective-permute-start.1 = (f32[6,32,256]{2,1,0:T(8,128)S(1)}, f32[6,32,256]{2,1,0:T(8,128)S(1)}, u32[]{:S(2)}, u32[]{:S(2)}) collective-permute-start(f32[6,32,256]{2,1,0:T(8,128)S(1)} %get-tuple-element.41), channel_id=1, source_target_pairs={{0,1},{1,0},{2,3},{3,2},{4,5},{5,4},{6,7},{7,6},{8,9},{9,8},{10,11... | collective-permute-start | bytes 589832 | tf_op jit(solution)/shard_map/ppermute | solution.py:541
  6.5 1.6 %copy-start.2 = (f32[8,256]{1,0:T(8,128)S(1)}, f32[8,256]{1,0:T(8,128)}, u32[]{:S(2)}) copy-start(f32[8,256]{1,0:T(8,128)} %constant.35.clone.squares_ref) | copy-start | bytes 24580
  6.5 1.6 %copy-start.10 = (bf16[1024,256]{1,0:T(8,128)(2,1)S(1)}, bf16[1024,256]{1,0:T(8,128)(2,1)}, u32[]{:S(2)}) copy-start(bf16[1024,256]{1,0:T(8,128)(2,1)} %constant.33.clone.coefs_ref) | copy-start | bytes 1572868
  6.5 1.6 %copy-start.11 = (bf16[512,512]{1,0:T(8,128)(2,1)S(1)}, bf16[512,512]{1,0:T(8,128)(2,1)}, u32[]{:S(2)}) copy-start(bf16[512,512]{1,0:T(8,128)(2,1)} %constant.32.clone.planes_ref) | copy-start | bytes 1572868
  6.5 1.6 %copy-start.12 = (f32[8,512]{1,0:T(8,128)S(1)}, f32[8,512]{1,0:T(8,128)}, u32[]{:S(2)}) copy-start(f32[8,512]{1,0:T(8,128)} %constant.34.clone.rotation_ref) | copy-start | bytes 49156
  12.2 6.2 %collective-permute-start.2 = (f32[6,32,256]{2,1,0:T(8,128)S(1)}, f32[6,32,256]{2,1,0:T(8,128)S(1)}, u32[]{:S(2)}, u32[]{:S(2)}) collective-permute-start(f32[6,32,256]{2,1,0:T(8,128)S(1)} %get-tuple-element.48), channel_id=1, source_target_pairs={{1,2},{2,1},{3,4},{4,3},{5,6},{6,5},{7,8},{8,7},{9,10},{10,9},{11,... | collective-permute-start | bytes 589832 | tf_op jit(solution)/shard_map/ppermute | solution.py:544
  13.3 5.1 %collective-permute-start.3 = (f32[6,32,256]{2,1,0:T(8,128)S(1)}, f32[6,32,256]{2,1,0:T(8,128)S(1)}, u32[]{:S(2)}, u32[]{:S(2)}) collective-permute-start(f32[6,32,256]{2,1,0:T(8,128)S(1)} %get-tuple-element.49), channel_id=1, source_target_pairs={{0,1},{1,0},{2,3},{3,2},{4,5},{5,4},{6,7},{7,6},{8,9},{9,8},{10,11... | collective-permute-start | bytes 589832 | tf_op jit(solution)/shard_map/ppermute | solution.py:541
  18.7 2.6 %collective-permute-start.4 = (f32[6,32,256]{2,1,0:T(8,128)S(1)}, f32[6,32,256]{2,1,0:T(8,128)S(1)}, u32[]{:S(2)}, u32[]{:S(2)}) collective-permute-start(f32[6,32,256]{2,1,0:T(8,128)S(1)} %get-tuple-element.55), channel_id=1, source_target_pairs={{0,1},{1,0},{2,3},{3,2},{4,5},{5,4},{6,7},{7,6},{8,9},{9,8},{10,11... | collective-permute-start | bytes 589832 | tf_op jit(solution)/shard_map/ppermute | solution.py:541
  19.8 5.7 %collective-permute-start.6 = (f32[6,32,256]{2,1,0:T(8,128)S(1)}, f32[6,32,256]{2,1,0:T(8,128)S(1)}, u32[]{:S(2)}, u32[]{:S(2)}) collective-permute-start(f32[6,32,256]{2,1,0:T(8,128)S(1)} %get-tuple-element.62), channel_id=1, source_target_pairs={{1,2},{2,1},{3,4},{4,3},{5,6},{6,5},{7,8},{8,7},{9,10},{10,9},{11,... | collective-permute-start | bytes 589832 | tf_op jit(solution)/shard_map/ppermute | solution.py:544
  23.5 6.3 %collective-permute-start.5 = (f32[6,32,256]{2,1,0:T(8,128)S(1)}, f32[6,32,256]{2,1,0:T(8,128)S(1)}, u32[]{:S(2)}, u32[]{:S(2)}) collective-permute-start(f32[6,32,256]{2,1,0:T(8,128)S(1)} %get-tuple-element.60), channel_id=1, source_target_pairs={{31,15},{15,31},{16,0},{0,16},{30,29},{29,30},{28,27},{27,28},{26,... | collective-permute-start | bytes 589832 | tf_op jit(solution)/shard_map/ppermute | solution.py:554
  26.0 3.8 %collective-permute-start.7 = (f32[6,32,256]{2,1,0:T(8,128)S(1)}, f32[6,32,256]{2,1,0:T(8,128)S(1)}, u32[]{:S(2)}, u32[]{:S(2)}) collective-permute-start(f32[6,32,256]{2,1,0:T(8,128)S(1)} %get-tuple-element.65), channel_id=1, source_target_pairs={{0,1},{1,0},{2,3},{3,2},{4,5},{5,4},{6,7},{7,6},{8,9},{9,8},{10,11... | collective-permute-start | bytes 589832 | tf_op jit(solution)/shard_map/ppermute | solution.py:541
  28.5 1.3 %collective-permute-start.8 = (f32[40,256]{1,0:T(8,128)S(1)}, f32[40,256]{1,0:T(8,128)S(1)}, u32[]{:S(2)}, u32[]{:S(2)}) collective-permute-start(f32[40,256]{1,0:T(8,128)S(1)} %get-tuple-element.71.moments), channel_id=1, source_target_pairs={{0,1},{1,0},{2,3},{3,2},{4,5},{5,4},{6,7},{7,6},{8,9},{9,8},{10,11... | collective-permute-start | bytes 122888 | tf_op jit(solution)/shard_map/ppermute | solution.py:541
  29.9 7.1 %collective-permute-start.12 = (f32[72,128]{1,0:T(8,128)S(1)}, f32[72,128]{1,0:T(8,128)S(1)}, u32[]{:S(2)}, u32[]{:S(2)}) collective-permute-start(f32[72,128]{1,0:T(8,128)S(1)} %shard_map.142), channel_id=1, source_target_pairs={{0,14},{1,12},{2,15},{3,13},{4,10},{5,8},{6,11},{7,9},{8,6},{9,4},... | collective-permute-start | bytes 110600 | tf_op jit(solution)/shard_map/ppermute | solution.py:646
  34.7 5.5 %collective-permute-start.11 = (f32[72,128]{1,0:T(8,128)S(1)}, f32[72,128]{1,0:T(8,128)S(1)}, u32[]{:S(2)}, u32[]{:S(2)}) collective-permute-start(f32[72,128]{1,0:T(8,128)S(1)} %shard_map.142), channel_id=1, source_target_pairs={{0,10},{1,8},{2,11},{3,9},{4,14},{5,12},{6,15},{7,13},{8,2},{9,0},... | collective-permute-start | bytes 110600 | tf_op jit(solution)/shard_map/ppermute | solution.py:646
  35.9 4.3 %collective-permute-start.10 = (f32[72,128]{1,0:T(8,128)S(1)}, f32[72,128]{1,0:T(8,128)S(1)}, u32[]{:S(2)}, u32[]{:S(2)}) collective-permute-start(f32[72,128]{1,0:T(8,128)S(1)} %shard_map.142), channel_id=1, source_target_pairs={{0,6},{1,4},{2,7},{3,5},{4,2},{5,0},{6,3},{7,1},{8,14},{9,12},{10,... | collective-permute-start | bytes 110600 | tf_op jit(solution)/shard_map/ppermute | solution.py:646
  36.1 4.1 %collective-permute-start.9 = (f32[72,128]{1,0:T(8,128)S(1)}, f32[72,128]{1,0:T(8,128)S(1)}, u32[]{:S(2)}, u32[]{:S(2)}) collective-permute-start(f32[72,128]{1,0:T(8,128)S(1)} %shard_map.142), channel_id=1, source_target_pairs={{0,2},{1,0},{2,3},{3,1},{4,6},{5,4},{6,7},{7,5},{8,10},{9,8},{10,1... | collective-permute-start | bytes 110600 | tf_op jit(solution)/shard_map/ppermute | solution.py:646
  40.2 1.3 %collective-permute-start.13 = (f32[72,128]{1,0:T(8,128)S(1)}, f32[72,128]{1,0:T(8,128)S(1)}, u32[]{:S(2)}, u32[]{:S(2)}) collective-permute-start(f32[72,128]{1,0:T(8,128)S(1)} %add_add_fusion.moments), channel_id=1, source_target_pairs={{0,1},{1,0},{2,3},{3,2},{4,5},{5,4},{6,7},{7,6},{8,9},{9,8},{10,11... | collective-permute-start | bytes 110600 | tf_op jit(solution)/shard_map/ppermute | solution.py:541

commit v10 on v9

--- a/solution.py
+++ b/solution.py
@@ -212,8 +212,8 @@
 
 
 def build_kernel(
-    info, pick_ref, mass_ref, stiff_ref, twist_ref, rates_ref, conn_ref, lists_ref,
-    dense_ref, mass_own_ref, rest_own_ref, mass_ghost_ref, rest_ghost_ref, z_ref,
+    info, pick_ref, mass_ref, stiff_ref, twist_ref, rates_ref, conn_ref, lists_ref, force, state, squares_ref,
+    dense_ref, mass_ghost_ref, rest_ghost_ref, packed_ref, z_ref,
 ):
     nodes = pick_ref.shape[1]
     elements = conn_ref.shape[1]
@@ -257,29 +257,24 @@
     def ghost_part(pair):
         return triple([item[:, nodes:] for item in pair])
 
-    mass_own_ref[...] = own_part(pairs[0])
+    mass_own = own_part(pairs[0])
+    rest_own = []
     mass_ghost_ref[...] = ghost_part(pairs[0])
     for f in range(2):
         used = (pairs[1], pairs[2]) if f == 0 else (pairs[3], pairs[4])
-        rest_own_ref[f] = jnp.concatenate([own_part(pair) for pair in used], axis=0)
+        rest_own.append(jnp.concatenate([own_part(pair) for pair in used], axis=0))
         rest_ghost_ref[f] = jnp.concatenate([ghost_part(pair) for pair in used], axis=0)
-
-
-def force_kernel(
-    state, planes_ref, coefs_ref, rotation_ref, squares_ref, mass_own, rest_own,
-    force_ref, packed_ref,
-):
-    nodes = state.shape[1]
-    count = packed_ref.shape[1]
-    value = state[...].reshape(6 * nodes, state.shape[2])
-    force_ref[...] = forcing(
-        value, nodes, planes_ref, coefs_ref, rotation_ref
-    ).reshape(force_ref.shape)
     square = squares_ref[0:1, :]
     for k in range(6):
-        from_force = dot(mass_own[...], stacked_rows(force_ref[k]))
+        from_force = dot(mass_own, stacked_rows(force[k]))
         from_state = dot(rest_own[k // 3], stacked_rows(state[k]))
         packed_ref[k] = from_force - (from_state[:count] + square * from_state[count:])
+
+
+def force_kernel(state, planes_ref, coefs_ref, rotation_ref, force_ref):
+    nodes = state.shape[1]
+    value = state[...].reshape(6 * nodes, state.shape[2])
+    force_ref[...] = forcing(value, nodes, planes_ref, coefs_ref, rotation_ref).reshape(force_ref.shape)
 
 
 def ghost_block(info, near, far, k):
@@ -570,24 +565,21 @@
         moved=1000,
     )
     near_state, far_state = exchange(near, far)
-    dense, mass_own, rest_own, mass_ghost, rest_ghost = call(
+    force = call(
+        force_kernel, whole, [state, plane_table, coef_table, rotation], flops=2_000_000_000
+    )
+    dense, mass_ghost, rest_ghost, packed = call(
         build_kernel,
         [
             shape(5 * nodes, nodes + both),
-            shape(both, 3 * nodes, dtype=bf16),
-            shape(2, 2 * both, 3 * nodes, dtype=bf16),
             shape(both, 3 * both, dtype=bf16),
             shape(2, 2 * both, 3 * both, dtype=bf16),
+            packs,
         ],
-        [info, pick, mass_blocks, stiff_blocks, twist_blocks, diffusivity.reshape(1, elements), conn, lists],
+        [info, pick, mass_blocks, stiff_blocks, twist_blocks, diffusivity.reshape(1, elements), conn, lists]
+        + [force, state, squares],
         scratch=[pltpu.VMEM((5 * nodes, 6 * elements), f32)],
         flops=1_000_000_000,
-    )
-    force, packed = call(
-        force_kernel,
-        [whole, packs],
-        [state, plane_table, coef_table, rotation, squares, mass_own, rest_own],
-        flops=2_000_000_000,
     )
     near, far, force_ghost = call(
         start_kernel,

time: 42.8 us -> 42.8 us (level)
  starting transfers between devices: 18.5 us -> 17.8 us
  Pallas kernels: 15.2 us -> 15.8 us
    ppermute x6, starting transfers between devices: 4.7 us -> 3.26 us  [swap_near(): return lax.ppermute(value, 'mesh', near_pairs)]
    pallas_call x13, Pallas kernels: 15.2 us -> 15.8 us  [call(): pl.pallas_call(kernel, out_shape=outs, in_specs=[VMEM] * len(operands), o...]
    ppermute x3, starting transfers between devices: 5.58 us -> 6.04 us  [swap_far(): return lax.ppermute(value, ('runs', 'mesh'), far_pairs)]
  transfers between devices with their start and end apart: 14 -> 14, of which waited for: 4 -> 5; matrix products, arithmetic and copies ran while one was open for 0% -> 0% of each run, Pallas kernels for 26% -> 28%
where the time goes in v10:
time: 42.8 us; the launch traced here: 42.6 us
  starting transfers between devices  17.8 us (42%)
  Pallas kernels  15.8 us (37%)
  waiting for transfers between devices  6.33 us (15%)
  local copies, waits for them, and re-layouts  1.71 us (4%)
  between operations  0.91 us (2%)
    pallas_call x13, Pallas kernels, call(): pl.pallas_call(kernel, out_shape=outs, in_specs=[VMEM] * len(operands), o...  15.8 us
    ppermute x4, starting transfers between devices, local(): term = lax.ppermute(joined, 'mesh', pairs)  7.39 us
    ppermute x3, starting transfers between devices, swap_far(): return lax.ppermute(value, ('runs', 'mesh'), far_pairs)  6.04 us
    ppermute x6, starting transfers between devices, swap_near(): return lax.ppermute(value, 'mesh', near_pairs)  3.26 us
    ppermute x4, waiting for transfers between devices, local(): term = lax.ppermute(joined, 'mesh', pairs)  2.96 us
    ppermute x6, waiting for transfers between devices, swap_near(): return lax.ppermute(value, 'mesh', near_pairs)  2.24 us
    unnamed x26, local copies, waits for them, and re-layouts  1.71 us
    ppermute x3, waiting for transfers between devices, swap_far(): return lax.ppermute(value, ('runs', 'mesh'), far_pairs)  1.13 us
  transfers between devices with their start and end apart: 14, of which 5 were waited for; matrix products, arithmetic and copies ran while one was open for 0% of the time, Pallas kernels for 28%

profile of v10, /device:TPU:0, one launch (start us, length us, event | category | flops | bytes accessed | tf_op | source)
XLA Modules:
  0.0 42.6 jit_solution(1893257736541726848)
XLA Ops:
  0.6 0.0 copy-start.1
  0.7 0.1 select_convert_fusion.info
  0.8 0.0 copy-start.6
  0.8 0.7 %copy-done.6 = s32[6,128]{1,0:T(8,128)S(1)} copy-done((s32[6,128]{1,0:T(8,128)S(1)}, s32[6,128]{1,0:T(8,128)}, u32[]{:S(2)}) %copy-start.6) | copy-done | bytes 3096
  1.5 0.0 copy-start
  1.5 0.3 shard_map.131.pick_ref
  1.8 0.0 copy-done.1
  1.8 0.3 shard_map.132
  2.1 0.4 copy-done
  2.5 0.3 shard_map.133
  2.8 3.0 %collective-permute-start = (f32[6,32,256]{2,1,0:T(8,128)S(1)}, f32[6,32,256]{2,1,0:T(8,128)S(1)}, u32[]{:S(2)}, u32[]{:S(2)}) collective-permute-start(f32[6,32,256]{2,1,0:T(8,128)S(1)} %get-tuple-element.37), channel_id=1, source_target_pairs={{1,2},{2,1},{3,4},{4,3},{5,6},{6,5},{7,8},{8,7},{9,10},{10,9},{11,... | collective-permute-start | bytes 589832 | tf_op jit(solution)/shard_map/ppermute | solution.py:539
  5.8 0.1 collective-permute-start.1
  6.0 0.0 copy-done.10
  6.0 0.0 copy-done.11
  6.0 0.0 copy-done.12
  6.0 0.0 copy-start.3
  6.0 0.0 copy-start.4
  6.0 0.0 copy-start.5
  6.0 0.0 copy-start.7
  6.1 2.2 %shard_map.134.force = f32[6,128,256]{2,1,0:T(8,128)S(1)} custom-call(f32[6,128,256]{2,1,0:T(8,128)S(1)} %get-tuple-element.39.state, bf16[512,512]{1,0:T(8,128)(2,1)S(1)} %copy-done.11, bf16[1024,256]{1,0:T(8,128)(2,1)S(1)} %copy-done.10, f32[8,512]{1,0:T(8,128)S(1)} %copy-done.12), custom_call_target="tpu_custom_call" | custom-call | flops 2000000000 | bytes 2637824 | tf_op jit(solution)/shard_map/pallas_call | solution.py:491
  8.2 0.0 copy-start.8
  8.2 0.0 copy-start.9
  8.3 0.0 copy-done.2
  8.3 0.0 copy-done.3
  8.3 0.0 copy-done.4
  8.3 0.0 copy-done.5
  8.3 0.0 copy-done.7
  8.3 0.6 %copy-done.8 = s32[2,32]{1,0:T(2,128)S(1)} copy-done((s32[2,32]{1,0:T(2,128)S(1)}, s32[2,32]{1,0:T(2,128)}, u32[]{:S(2)}) %copy-start.8) | copy-done | bytes 280
  8.9 0.0 copy-done.9
  8.9 2.5 %shard_map.135 = (f32[640,192]{1,0:T(8,128)S(1)}, bf16[64,192]{1,0:T(8,128)(2,1)S(1)}, bf16[2,128,192]{2,1,0:T(8,128)(2,1)S(1)}, f32[6,64,256]{2,1,0:T(8,128)S(1)}) custom-call(f32[8,256]{1,0:T(8,128)S(1)} %select_convert_fusion.info, bf16[64,128]{1,0:T(8,128)(2,1)S(1)} %shard_map.131.pick_ref, f32[6,6,128]{2,1,0:T(8,128)S(1)} %copy-done.3, ...), custom_call_target="tpu_custom_call" | custom-call | flops 1000000000 | bytes 2672384 | tf_op jit(solution)/shard_map/pallas_call | solution.py:491
  11.4 0.0 collective-permute-done.far
  11.4 0.0 collective-permute-done.1.near
  11.5 1.5 %shard_map.136 = (f32[6,32,256]{2,1,0:T(8,128)S(1)}, f32[6,32,256]{2,1,0:T(8,128)S(1)}, f32[6,64,256]{2,1,0:T(8,128)S(1)}) custom-call(f32[8,256]{1,0:T(8,128)S(1)} %select_convert_fusion.info, f32[6,32,256]{2,1,0:T(8,128)S(1)} %collective-permute-done.far, f32[6,32,256]{2,1,0:T(8,128)S(1)} %collective-permute-done.1.near, ...), custom_call_target="tpu_custom_call" | custom-call | flops 1000000000 | bytes 2777088 | tf_op jit(solution)/shard_map/pallas_call | solution.py:491
  12.9 1.6 %collective-permute-start.2 = (f32[6,32,256]{2,1,0:T(8,128)S(1)}, f32[6,32,256]{2,1,0:T(8,128)S(1)}, u32[]{:S(2)}, u32[]{:S(2)}) collective-permute-start(f32[6,32,256]{2,1,0:T(8,128)S(1)} %get-tuple-element.43), channel_id=1, source_target_pairs={{1,2},{2,1},{3,4},{4,3},{5,6},{6,5},{7,8},{8,7},{9,10},{10,9},{11,... | collective-permute-start | bytes 589832 | tf_op jit(solution)/shard_map/ppermute | solution.py:539
  14.5 0.2 collective-permute-start.3
  14.7 3.6 %shard_map.137 = (bf16[2,384,384]{2,1,0:T(8,128)(2,1)S(1)}, bf16[2,384,192]{2,1,0:T(8,128)(2,1)S(1)}, bf16[2,128,384]{2,1,0:T(8,128)(2,1)S(1)}, f32[6,128,256]{2...) custom-call(f32[8,256]{1,0:T(8,128)S(1)} %select_convert_fusion.info, ...), custom_call_target="tpu_custom_call" | custom-call | flops 2000000000 | bytes 5939200 | tf_op jit(solution)/shard_map/pallas_call | solution.py:491
  18.4 0.3 collective-permute-done.2.far
  18.7 0.0 collective-permute-done.3.near
  18.7 0.3 shard_map.138
  18.9 0.9 %collective-permute-start.4 = (f32[6,32,256]{2,1,0:T(8,128)S(1)}, f32[6,32,256]{2,1,0:T(8,128)S(1)}, u32[]{:S(2)}, u32[]{:S(2)}) collective-permute-start(f32[6,32,256]{2,1,0:T(8,128)S(1)} %get-tuple-element.49), channel_id=1, source_target_pairs={{0,1},{1,0},{2,3},{3,2},{4,5},{5,4},{6,7},{7,6},{8,9},{9,8},{10,11... | collective-permute-start | bytes 589832 | tf_op jit(solution)/shard_map/ppermute | solution.py:536
  19.8 1.5 %collective-permute-start.6 = (f32[6,32,256]{2,1,0:T(8,128)S(1)}, f32[6,32,256]{2,1,0:T(8,128)S(1)}, u32[]{:S(2)}, u32[]{:S(2)}) collective-permute-start(f32[6,32,256]{2,1,0:T(8,128)S(1)} %get-tuple-element.56), channel_id=1, source_target_pairs={{1,2},{2,1},{3,4},{4,3},{5,6},{6,5},{7,8},{8,7},{9,10},{10,9},{11,... | collective-permute-start | bytes 589832 | tf_op jit(solution)/shard_map/ppermute | solution.py:539
  21.3 0.0 collective-permute-done.4.near_next
  21.3 2.2 %shard_map.139 = (f32[6,128,256]{2,1,0:T(8,128)S(1)}, f32[6,32,256]{2,1,0:T(8,128)S(1)}, f32[6,32,256]{2,1,0:T(8,128)S(1)}, f32[6,128,256]{2,1,0:T(8,128)S(1)}, ...) custom-call(f32[8,256]{1,0:T(8,128)S(1)} %select_convert_fusion.info, f32[6,32,256]{2,1,0:T(8,128)S(1)} %collective-permute-done.2.far, ...), custom_call_target="tpu_custom_call" | custom-call | flops 1000000000 | bytes 5439488 | tf_op jit(solution)/shard_map/pallas_call | solution.py:491
  23.5 1.1 %collective-permute-start.5 = (f32[6,32,256]{2,1,0:T(8,128)S(1)}, f32[6,32,256]{2,1,0:T(8,128)S(1)}, u32[]{:S(2)}, u32[]{:S(2)}) collective-permute-start(f32[6,32,256]{2,1,0:T(8,128)S(1)} %get-tuple-element.54), channel_id=1, source_target_pairs={{31,15},{15,31},{16,0},{0,16},{30,29},{29,30},{28,27},{27,28},{26,... | collective-permute-start | bytes 589832 | tf_op jit(solution)/shard_map/ppermute | solution.py:549
  24.6 0.8 %collective-permute-done.6.far = f32[6,32,256]{2,1,0:T(8,128)S(1)} collective-permute-done((f32[6,32,256]{2,1,0:T(8,128)S(1)}, f32[6,32,256]{2,1,0:T(8,128)S(1)}, u32[]{:S(2)}, u32[]{:S(2)}) %collective-permute-start.6) | collective-permute-done | bytes 196640 | tf_op jit(solution)/shard_map/ppermute | solution.py:539
  25.5 0.5 %shard_map.140 = (f32[6,128,256]{2,1,0:T(8,128)S(1)}, f32[6,32,256]{2,1,0:T(8,128)S(1)}) custom-call(f32[8,256]{1,0:T(8,128)S(1)} %select_convert_fusion.info, f32[6,32,256]{2,1,0:T(8,128)S(1)} %collective-permute-done.6.far, f32[6,128,256]{2,1,0:T(8,128)S(1)} %get-tuple-element.57.image, f32[6,32,256]{2,1,0:T(8,128)S(1)} %get-tuple-element.58.packed_near, ...), custom_call_target="tpu_custom_call" | custom-call | flops 500000000 | bytes 2473984 | tf_op jit(solution)/shard_map/pallas_call | solution.py:491
  25.9 1.7 %collective-permute-start.7 = (f32[6,32,256]{2,1,0:T(8,128)S(1)}, f32[6,32,256]{2,1,0:T(8,128)S(1)}, u32[]{:S(2)}, u32[]{:S(2)}) collective-permute-start(f32[6,32,256]{2,1,0:T(8,128)S(1)} %get-tuple-element.59), channel_id=1, source_target_pairs={{0,1},{1,0},{2,3},{3,2},{4,5},{5,4},{6,7},{7,6},{8,9},{9,8},{10,11... | collective-permute-start | bytes 589832 | tf_op jit(solution)/shard_map/ppermute | solution.py:536
  27.6 0.8 %shard_map.141 = (f32[6,64,256]{2,1,0:T(8,128)S(1)}, f32[40,256]{1,0:T(8,128)S(1)}) custom-call(f32[6,128,256]{2,1,0:T(8,128)S(1)} %get-tuple-element.60.vector.third, f32[6,128,256]{2,1,0:T(8,128)S(1)} %get-tuple-element.61.before.second, bf16[2,384,384]{2,1,0:T(8,128)(2,1)S(1)} %get-tuple-element.52.own, ...), custom_call_target="tpu_custom_call" | custom-call | flops 1000000000 | bytes 2826240 | tf_op jit(solution)/shard_map/pallas_call | solution.py:491
  28.5 0.1 collective-permute-start.8
  28.5 1.2 %collective-permute-done.8.rest_0_ = f32[40,256]{1,0:T(8,128)S(1)} collective-permute-done((f32[40,256]{1,0:T(8,128)S(1)}, f32[40,256]{1,0:T(8,128)S(1)}, u32[]{:S(2)}, u32[]{:S(2)}) %collective-permute-start.8) | collective-permute-done | bytes 40992 | tf_op jit(solution)/shard_map/ppermute | solution.py:536
  29.7 0.0 collective-permute-done.5.far
  29.7 0.0 collective-permute-done.7.near
  29.8 0.1 shard_map.142
  29.8 5.1 %collective-permute-start.12 = (f32[72,128]{1,0:T(8,128)S(1)}, f32[72,128]{1,0:T(8,128)S(1)}, u32[]{:S(2)}, u32[]{:S(2)}) collective-permute-start(f32[72,128]{1,0:T(8,128)S(1)} %shard_map.142), channel_id=1, source_target_pairs={{0,14},{1,12},{2,15},{3,13},{4,10},{5,8},{6,11},{7,9},{8,6},{9,4},... | collective-permute-start | bytes 110600 | tf_op jit(solution)/shard_map/ppermute | solution.py:638
  35.0 0.9 %collective-permute-start.11 = (f32[72,128]{1,0:T(8,128)S(1)}, f32[72,128]{1,0:T(8,128)S(1)}, u32[]{:S(2)}, u32[]{:S(2)}) collective-permute-start(f32[72,128]{1,0:T(8,128)S(1)} %shard_map.142), channel_id=1, source_target_pairs={{0,10},{1,8},{2,11},{3,9},{4,14},{5,12},{6,15},{7,13},{8,2},{9,0},... | collective-permute-start | bytes 110600 | tf_op jit(solution)/shard_map/ppermute | solution.py:638
  35.9 0.1 collective-permute-start.10
  36.0 1.2 %collective-permute-start.9 = (f32[72,128]{1,0:T(8,128)S(1)}, f32[72,128]{1,0:T(8,128)S(1)}, u32[]{:S(2)}, u32[]{:S(2)}) collective-permute-start(f32[72,128]{1,0:T(8,128)S(1)} %shard_map.142), channel_id=1, source_target_pairs={{0,2},{1,0},{2,3},{3,1},{4,6},{5,4},{6,7},{7,5},{8,10},{9,8},{10,1... | collective-permute-start | bytes 110600 | tf_op jit(solution)/shard_map/ppermute | solution.py:638
  37.2 0.0 collective-permute-done.12
  37.2 3.0 %collective-permute-done.11 = f32[72,128]{1,0:T(8,128)S(1)} collective-permute-done((f32[72,128]{1,0:T(8,128)S(1)}, f32[72,128]{1,0:T(8,128)S(1)}, u32[]{:S(2)}, u32[]{:S(2)}) %collective-permute-start.11) | collective-permute-done | bytes 36896 | tf_op jit(solution)/shard_map/ppermute | solution.py:638
  40.2 0.0 collective-permute-done.10
  40.2 0.0 collective-permute-done.9
  40.2 0.3 collective-permute-start.13
  40.5 1.0 %collective-permute-done.13.other = f32[72,128]{1,0:T(8,128)S(1)} collective-permute-done((f32[72,128]{1,0:T(8,128)S(1)}, f32[72,128]{1,0:T(8,128)S(1)}, u32[]{:S(2)}, u32[]{:S(2)}) %collective-permute-start.13) | collective-permute-done | bytes 36896 | tf_op jit(solution)/shard_map/ppermute | solution.py:536
  41.5 1.2 %shard_map.143 = (f32[3,256,128]{2,1,0:T(8,128)}, f32[3,256,128]{2,1,0:T(8,128)}) custom-call(f32[72,128]{1,0:T(8,128)S(1)} %add_add_fusion.moments, f32[72,128]{1,0:T(8,128)S(1)} %collective-permute-done.13.other, f32[3,256,128]{2,1,0:T(8,128)S(1)} %copy-done.1, f32[3,256,128]{2,1,0:T(8,128)S(1)} %copy-done, ...), custom_call_target="tpu_custom_call" | custom-call | flops 10000000 | bytes 4005888 | tf_op jit(solution)/shard_map/pallas_call | solution.py:491
  (7 shorter events, 0.0 us)
Async XLA Ops:
  0.6 1.2 %copy-start.1 = (f32[3,256,128]{2,1,0:T(8,128)S(1)}, f32[3,256,128]{2,1,0:T(8,128)}, u32[]{:S(2)}) copy-start(f32[3,256,128]{2,1,0:T(8,128)} %velocity.3) | copy-start | bytes 1179652
  0.8 0.7 %copy-start.6 = (s32[6,128]{1,0:T(8,128)S(1)}, s32[6,128]{1,0:T(8,128)}, u32[]{:S(2)}) copy-start(s32[6,128]{1,0:T(8,128)} %conn_ref.3) | copy-start | bytes 9220
  1.5 1.0 %copy-start = (f32[3,256,128]{2,1,0:T(8,128)S(1)}, f32[3,256,128]{2,1,0:T(8,128)}, u32[]{:S(2)}) copy-start(f32[3,256,128]{2,1,0:T(8,128)} %magnetic.3) | copy-start | bytes 1179652
  2.5 3.5 %copy-start.10 = (bf16[1024,256]{1,0:T(8,128)(2,1)S(1)}, bf16[1024,256]{1,0:T(8,128)(2,1)}, u32[]{:S(2)}) copy-start(bf16[1024,256]{1,0:T(8,128)(2,1)} %constant.33.clone.coefs_ref) | copy-start | bytes 1572868
  2.5 3.5 %copy-start.11 = (bf16[512,512]{1,0:T(8,128)(2,1)S(1)}, bf16[512,512]{1,0:T(8,128)(2,1)}, u32[]{:S(2)}) copy-start(bf16[512,512]{1,0:T(8,128)(2,1)} %constant.32.clone.planes_ref) | copy-start | bytes 1572868
  2.5 3.5 %copy-start.12 = (f32[8,512]{1,0:T(8,128)S(1)}, f32[8,512]{1,0:T(8,128)}, u32[]{:S(2)}) copy-start(f32[8,512]{1,0:T(8,128)} %constant.34.clone.rotation_ref) | copy-start | bytes 49156
  2.8 8.6 %collective-permute-start = (f32[6,32,256]{2,1,0:T(8,128)S(1)}, f32[6,32,256]{2,1,0:T(8,128)S(1)}, u32[]{:S(2)}, u32[]{:S(2)}) collective-permute-start(f32[6,32,256]{2,1,0:T(8,128)S(1)} %get-tuple-element.37), channel_id=1, source_target_pairs={{1,2},{2,1},{3,4},{4,3},{5,6},{6,5},{7,8},{8,7},{9,10},{10,9},{11,... | collective-permute-start | bytes 589832 | tf_op jit(solution)/shard_map/ppermute | solution.py:539
  5.8 5.6 %collective-permute-start.1 = (f32[6,32,256]{2,1,0:T(8,128)S(1)}, f32[6,32,256]{2,1,0:T(8,128)S(1)}, u32[]{:S(2)}, u32[]{:S(2)}) collective-permute-start(f32[6,32,256]{2,1,0:T(8,128)S(1)} %get-tuple-element.38), channel_id=1, source_target_pairs={{0,1},{1,0},{2,3},{3,2},{4,5},{5,4},{6,7},{7,6},{8,9},{9,8},{10,11... | collective-permute-start | bytes 589832 | tf_op jit(solution)/shard_map/ppermute | solution.py:536
  6.0 2.3 %copy-start.2 = (f32[8,256]{1,0:T(8,128)S(1)}, f32[8,256]{1,0:T(8,128)}, u32[]{:S(2)}) copy-start(f32[8,256]{1,0:T(8,128)} %constant.35.clone.squares_ref) | copy-start | bytes 24580
  6.0 2.3 %copy-start.3 = (f32[6,6,128]{2,1,0:T(8,128)S(1)}, f32[6,6,128]{2,1,0:T(8,128)}, u32[]{:S(2)}) copy-start(f32[6,6,128]{2,1,0:T(8,128)} %mass_ref.1) | copy-start | bytes 55300
  6.0 2.3 %copy-start.4 = (f32[6,6,128]{2,1,0:T(8,128)S(1)}, f32[6,6,128]{2,1,0:T(8,128)}, u32[]{:S(2)}) copy-start(f32[6,6,128]{2,1,0:T(8,128)} %stiff_ref.1) | copy-start | bytes 55300
  6.0 2.3 %copy-start.5 = (f32[6,6,128]{2,1,0:T(8,128)S(1)}, f32[6,6,128]{2,1,0:T(8,128)}, u32[]{:S(2)}) copy-start(f32[6,6,128]{2,1,0:T(8,128)} %twist_ref.1) | copy-start | bytes 55300
  6.0 2.3 %copy-start.7 = (s32[6,128]{1,0:T(8,128)S(1)}, s32[6,128]{1,0:T(8,128)}, u32[]{:S(2)}) copy-start(s32[6,128]{1,0:T(8,128)} %conn_ref.3) | copy-start | bytes 9220
  8.2 0.7 %copy-start.8 = (s32[2,32]{1,0:T(2,128)S(1)}, s32[2,32]{1,0:T(2,128)}, u32[]{:S(2)}) copy-start(s32[2,32]{1,0:T(2,128)} %lists_ref.1) | copy-start | bytes 772
  8.2 0.7 %copy-start.9 = (f32[128]{0:T(128)S(1)}, f32[128]{0:T(128)}, u32[]{:S(2)}) copy-start(f32[128]{0:T(128)} %param.17) | copy-start | bytes 1540
  12.9 5.7 %collective-permute-start.2 = (f32[6,32,256]{2,1,0:T(8,128)S(1)}, f32[6,32,256]{2,1,0:T(8,128)S(1)}, u32[]{:S(2)}, u32[]{:S(2)}) collective-permute-start(f32[6,32,256]{2,1,0:T(8,128)S(1)} %get-tuple-element.43), channel_id=1, source_target_pairs={{1,2},{2,1},{3,4},{4,3},{5,6},{6,5},{7,8},{8,7},{9,10},{10,9},{11,... | collective-permute-start | bytes 589832 | tf_op jit(solution)/shard_map/ppermute | solution.py:539
  14.5 4.2 %collective-permute-start.3 = (f32[6,32,256]{2,1,0:T(8,128)S(1)}, f32[6,32,256]{2,1,0:T(8,128)S(1)}, u32[]{:S(2)}, u32[]{:S(2)}) collective-permute-start(f32[6,32,256]{2,1,0:T(8,128)S(1)} %get-tuple-element.44), channel_id=1, source_target_pairs={{0,1},{1,0},{2,3},{3,2},{4,5},{5,4},{6,7},{7,6},{8,9},{9,8},{10,11... | collective-permute-start | bytes 589832 | tf_op jit(solution)/shard_map/ppermute | solution.py:536
  18.9 2.3 %collective-permute-start.4 = (f32[6,32,256]{2,1,0:T(8,128)S(1)}, f32[6,32,256]{2,1,0:T(8,128)S(1)}, u32[]{:S(2)}, u32[]{:S(2)}) collective-permute-start(f32[6,32,256]{2,1,0:T(8,128)S(1)} %get-tuple-element.49), channel_id=1, source_target_pairs={{0,1},{1,0},{2,3},{3,2},{4,5},{5,4},{6,7},{7,6},{8,9},{9,8},{10,11... | collective-permute-start | bytes 589832 | tf_op jit(solution)/shard_map/ppermute | solution.py:536
  19.8 5.7 %collective-permute-start.6 = (f32[6,32,256]{2,1,0:T(8,128)S(1)}, f32[6,32,256]{2,1,0:T(8,128)S(1)}, u32[]{:S(2)}, u32[]{:S(2)}) collective-permute-start(f32[6,32,256]{2,1,0:T(8,128)S(1)} %get-tuple-element.56), channel_id=1, source_target_pairs={{1,2},{2,1},{3,4},{4,3},{5,6},{6,5},{7,8},{8,7},{9,10},{10,9},{11,... | collective-permute-start | bytes 589832 | tf_op jit(solution)/shard_map/ppermute | solution.py:539
  23.5 6.3 %collective-permute-start.5 = (f32[6,32,256]{2,1,0:T(8,128)S(1)}, f32[6,32,256]{2,1,0:T(8,128)S(1)}, u32[]{:S(2)}, u32[]{:S(2)}) collective-permute-start(f32[6,32,256]{2,1,0:T(8,128)S(1)} %get-tuple-element.54), channel_id=1, source_target_pairs={{31,15},{15,31},{16,0},{0,16},{30,29},{29,30},{28,27},{27,28},{26,... | collective-permute-start | bytes 589832 | tf_op jit(solution)/shard_map/ppermute | solution.py:549
  25.9 3.8 %collective-permute-start.7 = (f32[6,32,256]{2,1,0:T(8,128)S(1)}, f32[6,32,256]{2,1,0:T(8,128)S(1)}, u32[]{:S(2)}, u32[]{:S(2)}) collective-permute-start(f32[6,32,256]{2,1,0:T(8,128)S(1)} %get-tuple-element.59), channel_id=1, source_target_pairs={{0,1},{1,0},{2,3},{3,2},{4,5},{5,4},{6,7},{7,6},{8,9},{9,8},{10,11... | collective-permute-start | bytes 589832 | tf_op jit(solution)/shard_map/ppermute | solution.py:536
  28.5 1.3 %collective-permute-start.8 = (f32[40,256]{1,0:T(8,128)S(1)}, f32[40,256]{1,0:T(8,128)S(1)}, u32[]{:S(2)}, u32[]{:S(2)}) collective-permute-start(f32[40,256]{1,0:T(8,128)S(1)} %get-tuple-element.65.moments), channel_id=1, source_target_pairs={{0,1},{1,0},{2,3},{3,2},{4,5},{5,4},{6,7},{7,6},{8,9},{9,8},{10,11... | collective-permute-start | bytes 122888 | tf_op jit(solution)/shard_map/ppermute | solution.py:536
  29.8 7.4 %collective-permute-start.12 = (f32[72,128]{1,0:T(8,128)S(1)}, f32[72,128]{1,0:T(8,128)S(1)}, u32[]{:S(2)}, u32[]{:S(2)}) collective-permute-start(f32[72,128]{1,0:T(8,128)S(1)} %shard_map.142), channel_id=1, source_target_pairs={{0,14},{1,12},{2,15},{3,13},{4,10},{5,8},{6,11},{7,9},{8,6},{9,4},... | collective-permute-start | bytes 110600 | tf_op jit(solution)/shard_map/ppermute | solution.py:638
  35.0 5.2 %collective-permute-start.11 = (f32[72,128]{1,0:T(8,128)S(1)}, f32[72,128]{1,0:T(8,128)S(1)}, u32[]{:S(2)}, u32[]{:S(2)}) collective-permute-start(f32[72,128]{1,0:T(8,128)S(1)} %shard_map.142), channel_id=1, source_target_pairs={{0,10},{1,8},{2,11},{3,9},{4,14},{5,12},{6,15},{7,13},{8,2},{9,0},... | collective-permute-start | bytes 110600 | tf_op jit(solution)/shard_map/ppermute | solution.py:638
  35.9 4.3 %collective-permute-start.10 = (f32[72,128]{1,0:T(8,128)S(1)}, f32[72,128]{1,0:T(8,128)S(1)}, u32[]{:S(2)}, u32[]{:S(2)}) collective-permute-start(f32[72,128]{1,0:T(8,128)S(1)} %shard_map.142), channel_id=1, source_target_pairs={{0,6},{1,4},{2,7},{3,5},{4,2},{5,0},{6,3},{7,1},{8,14},{9,12},{10,... | collective-permute-start | bytes 110600 | tf_op jit(solution)/shard_map/ppermute | solution.py:638
  36.0 4.1 %collective-permute-start.9 = (f32[72,128]{1,0:T(8,128)S(1)}, f32[72,128]{1,0:T(8,128)S(1)}, u32[]{:S(2)}, u32[]{:S(2)}) collective-permute-start(f32[72,128]{1,0:T(8,128)S(1)} %shard_map.142), channel_id=1, source_target_pairs={{0,2},{1,0},{2,3},{3,1},{4,6},{5,4},{6,7},{7,5},{8,10},{9,8},{10,1... | collective-permute-start | bytes 110600 | tf_op jit(solution)/shard_map/ppermute | solution.py:638
  40.2 1.3 %collective-permute-start.13 = (f32[72,128]{1,0:T(8,128)S(1)}, f32[72,128]{1,0:T(8,128)S(1)}, u32[]{:S(2)}, u32[]{:S(2)}) collective-permute-start(f32[72,128]{1,0:T(8,128)S(1)} %add_add_fusion.moments), channel_id=1, source_target_pairs={{0,1},{1,0},{2,3},{3,2},{4,5},{5,4},{6,7},{7,6},{8,9},{9,8},{10,11... | collective-permute-start | bytes 110600 | tf_op jit(solution)/shard_map/ppermute | solution.py:536

commit v11 on v9

--- a/solution.py
+++ b/solution.py
@@ -153,8 +153,7 @@
         block = jnp.transpose(field[k])
         state_ref[at + k] = block
         first, rest = halves(block)
-        second = (block - first.astype(f32) - rest.astype(f32)).astype(bf16)
-        packed = dot(pick, first) + dot(pick, rest) + dot(pick, second)
+        packed = dot(pick, first) + dot(pick, rest)
         near_ref[at + k] = packed[:ghosts]
         far_ref[at + k] = packed[ghosts:]
 

time: 42.8 us -> 42.8 us (level)
  no operation moved by 1% of the time
where the time goes in v11:
time: 42.8 us; the launch traced here: 42.7 us
  starting transfers between devices  18.5 us (43%)
  Pallas kernels  15.2 us (36%)
  waiting for transfers between devices  6.34 us (15%)
  local copies, waits for them, and re-layouts  1.61 us (4%)
  between operations  0.87 us (2%)
    pallas_call x13, Pallas kernels, call(): pl.pallas_call(kernel, out_shape=outs, in_specs=[VMEM] * len(operands), o...  15.2 us
    ppermute x4, starting transfers between devices, local(): term = lax.ppermute(joined, 'mesh', pairs)  7.09 us
    ppermute x3, starting transfers between devices, swap_far(): return lax.ppermute(value, ('runs', 'mesh'), far_pairs)  5.58 us
    ppermute x6, starting transfers between devices, swap_near(): return lax.ppermute(value, 'mesh', near_pairs)  4.69 us
    ppermute x4, waiting for transfers between devices, local(): term = lax.ppermute(joined, 'mesh', pairs)  3.26 us
    ppermute x6, waiting for transfers between devices, swap_near(): return lax.ppermute(value, 'mesh', near_pairs)  2.24 us
    unnamed x26, local copies, waits for them, and re-layouts  1.61 us
    ppermute x1, starting transfers between devices, swap_far_beside(): return lax.ppermute(value, ('runs', 'mesh'), far_pairs[::-1])  1.14 us
  transfers between devices with their start and end apart: 14, of which 4 were waited for; matrix products, arithmetic and copies ran while one was open for 0% of the time, Pallas kernels for 26%

profile of v11, /device:TPU:0, one launch (start us, length us, event | category | flops | bytes accessed | tf_op | source)
XLA Modules:
  0.0 42.7 jit_solution(18321558008250703531)
XLA Ops:
  0.6 0.0 copy-start.1
  0.7 0.1 select_convert_fusion.info
  0.8 0.0 copy-start.6
  0.8 0.7 %copy-done.6 = s32[6,128]{1,0:T(8,128)S(1)} copy-done((s32[6,128]{1,0:T(8,128)S(1)}, s32[6,128]{1,0:T(8,128)}, u32[]{:S(2)}) %copy-start.6) | copy-done | bytes 3096
  1.5 0.0 copy-start
  1.5 0.3 shard_map.131.pick_ref
  1.8 0.0 copy-done.1
  1.8 0.3 shard_map.132
  2.1 0.4 copy-done
  2.5 0.0 copy-start.3
  2.5 0.0 copy-start.4
  2.5 0.0 copy-start.5
  2.5 0.3 shard_map.133
  2.8 0.0 copy-start.7
  2.9 3.0 %collective-permute-start = (f32[6,32,256]{2,1,0:T(8,128)S(1)}, f32[6,32,256]{2,1,0:T(8,128)S(1)}, u32[]{:S(2)}, u32[]{:S(2)}) collective-permute-start(f32[6,32,256]{2,1,0:T(8,128)S(1)} %get-tuple-element.40), channel_id=1, source_target_pairs={{1,2},{2,1},{3,4},{4,3},{5,6},{6,5},{7,8},{8,7},{9,10},{10,9},{11,... | collective-permute-start | bytes 589832 | tf_op jit(solution)/shard_map/ppermute | solution.py:543
  5.9 0.0 copy-start.8
  5.9 0.1 collective-permute-start.1
  6.0 0.0 copy-done.3
  6.0 0.0 copy-done.4
  6.0 0.0 copy-done.5
  6.0 0.0 copy-done.7
  6.0 0.5 %copy-done.8 = s32[2,32]{1,0:T(2,128)S(1)} copy-done((s32[2,32]{1,0:T(2,128)S(1)}, s32[2,32]{1,0:T(2,128)}, u32[]{:S(2)}) %copy-start.8) | copy-done | bytes 280
  6.5 0.0 copy-done.9
  6.5 0.0 copy-start.12
  6.6 1.6 %shard_map.134 = (f32[640,192]{1,0:T(8,128)S(1)}, bf16[64,384]{1,0:T(8,128)(2,1)S(1)}, bf16[2,128,384]{2,1,0:T(8,128)(2,1)S(1)}, bf16[64,192]{1,0:T(8,128)(2,1)S(1)}, bf16[2,128,192]{2,1,0:T(8,128)(2,1)S(1)}) custom-call(f32[8,256]{1,0:T(8,128)S(1)} %select_convert_fusion.info, bf16[64,128]{1,0:T(8,128)(2,1)S(1)} %shard_map.131.pick_ref, ...), custom_call_target="tpu_custom_call" | custom-call | flops 1000000000 | bytes 943872 | tf_op jit(solution)/shard_map/pallas_call | solution.py:495
  8.1 0.0 copy-done.2
  8.1 0.0 copy-done.10
  8.1 0.0 copy-done.11
  8.1 0.0 copy-done.12
  8.2 2.6 %shard_map.135 = (f32[6,128,256]{2,1,0:T(8,128)S(1)}, f32[6,64,256]{2,1,0:T(8,128)S(1)}) custom-call(f32[6,128,256]{2,1,0:T(8,128)S(1)} %get-tuple-element.42.state, bf16[512,512]{1,0:T(8,128)(2,1)S(1)} %copy-done.11, bf16[1024,256]{1,0:T(8,128)(2,1)S(1)} %copy-done.10, f32[8,512]{1,0:T(8,128)S(1)} %copy-done.12, f32[8,256]{1,0:T(8,128)S(1)} %copy-done.2, ...), custom_call_target="tpu_custom_call" | custom-call | flops 2000000000 | bytes 3284992 | tf_op jit(solution)/shard_map/pallas_call | solution.py:495
  10.7 0.0 collective-permute-done.far
  10.7 0.0 collective-permute-done.1.near
  10.8 1.5 %shard_map.136 = (f32[6,32,256]{2,1,0:T(8,128)S(1)}, f32[6,32,256]{2,1,0:T(8,128)S(1)}, f32[6,64,256]{2,1,0:T(8,128)S(1)}) custom-call(f32[8,256]{1,0:T(8,128)S(1)} %select_convert_fusion.info, f32[6,32,256]{2,1,0:T(8,128)S(1)} %collective-permute-done.far, f32[6,32,256]{2,1,0:T(8,128)S(1)} %collective-permute-done.1.near, ...), custom_call_target="tpu_custom_call" | custom-call | flops 1000000000 | bytes 2777088 | tf_op jit(solution)/shard_map/pallas_call | solution.py:495
  12.2 1.1 %collective-permute-start.2 = (f32[6,32,256]{2,1,0:T(8,128)S(1)}, f32[6,32,256]{2,1,0:T(8,128)S(1)}, u32[]{:S(2)}, u32[]{:S(2)}) collective-permute-start(f32[6,32,256]{2,1,0:T(8,128)S(1)} %get-tuple-element.48), channel_id=1, source_target_pairs={{1,2},{2,1},{3,4},{4,3},{5,6},{6,5},{7,8},{8,7},{9,10},{10,9},{11,... | collective-permute-start | bytes 589832 | tf_op jit(solution)/shard_map/ppermute | solution.py:543
  13.3 1.4 %collective-permute-start.3 = (f32[6,32,256]{2,1,0:T(8,128)S(1)}, f32[6,32,256]{2,1,0:T(8,128)S(1)}, u32[]{:S(2)}, u32[]{:S(2)}) collective-permute-start(f32[6,32,256]{2,1,0:T(8,128)S(1)} %get-tuple-element.49), channel_id=1, source_target_pairs={{0,1},{1,0},{2,3},{3,2},{4,5},{5,4},{6,7},{7,6},{8,9},{9,8},{10,11... | collective-permute-start | bytes 589832 | tf_op jit(solution)/shard_map/ppermute | solution.py:540
  14.7 3.6 %shard_map.137 = (bf16[2,384,384]{2,1,0:T(8,128)(2,1)S(1)}, bf16[2,384,192]{2,1,0:T(8,128)(2,1)S(1)}, bf16[2,128,384]{2,1,0:T(8,128)(2,1)S(1)}, f32[6,128,256]{2...) custom-call(f32[8,256]{1,0:T(8,128)S(1)} %select_convert_fusion.info, ...), custom_call_target="tpu_custom_call" | custom-call | flops 2000000000 | bytes 5939200 | tf_op jit(solution)/shard_map/pallas_call | solution.py:495
  18.4 0.0 collective-permute-done.2.far
  18.4 0.0 collective-permute-done.3.near
  18.4 0.3 shard_map.138
  18.7 1.1 %collective-permute-start.4 = (f32[6,32,256]{2,1,0:T(8,128)S(1)}, f32[6,32,256]{2,1,0:T(8,128)S(1)}, u32[]{:S(2)}, u32[]{:S(2)}) collective-permute-start(f32[6,32,256]{2,1,0:T(8,128)S(1)} %get-tuple-element.55), channel_id=1, source_target_pairs={{0,1},{1,0},{2,3},{3,2},{4,5},{5,4},{6,7},{7,6},{8,9},{9,8},{10,11... | collective-permute-start | bytes 589832 | tf_op jit(solution)/shard_map/ppermute | solution.py:540
  19.8 1.5 %collective-permute-start.6 = (f32[6,32,256]{2,1,0:T(8,128)S(1)}, f32[6,32,256]{2,1,0:T(8,128)S(1)}, u32[]{:S(2)}, u32[]{:S(2)}) collective-permute-start(f32[6,32,256]{2,1,0:T(8,128)S(1)} %get-tuple-element.62), channel_id=1, source_target_pairs={{1,2},{2,1},{3,4},{4,3},{5,6},{6,5},{7,8},{8,7},{9,10},{10,9},{11,... | collective-permute-start | bytes 589832 | tf_op jit(solution)/shard_map/ppermute | solution.py:543
  21.3 0.0 collective-permute-done.4.near_next
  21.3 2.2 %shard_map.139 = (f32[6,128,256]{2,1,0:T(8,128)S(1)}, f32[6,32,256]{2,1,0:T(8,128)S(1)}, f32[6,32,256]{2,1,0:T(8,128)S(1)}, f32[6,128,256]{2,1,0:T(8,128)S(1)}, ...) custom-call(f32[8,256]{1,0:T(8,128)S(1)} %select_convert_fusion.info, f32[6,32,256]{2,1,0:T(8,128)S(1)} %collective-permute-done.2.far, ...), custom_call_target="tpu_custom_call" | custom-call | flops 1000000000 | bytes 5439488 | tf_op jit(solution)/shard_map/pallas_call | solution.py:495
  23.5 1.1 %collective-permute-start.5 = (f32[6,32,256]{2,1,0:T(8,128)S(1)}, f32[6,32,256]{2,1,0:T(8,128)S(1)}, u32[]{:S(2)}, u32[]{:S(2)}) collective-permute-start(f32[6,32,256]{2,1,0:T(8,128)S(1)} %get-tuple-element.60), channel_id=1, source_target_pairs={{31,15},{15,31},{16,0},{0,16},{30,29},{29,30},{28,27},{27,28},{26,... | collective-permute-start | bytes 589832 | tf_op jit(solution)/shard_map/ppermute | solution.py:553
  24.6 0.8 %collective-permute-done.6.far = f32[6,32,256]{2,1,0:T(8,128)S(1)} collective-permute-done((f32[6,32,256]{2,1,0:T(8,128)S(1)}, f32[6,32,256]{2,1,0:T(8,128)S(1)}, u32[]{:S(2)}, u32[]{:S(2)}) %collective-permute-start.6) | collective-permute-done | bytes 196640 | tf_op jit(solution)/shard_map/ppermute | solution.py:543
  25.5 0.5 %shard_map.140 = (f32[6,128,256]{2,1,0:T(8,128)S(1)}, f32[6,32,256]{2,1,0:T(8,128)S(1)}) custom-call(f32[8,256]{1,0:T(8,128)S(1)} %select_convert_fusion.info, f32[6,32,256]{2,1,0:T(8,128)S(1)} %collective-permute-done.6.far, f32[6,128,256]{2,1,0:T(8,128)S(1)} %get-tuple-element.63.image, f32[6,32,256]{2,1,0:T(8,128)S(1)} %get-tuple-element.64.packed_near, ...), custom_call_target="tpu_custom_call" | custom-call | flops 500000000 | bytes 2473984 | tf_op jit(solution)/shard_map/pallas_call | solution.py:495
  25.9 1.7 %collective-permute-start.7 = (f32[6,32,256]{2,1,0:T(8,128)S(1)}, f32[6,32,256]{2,1,0:T(8,128)S(1)}, u32[]{:S(2)}, u32[]{:S(2)}) collective-permute-start(f32[6,32,256]{2,1,0:T(8,128)S(1)} %get-tuple-element.65), channel_id=1, source_target_pairs={{0,1},{1,0},{2,3},{3,2},{4,5},{5,4},{6,7},{7,6},{8,9},{9,8},{10,11... | collective-permute-start | bytes 589832 | tf_op jit(solution)/shard_map/ppermute | solution.py:540
  27.6 0.8 %shard_map.141 = (f32[6,64,256]{2,1,0:T(8,128)S(1)}, f32[40,256]{1,0:T(8,128)S(1)}) custom-call(f32[6,128,256]{2,1,0:T(8,128)S(1)} %get-tuple-element.66.vector.third, f32[6,128,256]{2,1,0:T(8,128)S(1)} %get-tuple-element.67.before.second, bf16[2,384,384]{2,1,0:T(8,128)(2,1)S(1)} %get-tuple-element.58.own, ...), custom_call_target="tpu_custom_call" | custom-call | flops 1000000000 | bytes 2826240 | tf_op jit(solution)/shard_map/pallas_call | solution.py:495
  28.5 0.1 collective-permute-start.8
  28.5 1.2 %collective-permute-done.8.rest_0_ = f32[40,256]{1,0:T(8,128)S(1)} collective-permute-done((f32[40,256]{1,0:T(8,128)S(1)}, f32[40,256]{1,0:T(8,128)S(1)}, u32[]{:S(2)}, u32[]{:S(2)}) %collective-permute-start.8) | collective-permute-done | bytes 40992 | tf_op jit(solution)/shard_map/ppermute | solution.py:540
  29.8 0.0 collective-permute-done.5.far
  29.8 0.0 collective-permute-done.7.near
  29.8 0.1 shard_map.142
  29.8 4.8 %collective-permute-start.12 = (f32[72,128]{1,0:T(8,128)S(1)}, f32[72,128]{1,0:T(8,128)S(1)}, u32[]{:S(2)}, u32[]{:S(2)}) collective-permute-start(f32[72,128]{1,0:T(8,128)S(1)} %shard_map.142), channel_id=1, source_target_pairs={{0,14},{1,12},{2,15},{3,13},{4,10},{5,8},{6,11},{7,9},{8,6},{9,4},... | collective-permute-start | bytes 110600 | tf_op jit(solution)/shard_map/ppermute | solution.py:645
  34.7 1.2 %collective-permute-start.11 = (f32[72,128]{1,0:T(8,128)S(1)}, f32[72,128]{1,0:T(8,128)S(1)}, u32[]{:S(2)}, u32[]{:S(2)}) collective-permute-start(f32[72,128]{1,0:T(8,128)S(1)} %shard_map.142), channel_id=1, source_target_pairs={{0,10},{1,8},{2,11},{3,9},{4,14},{5,12},{6,15},{7,13},{8,2},{9,0},... | collective-permute-start | bytes 110600 | tf_op jit(solution)/shard_map/ppermute | solution.py:645
  35.9 0.1 collective-permute-start.10
  36.1 0.9 %collective-permute-start.9 = (f32[72,128]{1,0:T(8,128)S(1)}, f32[72,128]{1,0:T(8,128)S(1)}, u32[]{:S(2)}, u32[]{:S(2)}) collective-permute-start(f32[72,128]{1,0:T(8,128)S(1)} %shard_map.142), channel_id=1, source_target_pairs={{0,2},{1,0},{2,3},{3,1},{4,6},{5,4},{6,7},{7,5},{8,10},{9,8},{10,1... | collective-permute-start | bytes 110600 | tf_op jit(solution)/shard_map/ppermute | solution.py:645
  36.9 0.0 collective-permute-done.12
  36.9 3.2 %collective-permute-done.11 = f32[72,128]{1,0:T(8,128)S(1)} collective-permute-done((f32[72,128]{1,0:T(8,128)S(1)}, f32[72,128]{1,0:T(8,128)S(1)}, u32[]{:S(2)}, u32[]{:S(2)}) %collective-permute-start.11) | collective-permute-done | bytes 36896 | tf_op jit(solution)/shard_map/ppermute | solution.py:645
  40.2 0.0 collective-permute-done.10
  40.2 0.0 collective-permute-done.9
  40.2 0.3 collective-permute-start.13
  40.5 1.0 %collective-permute-done.13.other = f32[72,128]{1,0:T(8,128)S(1)} collective-permute-done((f32[72,128]{1,0:T(8,128)S(1)}, f32[72,128]{1,0:T(8,128)S(1)}, u32[]{:S(2)}, u32[]{:S(2)}) %collective-permute-start.13) | collective-permute-done | bytes 36896 | tf_op jit(solution)/shard_map/ppermute | solution.py:540
  41.5 1.2 %shard_map.143 = (f32[3,256,128]{2,1,0:T(8,128)}, f32[3,256,128]{2,1,0:T(8,128)}) custom-call(f32[72,128]{1,0:T(8,128)S(1)} %add_add_fusion.moments, f32[72,128]{1,0:T(8,128)S(1)} %collective-permute-done.13.other, f32[3,256,128]{2,1,0:T(8,128)S(1)} %copy-done.1, f32[3,256,128]{2,1,0:T(8,128)S(1)} %copy-done, ...), custom_call_target="tpu_custom_call" | custom-call | flops 10000000 | bytes 4005888 | tf_op jit(solution)/shard_map/pallas_call | solution.py:495
  (7 shorter events, 0.0 us)
Async XLA Ops:
  0.6 1.2 %copy-start.1 = (f32[3,256,128]{2,1,0:T(8,128)S(1)}, f32[3,256,128]{2,1,0:T(8,128)}, u32[]{:S(2)}) copy-start(f32[3,256,128]{2,1,0:T(8,128)} %velocity.3) | copy-start | bytes 1179652
  0.8 0.7 %copy-start.6 = (s32[6,128]{1,0:T(8,128)S(1)}, s32[6,128]{1,0:T(8,128)}, u32[]{:S(2)}) copy-start(s32[6,128]{1,0:T(8,128)} %conn_ref.3) | copy-start | bytes 9220
  1.5 1.0 %copy-start = (f32[3,256,128]{2,1,0:T(8,128)S(1)}, f32[3,256,128]{2,1,0:T(8,128)}, u32[]{:S(2)}) copy-start(f32[3,256,128]{2,1,0:T(8,128)} %magnetic.3) | copy-start | bytes 1179652
  2.5 3.5 %copy-start.3 = (f32[6,6,128]{2,1,0:T(8,128)S(1)}, f32[6,6,128]{2,1,0:T(8,128)}, u32[]{:S(2)}) copy-start(f32[6,6,128]{2,1,0:T(8,128)} %mass_ref.1) | copy-start | bytes 55300
  2.5 3.5 %copy-start.4 = (f32[6,6,128]{2,1,0:T(8,128)S(1)}, f32[6,6,128]{2,1,0:T(8,128)}, u32[]{:S(2)}) copy-start(f32[6,6,128]{2,1,0:T(8,128)} %stiff_ref.1) | copy-start | bytes 55300
  2.5 3.5 %copy-start.5 = (f32[6,6,128]{2,1,0:T(8,128)S(1)}, f32[6,6,128]{2,1,0:T(8,128)}, u32[]{:S(2)}) copy-start(f32[6,6,128]{2,1,0:T(8,128)} %twist_ref.1) | copy-start | bytes 55300
  2.8 3.2 %copy-start.7 = (s32[6,128]{1,0:T(8,128)S(1)}, s32[6,128]{1,0:T(8,128)}, u32[]{:S(2)}) copy-start(s32[6,128]{1,0:T(8,128)} %conn_ref.3) | copy-start | bytes 9220
  2.9 7.9 %collective-permute-start = (f32[6,32,256]{2,1,0:T(8,128)S(1)}, f32[6,32,256]{2,1,0:T(8,128)S(1)}, u32[]{:S(2)}, u32[]{:S(2)}) collective-permute-start(f32[6,32,256]{2,1,0:T(8,128)S(1)} %get-tuple-element.40), channel_id=1, source_target_pairs={{1,2},{2,1},{3,4},{4,3},{5,6},{6,5},{7,8},{8,7},{9,10},{10,9},{11,... | collective-permute-start | bytes 589832 | tf_op jit(solution)/shard_map/ppermute | solution.py:543
  5.9 0.7 %copy-start.8 = (s32[2,32]{1,0:T(2,128)S(1)}, s32[2,32]{1,0:T(2,128)}, u32[]{:S(2)}) copy-start(s32[2,32]{1,0:T(2,128)} %lists_ref.1) | copy-start | bytes 772
  5.9 0.7 %copy-start.9 = (f32[128]{0:T(128)S(1)}, f32[128]{0:T(128)}, u32[]{:S(2)}) copy-start(f32[128]{0:T(128)} %param.17) | copy-start | bytes 1540
  5.9 4.9 %collective-permute-start.1 = (f32[6,32,256]{2,1,0:T(8,128)S(1)}, f32[6,32,256]{2,1,0:T(8,128)S(1)}, u32[]{:S(2)}, u32[]{:S(2)}) collective-permute-start(f32[6,32,256]{2,1,0:T(8,128)S(1)} %get-tuple-element.41), channel_id=1, source_target_pairs={{0,1},{1,0},{2,3},{3,2},{4,5},{5,4},{6,7},{7,6},{8,9},{9,8},{10,11... | collective-permute-start | bytes 589832 | tf_op jit(solution)/shard_map/ppermute | solution.py:540
  6.5 1.6 %copy-start.2 = (f32[8,256]{1,0:T(8,128)S(1)}, f32[8,256]{1,0:T(8,128)}, u32[]{:S(2)}) copy-start(f32[8,256]{1,0:T(8,128)} %constant.35.clone.squares_ref) | copy-start | bytes 24580
  6.5 1.6 %copy-start.10 = (bf16[1024,256]{1,0:T(8,128)(2,1)S(1)}, bf16[1024,256]{1,0:T(8,128)(2,1)}, u32[]{:S(2)}) copy-start(bf16[1024,256]{1,0:T(8,128)(2,1)} %constant.33.clone.coefs_ref) | copy-start | bytes 1572868
  6.5 1.6 %copy-start.11 = (bf16[512,512]{1,0:T(8,128)(2,1)S(1)}, bf16[512,512]{1,0:T(8,128)(2,1)}, u32[]{:S(2)}) copy-start(bf16[512,512]{1,0:T(8,128)(2,1)} %constant.32.clone.planes_ref) | copy-start | bytes 1572868
  6.5 1.6 %copy-start.12 = (f32[8,512]{1,0:T(8,128)S(1)}, f32[8,512]{1,0:T(8,128)}, u32[]{:S(2)}) copy-start(f32[8,512]{1,0:T(8,128)} %constant.34.clone.rotation_ref) | copy-start | bytes 49156
  12.2 6.2 %collective-permute-start.2 = (f32[6,32,256]{2,1,0:T(8,128)S(1)}, f32[6,32,256]{2,1,0:T(8,128)S(1)}, u32[]{:S(2)}, u32[]{:S(2)}) collective-permute-start(f32[6,32,256]{2,1,0:T(8,128)S(1)} %get-tuple-element.48), channel_id=1, source_target_pairs={{1,2},{2,1},{3,4},{4,3},{5,6},{6,5},{7,8},{8,7},{9,10},{10,9},{11,... | collective-permute-start | bytes 589832 | tf_op jit(solution)/shard_map/ppermute | solution.py:543
  13.3 5.1 %collective-permute-start.3 = (f32[6,32,256]{2,1,0:T(8,128)S(1)}, f32[6,32,256]{2,1,0:T(8,128)S(1)}, u32[]{:S(2)}, u32[]{:S(2)}) collective-permute-start(f32[6,32,256]{2,1,0:T(8,128)S(1)} %get-tuple-element.49), channel_id=1, source_target_pairs={{0,1},{1,0},{2,3},{3,2},{4,5},{5,4},{6,7},{7,6},{8,9},{9,8},{10,11... | collective-permute-start | bytes 589832 | tf_op jit(solution)/shard_map/ppermute | solution.py:540
  18.7 2.6 %collective-permute-start.4 = (f32[6,32,256]{2,1,0:T(8,128)S(1)}, f32[6,32,256]{2,1,0:T(8,128)S(1)}, u32[]{:S(2)}, u32[]{:S(2)}) collective-permute-start(f32[6,32,256]{2,1,0:T(8,128)S(1)} %get-tuple-element.55), channel_id=1, source_target_pairs={{0,1},{1,0},{2,3},{3,2},{4,5},{5,4},{6,7},{7,6},{8,9},{9,8},{10,11... | collective-permute-start | bytes 589832 | tf_op jit(solution)/shard_map/ppermute | solution.py:540
  19.8 5.7 %collective-permute-start.6 = (f32[6,32,256]{2,1,0:T(8,128)S(1)}, f32[6,32,256]{2,1,0:T(8,128)S(1)}, u32[]{:S(2)}, u32[]{:S(2)}) collective-permute-start(f32[6,32,256]{2,1,0:T(8,128)S(1)} %get-tuple-element.62), channel_id=1, source_target_pairs={{1,2},{2,1},{3,4},{4,3},{5,6},{6,5},{7,8},{8,7},{9,10},{10,9},{11,... | collective-permute-start | bytes 589832 | tf_op jit(solution)/shard_map/ppermute | solution.py:543
  23.5 6.3 %collective-permute-start.5 = (f32[6,32,256]{2,1,0:T(8,128)S(1)}, f32[6,32,256]{2,1,0:T(8,128)S(1)}, u32[]{:S(2)}, u32[]{:S(2)}) collective-permute-start(f32[6,32,256]{2,1,0:T(8,128)S(1)} %get-tuple-element.60), channel_id=1, source_target_pairs={{31,15},{15,31},{16,0},{0,16},{30,29},{29,30},{28,27},{27,28},{26,... | collective-permute-start | bytes 589832 | tf_op jit(solution)/shard_map/ppermute | solution.py:553
  25.9 3.8 %collective-permute-start.7 = (f32[6,32,256]{2,1,0:T(8,128)S(1)}, f32[6,32,256]{2,1,0:T(8,128)S(1)}, u32[]{:S(2)}, u32[]{:S(2)}) collective-permute-start(f32[6,32,256]{2,1,0:T(8,128)S(1)} %get-tuple-element.65), channel_id=1, source_target_pairs={{0,1},{1,0},{2,3},{3,2},{4,5},{5,4},{6,7},{7,6},{8,9},{9,8},{10,11... | collective-permute-start | bytes 589832 | tf_op jit(solution)/shard_map/ppermute | solution.py:540
  28.5 1.3 %collective-permute-start.8 = (f32[40,256]{1,0:T(8,128)S(1)}, f32[40,256]{1,0:T(8,128)S(1)}, u32[]{:S(2)}, u32[]{:S(2)}) collective-permute-start(f32[40,256]{1,0:T(8,128)S(1)} %get-tuple-element.71.moments), channel_id=1, source_target_pairs={{0,1},{1,0},{2,3},{3,2},{4,5},{5,4},{6,7},{7,6},{8,9},{9,8},{10,11... | collective-permute-start | bytes 122888 | tf_op jit(solution)/shard_map/ppermute | solution.py:540
  29.8 7.1 %collective-permute-start.12 = (f32[72,128]{1,0:T(8,128)S(1)}, f32[72,128]{1,0:T(8,128)S(1)}, u32[]{:S(2)}, u32[]{:S(2)}) collective-permute-start(f32[72,128]{1,0:T(8,128)S(1)} %shard_map.142), channel_id=1, source_target_pairs={{0,14},{1,12},{2,15},{3,13},{4,10},{5,8},{6,11},{7,9},{8,6},{9,4},... | collective-permute-start | bytes 110600 | tf_op jit(solution)/shard_map/ppermute | solution.py:645
  34.7 5.5 %collective-permute-start.11 = (f32[72,128]{1,0:T(8,128)S(1)}, f32[72,128]{1,0:T(8,128)S(1)}, u32[]{:S(2)}, u32[]{:S(2)}) collective-permute-start(f32[72,128]{1,0:T(8,128)S(1)} %shard_map.142), channel_id=1, source_target_pairs={{0,10},{1,8},{2,11},{3,9},{4,14},{5,12},{6,15},{7,13},{8,2},{9,0},... | collective-permute-start | bytes 110600 | tf_op jit(solution)/shard_map/ppermute | solution.py:645
  35.9 4.3 %collective-permute-start.10 = (f32[72,128]{1,0:T(8,128)S(1)}, f32[72,128]{1,0:T(8,128)S(1)}, u32[]{:S(2)}, u32[]{:S(2)}) collective-permute-start(f32[72,128]{1,0:T(8,128)S(1)} %shard_map.142), channel_id=1, source_target_pairs={{0,6},{1,4},{2,7},{3,5},{4,2},{5,0},{6,3},{7,1},{8,14},{9,12},{10,... | collective-permute-start | bytes 110600 | tf_op jit(solution)/shard_map/ppermute | solution.py:645
  36.1 4.1 %collective-permute-start.9 = (f32[72,128]{1,0:T(8,128)S(1)}, f32[72,128]{1,0:T(8,128)S(1)}, u32[]{:S(2)}, u32[]{:S(2)}) collective-permute-start(f32[72,128]{1,0:T(8,128)S(1)} %shard_map.142), channel_id=1, source_target_pairs={{0,2},{1,0},{2,3},{3,1},{4,6},{5,4},{6,7},{7,5},{8,10},{9,8},{10,1... | collective-permute-start | bytes 110600 | tf_op jit(solution)/shard_map/ppermute | solution.py:645
  40.2 1.3 %collective-permute-start.13 = (f32[72,128]{1,0:T(8,128)S(1)}, f32[72,128]{1,0:T(8,128)S(1)}, u32[]{:S(2)}, u32[]{:S(2)}) collective-permute-start(f32[72,128]{1,0:T(8,128)S(1)} %add_add_fusion.moments), channel_id=1, source_target_pairs={{0,1},{1,0},{2,3},{3,2},{4,5},{5,4},{6,7},{7,6},{8,9},{9,8},{10,11... | collective-permute-start | bytes 110600 | tf_op jit(solution)/shard_map/ppermute | solution.py:540
